TPU v7x, 32 devices: a whole 2x2x4 slice. The times are simulated.
32 devices in a mesh: ctx: 8 (over z, y), fsdp: 4 (over x, core).
Axes of the slice: x: 2, y: 2, z: 4, core: 2. Of those that a mesh axis runs over, the one named last changes fastest.
Arguments:
- tokens: bfloat16 [4, 2048, 768], P('fsdp', 'ctx'), may hold values from -6 to 6
- cotangent: bfloat16 [4, 2048, 768], P('fsdp', 'ctx'), may hold values from -6 to 6
- lengths: int32 [4, 4], P('fsdp'), may hold values from 1 to 1840, as said below
- piece_order: int32 [4, 16], P('fsdp'), may hold values from 0 to 15, each once within a row
- routes: int32 [4, 2048, 2], P('fsdp', 'ctx'), may hold values from 0 to 15, all different within a row; in each aligned block of 256 rows (0 to 255, 256 to 511, ..., all dimensions but the last counted through in order) at most 64 rows name the same one
- attn_in: bfloat16 [2, 768, 2304], P(None, 'fsdp'), may hold values from -0.21875 to 0.21875
- attn_out: bfloat16 [2, 768, 768], P(None, 'fsdp'), may hold values from -3.5 to 3.5
- norm_gain: bfloat16 [2, 2, 768], P(None, None, 'fsdp'), may hold values from 0.5 to 1.5
- mlp_in: bfloat16 [2, 768, 4096], P(None, 'fsdp'), may hold values from -0.21875 to 0.21875
- mlp_out: bfloat16 [2, 2048, 768], P(None, 'fsdp'), may hold values from -0.125 to 0.125
- router: bfloat16 [768, 16], P('fsdp'), may hold values from -0.14941406 to 0.14941406
- expert_in: bfloat16 [2, 32768, 768], P(None, 'ctx', 'fsdp'), may hold values from -0.21875 to 0.21875
- expert_out: bfloat16 [32768, 768], P('ctx', 'fsdp'), may hold values from -0.5 to 0.5
Outputs:
- output: float32 [4, 2048, 768], P('fsdp', 'ctx')
- tokens_grad: float32 [4, 2048, 768], P('fsdp', 'ctx')
- attn_in_grad: float32 [2, 768, 2304], P(None, 'fsdp')
- attn_out_grad: float32 [2, 768, 768], P(None, 'fsdp')
- norm_gain_grad: float32 [2, 2, 768], P(None, None, 'fsdp')
- mlp_in_grad: float32 [2, 768, 4096], P(None, 'fsdp')
- mlp_out_grad: float32 [2, 2048, 768], P(None, 'fsdp')
- router_grad: float32 [768, 16], P('fsdp')
- expert_in_grad: float32 [2, 32768, 768], P(None, 'ctx', 'fsdp')
- expert_out_grad: float32 [32768, 768], P('ctx', 'fsdp')
Inputs may be any that keep to these rules, and one draw needn't show every extreme that they name: `lengths`: each row sums to 1843; its largest length is 1840 and its smallest 1. `piece_order`: each row names every piece once. `routes`: a token's two experts differ; among the 256 slots of one device no expert is named more than 64 times, and that bound is reached.
All inputs are finite; a program needn't handle non-finite values.
Results may differ from a plain program's by a relative error of at most 0.028.
Values may be sent and summed in bfloat16 or wider, within the bound.
No kernel may reach another device: no remote copies, remote signals or barrier semaphores. Data moves between devices by JAX's collectives and lax.ppermute only.
A program may use at most 320 MiB of HBM per device.

v0:
```python
import math

import jax
import jax.numpy as jnp
from jax import lax
from jax.sharding import PartitionSpec as P

HEADS = 12
HD = 64
FF = 2048
TOP = 2


HIGHEST = lax.Precision.HIGHEST
EPSILON = 1e-06
NEGATIVE = -1e30


def layout(lengths_row, order_row, piece_len):
    all_slots = order_row.shape[0] * piece_len
    position = (
        order_row[:, None] * piece_len + jnp.arange(piece_len, dtype=jnp.int32)[None, :]
    ).reshape(all_slots)
    seq_ends = jnp.cumsum(lengths_row, dtype=jnp.int32)
    segment = jnp.sum(
        (position[:, None] >= seq_ends[None, :]).astype(jnp.int32), axis=1, dtype=jnp.int32
    )
    seq_index = jnp.arange(lengths_row.shape[0], dtype=jnp.int32)
    seq_start = jnp.sum(
        jnp.where(segment[:, None] > seq_index[None, :], lengths_row[None, :], 0),
        axis=1,
        dtype=jnp.int32,
    )
    return (position, segment, position - seq_start)


def visible(query_pos, query_seg, key_pos, key_seg, seq_count):
    same_seq = (query_seg[:, None] == key_seg[None, :]) & (query_seg[:, None] < seq_count)
    causal = key_pos[None, :] <= query_pos[:, None]
    return same_seq & causal | (key_pos[None, :] == query_pos[:, None])


def angles(offset, head_dim):
    freq_table = jnp.exp(
        jnp.arange(head_dim // 2, dtype=jnp.float32) * (-2.0 * math.log(10000.0) / head_dim)
    )
    theta = offset.astype(jnp.float32)[..., None] * freq_table
    return (jnp.cos(theta), jnp.sin(theta))


def rotate(values, cosine, sine_table):
    half_dim = values.shape[-1] // 2
    lead_half = values[..., :half_dim]
    tail_half = values[..., half_dim:]
    return jnp.concatenate(
        [lead_half * cosine - tail_half * sine_table, tail_half * cosine + lead_half * sine_table],
        axis=-1,
    )


def unrotate(grads, cosine, sine_table):
    half_dim = grads.shape[-1] // 2
    lead_half = grads[..., :half_dim]
    tail_half = grads[..., half_dim:]
    return jnp.concatenate(
        [lead_half * cosine + tail_half * sine_table, tail_half * cosine - lead_half * sine_table],
        axis=-1,
    )


def rounded(values):
    return lax.optimization_barrier(values.astype(jnp.bfloat16)).astype(jnp.float32)


def rms_apply(resid, gain_row):
    inv_rms = lax.rsqrt(jnp.mean(resid * resid, axis=-1, keepdims=True) + EPSILON)
    return (resid * inv_rms * gain_row, inv_rms)


def rms_back(resid, inv_rms, gain_row, grad_normed):
    weighted = grad_normed * gain_row
    grad_resid = inv_rms * weighted - resid * inv_rms**3 * jnp.mean(
        weighted * resid, axis=-1, keepdims=True
    )
    return (grad_resid, jnp.sum(grad_normed * resid * inv_rms, axis=0))


def feed_forward(normed, w_in, w_out):
    mixed_proj = jnp.dot(normed, w_in, preferred_element_type=jnp.float32)
    hidden_width = w_out.shape[0]
    hidden = (jax.nn.silu(mixed_proj[:, :hidden_width]) * mixed_proj[:, hidden_width:]).astype(
        jnp.bfloat16
    )
    return (jnp.dot(hidden, w_out, preferred_element_type=jnp.float32), mixed_proj, hidden)


def feed_back(normed, mixed_proj, hidden, grad_result, w_in, w_out):
    hidden_width = w_out.shape[0]
    grad_wout = jnp.einsum("tf,td->fd", hidden, grad_result, preferred_element_type=jnp.float32)
    grad_hidden = rounded(
        jnp.einsum("td,fd->tf", grad_result, w_out, preferred_element_type=jnp.float32)
    )
    gate_pre = mixed_proj[:, :hidden_width]
    up_pre = mixed_proj[:, hidden_width:]
    sigmoid_gate = jax.nn.sigmoid(gate_pre)
    grad_gate = grad_hidden * up_pre * sigmoid_gate * (1.0 + gate_pre * (1.0 - sigmoid_gate))
    grad_up = grad_hidden * gate_pre * sigmoid_gate
    grad_mixed = jnp.concatenate([grad_gate, grad_up], axis=1).astype(jnp.bfloat16)
    grad_win = jnp.einsum("td,tf->df", normed, grad_mixed, preferred_element_type=jnp.float32)
    grad_normed = jnp.einsum("tf,df->td", grad_mixed, w_in, preferred_element_type=jnp.float32)
    return (grad_normed, grad_win, grad_wout)


def attend_keys(queries, all_keys, all_values, geometry):
    local_pos, local_seg, cosine, sine_table, all_pos, all_seg, seq_count = geometry
    tok_rows = queries.shape[0]
    all_slots = all_keys.shape[0]
    key_span = min(512, all_slots)
    query_heads = queries.reshape(tok_rows, HEADS, HD)

    def advance(carried, block_idx):
        run_max, run_sum, accumulated = carried
        begin_at = block_idx * key_span
        key_block = lax.dynamic_slice_in_dim(all_keys, begin_at, key_span, 0).reshape(
            key_span, HEADS, HD
        )
        value_block = lax.dynamic_slice_in_dim(all_values, begin_at, key_span, 0).reshape(
            key_span, HEADS, HD
        )
        allowed = visible(
            local_pos,
            local_seg,
            lax.dynamic_slice_in_dim(all_pos, begin_at, key_span, 0),
            lax.dynamic_slice_in_dim(all_seg, begin_at, key_span, 0),
            seq_count,
        )[None]
        scores = jnp.where(
            allowed,
            jnp.einsum("thd,khd->htk", query_heads, key_block, preferred_element_type=jnp.float32),
            NEGATIVE,
        )
        new_max = jnp.maximum(run_max, jnp.max(scores, axis=-1))
        weights = jnp.where(allowed, jnp.exp(scores - new_max[..., None]), 0.0)
        factor = jnp.exp(run_max - new_max)
        run_sum = run_sum * factor + jnp.sum(weights, axis=-1)
        accumulated = accumulated * factor[..., None] + jnp.einsum(
            "htk,khd->htd",
            weights.astype(jnp.bfloat16),
            value_block,
            preferred_element_type=jnp.float32,
        )
        return ((new_max, run_sum, accumulated), None)

    start_state = (
        jnp.full((HEADS, tok_rows), NEGATIVE, jnp.float32),
        jnp.zeros((HEADS, tok_rows), jnp.float32),
        jnp.zeros((HEADS, tok_rows, HD), jnp.float32),
    )
    (run_max, run_sum, accumulated), ignored = lax.scan(
        advance, start_state, jnp.arange(all_slots // key_span)
    )
    context = jnp.transpose(accumulated / run_sum[..., None], (1, 0, 2))
    return (context, run_max + jnp.log(run_sum))


def attend_forward(resid, gain_row, w_in, w_out, geometry):
    local_pos, local_seg, cosine, sine_table, all_pos, all_seg, seq_count = geometry
    tok_rows, model_width = resid.shape
    normed, inv_rms = rms_apply(resid, gain_row)
    normed = normed.astype(jnp.bfloat16)
    mixed_proj = jnp.dot(normed, w_in, preferred_element_type=jnp.float32)
    queries = (
        (
            rotate(mixed_proj[:, :model_width].reshape(tok_rows, HEADS, HD), cosine, sine_table)
            * 0.125
        )
        .astype(jnp.bfloat16)
        .reshape(tok_rows, model_width)
    )
    keys_rot = (
        rotate(
            mixed_proj[:, model_width : 2 * model_width].reshape(tok_rows, HEADS, HD),
            cosine,
            sine_table,
        )
        .astype(jnp.bfloat16)
        .reshape(tok_rows, model_width)
    )
    values_rot = mixed_proj[:, 2 * model_width :].astype(jnp.bfloat16)
    all_keys, all_values = (
        lax.all_gather(keys_rot, "ctx", axis=0, tiled=True),
        lax.all_gather(values_rot, "ctx", axis=0, tiled=True),
    )
    context, log_sum = attend_keys(queries, all_keys, all_values, geometry)
    attended = context.reshape(tok_rows, model_width).astype(jnp.bfloat16)
    branch = jnp.dot(attended, w_out, preferred_element_type=jnp.float32)
    kept = (
        resid,
        inv_rms,
        normed,
        queries,
        keys_rot,
        values_rot,
        all_keys,
        all_values,
        context,
        log_sum,
        attended,
    )
    return (resid + branch, kept)


def attend_backward(grad_resid, kept, gain_row, w_in, w_out, geometry):
    (
        resid,
        inv_rms,
        normed,
        queries,
        keys_rot,
        values_rot,
        all_keys,
        all_values,
        context,
        log_sum,
        attended,
    ) = kept
    local_pos, local_seg, cosine, sine_table, all_pos, all_seg, seq_count = geometry
    tok_rows, model_width = resid.shape
    all_slots = all_keys.shape[0]
    key_span = min(512, all_slots)
    block_ids = jnp.arange(all_slots // key_span)
    grad_branch = grad_resid.astype(jnp.bfloat16)
    grad_wout = jnp.einsum("td,te->de", attended, grad_branch, preferred_element_type=jnp.float32)
    grad_attended = jnp.einsum(
        "te,de->td", grad_branch, w_out, preferred_element_type=jnp.float32
    ).astype(jnp.bfloat16)
    grad_heads = grad_attended.reshape(tok_rows, HEADS, HD)
    row_delta = jnp.transpose(jnp.sum(grad_heads.astype(jnp.float32) * context, axis=-1))
    query_heads = queries.reshape(tok_rows, HEADS, HD)
    zero_query = jnp.zeros((HEADS, tok_rows, HD), jnp.float32)

    def key_block_grads(block_idx):
        begin_at = block_idx * key_span
        key_block = lax.dynamic_slice_in_dim(all_keys, begin_at, key_span, 0).reshape(
            key_span, HEADS, HD
        )
        value_block = lax.dynamic_slice_in_dim(all_values, begin_at, key_span, 0).reshape(
            key_span, HEADS, HD
        )
        allowed = visible(
            local_pos,
            local_seg,
            lax.dynamic_slice_in_dim(all_pos, begin_at, key_span, 0),
            lax.dynamic_slice_in_dim(all_seg, begin_at, key_span, 0),
            seq_count,
        )[None]
        scores = jnp.einsum(
            "thd,khd->htk", query_heads, key_block, preferred_element_type=jnp.float32
        )
        prob_block = jnp.where(allowed, jnp.exp(scores - log_sum[..., None]), 0.0)
        grad_probs = jnp.einsum(
            "thd,khd->htk", grad_heads, value_block, preferred_element_type=jnp.float32
        )
        grad_scores = (prob_block * (grad_probs - row_delta[..., None])).astype(jnp.bfloat16)
        return (key_block, prob_block, grad_scores)

    def retreat(grad_query, block_idx):
        key_block, prob_block, grad_scores = key_block_grads(block_idx)
        grad_query = grad_query + jnp.einsum(
            "htk,khd->htd", grad_scores, key_block, preferred_element_type=jnp.float32
        )
        key_part = jnp.einsum(
            "htk,thd->khd", grad_scores, query_heads, preferred_element_type=jnp.float32
        ).reshape(key_span, model_width)
        value_part = jnp.einsum(
            "htk,thd->khd",
            prob_block.astype(jnp.bfloat16),
            grad_heads,
            preferred_element_type=jnp.float32,
        ).reshape(key_span, model_width)
        return (grad_query, (key_part, value_part))

    grad_query, (key_parts, value_parts) = lax.scan(retreat, zero_query, block_ids)
    grad_keys, grad_values = (
        lax.psum_scatter(
            key_parts.reshape(all_slots, model_width), "ctx", scatter_dimension=0, tiled=True
        ),
        lax.psum_scatter(
            value_parts.reshape(all_slots, model_width), "ctx", scatter_dimension=0, tiled=True
        ),
    )
    grad_query = unrotate(rounded(jnp.transpose(grad_query, (1, 0, 2))) * 0.125, cosine, sine_table)
    grad_key_rot = unrotate(rounded(grad_keys.reshape(tok_rows, HEADS, HD)), cosine, sine_table)
    grad_mixed = jnp.concatenate(
        [
            grad_query.reshape(tok_rows, model_width),
            grad_key_rot.reshape(tok_rows, model_width),
            grad_values,
        ],
        axis=1,
    ).astype(jnp.bfloat16)
    grad_win = jnp.einsum("td,te->de", normed, grad_mixed, preferred_element_type=jnp.float32)
    grad_normed = jnp.einsum("te,de->td", grad_mixed, w_in, preferred_element_type=jnp.float32)
    grad_in, grad_gain = rms_back(resid, inv_rms, gain_row, grad_normed)
    return (grad_resid + grad_in, grad_win, grad_wout, grad_gain)


def per_device(
    tokens,
    cotangent,
    lengths,
    piece_order,
    routes,
    attn_in,
    attn_out,
    norm_gain,
    mlp_in,
    mlp_out,
    router,
    expert_in,
    expert_out,
):
    tok_rows = tokens.shape[1]
    model_width = tokens.shape[2]
    seq_count = lengths.shape[1]
    position, segment, offset = layout(lengths[0], piece_order[0], tok_rows // 2)
    first_slot = lax.axis_index("ctx") * tok_rows
    local_pos = lax.dynamic_slice_in_dim(position, first_slot, tok_rows, 0)
    local_seg = lax.dynamic_slice_in_dim(segment, first_slot, tok_rows, 0)
    cosine, sine_table = angles(lax.dynamic_slice_in_dim(offset, first_slot, tok_rows, 0), HD)
    geometry = (
        local_pos,
        local_seg,
        cosine[:, None, :],
        sine_table[:, None, :],
        position,
        segment,
        seq_count,
    )
    dense_set = (
        lax.all_gather(attn_in[0], "fsdp", axis=0, tiled=True),
        lax.all_gather(attn_out[0], "fsdp", axis=0, tiled=True),
        lax.all_gather(mlp_in[0], "fsdp", axis=0, tiled=True),
        lax.all_gather(mlp_out[0], "fsdp", axis=0, tiled=True),
        lax.all_gather(norm_gain[0], "fsdp", axis=1, tiled=True),
    )
    moe_set = (
        lax.all_gather(attn_in[1], "fsdp", axis=0, tiled=True),
        lax.all_gather(attn_out[1], "fsdp", axis=0, tiled=True),
        lax.all_gather(mlp_in[1], "fsdp", axis=0, tiled=True),
        lax.all_gather(mlp_out[1], "fsdp", axis=0, tiled=True),
        lax.all_gather(norm_gain[1], "fsdp", axis=1, tiled=True),
        lax.all_gather(router, "fsdp", axis=0, tiled=True),
        lax.all_gather(expert_in, "fsdp", axis=2, tiled=True),
        lax.all_gather(expert_out, "fsdp", axis=1, tiled=True),
    )
    resid_in = tokens[0].astype(jnp.float32)
    after_one, kept_one = attend_forward(
        resid_in, dense_set[4][0], dense_set[0], dense_set[1], geometry
    )
    normed_two, inv_two = rms_apply(after_one, dense_set[4][1])
    normed_two = normed_two.astype(jnp.bfloat16)
    dense_branch, mixed_two, hidden_two = feed_forward(normed_two, dense_set[2], dense_set[3])
    middle = after_one + dense_branch
    after_two, kept_two = attend_forward(middle, moe_set[4][0], moe_set[0], moe_set[1], geometry)
    normed_three, inv_three = rms_apply(after_two, moe_set[4][1])
    normed_three = normed_three.astype(jnp.bfloat16)
    shared, mixed_three, hidden_three = feed_forward(normed_three, moe_set[2], moe_set[3])
    num_experts = router.shape[1]
    capacity = 2 * tok_rows * TOP // num_experts
    item_count = tok_rows * TOP
    hid_dev = expert_out.shape[0]
    per_slot = min(FF, hid_dev)
    local_count = hid_dev // per_slot
    split_count = FF // per_slot
    ctx_count = lax.axis_size("ctx")
    gate_rows = moe_set[6][0].reshape(local_count, per_slot, model_width)
    up_rows = moe_set[6][1].reshape(local_count, per_slot, model_width)
    down_rows = moe_set[7].reshape(local_count, per_slot, model_width)

    def spread(per_expert):
        return jnp.broadcast_to(
            per_expert[:, None], (num_experts, split_count, capacity, model_width)
        ).reshape(ctx_count, local_count, capacity, model_width)

    def collect(returned_parts):
        return jnp.sum(
            returned_parts.reshape(num_experts, split_count, capacity, model_width), axis=1
        ).reshape(num_experts * capacity, model_width)

    logits = jnp.dot(normed_three, moe_set[5], preferred_element_type=jnp.float32)
    chosen = routes[0][:, :, None] == jnp.arange(num_experts, dtype=jnp.int32)[None, None, :]
    picked = jnp.sum(jnp.where(chosen, logits[:, None, :], 0.0), axis=-1)
    gate_probs = jax.nn.softmax(picked, axis=-1)
    flat_chosen = chosen.reshape(item_count, num_experts).astype(jnp.int32)
    slot_rank = jnp.sum((jnp.cumsum(flat_chosen, axis=0) - flat_chosen) * flat_chosen, axis=1)
    slot_target = routes[0].reshape(item_count) * capacity + slot_rank
    slot_owner = (
        jnp.full((num_experts * capacity,), item_count, jnp.int32)
        .at[slot_target]
        .set(jnp.arange(item_count, dtype=jnp.int32))
    )
    filled = slot_owner < item_count
    padded = jnp.concatenate([normed_three, jnp.zeros((1, model_width), jnp.bfloat16)], axis=0)
    outgoing = spread(
        padded[jnp.where(filled, slot_owner // TOP, tok_rows)].reshape(
            num_experts, capacity, model_width
        )
    )
    arrived_rows = lax.all_to_all(outgoing, "ctx", split_axis=0, concat_axis=0, tiled=True)
    gate_pre = jnp.einsum(
        "sjkd,jfd->sjkf", arrived_rows, gate_rows, preferred_element_type=jnp.float32
    )
    up_pre = jnp.einsum("sjkd,jfd->sjkf", arrived_rows, up_rows, preferred_element_type=jnp.float32)
    hidden_rows = (jax.nn.silu(gate_pre) * up_pre).astype(jnp.bfloat16)
    partial_rows = jnp.einsum(
        "sjkf,jfd->sjkd", hidden_rows, down_rows, preferred_element_type=jnp.float32
    )
    returned = lax.all_to_all(partial_rows, "ctx", split_axis=0, concat_axis=0, tiled=True)
    expert_rows = collect(returned).astype(jnp.bfloat16)
    back_rows = expert_rows[slot_target].reshape(tok_rows, TOP, model_width).astype(jnp.float32)
    mixture = jnp.sum(gate_probs[..., None] * back_rows, axis=1)
    output = after_two + shared + mixture
    grad_out = cotangent[0].astype(jnp.float32)
    grad_gates = jnp.sum(back_rows * grad_out[:, None, :], axis=-1)
    grad_items = (
        (gate_probs[..., None] * grad_out[:, None, :])
        .astype(jnp.bfloat16)
        .reshape(item_count, model_width)
    )
    grad_padded = jnp.concatenate([grad_items, jnp.zeros((1, model_width), jnp.bfloat16)], axis=0)
    grad_outgoing = spread(
        grad_padded[jnp.where(filled, slot_owner, item_count)].reshape(
            num_experts, capacity, model_width
        )
    )
    grad_arrived = lax.all_to_all(grad_outgoing, "ctx", split_axis=0, concat_axis=0, tiled=True)
    hidden_again = (jax.nn.silu(gate_pre) * up_pre).astype(jnp.bfloat16)
    grad_ewout = jnp.einsum(
        "sjkf,sjkd->jfd", hidden_again, grad_arrived, preferred_element_type=jnp.float32
    ).reshape(hid_dev, model_width)
    grad_hidden = rounded(
        jnp.einsum("sjkd,jfd->sjkf", grad_arrived, down_rows, preferred_element_type=jnp.float32)
    )
    sigmoid_gate = jax.nn.sigmoid(gate_pre)
    grad_gate = (
        grad_hidden * up_pre * sigmoid_gate * (1.0 + gate_pre * (1.0 - sigmoid_gate))
    ).astype(jnp.bfloat16)
    grad_up = (grad_hidden * gate_pre * sigmoid_gate).astype(jnp.bfloat16)
    grad_wgate = jnp.einsum(
        "sjkf,sjkd->jfd", grad_gate, arrived_rows, preferred_element_type=jnp.float32
    ).reshape(hid_dev, model_width)
    grad_wup = jnp.einsum(
        "sjkf,sjkd->jfd", grad_up, arrived_rows, preferred_element_type=jnp.float32
    ).reshape(hid_dev, model_width)
    grad_ewin = jnp.stack([grad_wgate, grad_wup])
    grad_rows = jnp.einsum(
        "sjkf,jfd->sjkd", grad_gate, gate_rows, preferred_element_type=jnp.float32
    ) + jnp.einsum("sjkf,jfd->sjkd", grad_up, up_rows, preferred_element_type=jnp.float32)
    grad_back = lax.all_to_all(grad_rows, "ctx", split_axis=0, concat_axis=0, tiled=True)
    grad_copies = rounded(collect(grad_back))[slot_target].reshape(tok_rows, TOP, model_width)
    grad_picked = gate_probs * (
        grad_gates - jnp.sum(gate_probs * grad_gates, axis=-1, keepdims=True)
    )
    grad_logits = jnp.sum(jnp.where(chosen, grad_picked[..., None], 0.0), axis=1)
    router_full = moe_set[5].astype(jnp.float32)
    grad_router = jnp.einsum(
        "td,te->de", normed_three.astype(jnp.float32), grad_logits, precision=HIGHEST
    )
    grad_shared_in, grad_swin, grad_swout = feed_back(
        normed_three,
        mixed_three,
        hidden_three,
        grad_out.astype(jnp.bfloat16),
        moe_set[2],
        moe_set[3],
    )
    grad_normed = (
        grad_shared_in
        + jnp.sum(grad_copies, axis=1)
        + jnp.einsum("te,de->td", grad_logits, router_full, precision=HIGHEST)
    )
    grad_in, grad_gain_three = rms_back(after_two, inv_three, moe_set[4][1], grad_normed)
    grad_resid, grad_win_two, grad_wout_two, grad_gain_two = attend_backward(
        grad_out + grad_in, kept_two, moe_set[4][0], moe_set[0], moe_set[1], geometry
    )
    moe_grads = (
        lax.psum_scatter(grad_win_two, "fsdp", scatter_dimension=0, tiled=True),
        lax.psum_scatter(grad_wout_two, "fsdp", scatter_dimension=0, tiled=True),
        lax.psum_scatter(grad_swin, "fsdp", scatter_dimension=0, tiled=True),
        lax.psum_scatter(grad_swout, "fsdp", scatter_dimension=0, tiled=True),
        lax.psum_scatter(
            jnp.stack([grad_gain_two, grad_gain_three]), "fsdp", scatter_dimension=1, tiled=True
        ),
        lax.psum_scatter(grad_router, "fsdp", scatter_dimension=0, tiled=True),
        lax.psum_scatter(grad_ewin, "fsdp", scatter_dimension=2, tiled=True),
        lax.psum_scatter(grad_ewout, "fsdp", scatter_dimension=1, tiled=True),
    )
    grad_dense_in, grad_dwin, grad_dwout = feed_back(
        normed_two,
        mixed_two,
        hidden_two,
        grad_resid.astype(jnp.bfloat16),
        dense_set[2],
        dense_set[3],
    )
    grad_in_two, grad_gain_dense = rms_back(after_one, inv_two, dense_set[4][1], grad_dense_in)
    grad_resid, grad_win_one, grad_wout_one, grad_gain_one = attend_backward(
        grad_resid + grad_in_two, kept_one, dense_set[4][0], dense_set[0], dense_set[1], geometry
    )
    dense_grads = (
        lax.psum_scatter(grad_win_one, "fsdp", scatter_dimension=0, tiled=True),
        lax.psum_scatter(grad_wout_one, "fsdp", scatter_dimension=0, tiled=True),
        lax.psum_scatter(grad_dwin, "fsdp", scatter_dimension=0, tiled=True),
        lax.psum_scatter(grad_dwout, "fsdp", scatter_dimension=0, tiled=True),
        lax.psum_scatter(
            jnp.stack([grad_gain_one, grad_gain_dense]), "fsdp", scatter_dimension=1, tiled=True
        ),
    )
    summed = lax.psum(
        (
            dense_grads[0],
            dense_grads[1],
            dense_grads[2],
            dense_grads[3],
            dense_grads[4],
            moe_grads[0],
            moe_grads[1],
            moe_grads[2],
            moe_grads[3],
            moe_grads[4],
            moe_grads[5],
        ),
        "ctx",
    )
    return (
        output[None],
        grad_resid[None],
        jnp.stack([summed[0], summed[5]]),
        jnp.stack([summed[1], summed[6]]),
        jnp.stack([summed[4], summed[9]]),
        jnp.stack([summed[2], summed[7]]),
        jnp.stack([summed[3], summed[8]]),
        summed[10],
        moe_grads[6],
        moe_grads[7],
    )


def solution(mesh):
    placed = (
        P("fsdp", "ctx", None),
        P("fsdp", "ctx", None),
        P("fsdp", None),
        P("fsdp", None),
        P("fsdp", "ctx", None),
        P(None, "fsdp", None),
        P(None, "fsdp", None),
        P(None, None, "fsdp"),
        P(None, "fsdp", None),
        P(None, "fsdp", None),
        P("fsdp", None),
        P(None, "ctx", "fsdp"),
        P("ctx", "fsdp"),
    )
    return jax.shard_map(
        per_device,
        mesh=mesh,
        in_specs=placed,
        out_specs=(
            P("fsdp", "ctx", None),
            P("fsdp", "ctx", None),
            P(None, "fsdp", None),
            P(None, "fsdp", None),
            P(None, None, "fsdp"),
            P(None, "fsdp", None),
            P(None, "fsdp", None),
            P("fsdp", None),
            P(None, "ctx", "fsdp"),
            P("ctx", "fsdp"),
        ),
        check_vma=False,
    )
```

profile of v0, /device:TPU:0, one launch (start us, length us, event | category | flops | bytes accessed | tf_op | source)
XLA Modules:
  0.0 2838.0 jit_solution(18198430570639854257)
XLA Ops:
  10.3 7.9 all-gather
  23.6 20.1 all-gather.38.cloned.1.call-done
  67.4 6.5 all-gather.5
  78.6 31.1 %all-gather.28.cloned.1.call-done = bf16[2048,768]{1,0:T(8,128)(2,1)} async-done(((bf16[256,768]{1,0:T(8,128)(2,1)}), bf16[2048,768]{1,0:T(8,128)(2,1)}) %all-gather.28.cloned.1.call-update) | async-done | bytes 3145744 | tf_op jit(solution)/shard_map/all_gather | solution.py:192
  114.5 59.5 %all-gather.26.cloned.1.call-done = bf16[2048,768]{0,1:T(8,128)(2,1)} async-done(((bf16[256,768]{0,1:T(8,128)(2,1)}), bf16[2048,768]{0,1:T(8,128)(2,1)}) %all-gather.26.cloned.1.call-update) | async-done | bytes 3145744 | tf_op jit(solution)/shard_map/all_gather | solution.py:191
  174.0 65.4 %while.60 = (s32[]{:T(128)}, f32[12,256]{1,0:T(8,128)S(1)}, f32[12,256]{1,0:T(8,128)S(1)}, f32[12,256,64]{1,2,0:T(8,128)S(1)}, s32[256]{0:T(256)}, /*index=5*/s3...) while((s32[]{:T(128)}, f32[12,256]{1,0:T(8,128)S(1)}, ...), condition=%wide.region_7.8_spmd.clone, body=%wide.region_4.7_spmd.clone.sunk | while | flops 419773696 | bytes 51461896 | solution.py:159
  250.6 20.1 all-gather.44.cloned.1.call-done
  274.3 29.3 %all-gather.46.cloned.1.call-done = bf16[1,768,2304]{2,1,0:T(8,128)(2,1)} async-done(((bf16[1,192,2304]{2,1,0:T(8,128)(2,1)}), bf16[1,768,2304]{2,1,0:T(8,128)(2,1)}) %all-gather.46.cloned.1.call-update) | async-done | bytes 3538960 | tf_op jit(solution)/shard_map/all_gather | solution.py:348
  322.1 5.2 all-gather.10
  333.0 36.6 %all-gather.32.cloned.1.call-done = bf16[2048,768]{1,0:T(8,128)(2,1)} async-done(((bf16[256,768]{1,0:T(8,128)(2,1)}), bf16[2048,768]{1,0:T(8,128)(2,1)}) %all-gather.32.cloned.1.call-update) | async-done | bytes 3145744 | tf_op jit(solution)/shard_map/all_gather | solution.py:192
  374.3 59.7 %all-gather.30.cloned.1.call-done = bf16[2048,768]{0,1:T(8,128)(2,1)} async-done(((bf16[256,768]{0,1:T(8,128)(2,1)}), bf16[2048,768]{0,1:T(8,128)(2,1)}) %all-gather.30.cloned.1.call-update) | async-done | bytes 3145744 | tf_op jit(solution)/shard_map/all_gather | solution.py:191
  434.0 71.7 %while.61 = (s32[]{:T(128)}, f32[12,256]{1,0:T(8,128)S(1)}, f32[12,256]{1,0:T(8,128)S(1)}, f32[12,256,64]{1,2,0:T(8,128)}, s32[256]{0:T(256)}, /*index=5*/s32[4]...) while((s32[]{:T(128)}, f32[12,256]{1,0:T(8,128)S(1)}, ...), condition=%wide.region_13.14_spmd.clone, body=%wide.region_10.13_spmd.clone.sunk | while | flops 419773696 | bytes 51461896 | solution.py:159
  460.6 5.3 fusion.301
  514.7 5.2 gather_fusion.2
  524.4 5.2 gather_fusion
  529.6 31.2 %all-to-all-done.2 = bf16[8,2,64,768]{3,2,1,0:T(8,128)(2,1)} async-done(((bf16[8,2,64,768]{3,2,1,0:T(8,128)(2,1)}), bf16[8,2,64,768]{3,2,1,0:T(8,128)(2,1)}, u32[]{:S(2)}, u32[]{:S(2)}) %all-to-all-start.2) | async-done | bytes 1572896 | tf_op jit(solution)/shard_map/all_to_all | solution.py:437
  565.0 8.8 copy.279
  573.8 8.8 all-gather.34.cloned.1.call-done
  582.6 10.5 fusion.179
  593.1 8.7 copy.275
  601.8 8.7 copy.277
  610.5 8.7 convert_bitcast_fusion
  620.4 11.1 fusion.120
  631.5 11.5 fusion.42
  643.0 5.7 convolution_bitcast_fusion
  649.9 5.9 all-to-all-start.1
  655.8 9.3 fusion.192
  665.1 9.7 add_bitcast_fusion
  676.1 16.9 all-to-all-done.1
  719.8 14.1 all-to-all-done.3
  743.7 5.2 fusion.95
  761.6 114.5 %while.62 = (s32[]{:T(128)}, f32[12,256,64]{1,2,0:T(8,128)}, f32[4,512,768]{2,1,0:T(8,128)}, f32[4,512,768]{2,1,0:T(8,128)}, s32[256]{0:T(256)}, /*index=5*/s32[...) while((s32[]{:T(128)}, f32[12,256,64]{1,2,0:T(8,128)}, ...), condition=%wide.region_30.31_spmd.clone, body=%wide.region_29.30_spmd.clone.sunk | while | flops 1020395776 | bytes 88838064 | solution.py:283
  877.6 114.7 %reduce-scatter.24.cloned.1.call-done = f32[256,768]{1,0:T(8,128)} async-done(((f32[2048,768]{1,0:T(8,128)}), f32[256,768]{1,0:T(8,128)}) %reduce-scatter.24.cloned.1.call-update) | async-done | bytes 786448 | tf_op jit(solution)/shard_map/reduce_scatter | solution.py:285
  994.5 119.0 %reduce-scatter.26.cloned.1.call-done = f32[256,768]{1,0:T(8,128)} async-done(((f32[2048,768]{1,0:T(8,128)}), f32[256,768]{1,0:T(8,128)}) %reduce-scatter.26.cloned.1.call-update) | async-done | bytes 786448 | tf_op jit(solution)/shard_map/reduce_scatter | solution.py:288
  1124.2 6.0 multiply_reduce_fusion.4
  1141.8 115.2 %while.63 = (s32[]{:T(128)}, f32[12,256,64]{1,2,0:T(8,128)}, f32[4,512,768]{2,1,0:T(8,128)}, f32[4,512,768]{2,1,0:T(8,128)}, s32[256]{0:T(256)}, /*index=5*/s32[...) while((s32[]{:T(128)}, f32[12,256,64]{1,2,0:T(8,128)}, ...), condition=%wide.region_37.38_spmd.clone, body=%wide.region_36.37_spmd.clone.sunk | while | flops 1020395776 | bytes 88936432 | solution.py:283
  1156.5 5.1 fusion.330
  1185.2 5.1 fusion.330
  1214.0 5.1 fusion.330
  1242.7 5.1 fusion.330
  1267.1 8.0 fusion.94
  1282.3 5.2 fusion.137
  1288.7 8.2 fusion.93
  1298.1 76.1 %reduce-scatter.28.cloned.1.call-done = f32[256,768]{1,0:T(8,128)} async-done(((f32[2048,768]{1,0:T(8,128)}), f32[256,768]{1,0:T(8,128)}) %reduce-scatter.28.cloned.1.call-update) | async-done | bytes 786448 | tf_op jit(solution)/shard_map/reduce_scatter | solution.py:285
  1381.6 113.7 %reduce-scatter.30.cloned.1.call-done = f32[256,768]{1,0:T(8,128)} async-done(((f32[2048,768]{1,0:T(8,128)}), f32[256,768]{1,0:T(8,128)}) %reduce-scatter.30.cloned.1.call-update) | async-done | bytes 786448 | tf_op jit(solution)/shard_map/reduce_scatter | solution.py:288
  1510.3 20.5 reduce-scatter.38.cloned.1.call-done
  1530.7 60.9 %reduce-scatter.46.cloned.1.call-done = f32[512,768]{1,0:T(8,128)} async-done(((f32[2048,768]{1,0:T(8,128)}), f32[512,768]{1,0:T(8,128)}) %reduce-scatter.46.cloned.1.call-update) | async-done | bytes 1572880 | tf_op jit(solution)/shard_map/reduce_scatter | solution.py:491
  1591.6 36.3 %reduce-scatter.36.cloned.1.call-done = f32[192,768]{1,0:T(8,128)} async-done(((f32[768,768]{1,0:T(8,128)}), f32[192,768]{1,0:T(8,128)}) %reduce-scatter.36.cloned.1.call-update) | async-done | bytes 589840 | tf_op jit(solution)/shard_map/reduce_scatter | solution.py:513
  1627.9 101.8 %reduce-scatter.42.cloned.1.call-done = f32[192,4096]{1,0:T(8,128)} async-done(((f32[768,4096]{1,0:T(8,128)}), f32[192,4096]{1,0:T(8,128)}) %reduce-scatter.42.cloned.1.call-update) | async-done | bytes 3145744 | tf_op jit(solution)/shard_map/reduce_scatter | solution.py:490
  1729.8 61.1 %reduce-scatter.44.cloned.1.call-done = f32[512,768]{1,0:T(8,128)} async-done(((f32[2048,768]{1,0:T(8,128)}), f32[512,768]{1,0:T(8,128)}) %reduce-scatter.44.cloned.1.call-update) | async-done | bytes 1572880 | tf_op jit(solution)/shard_map/reduce_scatter | solution.py:515
  1790.8 66.0 %reduce-scatter.34.cloned.1.call-done = f32[192,2304]{1,0:T(8,128)} async-done(((f32[768,2304]{1,0:T(8,128)}), f32[192,2304]{1,0:T(8,128)}) %reduce-scatter.34.cloned.1.call-update) | async-done | bytes 1769488 | tf_op jit(solution)/shard_map/reduce_scatter | solution.py:488
  1856.9 101.8 %reduce-scatter.40.cloned.1.call-done = f32[192,4096]{1,0:T(8,128)} async-done(((f32[768,4096]{1,0:T(8,128)}), f32[192,4096]{1,0:T(8,128)}) %reduce-scatter.40.cloned.1.call-update) | async-done | bytes 3145744 | tf_op jit(solution)/shard_map/reduce_scatter | solution.py:514
  1958.7 66.3 %reduce-scatter.32.cloned.1.call-done = f32[192,2304]{1,0:T(8,128)} async-done(((f32[768,2304]{1,0:T(8,128)}), f32[192,2304]{1,0:T(8,128)}) %reduce-scatter.32.cloned.1.call-update) | async-done | bytes 1769488 | tf_op jit(solution)/shard_map/reduce_scatter | solution.py:512
  2025.1 10.7 fusion.90
  2035.8 12.6 copy.305
  2048.7 13.7 fusion.114
  2062.4 12.7 copy.303
  2075.1 10.7 fusion.116
  2085.8 12.6 copy.302
  2098.4 17.5 pad_maximum_fusion
  2126.1 40.2 %all-reduce.2 = (f32[1,2,192]{2,1,0:T(2,128)S(1)}, f32[1,2,192]{2,1,0:T(2,128)S(1)}, f32[192,16]{0,1:T(8,128)}) all-reduce(f32[1,2,192]{2,1,0:T(2,128)S(1)} %bitcast.531, f32[1,2,192]{2,1,0:T(2,128)S(1)} %bitcast.532, f32[192,16]{0,1:T(8,128)S(1)} %copy.325), channel_id=1, replica_groups=mesh['ctx'=8,'fsdp'=4] {'ctx'}, use_global_device_ids=true, to_apply=%region_56.57 | all-reduce | flops 3840 | bytes 30720 | tf_op jit(solution)/shard_map/psum | solution.py:520
  2167.0 379.4 %all-reduce.6.cloned.1.call-done = (f32[1,192,2304]{2,1,0:T(8,128)}, f32[1,192,2304]{2,1,0:T(8,128)}, f32[1,192,768]{2,1,0:T(8,128)}, f32[1,192,768]{2,1,0:T(8,1...) async-done(((f32[1,192,2304]{2,1,0:T(8,128)}, f32[1,192,2304]{2,1,0:T(8,128)}, ...) | async-done | bytes 14155792 | tf_op jit(solution)/shard_map/psum | solution.py:520
  2561.1 86.5 %reduce-scatter.50.cloned.1.call-done = f32[4096,192]{0,1:T(8,128)} async-done(((f32[4096,768]{0,1:T(8,128)}), f32[4096,192]{0,1:T(8,128)}) %reduce-scatter.50.cloned.1.call-update) | async-done | bytes 3145744 | tf_op jit(solution)/shard_map/reduce_scatter | solution.py:497
  2647.6 183.6 %reduce-scatter.48.cloned.1.call-done = f32[2,4096,192]{1,2,0:T(8,128)} async-done(((f32[2,4096,768]{1,2,0:T(8,128)}), f32[2,4096,192]{1,2,0:T(8,128)}) %reduce-scatter.48.cloned.1.call-update) | async-done | bytes 6291472 | tf_op jit(solution)/shard_map/reduce_scatter | solution.py:496
  (849 shorter events, 576.7 us)
Async XLA Ops:
  7.2 36.5 %all-gather.38.cloned.1.call-start = ((), (), s32[]{:S(2)}) async-start(), calls=%async_computation.41 | async-start | bytes 4423680 | tf_op jit(solution)/shard_map/all_gather | solution.py:341
  10.1 99.6 %all-gather.28.cloned.1.call-start = ((), (), s32[]{:S(2)}) async-start(), calls=%async_computation.22 | async-start | bytes 3538944 | tf_op jit(solution)/shard_map/all_gather | solution.py:192
  23.0 23.8 copy-start.98
  23.0 219.8 %copy-start.90 = (f32[768]{0:T(1024)}, f32[768]{0:T(1024)S(1)}, u32[]{:S(2)}) copy-start(f32[768]{0:T(1024)S(1)} %get-tuple-element.818) | copy-start | bytes 9220
  23.6 23.2 copy-start.112
  49.1 124.9 %all-gather.26.cloned.1.call-start = ((), (), s32[]{:S(2)}) async-start(), calls=%async_computation.21 | async-start | bytes 3538944 | tf_op jit(solution)/shard_map/all_gather | solution.py:191
  57.6 182.6 %all-gather.40.cloned.1.call-start = ((), (), s32[]{:S(2)}) async-start(), calls=%async_computation.42 | async-start | bytes 1474560 | tf_op jit(solution)/shard_map/all_gather | solution.py:342
  59.6 183.2 %all-gather.42.cloned.1.call-start = ((), (), s32[]{:S(2)}) async-start(), calls=%async_computation.43 | async-start | bytes 7864320 | tf_op jit(solution)/shard_map/all_gather | solution.py:343
  63.7 14.8 copy-start.74
  63.7 207.0 %all-gather.44.cloned.1.call-start = ((), (), s32[]{:S(2)}) async-start(), calls=%async_computation.44 | async-start | bytes 3932160 | tf_op jit(solution)/shard_map/all_gather | solution.py:344
  65.0 238.6 %all-gather.46.cloned.1.call-start = ((), (), s32[]{:S(2)}) async-start(), calls=%async_computation.45 | async-start | bytes 4423680 | tf_op jit(solution)/shard_map/all_gather | solution.py:348
  65.8 303.8 %all-gather.32.cloned.1.call-start = ((), (), s32[]{:S(2)}) async-start(), calls=%async_computation.24 | async-start | bytes 3538944 | tf_op jit(solution)/shard_map/all_gather | solution.py:192
  78.5 225.2 %copy-start.96 = (f32[768]{0:T(1024)}, f32[768]{0:T(1024)S(1)}, u32[]{:S(2)}) copy-start(f32[768]{0:T(1024)S(1)} %get-tuple-element.817) | copy-start | bytes 9220
  242.2 28.5 %copy-start.17 = (f32[256,768]{1,0:T(8,128)}, f32[256,768]{1,0:T(8,128)S(1)}, u32[]{:S(2)}) copy-start(f32[256,768]{1,0:T(8,128)S(1)} %get-tuple-element.1017) | copy-start | bytes 2359300
  250.6 56.1 %copy-start.41 = (bf16[256,2048]{1,0:T(8,128)(2,1)}, bf16[256,2048]{1,0:T(8,128)(2,1)S(1)}, u32[]{:S(2)}) copy-start(bf16[256,2048]{1,0:T(8,128)(2,1)S(1)} %multiply_convert_fusion.1) | copy-start | bytes 3145732
  273.7 233.5 %copy-start.27 = (f32[256,768]{1,0:T(8,128)}, f32[256,768]{1,0:T(8,128)S(1)}, u32[]{:S(2)}) copy-start(f32[256,768]{1,0:T(8,128)S(1)} %get-tuple-element.1019) | copy-start | bytes 2359300
  274.3 32.5 %copy-start.110 = (f32[256]{0:T(256)}, f32[256]{0:T(256)S(1)}, u32[]{:S(2)}) copy-start(f32[256]{0:T(256)S(1)} %get-tuple-element.1013) | copy-start | bytes 3076
  309.0 125.0 %all-gather.30.cloned.1.call-start = ((), (), s32[]{:S(2)}) async-start(), calls=%async_computation.23 | async-start | bytes 3538944 | tf_op jit(solution)/shard_map/all_gather | solution.py:191
  313.7 193.5 %all-gather.48.cloned.1.call-start = ((), (), s32[]{:S(2)}) async-start(), calls=%async_computation.46 | async-start | bytes 1474560 | tf_op jit(solution)/shard_map/all_gather | solution.py:349
  314.2 250.8 %all-gather.36.cloned.1.call-start = ((), (), s32[]{:S(2)}) async-start(), calls=%async_computation.26 | async-start | bytes 7864320 | tf_op jit(solution)/shard_map/all_gather | solution.py:355
  315.0 267.6 %all-gather.34.cloned.1.call-start = ((), (), s32[]{:S(2)}) async-start(), calls=%async_computation.25 | async-start | bytes 15728640 | tf_op jit(solution)/shard_map/all_gather | solution.py:354
  315.6 383.1 %all-gather.52.cloned.1.call-start = ((), (), s32[]{:S(2)}) async-start(), calls=%async_computation.48 | async-start | bytes 3932160 | tf_op jit(solution)/shard_map/all_gather | solution.py:351
  316.9 16.0 copy-start.73
  329.8 44.4 %copy-start.130 = (s32[512,1]{0,1:T(1,128)}, s32[512,1]{0,1:T(1,128)S(1)}, u32[]{:S(2)}) copy-start(s32[512,1]{0,1:T(1,128)S(1)} %compare_select_fusion) | copy-start | bytes 6148
  333.0 101.0 %copy-start.77 = (f32[12,256]{1,0:T(8,128)S(1)}, f32[12,256]{1,0:T(8,128)}, u32[]{:S(2)}) copy-start(f32[12,256]{1,0:T(8,128)} %custom-call.4) | copy-start | bytes 36868
  510.3 192.8 %copy-start.20 = (bf16[256,768]{1,0:T(8,128)(2,1)}, bf16[256,768]{1,0:T(8,128)(2,1)S(1)}, u32[]{:S(2)}) copy-start(bf16[256,768]{1,0:T(8,128)(2,1)S(1)} %multiply_convert_fusion.3) | copy-start | bytes 1179652
  519.9 40.8 %all-to-all-start.2 = ((bf16[8,2,64,768]{3,2,1,0:T(8,128)(2,1)}), bf16[8,2,64,768]{3,2,1,0:T(8,128)(2,1)}, u32[]{:S(2)}, u32[]{:S(2)}) async-start(bf16[8,2,64,768]{3,2,1,0:T(8,128)(2,1)} %bitcast.495), calls=%async_computation.2 | async-start | bytes 3145728 | tf_op jit(solution)/shard_map/all_to_all | solution.py:437
  560.8 58.5 %all-to-all-start = ((bf16[8,2,64,768]{3,2,1,0:T(8,128)(2,1)}), bf16[8,2,64,768]{3,2,1,0:T(8,128)(2,1)S(1)}, u32[]{:S(2)}, u32[]{:S(2)}) async-start(bf16[8,2,64,768]{3,2,1,0:T(8,128)(2,1)} %bitcast.494), calls=%async_computation | async-start | bytes 3145728 | tf_op jit(solution)/shard_map/all_to_all | solution.py:410
  564.4 138.7 %all-gather.50.cloned.1.call-start = ((), (), s32[]{:S(2)}) async-start(), calls=%async_computation.47 | async-start | bytes 7864320 | tf_op jit(solution)/shard_map/all_gather | solution.py:350
  620.4 11.1 copy-start.42
  620.4 22.6 slice-start
  631.5 11.5 slice-start.1
  649.9 43.1 %all-to-all-start.1 = ((bf16[8,2,64,768]{3,2,1,0:T(8,128)(2,1)}), bf16[8,2,64,768]{3,2,1,0:T(8,128)(2,1)S(1)}, u32[]{:S(2)}, u32[]{:S(2)}) async-start(bf16[8,2,64,768]{3,2,1,0:T(8,128)(2,1)} %copy.280), calls=%async_computation.1 | async-start | bytes 3145728 | tf_op jit(solution)/shard_map/all_to_all | solution.py:419
  693.0 40.9 %all-to-all-start.3 = ((bf16[8,2,64,768]{3,2,1,0:T(8,128)(2,1)}), bf16[8,2,64,768]{3,2,1,0:T(8,128)(2,1)}, u32[]{:S(2)}, u32[]{:S(2)}) async-start(bf16[8,2,64,768]{3,2,1,0:T(8,128)(2,1)} %copy.283), calls=%async_computation.3 | async-start | bytes 3145728 | tf_op jit(solution)/shard_map/all_to_all | solution.py:460
  697.3 295.0 %reduce-scatter.24.cloned.1.call-start = ((), (), s32[]{:S(2)}) async-start(), calls=%async_computation.27 | async-start | bytes 7077888 | tf_op jit(solution)/shard_map/reduce_scatter | solution.py:285
  876.1 237.3 %reduce-scatter.26.cloned.1.call-start = ((), (), s32[]{:S(2)}) async-start(), calls=%async_computation.28 | async-start | bytes 7077888 | tf_op jit(solution)/shard_map/reduce_scatter | solution.py:288
  876.7 117.0 %copy-start.85 = (f32[256,32]{0,1:T(8,128)S(1)}, f32[256,32]{0,1:T(8,128)}, u32[]{:S(2)}) copy-start(f32[256,32]{0,1:T(8,128)} %copy-done.84) | copy-start | bytes 98308
  876.7 117.0 %copy-start.88 = (f32[256,32]{0,1:T(8,128)S(1)}, f32[256,32]{0,1:T(8,128)}, u32[]{:S(2)}) copy-start(f32[256,32]{0,1:T(8,128)} %copy-done.87) | copy-start | bytes 98308
  876.7 497.5 %reduce-scatter.28.cloned.1.call-start = ((), (), s32[]{:S(2)}) async-start(), calls=%async_computation.29 | async-start | bytes 7077888 | tf_op jit(solution)/shard_map/reduce_scatter | solution.py:285
  993.7 120.9 %copy-start.28 = (f32[256,768]{1,0:T(8,128)S(1)}, f32[256,768]{1,0:T(8,128)}, u32[]{:S(2)}) copy-start(f32[256,768]{1,0:T(8,128)} %copy-done.27) | copy-start | bytes 2359300
  993.8 120.9 %copy-start.97 = (f32[768]{0:T(1024)S(1)}, f32[768]{0:T(1024)}, u32[]{:S(2)}) copy-start(f32[768]{0:T(1024)} %copy-done.96) | copy-start | bytes 9220
  993.8 120.9 %copy-start.111 = (f32[256]{0:T(256)S(1)}, f32[256]{0:T(256)}, u32[]{:S(2)}) copy-start(f32[256]{0:T(256)} %copy-done.110) | copy-start | bytes 3076
  994.3 124.4 %copy-start.65 = (bf16[256,768]{1,0:T(8,128)(2,1)}, bf16[256,768]{1,0:T(8,128)(2,1)S(1)}, u32[]{:S(2)}) copy-start(bf16[256,768]{1,0:T(8,128)(2,1)S(1)} %copy.292) | copy-start | bytes 1179652
  994.5 124.2 %copy-start.67 = (bf16[256,768]{1,0:T(8,128)(2,1)}, bf16[256,768]{1,0:T(8,128)(2,1)S(1)}, u32[]{:S(2)}) copy-start(bf16[256,768]{1,0:T(8,128)(2,1)S(1)} %copy.291) | copy-start | bytes 1179652
  1257.0 238.4 %reduce-scatter.30.cloned.1.call-start = ((), (), s32[]{:S(2)}) async-start(), calls=%async_computation.30 | async-start | bytes 7077888 | tf_op jit(solution)/shard_map/reduce_scatter | solution.py:288
  1257.6 273.1 %reduce-scatter.38.cloned.1.call-start = ((), (), s32[]{:S(2)}) async-start(), calls=%async_computation.34 | async-start | bytes 2949120 | tf_op jit(solution)/shard_map/reduce_scatter | solution.py:489
  1260.2 331.5 %reduce-scatter.46.cloned.1.call-start = ((), (), s32[]{:S(2)}) async-start(), calls=%async_computation.38 | async-start | bytes 7864320 | tf_op jit(solution)/shard_map/reduce_scatter | solution.py:491
  1264.0 364.0 %reduce-scatter.36.cloned.1.call-start = ((), (), s32[]{:S(2)}) async-start(), calls=%async_computation.33 | async-start | bytes 2949120 | tf_op jit(solution)/shard_map/reduce_scatter | solution.py:513
  1267.1 462.7 %reduce-scatter.42.cloned.1.call-start = ((), (), s32[]{:S(2)}) async-start(), calls=%async_computation.36 | async-start | bytes 15728640 | tf_op jit(solution)/shard_map/reduce_scatter | solution.py:490
  1275.1 515.7 %reduce-scatter.44.cloned.1.call-start = ((), (), s32[]{:S(2)}) async-start(), calls=%async_computation.37 | async-start | bytes 7864320 | tf_op jit(solution)/shard_map/reduce_scatter | solution.py:515
  1281.1 575.7 %reduce-scatter.34.cloned.1.call-start = ((), (), s32[]{:S(2)}) async-start(), calls=%async_computation.32 | async-start | bytes 8847360 | tf_op jit(solution)/shard_map/reduce_scatter | solution.py:488
  1287.6 671.2 %reduce-scatter.40.cloned.1.call-start = ((), (), s32[]{:S(2)}) async-start(), calls=%async_computation.35 | async-start | bytes 15728640 | tf_op jit(solution)/shard_map/reduce_scatter | solution.py:514
  1296.9 80.5 %copy-start.86 = (f32[256,32]{0,1:T(8,128)S(1)}, f32[256,32]{0,1:T(8,128)}, u32[]{:S(2)}) copy-start(f32[256,32]{0,1:T(8,128)} %copy-done.84) | copy-start | bytes 98308
  1296.9 80.5 %copy-start.89 = (f32[256,32]{0,1:T(8,128)S(1)}, f32[256,32]{0,1:T(8,128)}, u32[]{:S(2)}) copy-start(f32[256,32]{0,1:T(8,128)} %copy-done.87) | copy-start | bytes 98308
  1296.9 728.2 %reduce-scatter.32.cloned.1.call-start = ((), (), s32[]{:S(2)}) async-start(), calls=%async_computation.31 | async-start | bytes 8847360 | tf_op jit(solution)/shard_map/reduce_scatter | solution.py:512
  1377.4 119.9 %copy-start.38 = (bf16[1,256,768]{2,1,0:T(8,128)(2,1)S(1)}, bf16[1,256,768]{2,1,0:T(8,128)(2,1)}, u32[]{:S(2)}) copy-start(bf16[1,256,768]{2,1,0:T(8,128)(2,1)} %param.21) | copy-start | bytes 1179652
  1377.4 119.9 %copy-start.99 = (f32[768]{0:T(1024)S(1)}, f32[768]{0:T(1024)}, u32[]{:S(2)}) copy-start(f32[768]{0:T(1024)} %copy-done.98) | copy-start | bytes 9220
  1377.4 119.8 %copy-start.113 = (f32[256]{0:T(256)S(1)}, f32[256]{0:T(256)}, u32[]{:S(2)}) copy-start(f32[256]{0:T(256)} %copy-done.112) | copy-start | bytes 3076
  1501.5 619.5 %reduce-scatter.56.cloned.1.call-start = ((), (), s32[]{:S(2)}) async-start(), calls=%async_computation.51 | async-start | bytes 491520
  1503.5 618.4 %reduce-scatter.54.cloned.1.call-start = ((), (), s32[]{:S(2)}) async-start(), calls=%async_computation.50 | async-start | bytes 491520
  1504.6 620.6 %reduce-scatter.52.cloned.1.call-start = ((), (), s32[]{:S(2)}) async-start(), calls=%async_computation.49 | async-start | bytes 491520
  1510.2 1036.2 %all-reduce.6.cloned.1.call-start = ((), (), s32[]{:S(2)}) async-start(), calls=%async_computation.52 | async-start | bytes 28311552 | tf_op jit(solution)/shard_map/psum | solution.py:520
  2025.1 622.5 %reduce-scatter.50.cloned.1.call-start = ((), (), s32[]{:S(2)}) async-start(), calls=%async_computation.40 | async-start | bytes 15728640 | tf_op jit(solution)/shard_map/reduce_scatter | solution.py:497
  2048.4 782.8 %reduce-scatter.48.cloned.1.call-start = ((), (), s32[]{:S(2)}) async-start(), calls=%async_computation.39 | async-start | bytes 31457280 | tf_op jit(solution)/shard_map/reduce_scatter | solution.py:496
  (163 other events, 576.5 us)
Sparse Core Ops, SparseCore 0:
  10.2 33.4 all-gather.37
  49.2 60.4 all-gather.27
  112.3 61.6 all-gather.25
  176.0 15.6 all-gather.39
  193.7 46.3 all-gather.41
  242.1 28.5 all-gather.43
  272.8 30.7 all-gather.45
  309.1 60.4 all-gather.31
  372.2 61.6 all-gather.29
  435.4 15.6 all-gather.47
  452.6 46.3 all-gather.35
  500.5 82.0 all-gather.33
  584.7 28.5 all-gather.51
  614.7 46.3 all-gather.49
  876.2 116.0 reduce-scatter.23
  996.3 117.0 reduce-scatter.25
  1257.1 117.0 reduce-scatter.27
  1378.3 117.0 reduce-scatter.29
  1498.5 32.2 reduce-scatter.37
  1533.3 58.3 reduce-scatter.45
  1594.8 33.0 reduce-scatter.35
  1630.7 99.0 reduce-scatter.41
  1732.5 58.3 reduce-scatter.43
  1793.2 63.6 reduce-scatter.33
  1859.7 99.0 reduce-scatter.39
  1961.3 63.7 reduce-scatter.31
  2027.4 20.7 reduce-scatter.55
  2051.3 20.8 reduce-scatter.53
  2075.2 20.7 reduce-scatter.51
  2101.5 444.8 all-reduce.5
  2549.6 97.9 reduce-scatter.49
  2650.8 180.4 reduce-scatter.47
where the time goes:
time: 2850 us; the launch traced here: 2840 us
  waiting for transfers between devices  1920 us (67%)
  matrix products  347 us (12%)
  local copies, waits for them, and re-layouts  312 us (11%)
  other arithmetic  150 us (5%)
  blocking collectives  59.8 us (2%)
    psum x1, waiting for transfers between devices, per_device(): lax.psum((dense_grads[0], dense_grads[1], dense_grads[2], dense_grads[3],...  379 us
    reduce_scatter x2, waiting for transfers between devices, attend_backward(): lax.psum_scatter(value_parts.reshape(all_slots, model_width), 'ctx', scat...  233 us
    reduce_scatter x2, waiting for transfers between devices, attend_backward(): lax.psum_scatter(key_parts.reshape(all_slots, model_width), 'ctx', scatte...  191 us
    reduce_scatter x1, waiting for transfers between devices, per_device(): lax.psum_scatter(grad_ewin, 'fsdp', scatter_dimension=2, tiled=True)  184 us
    all_gather x2, waiting for transfers between devices, attend_forward(): lax.all_gather(keys_rot, 'ctx', axis=0, tiled=True)  119 us
    reduce_scatter x1, waiting for transfers between devices, per_device(): lax.psum_scatter(grad_dwin, 'fsdp', scatter_dimension=0, tiled=True)  102 us
    reduce_scatter x1, waiting for transfers between devices, per_device(): lax.psum_scatter(grad_swin, 'fsdp', scatter_dimension=0, tiled=True)  102 us
    reduce_scatter x1, waiting for transfers between devices, per_device(): lax.psum_scatter(grad_ewout, 'fsdp', scatter_dimension=1, tiled=True)  86.5 us
  transfers between devices with their start and end apart: 36, of which 26 were waited for; matrix products, arithmetic and copies ran while one was open for 17% of the time, Pallas kernels for 0%

commit v1 on v0

--- a/solution.py
+++ b/solution.py
@@ -21,7 +21,10 @@
     position = (
         order_row[:, None] * piece_len + jnp.arange(piece_len, dtype=jnp.int32)[None, :]
     ).reshape(all_slots)
-    seq_ends = jnp.cumsum(lengths_row, dtype=jnp.int32)
+    count = jnp.arange(lengths_row.shape[0], dtype=jnp.int32)
+    seq_ends = jnp.sum(
+        jnp.where(count[:, None] <= count[None, :], lengths_row[:, None], 0), axis=0, dtype=jnp.int32
+    )
     segment = jnp.sum(
         (position[:, None] >= seq_ends[None, :]).astype(jnp.int32), axis=1, dtype=jnp.int32
     )
@@ -393,7 +396,13 @@
     picked = jnp.sum(jnp.where(chosen, logits[:, None, :], 0.0), axis=-1)
     gate_probs = jax.nn.softmax(picked, axis=-1)
     flat_chosen = chosen.reshape(item_count, num_experts).astype(jnp.int32)
-    slot_rank = jnp.sum((jnp.cumsum(flat_chosen, axis=0) - flat_chosen) * flat_chosen, axis=1)
+    items = jnp.arange(item_count, dtype=jnp.int32)
+    earlier = jnp.dot(
+        (items[None, :] < items[:, None]).astype(jnp.bfloat16),
+        flat_chosen.astype(jnp.bfloat16),
+        preferred_element_type=jnp.float32,
+    ).astype(jnp.int32)
+    slot_rank = jnp.sum(earlier * flat_chosen, axis=1)
     slot_target = routes[0].reshape(item_count) * capacity + slot_rank
     slot_owner = (
         jnp.full((num_experts * capacity,), item_count, jnp.int32)

time: 2850 us -> 2850 us (level)
  no operation moved by 1% of the time
where the time goes in v1:
time: 2850 us; the launch traced here: 2840 us
  waiting for transfers between devices  1920 us (67%)
  matrix products  347 us (12%)
  local copies, waits for them, and re-layouts  312 us (11%)
  other arithmetic  147 us (5%)
  blocking collectives  60.1 us (2%)
    psum x1, waiting for transfers between devices, per_device(): lax.psum((dense_grads[0], dense_grads[1], dense_grads[2], dense_grads[3],...  379 us
    reduce_scatter x2, waiting for transfers between devices, attend_backward(): lax.psum_scatter(value_parts.reshape(all_slots, model_width), 'ctx', scat...  233 us
    reduce_scatter x2, waiting for transfers between devices, attend_backward(): lax.psum_scatter(key_parts.reshape(all_slots, model_width), 'ctx', scatte...  191 us
    reduce_scatter x1, waiting for transfers between devices, per_device(): lax.psum_scatter(grad_ewin, 'fsdp', scatter_dimension=2, tiled=True)  184 us
    all_gather x2, waiting for transfers between devices, attend_forward(): lax.all_gather(keys_rot, 'ctx', axis=0, tiled=True)  119 us
    reduce_scatter x1, waiting for transfers between devices, per_device(): lax.psum_scatter(grad_dwin, 'fsdp', scatter_dimension=0, tiled=True)  102 us
    reduce_scatter x1, waiting for transfers between devices, per_device(): lax.psum_scatter(grad_swin, 'fsdp', scatter_dimension=0, tiled=True)  102 us
    reduce_scatter x1, waiting for transfers between devices, per_device(): lax.psum_scatter(grad_ewout, 'fsdp', scatter_dimension=1, tiled=True)  86.5 us
  transfers between devices with their start and end apart: 36, of which 26 were waited for; matrix products, arithmetic and copies ran while one was open for 17% of the time, Pallas kernels for 0%

profile of v1, /device:TPU:0, one launch (start us, length us, event | category | flops | bytes accessed | tf_op | source)
XLA Modules:
  0.0 2837.0 jit_solution(11249591935880989323)
XLA Ops:
  10.3 7.9 all-gather
  23.6 20.1 all-gather.38.cloned.1.call-done
  67.2 6.5 all-gather.5
  78.4 31.3 %all-gather.28.cloned.1.call-done = bf16[2048,768]{1,0:T(8,128)(2,1)} async-done(((bf16[256,768]{1,0:T(8,128)(2,1)}), bf16[2048,768]{1,0:T(8,128)(2,1)}) %all-gather.28.cloned.1.call-update) | async-done | bytes 3145744 | tf_op jit(solution)/shard_map/all_gather | solution.py:195
  114.5 59.5 %all-gather.26.cloned.1.call-done = bf16[2048,768]{0,1:T(8,128)(2,1)} async-done(((bf16[256,768]{0,1:T(8,128)(2,1)}), bf16[2048,768]{0,1:T(8,128)(2,1)}) %all-gather.26.cloned.1.call-update) | async-done | bytes 3145744 | tf_op jit(solution)/shard_map/all_gather | solution.py:194
  174.0 65.2 %while.60 = (s32[]{:T(128)}, f32[12,256]{1,0:T(8,128)S(1)}, f32[12,256]{1,0:T(8,128)S(1)}, f32[12,256,64]{1,2,0:T(8,128)S(1)}, s32[256]{0:T(256)}, /*index=5*/s3...) while((s32[]{:T(128)}, f32[12,256]{1,0:T(8,128)S(1)}, ...), condition=%wide.region_7.8_spmd.clone, body=%wide.region_4.7_spmd.clone.sunk | while | flops 419773696 | bytes 51461896 | solution.py:162
  250.5 20.2 all-gather.44.cloned.1.call-done
  274.2 29.4 %all-gather.46.cloned.1.call-done = bf16[1,768,2304]{2,1,0:T(8,128)(2,1)} async-done(((bf16[1,192,2304]{2,1,0:T(8,128)(2,1)}), bf16[1,768,2304]{2,1,0:T(8,128)(2,1)}) %all-gather.46.cloned.1.call-update) | async-done | bytes 3538960 | tf_op jit(solution)/shard_map/all_gather | solution.py:351
  321.8 5.2 all-gather.10
  331.6 38.0 %all-gather.32.cloned.1.call-done = bf16[2048,768]{1,0:T(8,128)(2,1)} async-done(((bf16[256,768]{1,0:T(8,128)(2,1)}), bf16[2048,768]{1,0:T(8,128)(2,1)}) %all-gather.32.cloned.1.call-update) | async-done | bytes 3145744 | tf_op jit(solution)/shard_map/all_gather | solution.py:195
  374.2 59.7 %all-gather.30.cloned.1.call-done = bf16[2048,768]{0,1:T(8,128)(2,1)} async-done(((bf16[256,768]{0,1:T(8,128)(2,1)}), bf16[2048,768]{0,1:T(8,128)(2,1)}) %all-gather.30.cloned.1.call-update) | async-done | bytes 3145744 | tf_op jit(solution)/shard_map/all_gather | solution.py:194
  433.9 71.6 %while.61 = (s32[]{:T(128)}, f32[12,256]{1,0:T(8,128)S(1)}, f32[12,256]{1,0:T(8,128)S(1)}, f32[12,256,64]{1,2,0:T(8,128)}, s32[256]{0:T(256)}, /*index=5*/s32[4]...) while((s32[]{:T(128)}, f32[12,256]{1,0:T(8,128)S(1)}, ...), condition=%wide.region_13.14_spmd.clone, body=%wide.region_10.13_spmd.clone.sunk | while | flops 419773696 | bytes 51461896 | solution.py:162
  460.5 5.3 fusion.300
  514.5 5.2 gather_fusion.2
  524.2 5.3 gather_fusion
  529.5 31.2 %all-to-all-done.2 = bf16[8,2,64,768]{3,2,1,0:T(8,128)(2,1)} async-done(((bf16[8,2,64,768]{3,2,1,0:T(8,128)(2,1)}), bf16[8,2,64,768]{3,2,1,0:T(8,128)(2,1)}, u32[]{:S(2)}, u32[]{:S(2)}) %all-to-all-start.2) | async-done | bytes 1572896 | tf_op jit(solution)/shard_map/all_to_all | solution.py:446
  564.9 8.8 copy.269
  573.6 8.9 all-gather.34.cloned.1.call-done
  582.5 10.4 fusion.178
  593.0 8.7 copy.265
  601.7 8.7 copy.267
  610.4 8.7 convert_bitcast_fusion
  620.3 11.1 fusion.122
  631.4 11.5 fusion.42
  642.9 5.7 convolution_bitcast_fusion
  649.8 5.9 all-to-all-start.1
  655.8 9.3 fusion.191
  665.1 9.7 add_bitcast_fusion
  676.1 16.9 all-to-all-done.1
  719.8 14.1 all-to-all-done.3
  743.6 5.2 fusion.95
  761.6 114.2 %while.62 = (s32[]{:T(128)}, f32[12,256,64]{1,2,0:T(8,128)}, f32[4,512,768]{2,1,0:T(8,128)}, f32[4,512,768]{2,1,0:T(8,128)}, s32[256]{0:T(256)}, /*index=5*/s32[...) while((s32[]{:T(128)}, f32[12,256,64]{1,2,0:T(8,128)}, ...), condition=%wide.region_28.29_spmd.clone, body=%wide.region_27.28_spmd.clone.sunk | while | flops 1020395776 | bytes 88838064 | solution.py:286
  877.3 114.7 %reduce-scatter.24.cloned.1.call-done = f32[256,768]{1,0:T(8,128)} async-done(((f32[2048,768]{1,0:T(8,128)}), f32[256,768]{1,0:T(8,128)}) %reduce-scatter.24.cloned.1.call-update) | async-done | bytes 786448 | tf_op jit(solution)/shard_map/reduce_scatter | solution.py:288
  994.2 119.0 %reduce-scatter.26.cloned.1.call-done = f32[256,768]{1,0:T(8,128)} async-done(((f32[2048,768]{1,0:T(8,128)}), f32[256,768]{1,0:T(8,128)}) %reduce-scatter.26.cloned.1.call-update) | async-done | bytes 786448 | tf_op jit(solution)/shard_map/reduce_scatter | solution.py:291
  1123.9 6.0 multiply_reduce_fusion.4
  1141.5 114.5 %while.63 = (s32[]{:T(128)}, f32[12,256,64]{1,2,0:T(8,128)}, f32[4,512,768]{2,1,0:T(8,128)}, f32[4,512,768]{2,1,0:T(8,128)}, s32[256]{0:T(256)}, /*index=5*/s32[...) while((s32[]{:T(128)}, f32[12,256,64]{1,2,0:T(8,128)}, ...), condition=%wide.region_35.36_spmd.clone, body=%wide.region_34.35_spmd.clone.sunk | while | flops 1020395776 | bytes 88936432 | solution.py:286
  1156.0 5.1 fusion.329
  1184.6 5.1 fusion.329
  1213.2 5.1 fusion.329
  1241.8 5.1 fusion.329
  1266.1 7.9 fusion.94
  1281.3 5.2 fusion.139
  1287.7 8.2 fusion.93
  1297.1 76.2 %reduce-scatter.28.cloned.1.call-done = f32[256,768]{1,0:T(8,128)} async-done(((f32[2048,768]{1,0:T(8,128)}), f32[256,768]{1,0:T(8,128)}) %reduce-scatter.28.cloned.1.call-update) | async-done | bytes 786448 | tf_op jit(solution)/shard_map/reduce_scatter | solution.py:288
  1380.7 113.8 %reduce-scatter.30.cloned.1.call-done = f32[256,768]{1,0:T(8,128)} async-done(((f32[2048,768]{1,0:T(8,128)}), f32[256,768]{1,0:T(8,128)}) %reduce-scatter.30.cloned.1.call-update) | async-done | bytes 786448 | tf_op jit(solution)/shard_map/reduce_scatter | solution.py:291
  1509.4 20.4 reduce-scatter.38.cloned.1.call-done
  1529.8 61.0 %reduce-scatter.46.cloned.1.call-done = f32[512,768]{1,0:T(8,128)} async-done(((f32[2048,768]{1,0:T(8,128)}), f32[512,768]{1,0:T(8,128)}) %reduce-scatter.46.cloned.1.call-update) | async-done | bytes 1572880 | tf_op jit(solution)/shard_map/reduce_scatter | solution.py:500
  1590.7 36.2 %reduce-scatter.36.cloned.1.call-done = f32[192,768]{1,0:T(8,128)} async-done(((f32[768,768]{1,0:T(8,128)}), f32[192,768]{1,0:T(8,128)}) %reduce-scatter.36.cloned.1.call-update) | async-done | bytes 589840 | tf_op jit(solution)/shard_map/reduce_scatter | solution.py:522
  1626.9 101.9 %reduce-scatter.42.cloned.1.call-done = f32[192,4096]{1,0:T(8,128)} async-done(((f32[768,4096]{1,0:T(8,128)}), f32[192,4096]{1,0:T(8,128)}) %reduce-scatter.42.cloned.1.call-update) | async-done | bytes 3145744 | tf_op jit(solution)/shard_map/reduce_scatter | solution.py:499
  1728.8 61.1 %reduce-scatter.44.cloned.1.call-done = f32[512,768]{1,0:T(8,128)} async-done(((f32[2048,768]{1,0:T(8,128)}), f32[512,768]{1,0:T(8,128)}) %reduce-scatter.44.cloned.1.call-update) | async-done | bytes 1572880 | tf_op jit(solution)/shard_map/reduce_scatter | solution.py:524
  1789.9 66.0 %reduce-scatter.34.cloned.1.call-done = f32[192,2304]{1,0:T(8,128)} async-done(((f32[768,2304]{1,0:T(8,128)}), f32[192,2304]{1,0:T(8,128)}) %reduce-scatter.34.cloned.1.call-update) | async-done | bytes 1769488 | tf_op jit(solution)/shard_map/reduce_scatter | solution.py:497
  1855.9 101.9 %reduce-scatter.40.cloned.1.call-done = f32[192,4096]{1,0:T(8,128)} async-done(((f32[768,4096]{1,0:T(8,128)}), f32[192,4096]{1,0:T(8,128)}) %reduce-scatter.40.cloned.1.call-update) | async-done | bytes 3145744 | tf_op jit(solution)/shard_map/reduce_scatter | solution.py:523
  1957.8 66.3 %reduce-scatter.32.cloned.1.call-done = f32[192,2304]{1,0:T(8,128)} async-done(((f32[768,2304]{1,0:T(8,128)}), f32[192,2304]{1,0:T(8,128)}) %reduce-scatter.32.cloned.1.call-update) | async-done | bytes 1769488 | tf_op jit(solution)/shard_map/reduce_scatter | solution.py:521
  2024.2 10.7 fusion.90
  2034.9 12.7 copy.295
  2047.9 13.6 fusion.116
  2061.5 12.7 copy.293
  2074.2 10.7 fusion.118
  2084.9 12.7 copy.292
  2097.6 17.4 pad_maximum_fusion
  2125.2 40.5 %all-reduce.2 = (f32[1,2,192]{2,1,0:T(2,128)S(1)}, f32[1,2,192]{2,1,0:T(2,128)S(1)}, f32[192,16]{0,1:T(8,128)}) all-reduce(f32[1,2,192]{2,1,0:T(2,128)S(1)} %bitcast.510, f32[1,2,192]{2,1,0:T(2,128)S(1)} %bitcast.511, f32[192,16]{0,1:T(8,128)S(1)} %copy.315), channel_id=1, replica_groups=mesh['ctx'=8,'fsdp'=4] {'ctx'}, use_global_device_ids=true, to_apply=%region_54.55 | all-reduce | flops 3840 | bytes 30720 | tf_op jit(solution)/shard_map/psum | solution.py:529
  2166.4 379.1 %all-reduce.6.cloned.1.call-done = (f32[1,192,2304]{2,1,0:T(8,128)}, f32[1,192,2304]{2,1,0:T(8,128)}, f32[1,192,768]{2,1,0:T(8,128)}, f32[1,192,768]{2,1,0:T(8,1...) async-done(((f32[1,192,2304]{2,1,0:T(8,128)}, f32[1,192,2304]{2,1,0:T(8,128)}, ...) | async-done | bytes 14155792 | tf_op jit(solution)/shard_map/psum | solution.py:529
  2560.1 86.5 %reduce-scatter.50.cloned.1.call-done = f32[4096,192]{0,1:T(8,128)} async-done(((f32[4096,768]{0,1:T(8,128)}), f32[4096,192]{0,1:T(8,128)}) %reduce-scatter.50.cloned.1.call-update) | async-done | bytes 3145744 | tf_op jit(solution)/shard_map/reduce_scatter | solution.py:506
  2646.6 183.6 %reduce-scatter.48.cloned.1.call-done = f32[2,4096,192]{1,2,0:T(8,128)} async-done(((f32[2,4096,768]{1,2,0:T(8,128)}), f32[2,4096,192]{1,2,0:T(8,128)}) %reduce-scatter.48.cloned.1.call-update) | async-done | bytes 6291472 | tf_op jit(solution)/shard_map/reduce_scatter | solution.py:505
  (843 shorter events, 573.8 us)
Async XLA Ops:
  7.2 36.5 %all-gather.38.cloned.1.call-start = ((), (), s32[]{:S(2)}) async-start(), calls=%async_computation.41 | async-start | bytes 4423680 | tf_op jit(solution)/shard_map/all_gather | solution.py:344
  10.1 99.6 %all-gather.28.cloned.1.call-start = ((), (), s32[]{:S(2)}) async-start(), calls=%async_computation.22 | async-start | bytes 3538944 | tf_op jit(solution)/shard_map/all_gather | solution.py:195
  23.0 23.8 copy-start.98
  23.0 219.6 %copy-start.90 = (f32[768]{0:T(1024)}, f32[768]{0:T(1024)S(1)}, u32[]{:S(2)}) copy-start(f32[768]{0:T(1024)S(1)} %get-tuple-element.818) | copy-start | bytes 9220
  23.6 23.3 copy-start.112
  49.1 124.9 %all-gather.26.cloned.1.call-start = ((), (), s32[]{:S(2)}) async-start(), calls=%async_computation.21 | async-start | bytes 3538944 | tf_op jit(solution)/shard_map/all_gather | solution.py:194
  57.5 182.5 %all-gather.40.cloned.1.call-start = ((), (), s32[]{:S(2)}) async-start(), calls=%async_computation.42 | async-start | bytes 1474560 | tf_op jit(solution)/shard_map/all_gather | solution.py:345
  59.5 183.1 %all-gather.42.cloned.1.call-start = ((), (), s32[]{:S(2)}) async-start(), calls=%async_computation.43 | async-start | bytes 7864320 | tf_op jit(solution)/shard_map/all_gather | solution.py:346
  63.6 14.7 copy-start.74
  63.6 207.1 %all-gather.44.cloned.1.call-start = ((), (), s32[]{:S(2)}) async-start(), calls=%async_computation.44 | async-start | bytes 3932160 | tf_op jit(solution)/shard_map/all_gather | solution.py:347
  65.0 238.7 %all-gather.46.cloned.1.call-start = ((), (), s32[]{:S(2)}) async-start(), calls=%async_computation.45 | async-start | bytes 4423680 | tf_op jit(solution)/shard_map/all_gather | solution.py:351
  65.7 303.9 %all-gather.32.cloned.1.call-start = ((), (), s32[]{:S(2)}) async-start(), calls=%async_computation.24 | async-start | bytes 3538944 | tf_op jit(solution)/shard_map/all_gather | solution.py:195
  78.3 225.3 %copy-start.96 = (f32[768]{0:T(1024)}, f32[768]{0:T(1024)S(1)}, u32[]{:S(2)}) copy-start(f32[768]{0:T(1024)S(1)} %get-tuple-element.817) | copy-start | bytes 9220
  242.0 28.7 %copy-start.17 = (f32[256,768]{1,0:T(8,128)}, f32[256,768]{1,0:T(8,128)S(1)}, u32[]{:S(2)}) copy-start(f32[256,768]{1,0:T(8,128)S(1)} %get-tuple-element.1017) | copy-start | bytes 2359300
  250.5 56.3 %copy-start.41 = (bf16[256,2048]{1,0:T(8,128)(2,1)}, bf16[256,2048]{1,0:T(8,128)(2,1)S(1)}, u32[]{:S(2)}) copy-start(bf16[256,2048]{1,0:T(8,128)(2,1)S(1)} %multiply_convert_fusion.1) | copy-start | bytes 3145732
  273.6 233.3 %copy-start.27 = (f32[256,768]{1,0:T(8,128)}, f32[256,768]{1,0:T(8,128)S(1)}, u32[]{:S(2)}) copy-start(f32[256,768]{1,0:T(8,128)S(1)} %get-tuple-element.1019) | copy-start | bytes 2359300
  274.2 32.5 %copy-start.110 = (f32[256]{0:T(256)}, f32[256]{0:T(256)S(1)}, u32[]{:S(2)}) copy-start(f32[256]{0:T(256)S(1)} %get-tuple-element.1013) | copy-start | bytes 3076
  309.0 124.9 %all-gather.30.cloned.1.call-start = ((), (), s32[]{:S(2)}) async-start(), calls=%async_computation.23 | async-start | bytes 3538944 | tf_op jit(solution)/shard_map/all_gather | solution.py:194
  313.6 193.3 %all-gather.48.cloned.1.call-start = ((), (), s32[]{:S(2)}) async-start(), calls=%async_computation.46 | async-start | bytes 1474560 | tf_op jit(solution)/shard_map/all_gather | solution.py:352
  314.2 250.6 %all-gather.36.cloned.1.call-start = ((), (), s32[]{:S(2)}) async-start(), calls=%async_computation.26 | async-start | bytes 7864320 | tf_op jit(solution)/shard_map/all_gather | solution.py:358
  315.0 267.6 %all-gather.34.cloned.1.call-start = ((), (), s32[]{:S(2)}) async-start(), calls=%async_computation.25 | async-start | bytes 15728640 | tf_op jit(solution)/shard_map/all_gather | solution.py:357
  315.5 383.0 %all-gather.52.cloned.1.call-start = ((), (), s32[]{:S(2)}) async-start(), calls=%async_computation.48 | async-start | bytes 3932160 | tf_op jit(solution)/shard_map/all_gather | solution.py:354
  316.6 14.9 copy-start.73
  328.4 45.8 %copy-start.130 = (s32[512,1]{0,1:T(1,128)}, s32[512,1]{0,1:T(1,128)S(1)}, u32[]{:S(2)}) copy-start(s32[512,1]{0,1:T(1,128)S(1)} %compare_select_fusion) | copy-start | bytes 6148
  331.6 102.4 %copy-start.77 = (f32[12,256]{1,0:T(8,128)S(1)}, f32[12,256]{1,0:T(8,128)}, u32[]{:S(2)}) copy-start(f32[12,256]{1,0:T(8,128)} %custom-call.4) | copy-start | bytes 36868
  510.1 193.0 %copy-start.20 = (bf16[256,768]{1,0:T(8,128)(2,1)}, bf16[256,768]{1,0:T(8,128)(2,1)S(1)}, u32[]{:S(2)}) copy-start(bf16[256,768]{1,0:T(8,128)(2,1)S(1)} %multiply_convert_fusion.3) | copy-start | bytes 1179652
  519.7 40.9 %all-to-all-start.2 = ((bf16[8,2,64,768]{3,2,1,0:T(8,128)(2,1)}), bf16[8,2,64,768]{3,2,1,0:T(8,128)(2,1)}, u32[]{:S(2)}, u32[]{:S(2)}) async-start(bf16[8,2,64,768]{3,2,1,0:T(8,128)(2,1)} %bitcast.474), calls=%async_computation.2 | async-start | bytes 3145728 | tf_op jit(solution)/shard_map/all_to_all | solution.py:446
  560.6 58.5 %all-to-all-start = ((bf16[8,2,64,768]{3,2,1,0:T(8,128)(2,1)}), bf16[8,2,64,768]{3,2,1,0:T(8,128)(2,1)S(1)}, u32[]{:S(2)}, u32[]{:S(2)}) async-start(bf16[8,2,64,768]{3,2,1,0:T(8,128)(2,1)} %bitcast.473), calls=%async_computation | async-start | bytes 3145728 | tf_op jit(solution)/shard_map/all_to_all | solution.py:419
  564.3 138.8 %all-gather.50.cloned.1.call-start = ((), (), s32[]{:S(2)}) async-start(), calls=%async_computation.47 | async-start | bytes 7864320 | tf_op jit(solution)/shard_map/all_gather | solution.py:353
  620.3 11.1 copy-start.42
  620.3 22.6 slice-start
  631.4 11.5 slice-start.1
  649.8 43.1 %all-to-all-start.1 = ((bf16[8,2,64,768]{3,2,1,0:T(8,128)(2,1)}), bf16[8,2,64,768]{3,2,1,0:T(8,128)(2,1)S(1)}, u32[]{:S(2)}, u32[]{:S(2)}) async-start(bf16[8,2,64,768]{3,2,1,0:T(8,128)(2,1)} %copy.270), calls=%async_computation.1 | async-start | bytes 3145728 | tf_op jit(solution)/shard_map/all_to_all | solution.py:428
  692.9 40.9 %all-to-all-start.3 = ((bf16[8,2,64,768]{3,2,1,0:T(8,128)(2,1)}), bf16[8,2,64,768]{3,2,1,0:T(8,128)(2,1)}, u32[]{:S(2)}, u32[]{:S(2)}) async-start(bf16[8,2,64,768]{3,2,1,0:T(8,128)(2,1)} %copy.273), calls=%async_computation.3 | async-start | bytes 3145728 | tf_op jit(solution)/shard_map/all_to_all | solution.py:469
  697.2 294.8 %reduce-scatter.24.cloned.1.call-start = ((), (), s32[]{:S(2)}) async-start(), calls=%async_computation.27 | async-start | bytes 7077888 | tf_op jit(solution)/shard_map/reduce_scatter | solution.py:288
  875.8 237.4 %reduce-scatter.26.cloned.1.call-start = ((), (), s32[]{:S(2)}) async-start(), calls=%async_computation.28 | async-start | bytes 7077888 | tf_op jit(solution)/shard_map/reduce_scatter | solution.py:291
  876.4 117.1 %copy-start.85 = (f32[256,32]{0,1:T(8,128)S(1)}, f32[256,32]{0,1:T(8,128)}, u32[]{:S(2)}) copy-start(f32[256,32]{0,1:T(8,128)} %copy-done.84) | copy-start | bytes 98308
  876.4 117.1 %copy-start.88 = (f32[256,32]{0,1:T(8,128)S(1)}, f32[256,32]{0,1:T(8,128)}, u32[]{:S(2)}) copy-start(f32[256,32]{0,1:T(8,128)} %copy-done.87) | copy-start | bytes 98308
  876.4 496.9 %reduce-scatter.28.cloned.1.call-start = ((), (), s32[]{:S(2)}) async-start(), calls=%async_computation.29 | async-start | bytes 7077888 | tf_op jit(solution)/shard_map/reduce_scatter | solution.py:288
  993.5 120.9 %copy-start.28 = (f32[256,768]{1,0:T(8,128)S(1)}, f32[256,768]{1,0:T(8,128)}, u32[]{:S(2)}) copy-start(f32[256,768]{1,0:T(8,128)} %copy-done.27) | copy-start | bytes 2359300
  993.5 120.9 %copy-start.97 = (f32[768]{0:T(1024)S(1)}, f32[768]{0:T(1024)}, u32[]{:S(2)}) copy-start(f32[768]{0:T(1024)} %copy-done.96) | copy-start | bytes 9220
  993.5 120.9 %copy-start.111 = (f32[256]{0:T(256)S(1)}, f32[256]{0:T(256)}, u32[]{:S(2)}) copy-start(f32[256]{0:T(256)} %copy-done.110) | copy-start | bytes 3076
  994.0 124.4 %copy-start.65 = (bf16[256,768]{1,0:T(8,128)(2,1)}, bf16[256,768]{1,0:T(8,128)(2,1)S(1)}, u32[]{:S(2)}) copy-start(bf16[256,768]{1,0:T(8,128)(2,1)S(1)} %copy.282) | copy-start | bytes 1179652
  994.2 124.2 %copy-start.67 = (bf16[256,768]{1,0:T(8,128)(2,1)}, bf16[256,768]{1,0:T(8,128)(2,1)S(1)}, u32[]{:S(2)}) copy-start(bf16[256,768]{1,0:T(8,128)(2,1)S(1)} %copy.281) | copy-start | bytes 1179652
  1256.0 238.4 %reduce-scatter.30.cloned.1.call-start = ((), (), s32[]{:S(2)}) async-start(), calls=%async_computation.30 | async-start | bytes 7077888 | tf_op jit(solution)/shard_map/reduce_scatter | solution.py:291
  1256.6 273.2 %reduce-scatter.38.cloned.1.call-start = ((), (), s32[]{:S(2)}) async-start(), calls=%async_computation.34 | async-start | bytes 2949120 | tf_op jit(solution)/shard_map/reduce_scatter | solution.py:498
  1259.2 331.5 %reduce-scatter.46.cloned.1.call-start = ((), (), s32[]{:S(2)}) async-start(), calls=%async_computation.38 | async-start | bytes 7864320 | tf_op jit(solution)/shard_map/reduce_scatter | solution.py:500
  1263.0 364.0 %reduce-scatter.36.cloned.1.call-start = ((), (), s32[]{:S(2)}) async-start(), calls=%async_computation.33 | async-start | bytes 2949120 | tf_op jit(solution)/shard_map/reduce_scatter | solution.py:522
  1266.1 462.7 %reduce-scatter.42.cloned.1.call-start = ((), (), s32[]{:S(2)}) async-start(), calls=%async_computation.36 | async-start | bytes 15728640 | tf_op jit(solution)/shard_map/reduce_scatter | solution.py:499
  1274.1 515.8 %reduce-scatter.44.cloned.1.call-start = ((), (), s32[]{:S(2)}) async-start(), calls=%async_computation.37 | async-start | bytes 7864320 | tf_op jit(solution)/shard_map/reduce_scatter | solution.py:524
  1280.1 575.8 %reduce-scatter.34.cloned.1.call-start = ((), (), s32[]{:S(2)}) async-start(), calls=%async_computation.32 | async-start | bytes 8847360 | tf_op jit(solution)/shard_map/reduce_scatter | solution.py:497
  1286.6 671.2 %reduce-scatter.40.cloned.1.call-start = ((), (), s32[]{:S(2)}) async-start(), calls=%async_computation.35 | async-start | bytes 15728640 | tf_op jit(solution)/shard_map/reduce_scatter | solution.py:523
  1295.9 80.6 %copy-start.86 = (f32[256,32]{0,1:T(8,128)S(1)}, f32[256,32]{0,1:T(8,128)}, u32[]{:S(2)}) copy-start(f32[256,32]{0,1:T(8,128)} %copy-done.84) | copy-start | bytes 98308
  1295.9 80.6 %copy-start.89 = (f32[256,32]{0,1:T(8,128)S(1)}, f32[256,32]{0,1:T(8,128)}, u32[]{:S(2)}) copy-start(f32[256,32]{0,1:T(8,128)} %copy-done.87) | copy-start | bytes 98308
  1295.9 728.2 %reduce-scatter.32.cloned.1.call-start = ((), (), s32[]{:S(2)}) async-start(), calls=%async_computation.31 | async-start | bytes 8847360 | tf_op jit(solution)/shard_map/reduce_scatter | solution.py:521
  1376.5 119.9 %copy-start.38 = (bf16[1,256,768]{2,1,0:T(8,128)(2,1)S(1)}, bf16[1,256,768]{2,1,0:T(8,128)(2,1)}, u32[]{:S(2)}) copy-start(bf16[1,256,768]{2,1,0:T(8,128)(2,1)} %param.21) | copy-start | bytes 1179652
  1376.5 119.9 %copy-start.99 = (f32[768]{0:T(1024)S(1)}, f32[768]{0:T(1024)}, u32[]{:S(2)}) copy-start(f32[768]{0:T(1024)} %copy-done.98) | copy-start | bytes 9220
  1376.5 119.9 %copy-start.113 = (f32[256]{0:T(256)S(1)}, f32[256]{0:T(256)}, u32[]{:S(2)}) copy-start(f32[256]{0:T(256)} %copy-done.112) | copy-start | bytes 3076
  1500.6 619.5 %reduce-scatter.56.cloned.1.call-start = ((), (), s32[]{:S(2)}) async-start(), calls=%async_computation.51 | async-start | bytes 491520
  1502.6 618.4 %reduce-scatter.54.cloned.1.call-start = ((), (), s32[]{:S(2)}) async-start(), calls=%async_computation.50 | async-start | bytes 491520
  1503.7 620.6 %reduce-scatter.52.cloned.1.call-start = ((), (), s32[]{:S(2)}) async-start(), calls=%async_computation.49 | async-start | bytes 491520
  1509.3 1036.1 %all-reduce.6.cloned.1.call-start = ((), (), s32[]{:S(2)}) async-start(), calls=%async_computation.52 | async-start | bytes 28311552 | tf_op jit(solution)/shard_map/psum | solution.py:529
  2024.1 622.5 %reduce-scatter.50.cloned.1.call-start = ((), (), s32[]{:S(2)}) async-start(), calls=%async_computation.40 | async-start | bytes 15728640 | tf_op jit(solution)/shard_map/reduce_scatter | solution.py:506
  2047.6 782.7 %reduce-scatter.48.cloned.1.call-start = ((), (), s32[]{:S(2)}) async-start(), calls=%async_computation.39 | async-start | bytes 31457280 | tf_op jit(solution)/shard_map/reduce_scatter | solution.py:505
  (163 other events, 574.6 us)
Sparse Core Ops, SparseCore 0:
  10.2 33.4 all-gather.37
  49.2 60.4 all-gather.27
  112.3 61.6 all-gather.25
  176.0 15.6 all-gather.39
  193.7 46.3 all-gather.41
  242.1 28.5 all-gather.43
  272.8 30.7 all-gather.45
  309.1 60.4 all-gather.31
  372.2 61.6 all-gather.29
  435.3 15.6 all-gather.47
  452.6 46.3 all-gather.35
  500.4 82.0 all-gather.33
  584.7 28.5 all-gather.51
  614.7 46.3 all-gather.49
  875.9 116.0 reduce-scatter.23
  996.0 117.0 reduce-scatter.25
  1256.1 117.1 reduce-scatter.27
  1377.3 117.0 reduce-scatter.29
  1497.5 32.1 reduce-scatter.37
  1532.3 58.3 reduce-scatter.45
  1593.8 33.0 reduce-scatter.35
  1629.7 99.0 reduce-scatter.41
  1731.5 58.3 reduce-scatter.43
  1792.3 63.6 reduce-scatter.33
  1858.7 99.0 reduce-scatter.39
  1960.4 63.6 reduce-scatter.31
  2026.4 20.8 reduce-scatter.55
  2050.4 20.7 reduce-scatter.53
  2074.3 20.7 reduce-scatter.51
  2100.5 444.8 all-reduce.5
  2548.6 97.9 reduce-scatter.49
  2649.8 180.4 reduce-scatter.47

commit v2 on v0

v2 whole, which is shorter than its diff:
```python
import functools
import math

import jax
import jax.numpy as jnp
from jax import lax
from jax.experimental import pallas as pl
from jax.experimental.pallas import tpu as pltpu
from jax.sharding import PartitionSpec as P

HEADS = 12
HD = 64
FF = 2048
TOP = 2
HEAD_GROUPS = 4
KEY_SPAN = 512
VMEM_LIMIT = 60 * 1024 * 1024


HIGHEST = lax.Precision.HIGHEST
EPSILON = 1e-06
NEGATIVE = -1e30


def _mask(first_key, keys, query_pos, query_start, copies):
    key_pos = first_key + lax.broadcasted_iota(jnp.int32, (keys, query_pos.shape[1]), 0)
    allowed = (key_pos <= query_pos) & (key_pos >= query_start)
    return jnp.concatenate([allowed] * copies, axis=1)


def _starts(pos, ends_ref, count):
    start = jnp.zeros_like(pos)
    for k in range(count):
        start = jnp.where(pos >= ends_ref[k], ends_ref[k] if k < count - 1 else pos, start)
    return start


def _query_geometry(place, ends_ref, count, piece, key_span):
    query_pos = place * piece + lax.broadcasted_iota(jnp.int32, (1, piece), 1)
    query_start = _starts(query_pos, ends_ref, count)
    first = place * piece
    least = jnp.int32(0)
    for k in range(count):
        least = jnp.where(first >= ends_ref[k], ends_ref[k] if k < count - 1 else first, least)
    return (
        query_pos,
        query_start,
        least // key_span,
        (first + piece - 1) // key_span + 1,
    )


def _stack_heads(rows, heads):
    head_dim = rows.shape[1] // heads
    lane = lax.broadcasted_iota(jnp.int32, rows.shape, 1) // head_dim
    zero = jnp.zeros_like(rows)
    return jnp.concatenate([jnp.where(lane == h, rows, zero) for h in range(heads)], axis=0)


def _own_heads(acc, heads, piece):
    head_dim = acc.shape[0] // heads
    return jnp.concatenate(
        [
            acc[h * head_dim : (h + 1) * head_dim, h * piece : (h + 1) * piece]
            for h in range(heads)
        ],
        axis=0,
    )


NT = (((1,), (1,)), ((), ()))


def _dot(a, b):
    return jnp.dot(a, b, preferred_element_type=jnp.float32)


def _dot_nt(a, b):
    return lax.dot_general(a, b, NT, preferred_element_type=jnp.float32)


def _forward_kernel(
    heads,
    count,
    key_span,
    place_ref,
    ends_ref,
    own_ref,
    other_ref,
    out_ref,
    keep_ref,
    lse_ref,
    keys,
    values_t,
):
    step = pl.program_id(0)
    members, _, tok, width = own_ref.shape
    piece = tok // 2
    own_pieces = members * 2
    all_pieces = own_pieces * (1 + other_ref.shape[0])

    @pl.when(step == 0)
    def _():
        for s in range(all_pieces):
            part, rest = divmod(s, own_pieces)
            member, half = divmod(rest, 2)
            rows = pl.ds(half * piece, piece)
            if part == 0:
                k_rows, v_rows = own_ref[member, 1, rows, :], own_ref[member, 2, rows, :]
            else:
                k_rows = other_ref[part - 1, member, 0, rows, :]
                v_rows = other_ref[part - 1, member, 1, rows, :]
            at = pl.ds(pl.multiple_of(place_ref[s] * piece, piece), piece)
            keys[at, :] = k_rows
            values_t[:, at] = v_rows.astype(jnp.float32).T.astype(jnp.bfloat16)

    place = place_ref[step]
    query_pos, query_start, begin, end = _query_geometry(place, ends_ref, count, piece, key_span)
    rows = pl.ds(pl.multiple_of((step % 2) * piece, piece), piece)
    stacked = _stack_heads(own_ref[step // 2, 0, rows, :], heads)
    cols = heads * piece

    def advance(block, carried):
        run_max, run_sum, acc = carried
        first = pl.multiple_of(block * key_span, key_span)
        scores = _dot_nt(keys[pl.ds(first, key_span), :], stacked)
        allowed = _mask(first, key_span, query_pos, query_start, heads)
        scores = jnp.where(allowed, scores, NEGATIVE)
        new_max = jnp.maximum(run_max, jnp.max(scores, axis=0, keepdims=True))
        weights = jnp.exp(scores - new_max)
        factor = jnp.exp(run_max - new_max)
        run_sum = run_sum * factor + jnp.sum(weights, axis=0, keepdims=True)
        acc = acc * factor + _dot(values_t[:, pl.ds(first, key_span)], weights.astype(jnp.bfloat16))
        return (new_max, run_sum, acc)

    run_max, run_sum, acc = lax.fori_loop(
        begin,
        end,
        advance,
        (
            jnp.full((1, cols), NEGATIVE, jnp.float32),
            jnp.zeros((1, cols), jnp.float32),
            jnp.zeros((width, cols), jnp.float32),
        ),
    )
    kept = _own_heads(acc / run_sum, heads, piece)
    keep_ref[0] = kept
    out_ref[0] = kept.T.astype(jnp.bfloat16)
    lse_ref[0] = run_max + jnp.log(run_sum)


def _backward_kernel(
    heads,
    count,
    key_span,
    place_ref,
    ends_ref,
    own_ref,
    other_ref,
    grad_ref,
    keep_ref,
    lse_ref,
    gq_ref,
    gown_ref,
    gother_ref,
    keys,
    keys_t,
    values,
    gkeys,
    gvalues,
):
    step = pl.program_id(0)
    members, _, tok, width = own_ref.shape
    piece = tok // 2
    own_pieces = members * 2
    all_pieces = own_pieces * (1 + other_ref.shape[0])

    @pl.when(step == 0)
    def _():
        for s in range(all_pieces):
            part, rest = divmod(s, own_pieces)
            member, half = divmod(rest, 2)
            rows = pl.ds(half * piece, piece)
            if part == 0:
                k_rows, v_rows = own_ref[member, 1, rows, :], own_ref[member, 2, rows, :]
            else:
                k_rows = other_ref[part - 1, member, 0, rows, :]
                v_rows = other_ref[part - 1, member, 1, rows, :]
            at = pl.ds(pl.multiple_of(place_ref[s] * piece, piece), piece)
            keys[at, :] = k_rows
            keys_t[:, at] = k_rows.astype(jnp.float32).T.astype(jnp.bfloat16)
            values[at, :] = v_rows
        gkeys[...] = jnp.zeros_like(gkeys)
        gvalues[...] = jnp.zeros_like(gvalues)

    place = place_ref[step]
    query_pos, query_start, begin, end = _query_geometry(place, ends_ref, count, piece, key_span)
    rows = pl.ds(pl.multiple_of((step % 2) * piece, piece), piece)
    stacked = _stack_heads(own_ref[step // 2, 0, rows, :], heads)
    grad = grad_ref[step // 2, rows, :]
    grad_stacked = _stack_heads(grad, heads)
    product = grad.astype(jnp.float32).T * keep_ref[0]
    head_dim = width // heads
    delta = jnp.concatenate(
        [
            jnp.sum(product[h * head_dim : (h + 1) * head_dim, :], axis=0, keepdims=True)
            for h in range(heads)
        ],
        axis=1,
    )
    lse = lse_ref[0]

    def retreat(block, acc):
        first = pl.multiple_of(block * key_span, key_span)
        at = pl.ds(first, key_span)
        scores = _dot_nt(keys[at, :], stacked)
        allowed = _mask(first, key_span, query_pos, query_start, heads)
        probs = jnp.where(allowed, jnp.exp(scores - lse), 0.0)
        grad_probs = _dot_nt(values[at, :], grad_stacked)
        grad_scores = (probs * (grad_probs - delta)).astype(jnp.bfloat16)
        gvalues[at, :] += _dot(probs.astype(jnp.bfloat16), grad_stacked)
        gkeys[at, :] += _dot(grad_scores, stacked)
        return acc + _dot(keys_t[:, at], grad_scores)

    acc = lax.fori_loop(
        begin, end, retreat, jnp.zeros((width, heads * piece), jnp.float32)
    )
    gq_ref[0] = _own_heads(acc, heads, piece).T.astype(jnp.bfloat16)

    @pl.when(step == pl.num_programs(0) - 1)
    def _():
        for s in range(all_pieces):
            part, rest = divmod(s, own_pieces)
            member, half = divmod(rest, 2)
            rows = pl.ds(half * piece, piece)
            at = pl.ds(pl.multiple_of(place_ref[s] * piece, piece), piece)
            if part == 0:
                gown_ref[member, 0, rows, :] = gkeys[at, :]
                gown_ref[member, 1, rows, :] = gvalues[at, :]
            else:
                gother_ref[part - 1, member, 0, rows, :] = gkeys[at, :].astype(jnp.bfloat16)
                gother_ref[part - 1, member, 1, rows, :] = gvalues[at, :].astype(jnp.bfloat16)


def _whole(shape):
    return pl.BlockSpec(shape, lambda i, *_: (0,) * len(shape))


def attend(own, other, place, ends, heads, key_span):
    members, _, tok, width = own.shape
    piece = tok // 2
    steps = members * 2
    slots = tok * members * (1 + other.shape[0])
    return pl.pallas_call(
        functools.partial(_forward_kernel, heads, ends.shape[0], key_span),
        grid_spec=pltpu.PrefetchScalarGridSpec(
            num_scalar_prefetch=2,
            grid=(steps,),
            in_specs=[_whole(own.shape), _whole(other.shape)],
            out_specs=[
                pl.BlockSpec((1, piece, width), lambda i, *_: (i, 0, 0)),
                pl.BlockSpec((1, width, piece), lambda i, *_: (i, 0, 0)),
                pl.BlockSpec((1, 1, heads * piece), lambda i, *_: (i, 0, 0)),
            ],
            scratch_shapes=[
                pltpu.VMEM((slots, width), jnp.bfloat16),
                pltpu.VMEM((width, slots), jnp.bfloat16),
            ],
        ),
        out_shape=[
            jax.ShapeDtypeStruct((steps, piece, width), jnp.bfloat16),
            jax.ShapeDtypeStruct((steps, width, piece), jnp.float32),
            jax.ShapeDtypeStruct((steps, 1, heads * piece), jnp.float32),
        ],
        compiler_params=pltpu.CompilerParams(vmem_limit_bytes=VMEM_LIMIT),
        cost_estimate=pl.CostEstimate(
            flops=4 * steps * piece * slots * width, bytes_accessed=8 * slots * width,
            transcendentals=steps * piece * slots * heads // 2,
        ),
    )(place, ends, own, other)


def attend_grads(own, other, grad, keep, lse, place, ends, heads, key_span):
    members, _, tok, width = own.shape
    piece = tok // 2
    steps = members * 2
    slots = tok * members * (1 + other.shape[0])
    return pl.pallas_call(
        functools.partial(_backward_kernel, heads, ends.shape[0], key_span),
        grid_spec=pltpu.PrefetchScalarGridSpec(
            num_scalar_prefetch=2,
            grid=(steps,),
            in_specs=[
                _whole(own.shape),
                _whole(other.shape),
                _whole(grad.shape),
                pl.BlockSpec((1, width, piece), lambda i, *_: (i, 0, 0)),
                pl.BlockSpec((1, 1, heads * piece), lambda i, *_: (i, 0, 0)),
            ],
            out_specs=[
                pl.BlockSpec((1, piece, width), lambda i, *_: (i, 0, 0)),
                _whole((members, 2, tok, width)),
                _whole(other.shape),
            ],
            scratch_shapes=[
                pltpu.VMEM((slots, width), jnp.bfloat16),
                pltpu.VMEM((width, slots), jnp.bfloat16),
                pltpu.VMEM((slots, width), jnp.bfloat16),
                pltpu.VMEM((slots, width), jnp.float32),
                pltpu.VMEM((slots, width), jnp.float32),
            ],
        ),
        out_shape=[
            jax.ShapeDtypeStruct((steps, piece, width), jnp.bfloat16),
            jax.ShapeDtypeStruct((members, 2, tok, width), jnp.float32),
            jax.ShapeDtypeStruct(other.shape, jnp.bfloat16),
        ],
        compiler_params=pltpu.CompilerParams(vmem_limit_bytes=VMEM_LIMIT),
        cost_estimate=pl.CostEstimate(
            flops=10 * steps * piece * slots * width, bytes_accessed=12 * slots * width,
            transcendentals=steps * piece * slots * heads // 2,
        ),
    )(place, ends, own, other, grad, keep, lse)


BOTH = ("ctx", "fsdp")


def swap(values, axis, mask):
    count = lax.axis_size(axis)
    return lax.ppermute(values, axis, [(i, i ^ mask) for i in range(count)])


def gather_shards(shard):
    near = swap(shard, "fsdp", 1)
    far = swap(shard, "fsdp", 2)
    return (shard, near, far, swap(far, "fsdp", 1))


def in_order(shards):
    own = lax.axis_index("fsdp")
    buffer = jnp.zeros((len(shards),) + shards[0].shape, shards[0].dtype)
    for k, shard in enumerate(shards):
        buffer = lax.dynamic_update_index_in_dim(buffer, shard, own ^ k, 0)
    return buffer


def gather_rows(shard):
    return in_order(gather_shards(shard)).reshape(-1, shard.shape[1])


def weight_grad(left, right):
    own = lax.axis_index("fsdp")
    width = left.shape[1] // 4

    def pick(k):
        return lax.dynamic_slice_in_dim(left, (own ^ k) * width, width, 1)

    mine = jnp.concatenate([pick(0), pick(2)], axis=1)
    theirs = swap(jnp.concatenate([pick(1), pick(3)], axis=1), "fsdp", 1)
    right_all = jnp.concatenate([right, swap(right, "fsdp", 1)], axis=0)
    left_all = jnp.concatenate([mine, theirs], axis=0)
    grads = jnp.einsum("tr,tn->rn", left_all, right_all, preferred_element_type=jnp.float32)
    arrived = swap(grads[width:].astype(jnp.bfloat16), "fsdp", 2)
    return (grads[:width] + arrived.astype(jnp.float32)).astype(jnp.bfloat16)


def total(grads):
    return tuple(g.astype(jnp.float32) for g in lax.psum(grads, "ctx"))


def layout(lengths_row, order_row, piece_len):
    all_slots = order_row.shape[0] * piece_len
    position = (
        order_row[:, None] * piece_len + jnp.arange(piece_len, dtype=jnp.int32)[None, :]
    ).reshape(all_slots)
    count = jnp.arange(lengths_row.shape[0], dtype=jnp.int32)
    seq_ends = jnp.sum(
        jnp.where(count[:, None] <= count[None, :], lengths_row[:, None], 0), axis=0, dtype=jnp.int32
    )
    segment = jnp.sum(
        (position[:, None] >= seq_ends[None, :]).astype(jnp.int32), axis=1, dtype=jnp.int32
    )
    seq_start = jnp.sum(
        jnp.where(segment[:, None] > count[None, :], lengths_row[None, :], 0),
        axis=1,
        dtype=jnp.int32,
    )
    return (seq_ends, position - seq_start)


def angles(offset, head_dim):
    freq_table = jnp.exp(
        jnp.arange(head_dim // 2, dtype=jnp.float32) * (-2.0 * math.log(10000.0) / head_dim)
    )
    theta = offset.astype(jnp.float32)[..., None] * freq_table
    cosine, sine = jnp.cos(theta), jnp.sin(theta)
    return (
        jnp.tile(cosine, (1, 2 * HEADS)),
        jnp.tile(jnp.concatenate([-sine, sine], axis=1), (1, HEADS)),
    )


def partner(values):
    lane = lax.broadcasted_iota(jnp.int32, values.shape, 1)
    half = HD // 2
    return jnp.where(
        lane % HD < half, jnp.roll(values, -half, axis=1), jnp.roll(values, half, axis=1)
    )


def rotate(values, tables):
    return values * tables[0] + partner(values) * tables[1]


def unrotate(grads, tables):
    return grads * tables[0] - partner(grads) * tables[1]


def rms_apply(resid, gain_row):
    inv_rms = lax.rsqrt(jnp.mean(resid * resid, axis=-1, keepdims=True) + EPSILON)
    return ((resid * inv_rms * gain_row).astype(jnp.bfloat16), inv_rms)


def rms_back(resid, inv_rms, gain_row, grad_normed):
    weighted = grad_normed * gain_row
    grad_resid = inv_rms * weighted - resid * inv_rms**3 * jnp.mean(
        weighted * resid, axis=-1, keepdims=True
    )
    return (grad_resid, jnp.sum(grad_normed * resid * inv_rms, axis=0))


def feed_forward(normed, w_in, w_out):
    mixed_proj = jnp.dot(normed, w_in, preferred_element_type=jnp.float32)
    hidden_width = w_out.shape[0]
    hidden = (jax.nn.silu(mixed_proj[:, :hidden_width]) * mixed_proj[:, hidden_width:]).astype(
        jnp.bfloat16
    )
    return (jnp.dot(hidden, w_out, preferred_element_type=jnp.float32), mixed_proj, hidden)


def hidden_back(gate_pre, up_pre, grad_hidden):
    sigmoid_gate = jax.nn.sigmoid(gate_pre)
    grad_gate = grad_hidden * up_pre * sigmoid_gate * (1.0 + gate_pre * (1.0 - sigmoid_gate))
    grad_up = grad_hidden * gate_pre * sigmoid_gate
    return (grad_gate.astype(jnp.bfloat16), grad_up.astype(jnp.bfloat16))


def feed_back(mixed_proj, grad_result, w_in, w_out):
    hidden_width = w_out.shape[0]
    grad_hidden = (
        jnp.einsum("td,fd->tf", grad_result, w_out, preferred_element_type=jnp.float32)
        .astype(jnp.bfloat16)
        .astype(jnp.float32)
    )
    grad_mixed = jnp.concatenate(
        hidden_back(mixed_proj[:, :hidden_width], mixed_proj[:, hidden_width:], grad_hidden), axis=1
    )
    grad_normed = jnp.einsum("tf,df->td", grad_mixed, w_in, preferred_element_type=jnp.float32)
    return (grad_normed, grad_mixed)


def head_groups():
    count = lax.axis_size("ctx")
    parts = count // HEAD_GROUPS
    return (parts, [[h * parts + q for h in range(HEAD_GROUPS)] for q in range(parts)])


def to_heads(values):
    return lax.all_to_all(
        values, "ctx", 0, 0, tiled=True, axis_index_groups=head_groups()[1]
    )


def split_heads(values, kinds):
    rows = values.shape[0]
    return jnp.transpose(values.reshape(rows, kinds, HEAD_GROUPS, -1), (2, 1, 0, 3))


def join_heads(values):
    rows = values.shape[2]
    return jnp.transpose(values, (2, 1, 0, 3)).reshape(rows, -1)


def attend_forward(resid, gain_row, w_in, w_out, geometry):
    tables, place, ends = geometry
    tok_rows, model_width = resid.shape
    normed, inv_rms = rms_apply(resid, gain_row)
    mixed_proj = jnp.dot(normed, w_in, preferred_element_type=jnp.float32)
    queries = rotate(mixed_proj[:, :model_width], tables) * 0.125
    keys_rot = rotate(mixed_proj[:, model_width : 2 * model_width], tables)
    mixed = jnp.concatenate([queries, keys_rot, mixed_proj[:, 2 * model_width :]], axis=1).astype(
        jnp.bfloat16
    )
    own = to_heads(split_heads(mixed, 3))
    parts = head_groups()[0]
    other = jnp.stack([swap(own[:, 1:], "ctx", k) for k in range(1, parts)])
    out, keep, lse = attend(own, other, place, ends, HEADS // HEAD_GROUPS, KEY_SPAN)
    back = to_heads(out.reshape(HEAD_GROUPS, tok_rows, -1))
    attended = join_heads(back[:, None])
    branch = jnp.dot(attended, w_out, preferred_element_type=jnp.float32)
    return (resid + branch, (resid, inv_rms, normed, own, other, keep, lse, attended))


def attend_backward(grad_resid, kept, gain_row, w_in, w_out, geometry):
    resid, inv_rms, normed, own, other, keep, lse, attended = kept
    tables, place, ends = geometry
    tok_rows, model_width = resid.shape
    parts = head_groups()[0]
    grad_branch = grad_resid.astype(jnp.bfloat16)
    grad_attended = jnp.einsum(
        "te,de->td", grad_branch, w_out, preferred_element_type=jnp.float32
    ).astype(jnp.bfloat16)
    grad_heads = to_heads(split_heads(grad_attended, 1))[:, 0]
    grad_query, grad_own, grad_other = attend_grads(
        own, other, grad_heads, keep, lse, place, ends, HEADS // HEAD_GROUPS, KEY_SPAN
    )
    for k in range(1, parts):
        grad_own = grad_own + swap(grad_other[k - 1], "ctx", k).astype(jnp.float32)
    grad_out = jnp.concatenate(
        [grad_query.reshape(HEAD_GROUPS, 1, tok_rows, -1), grad_own.astype(jnp.bfloat16)], axis=1
    )
    grad_rot = join_heads(to_heads(grad_out)).astype(jnp.float32)
    grad_mixed = jnp.concatenate(
        [
            unrotate(grad_rot[:, :model_width] * 0.125, tables),
            unrotate(grad_rot[:, model_width : 2 * model_width], tables),
            grad_rot[:, 2 * model_width :],
        ],
        axis=1,
    ).astype(jnp.bfloat16)
    grad_normed = jnp.einsum("te,de->td", grad_mixed, w_in, preferred_element_type=jnp.float32)
    grad_in, grad_gain = rms_back(resid, inv_rms, gain_row, grad_normed)
    weights = (weight_grad(normed, grad_mixed), weight_grad(attended, grad_branch))
    return (grad_resid + grad_in, weights, grad_gain)


def per_device(
    tokens,
    cotangent,
    lengths,
    piece_order,
    routes,
    attn_in,
    attn_out,
    norm_gain,
    mlp_in,
    mlp_out,
    router,
    expert_in,
    expert_out,
):
    tok_rows, model_width = tokens.shape[1:]
    shard_width = router.shape[0]
    num_experts = router.shape[1]
    own_ctx, own_fsdp = lax.axis_index("ctx"), lax.axis_index("fsdp")
    ctx_count, fsdp_count = lax.axis_size("ctx"), lax.axis_size("fsdp")
    units = ctx_count * fsdp_count // num_experts
    hid_unit = expert_out.shape[0] // fsdp_count
    members = [
        [i for i in range(ctx_count * fsdp_count) if i % units == lane] for lane in range(units)
    ]

    def dispatch(values):
        return lax.all_to_all(values, BOTH, 0, 0, tiled=True, axis_index_groups=members)

    def to_units(values):
        return jnp.stack([values] + [swap(values, BOTH, k) for k in range(1, units)])

    def from_units(partial):
        summed = partial[0]
        for k in range(1, units):
            summed = summed + swap(partial[k].astype(jnp.bfloat16), BOTH, k).astype(jnp.float32)
        return summed.astype(jnp.bfloat16)

    small = gather_shards(jnp.concatenate([norm_gain.reshape(4, shard_width), router.T], axis=0))
    small = jnp.transpose(in_order(small), (1, 0, 2)).reshape(-1, model_width)
    gains = small[:4].astype(jnp.float32)
    router_full = small[4:].T
    weights = [
        [gather_rows(w[layer]) for w in (attn_in, attn_out, mlp_in, mlp_out)] for layer in range(2)
    ]

    seq_ends, offset = layout(lengths[0], piece_order[0], tok_rows // 2)
    tables = angles(lax.dynamic_slice_in_dim(offset, own_ctx * tok_rows, tok_rows, 0), HD)
    parts = ctx_count // HEAD_GROUPS
    order = piece_order[0].reshape(HEAD_GROUPS, parts, 2)
    place = jnp.stack(
        [
            lax.dynamic_index_in_dim(order, (own_ctx % parts) ^ k, 1, keepdims=False)
            for k in range(parts)
        ]
    ).reshape(-1)
    geometry = (tables, place, seq_ends)

    item_count = tok_rows * TOP
    capacity = 2 * item_count // num_experts
    slot_count = num_experts * capacity
    expert_ids = jnp.arange(num_experts, dtype=jnp.int32)
    chosen = routes[0][:, :, None] == expert_ids[None, None, :]
    flat_chosen = chosen.reshape(item_count, num_experts).astype(jnp.bfloat16)
    items = jnp.arange(item_count, dtype=jnp.int32)
    earlier = jnp.dot(
        (items[None, :] < items[:, None]).astype(jnp.bfloat16),
        flat_chosen,
        preferred_element_type=jnp.float32,
    )
    slot_rank = jnp.sum(earlier * flat_chosen.astype(jnp.float32), axis=1).astype(jnp.int32)
    slot_target = (routes[0].reshape(item_count) * capacity + slot_rank).reshape(tok_rows, TOP)
    slots = jnp.arange(slot_count, dtype=jnp.int32)
    at_slot = [slots[:, None] == slot_target[None, :, k] for k in range(TOP)]
    of_token = [(slots[None, :] == slot_target[:, k, None]).astype(jnp.bfloat16) for k in range(TOP)]
    fill = (at_slot[0] | at_slot[1]).astype(jnp.bfloat16)

    def to_slots(rows):
        return jnp.dot(fill, rows, preferred_element_type=jnp.float32).astype(jnp.bfloat16)

    def send_rows(rows):
        return to_units(
            dispatch(to_slots(rows).reshape(num_experts, capacity, model_width))
        ).reshape(-1, model_width)

    grad_arrived = send_rows(cotangent[0])
    expert_w = lax.all_to_all(
        jnp.concatenate([expert_in, expert_out[None]]).reshape(3, fsdp_count, hid_unit, -1),
        "fsdp",
        1,
        1,
        tiled=True,
    )
    expert_w = jnp.transpose(expert_w, (0, 2, 1, 3)).reshape(3, hid_unit, model_width)

    resid_in = tokens[0].astype(jnp.float32)
    after_one, kept_one = attend_forward(
        resid_in, gains[0], weights[0][0], weights[0][1], geometry
    )
    normed_two, inv_two = rms_apply(after_one, gains[1])
    dense_branch, mixed_two, hidden_two = feed_forward(normed_two, weights[0][2], weights[0][3])
    middle = after_one + dense_branch
    after_two, kept_two = attend_forward(
        middle, gains[2], weights[1][0], weights[1][1], geometry
    )
    normed_three, inv_three = rms_apply(after_two, gains[3])

    logits = jnp.dot(normed_three, router_full, preferred_element_type=jnp.float32)
    picked = jnp.sum(jnp.where(chosen, logits[:, None, :], 0.0), axis=-1)
    gate_probs = jax.nn.softmax(picked, axis=-1)
    arrived = send_rows(normed_three)
    slot_gates = sum(
        jnp.sum(jnp.where(at_slot[k], gate_probs[None, :, k], 0.0), axis=1) for k in range(TOP)
    )
    arrived_gates = to_units(dispatch(slot_gates.reshape(num_experts, capacity))).reshape(-1, 1)

    shared, mixed_three, hidden_three = feed_forward(normed_three, weights[1][2], weights[1][3])
    grad_shared_in, grad_mixed_three = feed_back(
        mixed_three, cotangent[0], weights[1][2], weights[1][3]
    )

    gate_pre = jnp.einsum("rd,fd->rf", arrived, expert_w[0], preferred_element_type=jnp.float32)
    up_pre = jnp.einsum("rd,fd->rf", arrived, expert_w[1], preferred_element_type=jnp.float32)
    hidden_rows = (jax.nn.silu(gate_pre) * up_pre).astype(jnp.bfloat16)
    partial_rows = jnp.dot(hidden_rows, expert_w[2], preferred_element_type=jnp.float32)
    expert_rows = dispatch(
        from_units(partial_rows.reshape(units, num_experts, capacity, model_width))
    ).reshape(slot_count, model_width)

    grad_rows = (arrived_gates * grad_arrived.astype(jnp.float32)).astype(jnp.bfloat16)
    grad_hidden = (
        jnp.einsum("rd,fd->rf", grad_rows, expert_w[2], preferred_element_type=jnp.float32)
        .astype(jnp.bfloat16)
        .astype(jnp.float32)
    )
    grad_gate, grad_up = hidden_back(gate_pre, up_pre, grad_hidden)
    grad_copies = jnp.dot(grad_gate, expert_w[0], preferred_element_type=jnp.float32) + jnp.dot(
        grad_up, expert_w[1], preferred_element_type=jnp.float32
    )
    grad_back = dispatch(
        from_units(grad_copies.reshape(units, num_experts, capacity, model_width))
    ).reshape(slot_count, model_width)
    grad_experts = jnp.stack(
        [
            jnp.einsum("rf,rd->fd", left, right, preferred_element_type=jnp.float32).astype(
                jnp.bfloat16
            )
            for left, right in ((grad_gate, arrived), (grad_up, arrived), (hidden_rows, grad_rows))
        ]
    ).reshape(3, hid_unit, fsdp_count, -1)
    grad_experts = lax.all_to_all(
        jnp.transpose(grad_experts, (0, 2, 1, 3)), "fsdp", 1, 1, tiled=True
    ).astype(jnp.float32)
    grad_experts = grad_experts.reshape(3, hid_unit * fsdp_count, -1)

    back_rows = [jnp.dot(p, expert_rows, preferred_element_type=jnp.float32) for p in of_token]
    output = after_two + shared + sum(gate_probs[:, k, None] * back_rows[k] for k in range(TOP))
    grad_out = cotangent[0].astype(jnp.float32)
    grad_gates = jnp.stack([jnp.sum(rows * grad_out, axis=-1) for rows in back_rows], axis=1)
    grad_picked = gate_probs * (
        grad_gates - jnp.sum(gate_probs * grad_gates, axis=-1, keepdims=True)
    )
    grad_logits = jnp.sum(jnp.where(chosen, grad_picked[..., None], 0.0), axis=1)
    grad_router = jnp.einsum(
        "te,td->ed", grad_logits, normed_three.astype(jnp.float32), precision=HIGHEST
    )
    grad_normed = (
        grad_shared_in
        + jnp.dot(of_token[0] + of_token[1], grad_back, preferred_element_type=jnp.float32)
        + jnp.einsum(
            "te,de->td", grad_logits, router_full.astype(jnp.float32), precision=HIGHEST
        )
    )
    grad_in, grad_gain_three = rms_back(after_two, inv_three, gains[3], grad_normed)
    shared_grads = (
        weight_grad(normed_three, grad_mixed_three),
        weight_grad(hidden_three, cotangent[0]),
    )
    shared_total = total(shared_grads)
    grad_resid, attn_grads, grad_gain_two = attend_backward(
        grad_out + grad_in, kept_two, gains[2], weights[1][0], weights[1][1], geometry
    )
    attn_total_two = total(attn_grads)
    grad_branch = grad_resid.astype(jnp.bfloat16)
    grad_dense_in, grad_mixed_two = feed_back(
        mixed_two, grad_branch, weights[0][2], weights[0][3]
    )
    dense_total = total(
        (weight_grad(normed_two, grad_mixed_two), weight_grad(hidden_two, grad_branch))
    )
    grad_in_two, grad_gain_dense = rms_back(after_one, inv_two, gains[1], grad_dense_in)
    grad_resid, attn_grads, grad_gain_one = attend_backward(
        grad_resid + grad_in_two, kept_one, gains[0], weights[0][0], weights[0][1], geometry
    )
    attn_total_one = total(attn_grads)
    small_grads = lax.psum(
        jnp.concatenate(
            [
                jnp.stack([grad_gain_one, grad_gain_dense, grad_gain_two, grad_gain_three]),
                grad_router,
            ]
        ),
        BOTH,
    )
    small_grads = lax.dynamic_slice_in_dim(small_grads, own_fsdp * shard_width, shard_width, 1)
    return (
        output[None],
        grad_resid[None],
        jnp.stack([attn_total_one[0], attn_total_two[0]]),
        jnp.stack([attn_total_one[1], attn_total_two[1]]),
        small_grads[:4].reshape(2, 2, shard_width),
        jnp.stack([dense_total[0], shared_total[0]]),
        jnp.stack([dense_total[1], shared_total[1]]),
        small_grads[4:].T,
        grad_experts[:2],
        grad_experts[2],
    )


def solution(mesh):
    placed = (
        P("fsdp", "ctx", None),
        P("fsdp", "ctx", None),
        P("fsdp", None),
        P("fsdp", None),
        P("fsdp", "ctx", None),
        P(None, "fsdp", None),
        P(None, "fsdp", None),
        P(None, None, "fsdp"),
        P(None, "fsdp", None),
        P(None, "fsdp", None),
        P("fsdp", None),
        P(None, "ctx", "fsdp"),
        P("ctx", "fsdp"),
    )
    return jax.shard_map(
        per_device,
        mesh=mesh,
        in_specs=placed,
        out_specs=(
            P("fsdp", "ctx", None),
            P("fsdp", "ctx", None),
            P(None, "fsdp", None),
            P(None, "fsdp", None),
            P(None, None, "fsdp"),
            P(None, "fsdp", None),
            P(None, "fsdp", None),
            P("fsdp", None),
            P(None, "ctx", "fsdp"),
            P("ctx", "fsdp"),
        ),
        check_vma=False,
    )
```

time: 2850 us -> 1190 us (0.42)
  waiting for transfers between devices: 1920 us -> 479 us
  matrix products: 347 us -> 144 us
  local copies, waits for them, and re-layouts: 312 us -> 177 us
  starting transfers between devices: 19.9 us -> 131 us
  Pallas kernels: 0 us -> 79.4 us
  other arithmetic: 150 us -> 89.4 us
    reduce_scatter x14 -> x0, waiting for transfers between devices: 1210 us -> none  [the longest x2 233 us: attend_backward(): lax.psum_scatter(value_parts.reshape(all_slots, model_width), 'ctx', scat...]
    psum x1, waiting for transfers between devices: 379 us -> 101 us  [total(): return tuple((g.astype(jnp.float32) for g in lax.psum(grads, 'ctx')))]
    all_gather x14 -> x0, waiting for transfers between devices: 265 us -> none  [the longest x2 119 us: attend_forward(): lax.all_gather(keys_rot, 'ctx', axis=0, tiled=True)]
    dot_general x75 -> x26, matrix products: 293 us -> 89.3 us  [the longest x8 31.8 us: weight_grad(): jnp.einsum('tr,tn->rn', left_all, right_all, preferred_element_type=jnp.f...]
    ppermute x0 -> x60, waiting for transfers between devices: none -> 187 us  [swap(): return lax.ppermute(values, axis, [(i, i ^ mask) for i in range(count)])]
    all_to_all x4 -> x14, waiting for transfers between devices: 62.1 us -> 190 us  [the longest x5 74.6 us: dispatch(): lax.all_to_all(values, BOTH, 0, 0, tiled=True, axis_index_groups=members)]
    pallas_call x0 -> x4, Pallas kernels: none -> 79.4 us  [the longest x2 45.2 us: attend_grads(): pl.pallas_call(functools.partial(_backward_kernel, heads, ends.shape[0],...]
    dynamic_slice x73 -> x11, local copies, waits for them, and re-layouts: 71.2 us -> 5.99 us  [the longest x8 5.79 us: pick(): return lax.dynamic_slice_in_dim(left, (own ^ k) * width, width, 1)]
  transfers between devices with their start and end apart: 36 -> 75, of which waited for: 26 -> 29; matrix products, arithmetic and copies ran while one was open for 17% -> 30% of each run, Pallas kernels for 0% -> 7%
where the time goes in v2:
time: 1190 us
  waiting for transfers between devices  479 us (40%)
  local copies, waits for them, and re-layouts  177 us (15%)
  matrix products  144 us (12%)
  starting transfers between devices  131 us (11%)
  other arithmetic  89.4 us (8%)
  Pallas kernels  79.4 us (7%)
  blocking collectives  69.1 us (6%)
  between operations  17.1 us (1%)
    ppermute x60, waiting for transfers between devices, swap(): return lax.ppermute(values, axis, [(i, i ^ mask) for i in range(count)])  187 us
    psum x1, waiting for transfers between devices, total(): return tuple((g.astype(jnp.float32) for g in lax.psum(grads, 'ctx')))  101 us
    all_to_all x5, waiting for transfers between devices, dispatch(): lax.all_to_all(values, BOTH, 0, 0, tiled=True, axis_index_groups=members)  74.6 us
    all_to_all x1, waiting for transfers between devices, per_device(): lax.all_to_all(jnp.concatenate([expert_in, expert_out[None]]).reshape(3,...  51.6 us
    ppermute x60, starting transfers between devices, swap(): return lax.ppermute(values, axis, [(i, i ^ mask) for i in range(count)])  50.6 us
    all_to_all x1, waiting for transfers between devices, per_device(): lax.all_to_all(jnp.transpose(grad_experts, (0, 2, 1, 3)), 'fsdp', 1, 1, t...  49.5 us
    dynamic_update_slice x31, local copies, waits for them, and re-layouts, in_order(): buffer = lax.dynamic_update_index_in_dim(buffer, shard, own ^ k, 0)  45.9 us
    pallas_call x2, Pallas kernels, attend_grads(): pl.pallas_call(functools.partial(_backward_kernel, heads, ends.shape[0],...  45.2 us
  transfers between devices with their start and end apart: 75, of which 29 were waited for; matrix products, arithmetic and copies ran while one was open for 30% of the time, Pallas kernels for 7%

profile of v2, /device:TPU:0, one launch (start us, length us, event | category | flops | bytes accessed | tf_op | source)
XLA Modules:
  0.0 1186.5 jit_solution(13569500622145773093)
XLA Ops:
  25.9 4.0 broadcast.262.clone.1
  49.7 4.5 collective-permute-done.8
  62.0 11.0 collective-permute-done.4
  89.4 5.1 all-to-all-start
  95.5 27.5 %collective-permute-done.14 = bf16[512,768]{1,0:T(8,128)(2,1)} collective-permute-done((bf16[512,768]{1,0:T(8,128)(2,1)}, bf16[512,768]{1,0:T(8,128)(2,1)}, u32[]{:S(2)}, u32[]{:S(2)}) %collective-permute-start.14) | collective-permute-done | bytes 786464 | tf_op jit(solution)/shard_map/ppermute | solution.py:331
  140.4 12.7 %collective-permute-done.6 = bf16[4,2,256,192]{2,3,1,0:T(8,128)(2,1)S(1)} collective-permute-done((bf16[4,2,256,192]{2,3,1,0:T(8,128)(2,1)}, bf16[4,2,256,192]{2,3,1,0:T(8,128)(2,1)S(1)}, u32[]{:S(2)}, u32[]{:S(2)}) %collective-permute-start.6) | collective-permute-done | bytes 786464 | tf_op jit(solution)/shard_map/ppermute | solution.py:331
  154.4 17.1 %shard_map.204 = (bf16[8,128,192]{2,1,0:T(8,128)(2,1)}, f32[8,192,128]{2,1,0:T(8,128)}, f32[8,1,384]{2,1,0:T(1,128)}) custom-call(s32[16]{0:T(128)} %reshape.454.place_ref, s32[4]{0:T(128)} %copy-done.166, bf16[4,3,256,192]{3,2,1,0:T(8,128)(2,1)} %copy.294.own_ref, bf16[1,4,2,256,192]{4,3,2,1,0:T(8,128)(2,1)} %bitcast.368), custom_call_target="tpu_custom_call" | custom-call | flops 1610612736 | bytes 3145728 | tf_op jit(solution)/shard_map/pallas_call | solution.py:254
  173.5 5.1 all-to-all-start.1
  181.3 6.3 all-to-all-done.1
  188.9 4.8 fusion.229
  213.5 27.4 %all_to_all.79 = bf16[4,3,256,192]{2,3,1,0:T(8,128)(2,1)S(1)} all-to-all(bf16[4,3,256,192]{2,3,1,0:T(8,128)(2,1)S(1)} %copy.303), channel_id=1, replica_groups={{0,8,16,24},{4,12,20,28},{1,9,17,25},{5,13,21,29},{2,10,18,26},{6,14,22..., dimensions={0} | all-to-all | bytes 2359296 | tf_op jit(solution)/shard_map/all_to_all | solution.py:470
  240.9 10.9 collective-permute-start.19
  252.9 8.7 collective-permute-done.21
  263.1 5.6 collective-permute-done.19
  269.9 17.1 %shard_map.205 = (bf16[8,128,192]{2,1,0:T(8,128)(2,1)}, f32[8,192,128]{2,1,0:T(8,128)}, f32[8,1,384]{2,1,0:T(1,128)}) custom-call(s32[16]{0:T(128)} %reshape.454.place_ref, s32[4]{0:T(128)} %copy-done.166, bf16[4,3,256,192]{3,2,1,0:T(8,128)(2,1)} %copy.305.own_ref, bf16[1,4,2,256,192]{4,3,2,1,0:T(8,128)(2,1)} %bitcast.370), custom_call_target="tpu_custom_call" | custom-call | flops 1610612736 | bytes 3145728 | tf_op jit(solution)/shard_map/pallas_call | solution.py:254
  296.7 4.7 all-to-all-done.3
  306.3 8.3 all-to-all-start.4
  316.9 4.8 concatenate.228
  321.7 4.8 pad_maximum_fusion
  330.2 17.8 %all-to-all-done.4 = bf16[16,64,768]{2,1,0:T(8,128)(2,1)} async-done(((bf16[16,64,768]{2,1,0:T(8,128)(2,1)}), bf16[16,64,768]{2,1,0:T(8,128)(2,1)}, u32[]{:S(2)}, u32[]{:S(2)}) %all-to-all-start.4) | async-done | bytes 1572896 | tf_op jit(solution)/shard_map/all_to_all | solution.py:565
  348.0 5.0 all-to-all-start.5
  355.3 51.6 %all-to-all-done.5 = bf16[3,4,1024,192]{2,3,0,1:T(8,128)(2,1)} async-done(((bf16[3,4,1024,192]{2,3,0,1:T(8,128)(2,1)}), bf16[3,4,1024,192]{2,3,0,1:T(8,128)(2,1)}, u32[]{:S(2)}, u32[]{:S(2)}) %all-to-all-start.5) | async-done | bytes 4718624 | tf_op jit(solution)/shard_map/all_to_all | solution.py:624
  406.9 7.9 all-to-all-start.8
  418.2 3.9 pad_maximum_fusion.1
  425.6 6.3 multiply_convert_fusion
  440.6 8.2 all-to-all-done.8
  448.9 7.6 all-to-all-start.6
  461.4 28.8 %all-to-all-done.6 = bf16[16,64,768]{2,1,0:T(8,128)(2,1)} async-done(((bf16[16,64,768]{2,1,0:T(8,128)(2,1)}), bf16[16,64,768]{2,1,0:T(8,128)(2,1)}, u32[]{:S(2)}, u32[]{:S(2)}) %all-to-all-start.6) | async-done | bytes 1572896 | tf_op jit(solution)/shard_map/all_to_all | solution.py:565
  499.2 7.6 all-to-all-start.7
  509.0 16.4 %collective-permute-done.27 = bf16[512,768]{1,0:T(8,128)(2,1)} collective-permute-done((bf16[512,768]{1,0:T(8,128)(2,1)}, bf16[512,768]{1,0:T(8,128)(2,1)}, u32[]{:S(2)}, u32[]{:S(2)}) %collective-permute-start.27) | collective-permute-done | bytes 786464 | tf_op jit(solution)/shard_map/ppermute | solution.py:331
  531.0 10.1 fusion.4
  556.2 4.9 all-to-all-start.9
  566.0 4.6 fusion.231
  570.6 5.3 multiply_convert_fusion.3
  576.6 18.9 %all-to-all-done.9 = bf16[16,64,768]{2,1,0:T(8,128)(2,1)} async-done(((bf16[16,64,768]{2,1,0:T(8,128)(2,1)}), bf16[16,64,768]{2,1,0:T(8,128)(2,1)}, u32[]{:S(2)}, u32[]{:S(2)}) %all-to-all-start.9) | async-done | bytes 1572896 | tf_op jit(solution)/shard_map/all_to_all | solution.py:565
  597.8 5.4 multiply_reduce_fusion
  607.3 6.5 all-to-all-start.10
  613.8 4.5 maximum_convert_fusion
  625.3 22.6 %shard_map.206 = (bf16[8,128,192]{2,1,0:T(8,128)(2,1)}, f32[4,2,256,192]{3,2,1,0:T(8,128)}, bf16[1,4,2,256,192]{4,3,2,1,0:T(8,128)(2,1)}) custom-call(s32[16]{0:T(128)} %reshape.454.place_ref, s32[4]{0:T(128)} %copy-done.166, bf16[4,3,256,192]{3,2,1,0:T(8,128)(2,1)} %copy.305.own_ref, bf16[1,4,2,256,192]{4,3,2,1,0:T(8,128)(2,1)} %bitcast.371, ...), custom_call_target="tpu_custom_call" | custom-call | flops 4026531840 | bytes 4718592 | tf_op jit(solution)/shard_map/pallas_call | solution.py:288
  657.8 12.9 %collective-permute-done.34 = bf16[4,2,256,192]{2,3,1,0:T(8,128)(2,1)} collective-permute-done((bf16[4,2,256,192]{2,3,1,0:T(8,128)(2,1)}, bf16[4,2,256,192]{2,3,1,0:T(8,128)(2,1)}, u32[]{:S(2)}, u32[]{:S(2)}) %collective-permute-start.34) | collective-permute-done | bytes 786464 | tf_op jit(solution)/shard_map/ppermute | solution.py:331
  675.8 3.9 all-to-all-start.11
  690.0 13.7 %collective-permute-done.59 = bf16[512,768]{1,0:T(8,128)(2,1)S(1)} collective-permute-done((bf16[512,768]{1,0:T(8,128)(2,1)S(1)}, bf16[512,768]{1,0:T(8,128)(2,1)S(1)}, u32[]{:S(2)}, u32[]{:S(2)}) %collective-permute-start.59) | collective-permute-done | bytes 786464 | tf_op jit(solution)/shard_map/ppermute | solution.py:331
  705.2 10.0 fusion.12
  724.8 4.0 multiply_reduce_fusion.1
  742.5 5.1 all-to-all-start.12
  747.7 5.8 collective-permute-done.53
  753.5 3.9 fusion.46
  761.9 22.6 %shard_map.207 = (bf16[8,128,192]{2,1,0:T(8,128)(2,1)}, f32[4,2,256,192]{3,2,1,0:T(8,128)}, bf16[1,4,2,256,192]{4,3,2,1,0:T(8,128)(2,1)}) custom-call(s32[16]{0:T(128)} %reshape.454.place_ref, s32[4]{0:T(128)} %copy-done.166, bf16[4,3,256,192]{3,2,1,0:T(8,128)(2,1)} %copy.294.own_ref, bf16[1,4,2,256,192]{4,3,2,1,0:T(8,128)(2,1)} %bitcast.369, ...), custom_call_target="tpu_custom_call" | custom-call | flops 4026531840 | bytes 4718592 | tf_op jit(solution)/shard_map/pallas_call | solution.py:288
  795.1 11.8 collective-permute-done.35
  816.2 5.1 all-to-all-start.13
  845.1 10.4 collective-permute-done.56
  856.6 10.0 fusion.6
  877.1 3.8 fusion.88
  887.6 20.7 %collective-permute-done.50 = bf16[192,4096]{1,0:T(8,128)(2,1)} collective-permute-done((bf16[192,4096]{1,0:T(8,128)(2,1)}, bf16[192,4096]{1,0:T(8,128)(2,1)}, u32[]{:S(2)}, u32[]{:S(2)}) %collective-permute-start.50) | collective-permute-done | bytes 1572896 | tf_op jit(solution)/shard_map/ppermute | solution.py:331
  911.2 15.0 %collective-permute-done.38 = bf16[192,2304]{1,0:T(8,128)(2,1)S(1)} collective-permute-done((bf16[192,2304]{1,0:T(8,128)(2,1)S(1)}, bf16[192,2304]{1,0:T(8,128)(2,1)S(1)}, u32[]{:S(2)}, u32[]{:S(2)}) %collective-permute-start.38) | collective-permute-done | bytes 884768 | tf_op jit(solution)/shard_map/ppermute | solution.py:331
  927.3 6.6 convolution_convert_fusion.4
  934.1 3.9 fusion.5
  939.6 3.9 convolution_convert_fusion.5
  949.6 5.1 all-to-all-start.14
  955.1 4.0 fusion.50
  959.1 49.5 %all-to-all-done.14 = bf16[3,4,1024,192]{2,3,0,1:T(8,128)(2,1)} async-done(((bf16[3,4,1024,192]{2,3,0,1:T(8,128)(2,1)}), bf16[3,4,1024,192]{2,3,0,1:T(8,128)(2,1)}, u32[]{:S(2)}, u32[]{:S(2)}) %all-to-all-start.14) | async-done | bytes 4718624 | tf_op jit(solution)/shard_map/all_to_all | solution.py:688
  1020.4 4.4 copy.348
  1025.0 41.7 %psum.67 = f32[20,768]{1,0:T(8,128)S(1)} all-reduce(f32[20,768]{1,0:T(8,128)S(1)} %concatenate.261), channel_id=1, replica_groups=mesh['ctx'=8,'fsdp'=4] {'ctx','fsdp'}, use_global_device_ids=true, to_apply=%region_29.30 | all-reduce | flops 15360 | bytes 122880 | tf_op jit(solution)/shard_map/psum | solution.py:733
  1068.1 101.4 %all-reduce.3.cloned.1.call-done = (bf16[1,192,2304]{2,1,0:T(8,128)(2,1)}, bf16[1,192,2304]{2,1,0:T(8,128)(2,1)}, bf16[1,192,768]{2,1,0:T(8,128)(2,1)}, bf16[1,1...) async-done(((bf16[1,192,2304]{2,1,0:T(8,128)(2,1)}, ...) | async-done | bytes 7077904 | tf_op jit(solution)/shard_map/psum | solution.py:369
  (742 shorter events, 356.0 us)
Async XLA Ops:
  10.9 44.3 %collective-permute-start.16 = (bf16[192,2304]{1,0:T(8,128)(2,1)}, bf16[192,2304]{1,0:T(8,128)(2,1)}, u32[]{:S(2)}, u32[]{:S(2)}) collective-permute-start(bf16[192,2304]{1,0:T(8,128)(2,1)} %get-tuple-element.99), channel_id=1, source_target_pairs={{0,1},{1,0},{2,3},{3,2},{4,5},{5,4},{6,7},{7,6},{8,9},{9,8},{10,11... | collective-permute-start | bytes 2654216 | tf_op jit(solution)/shard_map/ppermute | solution.py:331
  11.3 48.0 %collective-permute-start.17 = (bf16[192,2304]{1,0:T(8,128)(2,1)}, bf16[192,2304]{1,0:T(8,128)(2,1)}, u32[]{:S(2)}, u32[]{:S(2)}) collective-permute-start(bf16[192,2304]{1,0:T(8,128)(2,1)} %get-tuple-element.99), channel_id=1, source_target_pairs={{0,2},{1,3},{2,0},{3,1},{4,6},{5,7},{6,4},{7,5},{8,10},{9,11},{10,... | collective-permute-start | bytes 2654216 | tf_op jit(solution)/shard_map/ppermute | solution.py:331
  14.5 29.6 %collective-permute-start = (bf16[20,192]{1,0:T(8,128)(2,1)}, bf16[20,192]{1,0:T(8,128)(2,1)}, u32[]{:S(2)}, u32[]{:S(2)}) collective-permute-start(bf16[20,192]{1,0:T(8,128)(2,1)} %get-tuple-element.162), channel_id=1, source_target_pairs={{0,1},{1,0},{2,3},{3,2},{4,5},{5,4},{6,7},{7,6},{8,9},{9,8},{10,11... | collective-permute-start | bytes 23048 | tf_op jit(solution)/shard_map/ppermute | solution.py:331
  14.7 24.7 %collective-permute-start.1 = (bf16[20,192]{1,0:T(8,128)(2,1)}, bf16[20,192]{1,0:T(8,128)(2,1)}, u32[]{:S(2)}, u32[]{:S(2)}) collective-permute-start(bf16[20,192]{1,0:T(8,128)(2,1)} %get-tuple-element.162), channel_id=1, source_target_pairs={{0,2},{1,3},{2,0},{3,1},{4,6},{5,7},{6,4},{7,5},{8,10},{9,11},{10,... | collective-permute-start | bytes 23048 | tf_op jit(solution)/shard_map/ppermute | solution.py:331
  17.0 32.4 %collective-permute-start.7 = (bf16[192,768]{1,0:T(8,128)(2,1)}, bf16[192,768]{1,0:T(8,128)(2,1)S(1)}, u32[]{:S(2)}, u32[]{:S(2)}) collective-permute-start(bf16[192,768]{1,0:T(8,128)(2,1)} %get-tuple-element.130), channel_id=1, source_target_pairs={{0,1},{1,0},{2,3},{3,2},{4,5},{5,4},{6,7},{7,6},{8,9},{9,8},{10,11... | collective-permute-start | bytes 884744 | tf_op jit(solution)/shard_map/ppermute | solution.py:331
  47.6 14.1 %collective-permute-start.3 = (bf16[192,2304]{1,0:T(8,128)(2,1)}, bf16[192,2304]{1,0:T(8,128)(2,1)}, u32[]{:S(2)}, u32[]{:S(2)}) collective-permute-start(bf16[192,2304]{1,0:T(8,128)(2,1)} %get-tuple-element.100), channel_id=1, source_target_pairs={{0,1},{1,0},{2,3},{3,2},{4,5},{5,4},{6,7},{7,6},{8,9},{9,8},{10,11... | collective-permute-start | bytes 2654216 | tf_op jit(solution)/shard_map/ppermute | solution.py:331
  49.4 23.6 %collective-permute-start.4 = (bf16[192,2304]{1,0:T(8,128)(2,1)}, bf16[192,2304]{1,0:T(8,128)(2,1)S(1)}, u32[]{:S(2)}, u32[]{:S(2)}) collective-permute-start(bf16[192,2304]{1,0:T(8,128)(2,1)} %get-tuple-element.100), channel_id=1, source_target_pairs={{0,2},{1,3},{2,0},{3,1},{4,6},{5,7},{6,4},{7,5},{8,10},{9,11},{10,... | collective-permute-start | bytes 2654216 | tf_op jit(solution)/shard_map/ppermute | solution.py:331
  54.2 73.5 %collective-permute-start.10 = (bf16[192,4096]{1,0:T(8,128)(2,1)}, bf16[192,4096]{1,0:T(8,128)(2,1)}, u32[]{:S(2)}, u32[]{:S(2)}) collective-permute-start(bf16[192,4096]{1,0:T(8,128)(2,1)} %get-tuple-element.81), channel_id=1, source_target_pairs={{0,1},{1,0},{2,3},{3,2},{4,5},{5,4},{6,7},{7,6},{8,9},{9,8},{10,11... | collective-permute-start | bytes 4718600 | tf_op jit(solution)/shard_map/ppermute | solution.py:331
  55.2 72.0 %collective-permute-start.11 = (bf16[192,4096]{1,0:T(8,128)(2,1)}, bf16[192,4096]{1,0:T(8,128)(2,1)}, u32[]{:S(2)}, u32[]{:S(2)}) collective-permute-start(bf16[192,4096]{1,0:T(8,128)(2,1)} %get-tuple-element.81), channel_id=1, source_target_pairs={{0,2},{1,3},{2,0},{3,1},{4,6},{5,7},{6,4},{7,5},{8,10},{9,11},{10,... | collective-permute-start | bytes 4718600 | tf_op jit(solution)/shard_map/ppermute | solution.py:331
  59.4 63.7 %collective-permute-start.13 = (bf16[512,768]{1,0:T(8,128)(2,1)}, bf16[512,768]{1,0:T(8,128)(2,1)}, u32[]{:S(2)}, u32[]{:S(2)}) collective-permute-start(bf16[512,768]{1,0:T(8,128)(2,1)} %get-tuple-element.103), channel_id=1, source_target_pairs={{0,1},{1,0},{2,3},{3,2},{4,5},{5,4},{6,7},{7,6},{8,9},{9,8},{10,11... | collective-permute-start | bytes 2359304 | tf_op jit(solution)/shard_map/ppermute | solution.py:331
  61.7 14.4 %collective-permute-start.18 = (bf16[192,2304]{1,0:T(8,128)(2,1)}, bf16[192,2304]{1,0:T(8,128)(2,1)S(1)}, u32[]{:S(2)}, u32[]{:S(2)}) collective-permute-start(bf16[192,2304]{1,0:T(8,128)(2,1)} %collective-permute-done.17), channel_id=1, source_target_pairs={{0,1},{1,0},{2,3},{3,2},{4,5},{5,4},{6,7},{7,6},{8,9},{9,8},{10,11... | collective-permute-start | bytes 2654216 | tf_op jit(solution)/shard_map/ppermute | solution.py:331
  76.2 46.9 %collective-permute-start.14 = (bf16[512,768]{1,0:T(8,128)(2,1)}, bf16[512,768]{1,0:T(8,128)(2,1)}, u32[]{:S(2)}, u32[]{:S(2)}) collective-permute-start(bf16[512,768]{1,0:T(8,128)(2,1)} %get-tuple-element.103), channel_id=1, source_target_pairs={{0,2},{1,3},{2,0},{3,1},{4,6},{5,7},{6,4},{7,5},{8,10},{9,11},{10,... | collective-permute-start | bytes 2359304 | tf_op jit(solution)/shard_map/ppermute | solution.py:331
  78.2 16.3 %collective-permute-start.9 = (bf16[192,768]{1,0:T(8,128)(2,1)}, bf16[192,768]{1,0:T(8,128)(2,1)}, u32[]{:S(2)}, u32[]{:S(2)}) collective-permute-start(bf16[192,768]{1,0:T(8,128)(2,1)} %collective-permute-done.8), channel_id=1, source_target_pairs={{0,1},{1,0},{2,3},{3,2},{4,5},{5,4},{6,7},{7,6},{8,9},{9,8},{10,11... | collective-permute-start | bytes 884744 | tf_op jit(solution)/shard_map/ppermute | solution.py:331
  89.4 41.9 %all-to-all-start = ((bf16[4,3,256,192]{2,3,1,0:T(8,128)(2,1)}), bf16[4,3,256,192]{2,3,1,0:T(8,128)(2,1)}, u32[]{:S(2)}, u32[]{:S(2)}) async-start(bf16[4,3,256,192]{2,3,1,0:T(8,128)(2,1)} %copy.292), calls=%async_computation | async-start | bytes 2359296 | tf_op jit(solution)/shard_map/all_to_all | solution.py:470
  127.2 51.4 %collective-permute-start.12 = (bf16[192,4096]{1,0:T(8,128)(2,1)}, bf16[192,4096]{1,0:T(8,128)(2,1)}, u32[]{:S(2)}, u32[]{:S(2)}) collective-permute-start(bf16[192,4096]{1,0:T(8,128)(2,1)} %collective-permute-done.11), channel_id=1, source_target_pairs={{0,1},{1,0},{2,3},{3,2},{4,5},{5,4},{6,7},{7,6},{8,9},{9,8},{10,11... | collective-permute-start | bytes 4718600 | tf_op jit(solution)/shard_map/ppermute | solution.py:331
  133.4 19.7 %collective-permute-start.6 = (bf16[4,2,256,192]{2,3,1,0:T(8,128)(2,1)}, bf16[4,2,256,192]{2,3,1,0:T(8,128)(2,1)S(1)}, u32[]{:S(2)}, u32[]{:S(2)}) collective-permute-start(bf16[4,2,256,192]{2,3,1,0:T(8,128)(2,1)} %slice.471), channel_id=1, source_target_pairs={{0,4},{4,0},{8,12},{12,8},{16,20},{20,16},{24,28},{28,24},{1,5},{5... | collective-permute-start | bytes 2359304 | tf_op jit(solution)/shard_map/ppermute | solution.py:331
  173.5 14.1 %all-to-all-start.1 = ((bf16[4,256,192]{1,2,0:T(8,128)(2,1)}), bf16[4,256,192]{1,2,0:T(8,128)(2,1)S(1)}, u32[]{:S(2)}, u32[]{:S(2)}) async-start(bf16[4,256,192]{1,2,0:T(8,128)(2,1)} %copy.295), calls=%async_computation.1 | async-start | bytes 786432 | tf_op jit(solution)/shard_map/all_to_all | solution.py:470
  240.9 27.7 %collective-permute-start.19 = (bf16[4,2,256,192]{2,3,1,0:T(8,128)(2,1)S(1)}, bf16[4,2,256,192]{2,3,1,0:T(8,128)(2,1)S(1)}, u32[]{:S(2)}, u32[]{:S(2)}) collective-permute-start(bf16[4,2,256,192]{2,3,1,0:T(8,128)(2,1)S(1)} %slice.487), channel_id=1, source_target_pairs={{0,4},{4,0},{8,12},{12,8},{16,20},{20,16},{24,28},{28,24},{1,5},{5... | collective-permute-start | bytes 2359304 | tf_op jit(solution)/shard_map/ppermute | solution.py:331
  251.8 40.8 %collective-permute-start.20 = (bf16[192,768]{1,0:T(8,128)(2,1)}, bf16[192,768]{1,0:T(8,128)(2,1)S(1)}, u32[]{:S(2)}, u32[]{:S(2)}) collective-permute-start(bf16[192,768]{1,0:T(8,128)(2,1)} %get-tuple-element.129), channel_id=1, source_target_pairs={{0,1},{1,0},{2,3},{3,2},{4,5},{5,4},{6,7},{7,6},{8,9},{9,8},{10,11... | collective-permute-start | bytes 884744 | tf_op jit(solution)/shard_map/ppermute | solution.py:331
  261.5 33.5 %collective-permute-start.22 = (bf16[192,768]{1,0:T(8,128)(2,1)}, bf16[192,768]{1,0:T(8,128)(2,1)}, u32[]{:S(2)}, u32[]{:S(2)}) collective-permute-start(bf16[192,768]{1,0:T(8,128)(2,1)} %collective-permute-done.21), channel_id=1, source_target_pairs={{0,1},{1,0},{2,3},{3,2},{4,5},{5,4},{6,7},{7,6},{8,9},{9,8},{10,11... | collective-permute-start | bytes 884744 | tf_op jit(solution)/shard_map/ppermute | solution.py:331
  289.1 12.3 %all-to-all-start.3 = ((bf16[4,256,192]{1,2,0:T(8,128)(2,1)}), bf16[4,256,192]{1,2,0:T(8,128)(2,1)S(1)}, u32[]{:S(2)}, u32[]{:S(2)}) async-start(bf16[4,256,192]{1,2,0:T(8,128)(2,1)} %copy.306), calls=%async_computation.3 | async-start | bytes 786432 | tf_op jit(solution)/shard_map/all_to_all | solution.py:470
  306.3 41.7 %all-to-all-start.4 = ((bf16[16,64,768]{2,1,0:T(8,128)(2,1)}), bf16[16,64,768]{2,1,0:T(8,128)(2,1)}, u32[]{:S(2)}, u32[]{:S(2)}) async-start(bf16[16,64,768]{2,1,0:T(8,128)(2,1)} %bitcast.360), calls=%async_computation.4 | async-start | bytes 3145728 | tf_op jit(solution)/shard_map/all_to_all | solution.py:565
  348.0 58.9 %all-to-all-start.5 = ((bf16[3,4,1024,192]{2,3,0,1:T(8,128)(2,1)}), bf16[3,4,1024,192]{2,3,0,1:T(8,128)(2,1)}, u32[]{:S(2)}, u32[]{:S(2)}) async-start(bf16[3,4,1024,192]{2,3,0,1:T(8,128)(2,1)} %copy.310), calls=%async_computation.5 | async-start | bytes 9437184 | tf_op jit(solution)/shard_map/all_to_all | solution.py:624
  353.0 65.2 %collective-permute-start.29 = (bf16[16,64,768]{2,1,0:T(8,128)(2,1)}, bf16[16,64,768]{2,1,0:T(8,128)(2,1)}, u32[]{:S(2)}, u32[]{:S(2)}) collective-permute-start(bf16[16,64,768]{2,1,0:T(8,128)(2,1)} %all-to-all-done.4), channel_id=1, source_target_pairs={{0,1},{1,0},{2,3},{3,2},{4,5},{5,4},{6,7},{7,6},{8,9},{9,8},{10,11... | collective-permute-start | bytes 4718600 | tf_op jit(solution)/shard_map/ppermute | solution.py:331
  406.9 42.0 %all-to-all-start.8 = ((bf16[16,64,768]{2,1,0:T(8,128)(2,1)}), bf16[16,64,768]{2,1,0:T(8,128)(2,1)S(1)}, u32[]{:S(2)}, u32[]{:S(2)}) async-start(bf16[16,64,768]{2,1,0:T(8,128)(2,1)} %bitcast.93), calls=%async_computation.8 | async-start | bytes 3145728 | tf_op jit(solution)/shard_map/all_to_all | solution.py:565
  448.9 41.3 %all-to-all-start.6 = ((bf16[16,64,768]{2,1,0:T(8,128)(2,1)}), bf16[16,64,768]{2,1,0:T(8,128)(2,1)}, u32[]{:S(2)}, u32[]{:S(2)}) async-start(bf16[16,64,768]{2,1,0:T(8,128)(2,1)} %add_convert_fusion.1), calls=%async_computation.6 | async-start | bytes 3145728 | tf_op jit(solution)/shard_map/all_to_all | solution.py:565
  456.5 92.5 %collective-permute-start.23 = (bf16[192,4096]{1,0:T(8,128)(2,1)}, bf16[192,4096]{1,0:T(8,128)(2,1)}, u32[]{:S(2)}, u32[]{:S(2)}) collective-permute-start(bf16[192,4096]{1,0:T(8,128)(2,1)} %get-tuple-element.80), channel_id=1, source_target_pairs={{0,1},{1,0},{2,3},{3,2},{4,5},{5,4},{6,7},{7,6},{8,9},{9,8},{10,11... | collective-permute-start | bytes 4718600 | tf_op jit(solution)/shard_map/ppermute | solution.py:331
  456.5 71.9 %collective-permute-start.24 = (bf16[192,4096]{1,0:T(8,128)(2,1)}, bf16[192,4096]{1,0:T(8,128)(2,1)}, u32[]{:S(2)}, u32[]{:S(2)}) collective-permute-start(bf16[192,4096]{1,0:T(8,128)(2,1)} %get-tuple-element.80), channel_id=1, source_target_pairs={{0,2},{1,3},{2,0},{3,1},{4,6},{5,7},{6,4},{7,5},{8,10},{9,11},{10,... | collective-permute-start | bytes 4718600 | tf_op jit(solution)/shard_map/ppermute | solution.py:331
  458.4 48.4 %collective-permute-start.26 = (bf16[512,768]{1,0:T(8,128)(2,1)}, bf16[512,768]{1,0:T(8,128)(2,1)}, u32[]{:S(2)}, u32[]{:S(2)}) collective-permute-start(bf16[512,768]{1,0:T(8,128)(2,1)} %get-tuple-element.102), channel_id=1, source_target_pairs={{0,1},{1,0},{2,3},{3,2},{4,5},{5,4},{6,7},{7,6},{8,9},{9,8},{10,11... | collective-permute-start | bytes 2359304 | tf_op jit(solution)/shard_map/ppermute | solution.py:331
  458.6 66.8 %collective-permute-start.27 = (bf16[512,768]{1,0:T(8,128)(2,1)}, bf16[512,768]{1,0:T(8,128)(2,1)}, u32[]{:S(2)}, u32[]{:S(2)}) collective-permute-start(bf16[512,768]{1,0:T(8,128)(2,1)} %get-tuple-element.102), channel_id=1, source_target_pairs={{0,2},{1,3},{2,0},{3,1},{4,6},{5,7},{6,4},{7,5},{8,10},{9,11},{10,... | collective-permute-start | bytes 2359304 | tf_op jit(solution)/shard_map/ppermute | solution.py:331
  459.7 69.3 %collective-permute-start.32 = (bf16[16,64,768]{2,1,0:T(8,128)(2,1)S(1)}, bf16[16,64,768]{2,1,0:T(8,128)(2,1)S(1)}, u32[]{:S(2)}, u32[]{:S(2)}) collective-permute-start(bf16[16,64,768]{2,1,0:T(8,128)(2,1)S(1)} %all-to-all-done.8), channel_id=1, source_target_pairs={{0,1},{1,0},{2,3},{3,2},{4,5},{5,4},{6,7},{7,6},{8,9},{9,8},{10,11... | collective-permute-start | bytes 4718600 | tf_op jit(solution)/shard_map/ppermute | solution.py:331
  499.2 27.2 %all-to-all-start.7 = ((f32[16,1,64]{2,1,0:T(1,128)}), f32[16,1,64]{2,1,0:T(1,128)S(1)}, u32[]{:S(2)}, u32[]{:S(2)}) async-start(f32[16,1,64]{2,1,0:T(1,128)} %add.397), calls=%async_computation.7 | async-start | bytes 16384 | tf_op jit(solution)/shard_map/all_to_all | solution.py:565
  506.8 174.0 %collective-permute-start.58 = (bf16[256,768]{1,0:T(8,128)(2,1)}, bf16[256,768]{1,0:T(8,128)(2,1)}, u32[]{:S(2)}, u32[]{:S(2)}) collective-permute-start(bf16[256,768]{1,0:T(8,128)(2,1)} %bitcast.357), channel_id=1, source_target_pairs={{0,1},{1,0},{2,3},{3,2},{4,5},{5,4},{6,7},{7,6},{8,9},{9,8},{10,11... | collective-permute-start | bytes 1179656 | tf_op jit(solution)/shard_map/ppermute | solution.py:331
  528.4 32.7 %collective-permute-start.28 = (bf16[512,768]{1,0:T(8,128)(2,1)}, bf16[512,768]{1,0:T(8,128)(2,1)}, u32[]{:S(2)}, u32[]{:S(2)}) collective-permute-start(bf16[512,768]{1,0:T(8,128)(2,1)} %collective-permute-done.27), channel_id=1, source_target_pairs={{0,1},{1,0},{2,3},{3,2},{4,5},{5,4},{6,7},{7,6},{8,9},{9,8},{10,11... | collective-permute-start | bytes 2359304 | tf_op jit(solution)/shard_map/ppermute | solution.py:331
  528.9 34.3 %collective-permute-start.25 = (bf16[192,4096]{1,0:T(8,128)(2,1)}, bf16[192,4096]{1,0:T(8,128)(2,1)}, u32[]{:S(2)}, u32[]{:S(2)}) collective-permute-start(bf16[192,4096]{1,0:T(8,128)(2,1)} %collective-permute-done.24), channel_id=1, source_target_pairs={{0,1},{1,0},{2,3},{3,2},{4,5},{5,4},{6,7},{7,6},{8,9},{9,8},{10,11... | collective-permute-start | bytes 4718600 | tf_op jit(solution)/shard_map/ppermute | solution.py:331
  556.2 39.2 %all-to-all-start.9 = ((bf16[16,64,768]{2,1,0:T(8,128)(2,1)}), bf16[16,64,768]{2,1,0:T(8,128)(2,1)}, u32[]{:S(2)}, u32[]{:S(2)}) async-start(bf16[16,64,768]{2,1,0:T(8,128)(2,1)} %add_convert_fusion), calls=%async_computation.9 | async-start | bytes 3145728 | tf_op jit(solution)/shard_map/all_to_all | solution.py:565
  607.3 17.0 %all-to-all-start.10 = ((bf16[4,1,256,192]{2,3,1,0:T(8,128)(2,1)}), bf16[4,1,256,192]{2,3,1,0:T(8,128)(2,1)S(1)}, u32[]{:S(2)}, u32[]{:S(2)}) async-start(bf16[4,1,256,192]{2,3,1,0:T(8,128)(2,1)} %bitcast.104), calls=%async_computation.10 | async-start | bytes 786432 | tf_op jit(solution)/shard_map/all_to_all | solution.py:470
  619.7 190.4 %collective-permute-start.42 = (bf16[256,384]{0,1:T(8,128)(2,1)}, bf16[256,384]{0,1:T(8,128)(2,1)}, u32[]{:S(2)}, u32[]{:S(2)}) collective-permute-start(bf16[256,384]{0,1:T(8,128)(2,1)} %pad_maximum_fusion.12), channel_id=1, source_target_pairs={{0,1},{1,0},{2,3},{3,2},{4,5},{5,4},{6,7},{7,6},{8,9},{9,8},{10,11... | collective-permute-start | bytes 589832 | tf_op jit(solution)/shard_map/ppermute | solution.py:331
  650.3 20.3 %collective-permute-start.34 = (bf16[4,2,256,192]{2,3,1,0:T(8,128)(2,1)}, bf16[4,2,256,192]{2,3,1,0:T(8,128)(2,1)}, u32[]{:S(2)}, u32[]{:S(2)}) collective-permute-start(bf16[4,2,256,192]{2,3,1,0:T(8,128)(2,1)} %copy.317), channel_id=1, source_target_pairs={{0,4},{4,0},{8,12},{12,8},{16,20},{20,16},{24,28},{28,24},{1,5},{5... | collective-permute-start | bytes 2359304 | tf_op jit(solution)/shard_map/ppermute | solution.py:331
  655.5 49.7 %collective-permute-start.52 = (bf16[256,4096]{1,0:T(8,128)(2,1)}, bf16[256,4096]{1,0:T(8,128)(2,1)}, u32[]{:S(2)}, u32[]{:S(2)}) collective-permute-start(bf16[256,4096]{1,0:T(8,128)(2,1)} %pad_maximum_fusion.2), channel_id=1, source_target_pairs={{0,1},{1,0},{2,3},{3,2},{4,5},{5,4},{6,7},{7,6},{8,9},{9,8},{10,11... | collective-permute-start | bytes 6291464 | tf_op jit(solution)/shard_map/ppermute | solution.py:331
  657.2 23.6 %collective-permute-start.57 = (bf16[256,1024]{1,0:T(8,128)(2,1)}, bf16[256,1024]{1,0:T(8,128)(2,1)}, u32[]{:S(2)}, u32[]{:S(2)}) collective-permute-start(bf16[256,1024]{1,0:T(8,128)(2,1)} %pad_maximum_fusion.9), channel_id=1, source_target_pairs={{0,1},{1,0},{2,3},{3,2},{4,5},{5,4},{6,7},{7,6},{8,9},{9,8},{10,11... | collective-permute-start | bytes 1572872 | tf_op jit(solution)/shard_map/ppermute | solution.py:331
  675.8 42.8 %all-to-all-start.11 = ((bf16[4,3,256,192]{2,3,1,0:T(8,128)(2,1)}), bf16[4,3,256,192]{2,3,1,0:T(8,128)(2,1)S(1)}, u32[]{:S(2)}, u32[]{:S(2)}) async-start(bf16[4,3,256,192]{2,3,1,0:T(8,128)(2,1)} %copy.319), calls=%async_computation.11 | async-start | bytes 2359296 | tf_op jit(solution)/shard_map/all_to_all | solution.py:470
  680.5 145.6 %collective-permute-start.54 = (bf16[256,1024]{1,0:T(8,128)(2,1)}, bf16[256,1024]{1,0:T(8,128)(2,1)}, u32[]{:S(2)}, u32[]{:S(2)}) collective-permute-start(bf16[256,1024]{1,0:T(8,128)(2,1)} %pad_maximum_fusion.8), channel_id=1, source_target_pairs={{0,1},{1,0},{2,3},{3,2},{4,5},{5,4},{6,7},{7,6},{8,9},{9,8},{10,11... | collective-permute-start | bytes 1572872 | tf_op jit(solution)/shard_map/ppermute | solution.py:331
  683.3 20.5 %collective-permute-start.59 = (bf16[512,768]{1,0:T(8,128)(2,1)S(1)}, bf16[512,768]{1,0:T(8,128)(2,1)S(1)}, u32[]{:S(2)}, u32[]{:S(2)}) collective-permute-start(bf16[512,768]{1,0:T(8,128)(2,1)S(1)} %slice.671), channel_id=1, source_target_pairs={{0,2},{1,3},{2,0},{3,1},{4,6},{5,7},{6,4},{7,5},{8,10},{9,11},{10,... | collective-permute-start | bytes 2359304 | tf_op jit(solution)/shard_map/ppermute | solution.py:331
  689.4 68.0 %collective-permute-start.45 = (bf16[256,384]{0,1:T(8,128)(2,1)}, bf16[256,384]{0,1:T(8,128)(2,1)}, u32[]{:S(2)}, u32[]{:S(2)}) collective-permute-start(bf16[256,384]{0,1:T(8,128)(2,1)} %pad_maximum_fusion.13), channel_id=1, source_target_pairs={{0,1},{1,0},{2,3},{3,2},{4,5},{5,4},{6,7},{7,6},{8,9},{9,8},{10,11... | collective-permute-start | bytes 589832 | tf_op jit(solution)/shard_map/ppermute | solution.py:331
  716.8 36.7 %collective-permute-start.53 = (bf16[192,4096]{1,0:T(8,128)(2,1)}, bf16[192,4096]{1,0:T(8,128)(2,1)}, u32[]{:S(2)}, u32[]{:S(2)}) collective-permute-start(bf16[192,4096]{1,0:T(8,128)(2,1)} %slice.665), channel_id=1, source_target_pairs={{0,2},{1,3},{2,0},{3,1},{4,6},{5,7},{6,4},{7,5},{8,10},{9,11},{10,... | collective-permute-start | bytes 4718600 | tf_op jit(solution)/shard_map/ppermute | solution.py:331
  718.5 38.9 %collective-permute-start.46 = (bf16[256,768]{1,0:T(8,128)(2,1)}, bf16[256,768]{1,0:T(8,128)(2,1)}, u32[]{:S(2)}, u32[]{:S(2)}) collective-permute-start(bf16[256,768]{1,0:T(8,128)(2,1)} %get-tuple-element.58), channel_id=1, source_target_pairs={{0,1},{1,0},{2,3},{3,2},{4,5},{5,4},{6,7},{7,6},{8,9},{9,8},{10,11... | collective-permute-start | bytes 1179656 | tf_op jit(solution)/shard_map/ppermute | solution.py:331
  742.5 18.3 %all-to-all-start.12 = ((bf16[4,1,256,192]{2,3,1,0:T(8,128)(2,1)}), bf16[4,1,256,192]{2,3,1,0:T(8,128)(2,1)S(1)}, u32[]{:S(2)}, u32[]{:S(2)}) async-start(bf16[4,1,256,192]{2,3,1,0:T(8,128)(2,1)} %bitcast.113), calls=%async_computation.12 | async-start | bytes 786432 | tf_op jit(solution)/shard_map/all_to_all | solution.py:470
  786.7 20.2 %collective-permute-start.35 = (bf16[4,2,256,192]{2,3,1,0:T(8,128)(2,1)}, bf16[4,2,256,192]{2,3,1,0:T(8,128)(2,1)}, u32[]{:S(2)}, u32[]{:S(2)}) collective-permute-start(bf16[4,2,256,192]{2,3,1,0:T(8,128)(2,1)} %copy.331), channel_id=1, source_target_pairs={{0,4},{4,0},{8,12},{12,8},{16,20},{20,16},{24,28},{28,24},{1,5},{5... | collective-permute-start | bytes 2359304 | tf_op jit(solution)/shard_map/ppermute | solution.py:331
  792.4 64.1 %collective-permute-start.49 = (bf16[256,4096]{1,0:T(8,128)(2,1)}, bf16[256,4096]{1,0:T(8,128)(2,1)}, u32[]{:S(2)}, u32[]{:S(2)}) collective-permute-start(bf16[256,4096]{1,0:T(8,128)(2,1)} %pad_maximum_fusion.3), channel_id=1, source_target_pairs={{0,1},{1,0},{2,3},{3,2},{4,5},{5,4},{6,7},{7,6},{8,9},{9,8},{10,11... | collective-permute-start | bytes 6291464 | tf_op jit(solution)/shard_map/ppermute | solution.py:331
  795.1 26.4 %collective-permute-start.43 = (bf16[256,768]{1,0:T(8,128)(2,1)}, bf16[256,768]{1,0:T(8,128)(2,1)}, u32[]{:S(2)}, u32[]{:S(2)}) collective-permute-start(bf16[256,768]{1,0:T(8,128)(2,1)} %get-tuple-element.54), channel_id=1, source_target_pairs={{0,1},{1,0},{2,3},{3,2},{4,5},{5,4},{6,7},{7,6},{8,9},{9,8},{10,11... | collective-permute-start | bytes 1179656 | tf_op jit(solution)/shard_map/ppermute | solution.py:331
  806.9 19.3 %collective-permute-start.55 = (bf16[256,768]{1,0:T(8,128)(2,1)}, bf16[256,768]{1,0:T(8,128)(2,1)}, u32[]{:S(2)}, u32[]{:S(2)}) collective-permute-start(bf16[256,768]{1,0:T(8,128)(2,1)} %get-tuple-element.56), channel_id=1, source_target_pairs={{0,1},{1,0},{2,3},{3,2},{4,5},{5,4},{6,7},{7,6},{8,9},{9,8},{10,11... | collective-permute-start | bytes 1179656 | tf_op jit(solution)/shard_map/ppermute | solution.py:331
  810.1 29.3 %collective-permute-start.40 = (bf16[256,2304]{1,0:T(8,128)(2,1)}, bf16[256,2304]{1,0:T(8,128)(2,1)}, u32[]{:S(2)}, u32[]{:S(2)}) collective-permute-start(bf16[256,2304]{1,0:T(8,128)(2,1)} %pad_maximum_fusion.6), channel_id=1, source_target_pairs={{0,1},{1,0},{2,3},{3,2},{4,5},{5,4},{6,7},{7,6},{8,9},{9,8},{10,11... | collective-permute-start | bytes 3538952 | tf_op jit(solution)/shard_map/ppermute | solution.py:331
  816.2 55.7 %all-to-all-start.13 = ((bf16[4,3,256,192]{2,3,1,0:T(8,128)(2,1)}), bf16[4,3,256,192]{2,3,1,0:T(8,128)(2,1)S(1)}, u32[]{:S(2)}, u32[]{:S(2)}) async-start(bf16[4,3,256,192]{2,3,1,0:T(8,128)(2,1)} %copy.333), calls=%async_computation.13 | async-start | bytes 2359296 | tf_op jit(solution)/shard_map/all_to_all | solution.py:470
  821.3 348.2 %all-reduce.3.cloned.1.call-start = ((), (), s32[]{:S(2)}) async-start(), calls=%async_computation.15 | async-start | bytes 14155776 | tf_op jit(solution)/shard_map/psum | solution.py:369
  821.5 10.8 collective-permute-start.47
  826.1 13.3 %collective-permute-start.39 = (bf16[256,384]{1,0:T(8,128)(2,1)S(1)}, bf16[256,384]{1,0:T(8,128)(2,1)S(1)}, u32[]{:S(2)}, u32[]{:S(2)}) collective-permute-start(bf16[256,384]{1,0:T(8,128)(2,1)S(1)} %copy-done.100), channel_id=1, source_target_pairs={{0,1},{1,0},{2,3},{3,2},{4,5},{5,4},{6,7},{7,6},{8,9},{9,8},{10,11... | collective-permute-start | bytes 589832 | tf_op jit(solution)/shard_map/ppermute | solution.py:331
  826.2 12.4 %collective-permute-start.44 = (bf16[192,768]{1,0:T(8,128)(2,1)S(1)}, bf16[192,768]{1,0:T(8,128)(2,1)S(1)}, u32[]{:S(2)}, u32[]{:S(2)}) collective-permute-start(bf16[192,768]{1,0:T(8,128)(2,1)S(1)} %slice.676), channel_id=1, source_target_pairs={{0,2},{1,3},{2,0},{3,1},{4,6},{5,7},{6,4},{7,5},{8,10},{9,11},{10,... | collective-permute-start | bytes 884744 | tf_op jit(solution)/shard_map/ppermute | solution.py:331
  832.3 23.2 %collective-permute-start.56 = (bf16[512,768]{1,0:T(8,128)(2,1)S(1)}, bf16[512,768]{1,0:T(8,128)(2,1)S(1)}, u32[]{:S(2)}, u32[]{:S(2)}) collective-permute-start(bf16[512,768]{1,0:T(8,128)(2,1)S(1)} %slice.672), channel_id=1, source_target_pairs={{0,2},{1,3},{2,0},{3,1},{4,6},{5,7},{6,4},{7,5},{8,10},{9,11},{10,... | collective-permute-start | bytes 2359304 | tf_op jit(solution)/shard_map/ppermute | solution.py:331
  838.6 17.9 %collective-permute-start.48 = (bf16[256,384]{1,0:T(8,128)(2,1)S(1)}, bf16[256,384]{1,0:T(8,128)(2,1)S(1)}, u32[]{:S(2)}, u32[]{:S(2)}) collective-permute-start(bf16[256,384]{1,0:T(8,128)(2,1)S(1)} %copy-done.99), channel_id=1, source_target_pairs={{0,1},{1,0},{2,3},{3,2},{4,5},{5,4},{6,7},{7,6},{8,9},{9,8},{10,11... | collective-permute-start | bytes 589832 | tf_op jit(solution)/shard_map/ppermute | solution.py:331
  843.0 40.8 %collective-permute-start.41 = (bf16[192,2304]{1,0:T(8,128)(2,1)}, bf16[192,2304]{1,0:T(8,128)(2,1)}, u32[]{:S(2)}, u32[]{:S(2)}) collective-permute-start(bf16[192,2304]{1,0:T(8,128)(2,1)} %slice.669), channel_id=1, source_target_pairs={{0,2},{1,3},{2,0},{3,1},{4,6},{5,7},{6,4},{7,5},{8,10},{9,11},{10,... | collective-permute-start | bytes 2654216 | tf_op jit(solution)/shard_map/ppermute | solution.py:331
  869.8 38.4 %collective-permute-start.50 = (bf16[192,4096]{1,0:T(8,128)(2,1)}, bf16[192,4096]{1,0:T(8,128)(2,1)}, u32[]{:S(2)}, u32[]{:S(2)}) collective-permute-start(bf16[192,4096]{1,0:T(8,128)(2,1)} %slice.666), channel_id=1, source_target_pairs={{0,2},{1,3},{2,0},{3,1},{4,6},{5,7},{6,4},{7,5},{8,10},{9,11},{10,... | collective-permute-start | bytes 4718600 | tf_op jit(solution)/shard_map/ppermute | solution.py:331
  887.5 38.7 %collective-permute-start.38 = (bf16[192,2304]{1,0:T(8,128)(2,1)S(1)}, bf16[192,2304]{1,0:T(8,128)(2,1)S(1)}, u32[]{:S(2)}, u32[]{:S(2)}) collective-permute-start(bf16[192,2304]{1,0:T(8,128)(2,1)S(1)} %slice.670), channel_id=1, source_target_pairs={{0,2},{1,3},{2,0},{3,1},{4,6},{5,7},{6,4},{7,5},{8,10},{9,11},{10,... | collective-permute-start | bytes 2654216 | tf_op jit(solution)/shard_map/ppermute | solution.py:331
  949.6 58.9 %all-to-all-start.14 = ((bf16[3,4,1024,192]{2,3,0,1:T(8,128)(2,1)}), bf16[3,4,1024,192]{2,3,0,1:T(8,128)(2,1)}, u32[]{:S(2)}, u32[]{:S(2)}) async-start(bf16[3,4,1024,192]{2,3,0,1:T(8,128)(2,1)} %maximum_bitcast_fusion), calls=%async_computation.14 | async-start | bytes 9437184 | tf_op jit(solution)/shard_map/all_to_all | solution.py:688
  (189 other events, 2772.0 us)
Sparse Core Ops, SparseCore 0:
  927.4 242.0 all-reduce.2

commit v3 on v2

v3 whole, which is shorter than its diff:
```python
import functools
import math

import jax
import jax.numpy as jnp
from jax import lax
from jax.experimental import pallas as pl
from jax.experimental.pallas import tpu as pltpu
from jax.sharding import PartitionSpec as P

HEADS = 12
HD = 64
FF = 2048
TOP = 2
HEAD_GROUPS = 4
KEY_SPAN = 512
VMEM_LIMIT = 60 * 1024 * 1024


HIGHEST = lax.Precision.HIGHEST
EPSILON = 1e-06
NEGATIVE = -1e30


BOTH = ("ctx", "fsdp")


def swap(values, axis, mask):
    count = lax.axis_size(axis)
    return lax.ppermute(values, axis, [(i, i ^ mask) for i in range(count)])


def gather_shards(shard):
    near = swap(shard, "fsdp", 1)
    far = swap(shard, "fsdp", 2)
    return (shard, near, far, swap(far, "fsdp", 1))


def in_order(shards):
    own = lax.axis_index("fsdp")
    buffer = jnp.zeros((len(shards),) + shards[0].shape, shards[0].dtype)
    for k, shard in enumerate(shards):
        buffer = lax.dynamic_update_index_in_dim(buffer, shard, own ^ k, 0)
    return buffer


NT = (((1,), (1,)), ((), ()))


def _dot(a, b):
    return jnp.dot(a, b, preferred_element_type=jnp.float32)


def _dot_nt(a, b):
    return lax.dot_general(a, b, NT, preferred_element_type=jnp.float32)


def _flip(values):
    return values.astype(jnp.float32).T.astype(values.dtype)


def _shape(shape, dtype=jnp.bfloat16):
    return jax.ShapeDtypeStruct(shape, dtype)


def _whole(shape):
    return pl.BlockSpec(tuple(shape), lambda *_: (0,) * len(shape))


def operands(shards, part=None):
    if isinstance(shards, (tuple, list)):
        arrays, rows, place = shards, shards[0].shape[0], lambda m, k: 0
    else:
        arrays, rows, place = (shards,) * 4, shards.shape[0] // 4, lambda m, k: m[0] ^ k
    width = arrays[0].shape[1]
    if part is None:
        specs = [
            pl.BlockSpec((rows, width), lambda i, m, k=k: (place(m, k), 0)) for k in range(4)
        ]
    else:
        size, first = part
        specs = [
            pl.BlockSpec((rows, size), lambda i, m, k=k: (place(m, k), first + (m[0] ^ i)))
            for k in range(4)
        ]
    return list(arrays), specs


def call(body, meta, inputs, outputs, scratch=(), flops=0, in_specs=None, out_specs=None, grid=(1,)):
    moved = sum(math.prod(a.shape) * a.dtype.itemsize for a in (*inputs, *outputs))
    return pl.pallas_call(
        body,
        grid_spec=pltpu.PrefetchScalarGridSpec(
            num_scalar_prefetch=1,
            grid=grid,
            in_specs=in_specs or [_whole(a.shape) for a in inputs],
            out_specs=out_specs or [_whole(a.shape) for a in outputs],
            scratch_shapes=list(scratch),
        ),
        out_shape=list(outputs),
        compiler_params=pltpu.CompilerParams(vmem_limit_bytes=VMEM_LIMIT),
        cost_estimate=pl.CostEstimate(flops=flops, bytes_accessed=moved, transcendentals=0),
    )(meta, *inputs)


def _stack(refs, cols=slice(None)):
    return jnp.concatenate([w[:, cols] for w in refs], axis=0)


def _mine(blocks, own):
    return jnp.concatenate([blocks[own ^ k] for k in range(4)], axis=1)


def _norm(rows, gain):
    inverse = lax.rsqrt(jnp.mean(rows * rows, axis=-1, keepdims=True) + EPSILON)
    return rows * inverse * gain


def _norm_back(rows, gain, grad):
    inverse = lax.rsqrt(jnp.mean(rows * rows, axis=-1, keepdims=True) + EPSILON)
    weighted = grad * gain
    scaled = rows * inverse
    back = inverse * (weighted - scaled * jnp.mean(weighted * scaled, axis=-1, keepdims=True))
    return back, jnp.sum(grad * scaled, axis=0, keepdims=True)


def _split(rows, blocks):
    width = rows.shape[1] // len(blocks)
    for b, ref in enumerate(blocks):
        ref[...] = rows[:, b * width : (b + 1) * width]


def _turn(rows, cosine, sine, sign):
    lane = lax.broadcasted_iota(jnp.int32, cosine.shape, 1)
    low = lane % HD < HD // 2
    turned = []
    for b in range(rows.shape[1] // 128):
        part = rows[:, b * 128 : (b + 1) * 128]
        other = jnp.where(low, pltpu.roll(part, 128 - HD // 2, 1), pltpu.roll(part, HD // 2, 1))
        turned.append(part * cosine + sign * (other * sine))
    return jnp.concatenate(turned, axis=1)


def _pre_kernel(meta, x, gain, cosine, sine, w0, w1, w2, w3, keep, send, *rest):
    qkv, (blocks, heads) = rest[:4], rest[4:]
    own, line = meta[0], meta[1]
    width = x.shape[1]
    normed = _norm(x[...], gain[...]).astype(jnp.bfloat16)
    _split(normed, [blocks.at[b] for b in range(4)])
    for j in range(2):
        keep[j] = blocks[own ^ (2 * j)]
        send[j] = blocks[own ^ (2 * j + 1)]
    piece = x.shape[0] // 2
    mine = _mine(blocks, own)
    for kind in range(3):
        mixed = _dot(mine, _stack((w0, w1, w2, w3), slice(kind * width, (kind + 1) * width)))
        if kind < 2:
            mixed = _turn(mixed, cosine[...], sine[...], 1.0)
        if kind == 0:
            mixed = mixed * 0.125
        turned = mixed.T.astype(jnp.bfloat16)
        block = width // 4
        for b in range(4):
            for p in range(2):
                heads[b, p, kind] = turned[
                    b * block : (b + 1) * block, p * piece : (p + 1) * piece
                ]
    for k in range(4):
        qkv[k][...] = heads[line ^ k]


def pre(meta, x, gain, tables, shards):
    rows, width = x.shape
    block = width // 4
    outs = [_shape((2, rows, block))] * 2 + [_shape((2, 3, block, rows // 2))] * 4
    shards, specs = operands(shards)
    inputs = (x, gain, *tables)
    got = call(
        _pre_kernel,
        meta,
        (*inputs, *shards),
        outs,
        [
            pltpu.VMEM((4, rows, block), jnp.bfloat16),
            pltpu.VMEM((4, 2, 3, block, rows // 2), jnp.bfloat16),
        ],
        flops=6 * rows * width * width,
        in_specs=[_whole(a.shape) for a in inputs] + specs,
    )
    return got[0], got[1], got[2:6]


def _pre_back_kernel(meta, x, gain, cosine, sine, resid, *rest):
    qkv, w = rest[:4], rest[4:8]
    mixed_out, resid_out, gain_out, heads, blocks = rest[8:]
    own, line = meta[0], meta[1]
    width = x.shape[1]
    for k in range(4):
        heads[line ^ k] = qkv[k][...]
    for kind in range(3):
        mixed = jnp.concatenate(
            [
                jnp.concatenate([heads[b, p, kind] for b in range(4)], axis=0)
                for p in range(2)
            ],
            axis=1,
        )
        mixed = mixed.astype(jnp.float32).T
        if kind < 2:
            mixed = mixed * (0.125 if kind == 0 else 1.0)
            mixed = _turn(mixed, cosine[...], sine[...], -1.0)
        mixed_out[0, :, kind * width : (kind + 1) * width] = mixed.astype(jnp.bfloat16)
    grads = _dot_nt(mixed_out[0], _stack(w))
    _split(grads, [blocks.at[own ^ k] for k in range(4)])
    grad = jnp.concatenate([blocks[b] for b in range(4)], axis=1)
    back, grad_gain = _norm_back(x[...], gain[...], grad)
    resid_out[...] = resid[...] + back
    gain_out[...] = grad_gain


def pre_back(meta, x, gain, tables, resid, qkv, shards):
    rows, width = x.shape
    shards, specs = operands(shards)
    inputs = (x, gain, *tables, resid, *qkv)
    return call(
        _pre_back_kernel,
        meta,
        (*inputs, *shards),
        [
            _shape((1, rows, 3 * width)),
            _shape((rows, width), jnp.float32),
            _shape((1, width), jnp.float32),
        ],
        [
            pltpu.VMEM((4, 2, 3, width // 4, rows // 2), jnp.bfloat16),
            pltpu.VMEM((4, rows, width // 4), jnp.float32),
        ],
        flops=6 * rows * width * width,
        in_specs=[_whole(a.shape) for a in inputs] + specs,
    )


def _post_kernel(meta, x, gain, o0, o1, o2, o3, w0, w1, w2, w3, *rest):
    after, plain, blocks_out, keep, send, att_keep, att_send, att = rest
    own, line = meta[0], meta[1]
    piece = x.shape[0] // 2
    for k, o in enumerate((o0, o1, o2, o3)):
        for p in range(2):
            att[line ^ k, p * piece : (p + 1) * piece, :] = _flip(o[p])
    for j in range(2):
        att_keep[j] = att[own ^ (2 * j)]
        att_send[j] = att[own ^ (2 * j + 1)]
    rows = x[...] + _dot(_mine(att, own), _stack((w0, w1, w2, w3)))
    after[...] = rows
    normed = _norm(rows, gain[...]).astype(jnp.bfloat16)
    plain[...] = normed
    _split(normed, [att.at[b] for b in range(4)])
    blocks_out[...] = att[...]
    for j in range(2):
        keep[j] = att[own ^ (2 * j)]
        send[j] = att[own ^ (2 * j + 1)]


def post(meta, x, gain, heads, shards):
    rows, width = x.shape
    block = width // 4
    shards, specs = operands(shards)
    inputs = (x, gain, *heads)
    return call(
        _post_kernel,
        meta,
        (*inputs, *shards),
        [_shape((rows, width), jnp.float32), _shape((rows, width)), _shape((4, rows, block))]
        + [_shape((2, rows, block))] * 4,
        [pltpu.VMEM((4, rows, block), jnp.bfloat16)],
        flops=2 * rows * width * width,
        in_specs=[_whole(a.shape) for a in inputs] + specs,
    )


def _post_back_kernel(meta, x, gain, resid, grad, w0, w1, w2, w3, *rest):
    heads, (resid_out, branch, gain_out, att) = rest[:4], rest[4:]
    own, line = meta[0], meta[1]
    back, grad_gain = _norm_back(x[...], gain[...], grad[...])
    gain_out[...] = grad_gain
    rows = resid[...] + back
    resid_out[...] = rows
    rows = rows.astype(jnp.bfloat16)
    branch[0] = rows
    grads = _dot_nt(rows, _stack((w0, w1, w2, w3))).astype(jnp.bfloat16)
    _split(grads, [att.at[own ^ k] for k in range(4)])
    piece = x.shape[0] // 2
    for k in range(4):
        for p in range(2):
            heads[k][p] = _flip(att[line ^ k, p * piece : (p + 1) * piece, :])


def post_back(meta, x, gain, resid, grad, shards):
    rows, width = x.shape
    block = width // 4
    shards, specs = operands(shards)
    inputs = (x, gain, resid, grad)
    got = call(
        _post_back_kernel,
        meta,
        (*inputs, *shards),
        [_shape((2, block, rows // 2))] * 4
        + [
            _shape((rows, width), jnp.float32),
            _shape((1, rows, width)),
            _shape((1, width), jnp.float32),
        ],
        [pltpu.VMEM((4, rows, block), jnp.bfloat16)],
        flops=2 * rows * width * width,
        in_specs=[_whole(a.shape) for a in inputs] + specs,
    )
    return got[:4], got[4], got[5], got[6]


def _mlp_kernel(meta, x, blocks, *rest):
    gates, ups, downs = rest[:4], rest[4:8], rest[8:12]
    out, mixed, keep, send, acc = rest[12:]
    own, step = meta[0], pl.program_id(0)
    rows = _mine(blocks, own)
    gate = _dot(rows, _stack(gates))
    up = _dot(rows, _stack(ups))
    mixed[0], mixed[1] = gate, up
    hidden = (gate * jax.nn.sigmoid(gate) * up).astype(jnp.bfloat16)
    for k in range(4):

        @pl.when(step == k)
        def _(k=k):
            (send if k % 2 else keep)[k // 2] = hidden
            part = _dot(hidden, downs[k][...])
            if k == 0:
                acc[...] = x[...] + part
            elif k < 3:
                acc[...] += part
            else:
                out[...] = acc[...] + part


def mlp_width(shards):
    first = shards[0] if isinstance(shards, (tuple, list)) else shards
    return first.shape[1] // 2


def mlp(meta, x, blocks, shards_in, shards_out):
    rows, width = x.shape
    hidden = mlp_width(shards_in)
    part = hidden // 4
    gates, gate_specs = operands(shards_in, (part, 0))
    ups, up_specs = operands(shards_in, (part, 4))
    downs, down_specs = operands(shards_out)
    return call(
        _mlp_kernel,
        meta,
        (x, blocks, *gates, *ups, *downs),
        [
            _shape((rows, width), jnp.float32),
            _shape((2, rows, hidden), jnp.float32),
            _shape((2, rows, part)),
            _shape((2, rows, part)),
        ],
        [pltpu.VMEM((rows, width), jnp.float32)],
        flops=6 * rows * width * hidden,
        in_specs=[_whole(x.shape), _whole(blocks.shape), *gate_specs, *up_specs, *down_specs],
        out_specs=[
            _whole((rows, width)),
            pl.BlockSpec((2, rows, part), lambda i, m: (0, 0, m[0] ^ i)),
            _whole((2, rows, part)),
            _whole((2, rows, part)),
        ],
        grid=(4,),
    )


def _mlp_back_kernel(meta, branch, mixed, *rest):
    gates, ups, downs = rest[:4], rest[4:8], rest[8:12]
    grad_mixed, grad_out, grad_hidden, acc, turned = rest[12:]
    own, step = meta[0], pl.program_id(0)
    for k in range(4):

        @pl.when(step == k)
        def _(k=k):
            grad_hidden[...] = _dot_nt(branch[0], downs[k][...]).astype(jnp.bfloat16)

    grad_h = grad_hidden[...].astype(jnp.float32)
    gate, up = mixed[0], mixed[1]
    sigmoid = jax.nn.sigmoid(gate)
    grad_gate = (grad_h * up * sigmoid * (1.0 + gate * (1.0 - sigmoid))).astype(jnp.bfloat16)
    grad_up = (grad_h * gate * sigmoid).astype(jnp.bfloat16)
    grad_mixed[0], grad_mixed[1] = grad_gate, grad_up
    part = _dot_nt(grad_gate, _stack(gates)) + _dot_nt(grad_up, _stack(ups))

    @pl.when(step == 0)
    def _():
        acc[...] = part

    @pl.when((step > 0) & (step < 3))
    def _():
        acc[...] += part

    @pl.when(step == 3)
    def _():
        _split(acc[...] + part, [turned.at[own ^ k] for k in range(4)])
        grad_out[...] = jnp.concatenate([turned[b] for b in range(4)], axis=1)


def mlp_back(meta, branch, mixed, shards_in, shards_out):
    _, rows, width = branch.shape
    hidden = mixed.shape[2]
    part = hidden // 4
    block = width // 4
    gates, gate_specs = operands(shards_in, (part, 0))
    ups, up_specs = operands(shards_in, (part, 4))
    downs, down_specs = operands(shards_out)
    return call(
        _mlp_back_kernel,
        meta,
        (branch, mixed, *gates, *ups, *downs),
        [_shape((2, rows, hidden)), _shape((rows, width), jnp.float32)],
        [
            pltpu.VMEM((rows, part), jnp.bfloat16),
            pltpu.VMEM((rows, width), jnp.float32),
            pltpu.VMEM((4, rows, block), jnp.float32),
        ],
        flops=6 * rows * width * hidden,
        in_specs=[
            _whole(branch.shape),
            pl.BlockSpec((2, rows, part), lambda i, m: (0, 0, m[0] ^ i)),
            *gate_specs,
            *up_specs,
            *down_specs,
        ],
        out_specs=[
            pl.BlockSpec((2, rows, part), lambda i, m: (0, 0, m[0] ^ i)),
            _whole((rows, width)),
        ],
        grid=(4,),
    )


def _grad_kernel(meta, left, left_near, right, right_near, own, send, flipped):
    rows, depth = left.shape[1:]

    @pl.when((pl.program_id(0) == 0) & (pl.program_id(1) == 0))
    def _():
        for j in range(2):
            flipped[j * depth : (j + 1) * depth, :rows] = _flip(left[j])
            flipped[j * depth : (j + 1) * depth, rows:] = _flip(left_near[j])

    both = jnp.concatenate([right[0], right_near[0]], axis=0)
    grads = _dot(flipped[...], both).astype(jnp.bfloat16)
    own[...] = grads[:depth]
    send[...] = grads[depth:]


def weight_grad(meta, left, left_near, right, right_near):
    groups, rows, width = right.shape
    depth = left.shape[2]
    chunk = 512 if width % 768 else 768
    steps = width // chunk
    right_spec = pl.BlockSpec((1, rows, chunk), lambda g, i, m: (g, 0, i))
    out_spec = pl.BlockSpec((depth, chunk), lambda g, i, m: (0, g * steps + i))
    return call(
        _grad_kernel,
        meta,
        (left, left_near, right, right_near),
        [_shape((depth, groups * width))] * 2,
        [pltpu.VMEM((2 * depth, 2 * rows), jnp.bfloat16)],
        flops=8 * rows * depth * groups * width,
        in_specs=[_whole(left.shape), _whole(left.shape), right_spec, right_spec],
        out_specs=[out_spec, out_spec],
        grid=(groups, steps),
    )


def _mask(first_key, keys, query_pos, query_start, copies):
    key_pos = first_key + lax.broadcasted_iota(jnp.int32, (keys, query_pos.shape[1]), 0)
    allowed = (key_pos <= query_pos) & (key_pos >= query_start)
    return jnp.concatenate([allowed] * copies, axis=1)


def _tables(meta, parts):
    return (lambda s: meta[2 + s], lambda k: meta[2 + 8 * parts + k])


def _query_geometry(place, ends, count, piece, key_span):
    query_pos = place * piece + lax.broadcasted_iota(jnp.int32, (1, piece), 1)
    query_start = jnp.zeros_like(query_pos)
    first = place * piece
    least = jnp.int32(0)
    for k in range(count):
        last = k == count - 1
        query_start = jnp.where(query_pos >= ends(k), query_pos if last else ends(k), query_start)
        least = jnp.where(first >= ends(k), first if last else ends(k), least)
    return (query_pos, query_start, least // key_span, (first + piece - 1) // key_span + 1)


def _stack_heads(rows, heads):
    head_dim = rows.shape[0] // heads
    head = lax.broadcasted_iota(jnp.int32, rows.shape, 0) // head_dim
    zero = jnp.zeros_like(rows)
    return jnp.concatenate([jnp.where(head == h, rows, zero) for h in range(heads)], axis=1)


def _own_heads(acc, heads, piece):
    head_dim = acc.shape[0] // heads
    return jnp.concatenate(
        [
            acc[h * head_dim : (h + 1) * head_dim, h * piece : (h + 1) * piece]
            for h in range(heads)
        ],
        axis=0,
    )


def _attend_kernel(heads, count, key_span, parts, meta, *refs):
    inputs, o, (keep, lse, keys, values_t) = (
        refs[: 4 * parts],
        refs[4 * parts : 4 * parts + 4],
        refs[4 * parts + 4 :],
    )
    width, piece = inputs[0].shape[2:]
    place, ends = _tables(meta, parts)
    for s in range(8 * parts):
        at = pl.ds(pl.multiple_of(place(s) * piece, piece), piece)
        keys[at, :] = _flip(inputs[s // 2][s % 2, 1])
        values_t[:, at] = inputs[s // 2][s % 2, 2]
    cols = heads * piece
    for s in range(8):
        query_pos, query_start, begin, end = _query_geometry(
            place(s), ends, count, piece, key_span
        )
        stacked = _stack_heads(inputs[s // 2][s % 2, 0], heads)

        def advance(block, carried):
            run_max, run_sum, acc = carried
            first = pl.multiple_of(block * key_span, key_span)
            scores = _dot(keys[pl.ds(first, key_span), :], stacked)
            allowed = _mask(first, key_span, query_pos, query_start, heads)
            scores = jnp.where(allowed, scores, NEGATIVE)
            new_max = jnp.maximum(run_max, jnp.max(scores, axis=0, keepdims=True))
            weights = jnp.exp(scores - new_max)
            factor = jnp.exp(run_max - new_max)
            run_sum = run_sum * factor + jnp.sum(weights, axis=0, keepdims=True)
            part = _dot(values_t[:, pl.ds(first, key_span)], weights.astype(jnp.bfloat16))
            return (new_max, run_sum, acc * factor + part)

        run_max, run_sum, acc = lax.fori_loop(
            begin,
            end,
            advance,
            (
                jnp.full((1, cols), NEGATIVE, jnp.float32),
                jnp.zeros((1, cols), jnp.float32),
                jnp.zeros((width, cols), jnp.float32),
            ),
        )
        kept = _own_heads(acc / run_sum, heads, piece)
        keep[s] = kept
        o[s // 2][s % 2] = kept.astype(jnp.bfloat16)
        lse[s] = run_max + jnp.log(run_sum)


def attend(meta, inputs, count):
    _, _, width, piece = inputs[0].shape
    heads = width // HD
    parts = len(inputs) // 4
    slots = parts * 8 * piece
    got = call(
        functools.partial(_attend_kernel, heads, count, KEY_SPAN, parts),
        meta,
        inputs,
        [_shape((2, width, piece))] * 4
        + [_shape((8, width, piece), jnp.float32), _shape((8, 1, heads * piece), jnp.float32)],
        [
            pltpu.VMEM((slots, width), jnp.bfloat16),
            pltpu.VMEM((width, slots), jnp.bfloat16),
        ],
        flops=32 * piece * slots * width,
    )
    return got[:4], got[4], got[5]


def _attend_back_kernel(heads, count, key_span, parts, meta, *refs):
    inputs, grads, (keep, lse), rest = (
        refs[: 4 * parts],
        refs[4 * parts : 4 * parts + 4],
        refs[4 * parts + 4 : 4 * parts + 6],
        refs[4 * parts + 6 :],
    )
    gq, gkv = rest[0], rest[1 : 1 + parts]
    keys, keys_t, values, gkeys, gvalues = rest[1 + parts :]
    width, piece = inputs[0].shape[2:]
    head_dim = width // heads
    place, ends = _tables(meta, parts)
    for s in range(8 * parts):
        at = pl.ds(pl.multiple_of(place(s) * piece, piece), piece)
        key_rows = inputs[s // 2][s % 2, 1]
        keys_t[:, at] = key_rows
        keys[at, :] = _flip(key_rows)
        values[at, :] = _flip(inputs[s // 2][s % 2, 2])
    gkeys[...] = jnp.zeros_like(gkeys)
    gvalues[...] = jnp.zeros_like(gvalues)
    for s in range(8):
        query_pos, query_start, begin, end = _query_geometry(
            place(s), ends, count, piece, key_span
        )
        stacked = _stack_heads(inputs[s // 2][s % 2, 0], heads)
        grad = grads[s // 2][s % 2]
        grad_stacked = _stack_heads(grad, heads)
        product = grad.astype(jnp.float32) * keep[s]
        delta = jnp.concatenate(
            [
                jnp.sum(product[h * head_dim : (h + 1) * head_dim, :], axis=0, keepdims=True)
                for h in range(heads)
            ],
            axis=1,
        )
        log_sum = lse[s]

        def retreat(block, acc):
            first = pl.multiple_of(block * key_span, key_span)
            at = pl.ds(first, key_span)
            scores = _dot(keys[at, :], stacked)
            allowed = _mask(first, key_span, query_pos, query_start, heads)
            probs = jnp.where(allowed, jnp.exp(scores - log_sum), 0.0)
            grad_probs = _dot(values[at, :], grad_stacked)
            grad_scores = (probs * (grad_probs - delta)).astype(jnp.bfloat16)
            gvalues[:, at] += _dot_nt(grad_stacked, probs.astype(jnp.bfloat16))
            gkeys[:, at] += _dot_nt(stacked, grad_scores)
            return acc + _dot(keys_t[:, at], grad_scores)

        acc = lax.fori_loop(begin, end, retreat, jnp.zeros((width, heads * piece), jnp.float32))
        gq[s] = _own_heads(acc, heads, piece).astype(jnp.bfloat16)
    for s in range(8 * parts):
        at = pl.ds(pl.multiple_of(place(s) * piece, piece), piece)
        out = gkv[s // 8]
        out[s % 8, 0] = gkeys[:, at].astype(out.dtype)
        out[s % 8, 1] = gvalues[:, at].astype(out.dtype)


def attend_back(meta, inputs, grads, keep, lse, count):
    _, _, width, piece = inputs[0].shape
    heads = width // HD
    parts = len(inputs) // 4
    slots = parts * 8 * piece
    got = call(
        functools.partial(_attend_back_kernel, heads, count, KEY_SPAN, parts),
        meta,
        (*inputs, *grads, keep, lse),
        [_shape((8, width, piece)), _shape((8, 2, width, piece), jnp.float32)]
        + [_shape((8, 2, width, piece))] * (parts - 1),
        [
            pltpu.VMEM((slots, width), jnp.bfloat16),
            pltpu.VMEM((width, slots), jnp.bfloat16),
            pltpu.VMEM((slots, width), jnp.bfloat16),
            pltpu.VMEM((width, slots), jnp.float32),
            pltpu.VMEM((width, slots), jnp.float32),
        ],
        flops=80 * piece * slots * width,
    )
    return got[0], got[1], got[2:]


def _merge_kernel(meta, gq, own, *rest):
    arrived, out = rest[:-4], rest[-4:]
    for s in range(8):
        total = own[s]
        for other in arrived:
            total = total + other[s].astype(jnp.float32)
        out[s // 2][s % 2, 0] = gq[s]
        out[s // 2][s % 2, 1:3] = total.astype(jnp.bfloat16)


def merge(meta, gq, own, arrived):
    _, width, piece = gq.shape
    return call(
        _merge_kernel, meta, (gq, own, *arrived), [_shape((2, 3, width, piece))] * 4
    )


def _halve_kernel(meta, first, second, sent, kept):
    summed = (first[...].astype(jnp.float32) + second[...].astype(jnp.float32)).astype(jnp.bfloat16)
    half = sent.shape[1]
    left, right = summed[:, :half], summed[:, half:]
    side = meta[0] == 0
    sent[...] = jnp.where(side, right, left)
    kept[...] = jnp.where(side, left, right)


def _quarter_kernel(meta, first, second, *rest):
    parts, summed = rest[:-1], rest[-1]
    summed[...] = (first[...].astype(jnp.float32) + second[...].astype(jnp.float32)).astype(
        jnp.bfloat16
    )
    chunk = parts[0].shape[0]
    for k, part in enumerate(parts):
        at = pl.multiple_of((meta[1] ^ k) * chunk, chunk)
        part[...] = summed[pl.ds(at, chunk), :]


def _place_kernel(meta, other, *refs):
    out, parts = refs[-1], refs[:-1]
    _, rows, width = out.shape
    lines = len(parts) // 2
    chunk, half = rows // lines, width // 2
    side = meta[0] == 0
    for k in range(lines):
        at = pl.multiple_of((meta[1] ^ k) * chunk, chunk)
        own = parts[k][...].astype(jnp.float32)
        near = parts[lines + k][...].astype(jnp.float32)
        out[0, pl.ds(at, chunk), :half] = jnp.where(side, own, near)
        out[0, pl.ds(at, chunk), half:] = jnp.where(side, near, own)
    out[1] = other[...].astype(jnp.float32)


def reduce_last(place, own, arrived, other, held):
    lines = lax.axis_size("ctx") // 2
    rows, width = own.shape
    chunk, half = rows // lines, width // 2
    if chunk % 16:
        summed = lax.psum(own + arrived, "ctx")
        return jnp.stack([summed, other]).astype(jnp.float32), held
    sent, kept = call(_halve_kernel, place, (own, arrived), [_shape((rows, half))] * 2)
    parts = call(
        _quarter_kernel,
        place,
        (kept, swap(sent, "ctx", 1)),
        [_shape((chunk, half))] * lines,
        [pltpu.VMEM((rows, half), jnp.bfloat16)],
    )
    summed = parts[0].astype(jnp.float32)
    for k in range(1, lines):
        summed = summed + swap(parts[k], "ctx", 2 * k).astype(jnp.float32)
    summed = summed.astype(jnp.bfloat16)
    column = [swap(summed, "ctx", 2 * k) if k else summed for k in range(lines)]
    column, held = lax.optimization_barrier((column, held))
    parts = column + [swap(c, "ctx", 1) for c in column]
    return (
        call(
            _place_kernel, place, (other, *parts), [_shape((2, rows, width), jnp.float32)]
        )[0],
        held,
    )


def _expert_kernel(units, meta, *refs):
    xs, cs = refs[:units], refs[units : 2 * units]
    router, ids, w_in, w_out = refs[2 * units : 2 * units + 4]
    outs = refs[2 * units + 4 :]
    parts, backs = outs[:units], outs[units : 2 * units]
    rows_out, grads_out, hidden_out, gate_out, up_out, dots_out = outs[2 * units : 2 * units + 6]
    gates, ups, downs, x, c = outs[2 * units + 6 :]
    step = pl.program_id(0)
    tiles = pl.num_programs(0) // units

    @pl.when(step == 0)
    def _():
        width = w_in.shape[2]
        for f in range(4):
            part = slice(f * width, (f + 1) * width)
            gates[part, :] = w_in[f, 0]
            ups[part, :] = w_in[f, 1]
            downs[part, :] = w_out[f]

    for u in range(units):

        @pl.when(step // tiles == u)
        def _(u=u):
            x[...] = xs[u][...]
            c[...] = cs[u][...]

    rows = x[...]
    rows_out[...] = rows
    incoming = c[...].astype(jnp.float32)
    logits = _dot(rows, router[...])
    lane = lax.broadcasted_iota(jnp.int32, logits.shape, 1)
    gap = jnp.sum(
        jnp.where(lane == meta[0], logits, 0.0)
        - jnp.where(lane.astype(jnp.float32) == ids[...], logits, 0.0),
        axis=1,
        keepdims=True,
    )
    grads = (jax.nn.sigmoid(gap) * incoming).astype(jnp.bfloat16)
    grads_out[...] = grads
    gate = _dot(rows, gates[...])
    up = _dot(rows, ups[...])
    sigmoid = jax.nn.sigmoid(gate)
    silu = gate * sigmoid
    hidden = (silu * up).astype(jnp.bfloat16)
    hidden_out[...] = hidden
    part = _dot_nt(hidden, downs[...])
    dots_out[...] = jnp.sum(part * incoming, axis=1, keepdims=True)
    grad_h = _dot(grads, downs[...]).astype(jnp.bfloat16).astype(jnp.float32)
    grad_gate = (grad_h * up * sigmoid * (1.0 + gate * (1.0 - sigmoid))).astype(jnp.bfloat16)
    grad_up = (grad_h * silu).astype(jnp.bfloat16)
    gate_out[...] = grad_gate
    up_out[...] = grad_up
    back = _dot_nt(grad_gate, gates[...]) + _dot_nt(grad_up, ups[...])
    for u in range(units):

        @pl.when(step // tiles == u)
        def _(u=u):
            parts[u][...] = part.astype(jnp.bfloat16)
            backs[u][...] = back.astype(jnp.bfloat16)


def experts(meta, xs, cs, router, ids, w_in, w_out):
    units, (rows, width), tile = len(xs), xs[0].shape, 256
    tiles, hidden = rows // tile, w_out.shape[2]
    total_rows = units * rows
    slabs = [
        pl.BlockSpec((tile, width), lambda i, m, u=u: (jnp.clip(i - u * tiles, 0, tiles - 1), 0))
        for u in range(units)
    ]

    def rowed(columns):
        return pl.BlockSpec((tile, columns), lambda i, m: (i, 0))

    got = call(
        functools.partial(_expert_kernel, units),
        meta,
        (*xs, *cs, router, ids, w_in, w_out),
        [_shape((rows, width))] * (2 * units)
        + [_shape((total_rows, width))] * 2
        + [_shape((total_rows, hidden))] * 3
        + [_shape((total_rows, 1), jnp.float32)],
        [pltpu.VMEM((width, hidden), jnp.bfloat16)] * 3
        + [pltpu.VMEM((tile, width), jnp.bfloat16)] * 2,
        flops=12 * total_rows * width * hidden,
        in_specs=slabs
        + slabs
        + [_whole(router.shape), rowed(1), _whole(w_in.shape), _whole(w_out.shape)],
        out_specs=slabs + slabs + [rowed(width)] * 2 + [rowed(hidden)] * 3 + [rowed(1)],
        grid=(units * tiles,),
    )
    return got[:units], got[units : 2 * units], got[2 * units :]


def layout(lengths_row, order_row, piece_len):
    all_slots = order_row.shape[0] * piece_len
    position = (
        order_row[:, None] * piece_len + jnp.arange(piece_len, dtype=jnp.int32)[None, :]
    ).reshape(all_slots)
    count = jnp.arange(lengths_row.shape[0], dtype=jnp.int32)
    seq_ends = jnp.sum(
        jnp.where(count[:, None] <= count[None, :], lengths_row[:, None], 0), axis=0, dtype=jnp.int32
    )
    segment = jnp.sum(
        (position[:, None] >= seq_ends[None, :]).astype(jnp.int32), axis=1, dtype=jnp.int32
    )
    seq_start = jnp.sum(
        jnp.where(segment[:, None] > count[None, :], lengths_row[None, :], 0),
        axis=1,
        dtype=jnp.int32,
    )
    return (seq_ends, position - seq_start)


def angles(offset):
    freq_table = jnp.exp(
        jnp.arange(HD // 2, dtype=jnp.float32) * (-2.0 * math.log(10000.0) / HD)
    )
    theta = offset.astype(jnp.float32)[..., None] * freq_table
    cosine, sine = jnp.cos(theta), jnp.sin(theta)
    return (
        jnp.tile(cosine, (1, 256 // HD)),
        jnp.tile(jnp.concatenate([-sine, sine], axis=1), (1, 128 // HD)),
    )


def hidden_back(gate_pre, up_pre, grad_hidden):
    sigmoid_gate = jax.nn.sigmoid(gate_pre)
    grad_gate = grad_hidden * up_pre * sigmoid_gate * (1.0 + gate_pre * (1.0 - sigmoid_gate))
    grad_up = grad_hidden * gate_pre * sigmoid_gate
    return (grad_gate.astype(jnp.bfloat16), grad_up.astype(jnp.bfloat16))


def head_parts():
    return lax.axis_size("ctx") // HEAD_GROUPS


def exchange(values):
    return [values[0]] + [swap(values[k], "ctx", k * head_parts()) for k in range(1, 4)]


def attend_forward(meta, count, resid, gain, tables, w_in, early):
    keep, send, qkv = pre(meta, resid, gain, tables, w_in)
    qkv = exchange(qkv)
    inputs = list(qkv)
    for part in range(1, head_parts()):
        inputs += [swap(values, "ctx", part) for values in qkv]
    qkv[1], early = lax.optimization_barrier((qkv[1], early))
    inputs[1] = qkv[1]
    heads, acc, lse = attend(meta, inputs, count)
    return heads, (keep, send, inputs, acc, lse), early


def near(*values):
    return [swap(v, "fsdp", 1) for v in values]


def add_arrived(grads):
    return grads[0] + swap(grads[1], "fsdp", 2)


def total(bucket, grads):
    count = lax.axis_size("ctx")
    ring = [[(i + bucket) % count for i in range(count)]]
    return lax.psum(tuple(grads), "ctx", axis_index_groups=ring)


def total_small(values):
    for axis in BOTH:
        step = 1
        while step < lax.axis_size(axis):
            values = values + swap(values, axis, step)
            step *= 2
    return values


def per_device(
    tokens,
    cotangent,
    lengths,
    piece_order,
    routes,
    attn_in,
    attn_out,
    norm_gain,
    mlp_in,
    mlp_out,
    router,
    expert_in,
    expert_out,
):
    tok_rows, model_width = tokens.shape[1:]
    shard_width = router.shape[0]
    num_experts = router.shape[1]
    own_ctx, own_fsdp = lax.axis_index("ctx"), lax.axis_index("fsdp")
    ctx_count, fsdp_count = lax.axis_size("ctx"), lax.axis_size("fsdp")
    units = ctx_count * fsdp_count // num_experts
    hid_unit = expert_out.shape[0] // fsdp_count
    members = [
        [i for i in range(ctx_count * fsdp_count) if i % units == lane] for lane in range(units)
    ]

    def dispatch(values):
        return lax.all_to_all(values, BOTH, 0, 0, tiled=True, axis_index_groups=members)

    def to_units(values):
        return [values] + [swap(values, BOTH, k) for k in range(1, units)]

    def from_units(partial):
        summed = partial[0].astype(jnp.float32)
        for k in range(1, units):
            summed = summed + swap(partial[k], BOTH, k).astype(jnp.float32)
        return summed

    def gathered(shard):
        return lax.all_gather(shard, "fsdp", axis=0, tiled=True)

    seq_ends, offset = layout(lengths[0], piece_order[0], tok_rows // 2)
    tables = angles(lax.dynamic_slice_in_dim(offset, own_ctx * tok_rows, tok_rows, 0))
    parts = ctx_count // HEAD_GROUPS
    line, side = own_ctx // parts, own_ctx % parts
    order = piece_order[0].reshape(HEAD_GROUPS, parts, 2)
    place = [order[line ^ k, side ^ part] for part in range(parts) for k in range(HEAD_GROUPS)]
    meta = jnp.concatenate([jnp.stack([own_fsdp, line]), jnp.concatenate(place), seq_ends])
    at_ctx = jnp.stack([own_ctx % 2, own_ctx // 2])
    count = lengths.shape[1]

    item_count = tok_rows * TOP
    capacity = 2 * item_count // num_experts
    slot_count = num_experts * capacity
    expert_ids = jnp.arange(num_experts, dtype=jnp.int32)
    chosen = routes[0][:, :, None] == expert_ids[None, None, :]
    flat_chosen = chosen.reshape(item_count, num_experts).astype(jnp.bfloat16)
    items = jnp.arange(item_count, dtype=jnp.int32)
    earlier = jnp.dot(
        (items[None, :] < items[:, None]).astype(jnp.bfloat16),
        flat_chosen,
        preferred_element_type=jnp.float32,
    )
    slot_rank = jnp.sum(earlier * flat_chosen.astype(jnp.float32), axis=1).astype(jnp.int32)
    slot_target = (routes[0].reshape(item_count) * capacity + slot_rank).reshape(tok_rows, TOP)
    slots = jnp.arange(slot_count, dtype=jnp.int32)
    at_slot = [slots[:, None] == slot_target[None, :, k] for k in range(TOP)]
    of_token = [(slots[None, :] == slot_target[:, k, None]).astype(jnp.bfloat16) for k in range(TOP)]
    fill = (at_slot[0] | at_slot[1]).astype(jnp.bfloat16)

    def to_slots(rows):
        return jnp.dot(fill, rows, preferred_element_type=jnp.float32).astype(jnp.bfloat16)

    def send_rows(rows):
        return dispatch(to_slots(rows).reshape(num_experts, capacity, model_width))

    other_ids = sum(
        jnp.sum(
            jnp.where(at_slot[k], routes[0][None, :, 1 - k].astype(jnp.float32), 0.0), axis=1
        )
        for k in range(TOP)
    )

    def with_notes(rows, *notes):
        extra = jnp.stack(notes, axis=1).astype(jnp.bfloat16)
        extra = jnp.pad(extra, ((0, 0), (0, 8 - len(notes)), (0, model_width - capacity)))
        return jnp.concatenate([rows, extra], axis=1)

    shard = attn_in[0]
    near_shard, far_shard = swap(shard, "fsdp", 1), swap(shard, "fsdp", 2)
    small = gather_shards(jnp.concatenate([norm_gain.reshape(4, shard_width), router.T], axis=0))
    ordered = []
    for i in range(4):
        block = small[3]
        for j in range(3):
            block = jnp.where(own_fsdp ^ j == i, small[j], block)
        ordered.append(block)
    small = jnp.concatenate(ordered, axis=1)
    gains = [small[i : i + 1].astype(jnp.float32) for i in range(4)]
    router_full = small[4:].T
    grad_rows = to_slots(cotangent[0]).reshape(num_experts, capacity, model_width)
    grad_sent = dispatch(with_notes(grad_rows, other_ids.reshape(num_experts, capacity)))
    far_shard, tables, meta, gains = lax.optimization_barrier((far_shard, tables, meta, gains))
    w_attn_in_one = (shard, near_shard, far_shard, swap(far_shard, "fsdp", 1))
    near_shard, attn_in, attn_out, mlp_in, mlp_out = lax.optimization_barrier(
        (near_shard, attn_in, attn_out, mlp_in, mlp_out)
    )
    w_attn_out_one, w_mlp_in_one, w_mlp_out_one = (
        gathered(attn_out[0]), gathered(mlp_in[0]), gathered(mlp_out[0])
    )
    w_attn_in_two, w_attn_out_two = gathered(attn_in[1]), gathered(attn_out[1])
    w_mlp_in_two, w_mlp_out_two = gathered(mlp_in[1]), gathered(mlp_out[1])

    resid_in = tokens[0].astype(jnp.float32)
    heads_one, kept_one, (grad_sent, expert_parts) = attend_forward(
        meta,
        count,
        resid_in,
        gains[0],
        tables,
        w_attn_in_one,
        (
            grad_sent,
            (
                jnp.swapaxes(expert_in, 1, 2).reshape(2, shard_width, fsdp_count, hid_unit),
                jnp.swapaxes(expert_out, 0, 1).reshape(shard_width, fsdp_count, hid_unit),
            ),
        ),
    )
    expert_w_out = lax.all_to_all(
        jnp.transpose(expert_parts[1], (1, 0, 2)), "fsdp", 0, 0, tiled=True
    )
    heads_one, expert_w_out, expert_part = lax.optimization_barrier(
        (heads_one, expert_w_out, expert_parts[0])
    )
    heads_one = exchange(heads_one)
    after_one, _, blocks_one, keep_one, send_one, att_keep_one, att_send_one = post(
        meta, resid_in, gains[1], heads_one, w_attn_out_one
    )
    middle, mixed_one, hid_keep_one, hid_send_one = mlp(
        meta, after_one, blocks_one, w_mlp_in_one, w_mlp_out_one
    )
    near_one = near(send_one, att_send_one, hid_send_one)
    heads_two, kept_two, (expert_part, grad_sent) = attend_forward(
        meta, count, middle, gains[2], tables, w_attn_in_two, (expert_part, grad_sent)
    )
    expert_w = lax.all_to_all(
        jnp.transpose(expert_part, (2, 0, 1, 3)), "fsdp", 0, 0, tiled=True
    )
    grad_arrived = to_units(grad_sent[:, :capacity].reshape(slot_count, model_width))
    arrived_ids = jnp.concatenate(
        to_units(grad_sent[:, capacity, :capacity].astype(jnp.float32))
    ).reshape(-1, 1)
    heads_two, grad_arrived, arrived_ids = lax.optimization_barrier(
        (heads_two, grad_arrived, arrived_ids)
    )
    heads_two = exchange(heads_two)
    heads_two, w_attn_out_two, expert_w = lax.optimization_barrier(
        (heads_two, w_attn_out_two, expert_w)
    )
    after_two, normed_three, blocks_two, keep_two, send_two, att_keep_two, att_send_two = post(
        meta, middle, gains[3], heads_two, w_attn_out_two
    )

    rows_sent = send_rows(normed_three)
    shared, mixed_two, hid_keep_two, hid_send_two = mlp(
        meta, after_two, blocks_two, w_mlp_in_two, w_mlp_out_two
    )
    grad_mixed_two, grad_shared_in = mlp_back(
        meta, cotangent, mixed_two, w_mlp_in_two, w_mlp_out_two
    )
    grad_mlp_out_two = weight_grad(
        meta, hid_keep_two, *near(hid_send_two), cotangent, *near(cotangent)
    )
    logits = jnp.dot(normed_three, router_full, preferred_element_type=jnp.float32)
    picked = jnp.sum(jnp.where(chosen, logits[:, None, :], 0.0), axis=-1)
    gate_probs = jax.nn.softmax(picked, axis=-1)
    rows_sent, grad_shared_in, grad_mlp_out_two, gate_probs = lax.optimization_barrier(
        (rows_sent, grad_shared_in, grad_mlp_out_two, gate_probs)
    )
    sum_mlp_out_two = add_arrived(grad_mlp_out_two)
    router_wide = jnp.pad(router_full, ((0, 0), (0, 128 - num_experts)))
    own_expert = ((own_ctx * fsdp_count + own_fsdp) // units).reshape(1)
    partial_rows, partial_back, kept_rows = experts(
        own_expert,
        to_units(rows_sent.reshape(slot_count, model_width)),
        grad_arrived,
        router_wide,
        arrived_ids,
        expert_w,
        expert_w_out,
    )
    arrived, grad_rows, hidden_rows, grad_gate, grad_up, dots = kept_rows
    dots = from_units(dots.reshape(units, num_experts, capacity))
    coarse = lax.optimization_barrier(dots.astype(jnp.bfloat16))
    payload = with_notes(
        from_units(partial_back).astype(jnp.bfloat16).reshape(num_experts, capacity, model_width),
        coarse,
        dots - coarse.astype(jnp.float32),
    )
    payload, kept_rows, partial_rows = lax.optimization_barrier((payload, kept_rows, partial_rows))
    arrived, grad_rows, hidden_rows, grad_gate, grad_up, _ = kept_rows
    back = dispatch(payload)
    grad_experts = jnp.stack(
        [
            jnp.einsum("rd,rf->df", left, right, preferred_element_type=jnp.float32)
            .astype(jnp.bfloat16)
            .reshape(fsdp_count, shard_width, hid_unit)
            for left, right in ((arrived, grad_gate), (arrived, grad_up), (grad_rows, hidden_rows))
        ],
        axis=1,
    )
    grad_mlp_in_two = weight_grad(
        meta, keep_two, *near(send_two), grad_mixed_two, *near(grad_mixed_two)
    )
    back, grad_experts, grad_mlp_in_two, sum_mlp_out_two = lax.optimization_barrier(
        (back, grad_experts, grad_mlp_in_two, sum_mlp_out_two)
    )
    grad_out = cotangent[0].astype(jnp.float32)
    stride = back.shape[1]
    notes = back[:, capacity : capacity + 2, :capacity].astype(jnp.float32)
    slot_dots = jnp.sum(notes, axis=1).reshape(1, slot_count)
    grad_gates = jnp.stack(
        [
            jnp.sum(
                jnp.where(slots[None, :] == slot_target[:, k, None], slot_dots, 0.0), axis=-1
            )
            for k in range(TOP)
        ],
        axis=1,
    )
    grad_picked = gate_probs * (
        grad_gates - jnp.sum(gate_probs * grad_gates, axis=-1, keepdims=True)
    )
    grad_logits = jnp.sum(jnp.where(chosen, grad_picked[..., None], 0.0), axis=1)
    grad_router = jnp.einsum(
        "te,td->ed", grad_logits, normed_three.astype(jnp.float32), precision=HIGHEST
    )
    wide = jnp.arange(num_experts * stride, dtype=jnp.int32)[None, :]
    wide_target = slot_target + (stride - capacity) * routes[0]
    spread = (wide == wide_target[:, 0, None]) | (wide == wide_target[:, 1, None])
    grad_normed = (
        grad_shared_in
        + jnp.dot(
            spread.astype(jnp.bfloat16),
            back.reshape(num_experts * stride, model_width),
            preferred_element_type=jnp.float32,
        )
        + jnp.einsum(
            "te,de->td", grad_logits, router_full.astype(jnp.float32), precision=HIGHEST
        )
    )
    grad_heads, grad_resid, branch, gain_three = post_back(
        meta, after_two, gains[3], grad_out, grad_normed, w_attn_out_two
    )
    grad_heads = exchange(grad_heads)
    grad_attn_out_two = weight_grad(
        meta, att_keep_two, *near(att_send_two), branch, *near(branch)
    )
    grad_heads, grad_attn_out_two = lax.optimization_barrier((grad_heads, grad_attn_out_two))
    grad_q, own, others = attend_back(
        meta, kept_two[2], grad_heads, kept_two[3], kept_two[4], count
    )
    arrived_kv = [swap(values, "ctx", part + 1) for part, values in enumerate(others)]
    sum_mlp_in_two = add_arrived(grad_mlp_in_two)
    sum_attn_out_two = add_arrived(grad_attn_out_two)
    arrived_kv, grad_experts, *sums_two = lax.optimization_barrier(
        (arrived_kv, grad_experts, sum_mlp_in_two, sum_mlp_out_two, sum_attn_out_two)
    )
    sums_two = total(0, sums_two)
    grad_qkv = exchange(merge(meta, grad_q, own, arrived_kv))
    expert_rows = from_units(partial_rows).astype(jnp.bfloat16)
    grad_qkv, expert_rows = lax.optimization_barrier((grad_qkv, expert_rows))
    grad_experts = lax.all_to_all(grad_experts, "fsdp", 0, 0, tiled=True)
    grad_mixed, grad_resid, gain_two = pre_back(
        meta, middle, gains[2], tables, grad_resid, grad_qkv, w_attn_in_two
    )
    branch = grad_resid.astype(jnp.bfloat16)[None]
    grad_mixed_one, grad_normed = mlp_back(
        meta, branch, mixed_one, w_mlp_in_one, w_mlp_out_one
    )
    near_mixed = near(grad_mixed, branch, grad_mixed_one)
    grad_heads, grad_resid, att_branch, gain_one = post_back(
        meta, after_one, gains[1], grad_resid, grad_normed, w_attn_out_one
    )
    near_branch = near(att_branch)[0]
    grad_heads = exchange(grad_heads)
    grad_mlp_in_one = weight_grad(meta, keep_one, near_one[0], grad_mixed_one, near_mixed[2])
    grad_mlp_out_one = weight_grad(meta, hid_keep_one, near_one[2], branch, near_mixed[1])
    grad_heads, grad_mlp_out_one, grad_mlp_in_one = lax.optimization_barrier(
        (grad_heads, grad_mlp_out_one, grad_mlp_in_one)
    )
    grad_q, own, others = attend_back(
        meta, kept_one[2], grad_heads, kept_one[3], kept_one[4], count
    )
    arrived_kv = [swap(values, "ctx", part + 1) for part, values in enumerate(others)]
    grad_attn_in_two = weight_grad(
        meta, kept_two[0], *near(kept_two[1]), grad_mixed, near_mixed[0]
    )
    grad_attn_out_one = weight_grad(meta, att_keep_one, near_one[1], att_branch, near_branch)
    arrived_kv, grad_attn_in_two, grad_attn_out_one, grad_experts = lax.optimization_barrier(
        (arrived_kv, grad_attn_in_two, grad_attn_out_one, grad_experts)
    )
    grad_qkv = exchange(merge(meta, grad_q, own, arrived_kv))
    sums_one = [
        add_arrived(g)
        for g in (grad_attn_in_two, grad_mlp_in_one, grad_mlp_out_one, grad_attn_out_one)
    ]
    grad_experts = jnp.transpose(grad_experts, (1, 2, 0, 3)).astype(jnp.float32)
    grad_experts = grad_experts.reshape(3, shard_width, hid_unit * fsdp_count)
    grad_qkv, sums_two, expert_rows, grad_experts, *sums_one = lax.optimization_barrier(
        (grad_qkv, sums_two, expert_rows, grad_experts, *sums_one)
    )
    sums_one = total(1, sums_one)
    grad_mixed, grad_resid, gain_zero = pre_back(
        meta, resid_in, gains[0], tables, grad_resid, grad_qkv, w_attn_in_one
    )
    grad_attn_in_one = weight_grad(
        meta, kept_one[0], *near(kept_one[1]), grad_mixed, *near(grad_mixed)
    )
    grad_attn_in_one, expert_rows = lax.optimization_barrier((grad_attn_in_one, expert_rows))
    expert_rows = dispatch(expert_rows.reshape(num_experts, capacity, model_width))
    expert_rows = expert_rows.reshape(slot_count, model_width)
    back_rows = [jnp.dot(p, expert_rows, preferred_element_type=jnp.float32) for p in of_token]
    output = shared + sum(gate_probs[:, k, None] * back_rows[k] for k in range(TOP))
    small_grads = total_small(
        jnp.concatenate([gain_zero, gain_one, gain_two, gain_three, grad_router])
    )
    small_grads = lax.dynamic_slice_in_dim(small_grads, own_fsdp * shard_width, shard_width, 1)
    attn_in_grad, sums_one = reduce_last(
        at_ctx,
        grad_attn_in_one[0],
        swap(grad_attn_in_one[1], "fsdp", 2),
        sums_one[0],
        sums_one,
    )
    dense_grads = [attn_in_grad] + [
        jnp.stack(pair).astype(jnp.float32)
        for pair in (
            (sums_one[3], sums_two[2]),
            (sums_one[1], sums_two[0]),
            (sums_one[2], sums_two[1]),
        )
    ]
    return (
        output[None],
        grad_resid[None],
        dense_grads[0],
        dense_grads[1],
        small_grads[:4].reshape(2, 2, shard_width),
        dense_grads[2],
        dense_grads[3],
        small_grads[4:].T,
        jnp.swapaxes(grad_experts[:2], 1, 2),
        grad_experts[2].T,
    )


def solution(mesh):
    placed = (
        P("fsdp", "ctx", None),
        P("fsdp", "ctx", None),
        P("fsdp", None),
        P("fsdp", None),
        P("fsdp", "ctx", None),
        P(None, "fsdp", None),
        P(None, "fsdp", None),
        P(None, None, "fsdp"),
        P(None, "fsdp", None),
        P(None, "fsdp", None),
        P("fsdp", None),
        P(None, "ctx", "fsdp"),
        P("ctx", "fsdp"),
    )
    return jax.shard_map(
        per_device,
        mesh=mesh,
        in_specs=placed,
        out_specs=(
            P("fsdp", "ctx", None),
            P("fsdp", "ctx", None),
            P(None, "fsdp", None),
            P(None, "fsdp", None),
            P(None, None, "fsdp"),
            P(None, "fsdp", None),
            P(None, "fsdp", None),
            P("fsdp", None),
            P(None, "ctx", "fsdp"),
            P("ctx", "fsdp"),
        ),
        check_vma=False,
    )
```

time: 1190 us -> 941 us (0.79)
  Pallas kernels: 79.4 us -> 278 us
  matrix products: 144 us -> 21.4 us
  waiting for transfers between devices: 479 us -> 360 us
  local copies, waits for them, and re-layouts: 177 us -> 66.6 us
  blocking collectives: 69.1 us -> 0 us
  other arithmetic: 89.4 us -> 44 us
    pallas_call x4 -> x30, Pallas kernels: 79.4 us -> 278 us  [call(): pl.pallas_call(body, grid_spec=pltpu.PrefetchScalarGridSpec(num_scalar_pr...]
    dot_general x34 -> x4, matrix products: 133 us -> 14.6 us  [the longest x3 13.8 us: per_device(): jnp.einsum('rd,rf->df', left, right, preferred_element_type=jnp.float32)]
    all_to_all x9 -> x3, waiting for transfers between devices: 116 us -> 0.01 us  [the longest x1 0.01 us: per_device(): lax.all_to_all(jnp.transpose(expert_parts[1], (1, 0, 2)), 'fsdp', 0, 0, t...]
    ppermute x60 -> x86, waiting for transfers between devices: 187 us -> 286 us  [swap(): return lax.ppermute(values, axis, [(i, i ^ mask) for i in range(count)])]
    all_to_all x5 -> x4, waiting for transfers between devices: 74.6 us -> 12.8 us  [dispatch(): lax.all_to_all(values, BOTH, 0, 0, tiled=True, axis_index_groups=members)]
    ppermute x60 -> x86, starting transfers between devices: 50.6 us -> 102 us  [swap(): return lax.ppermute(values, axis, [(i, i ^ mask) for i in range(count)])]
    dynamic_update_slice x31 -> x0, local copies, waits for them, and re-layouts: 45.9 us -> none  [in_order(): buffer = lax.dynamic_update_index_in_dim(buffer, shard, own ^ k, 0)]
    psum x1 -> x2, waiting for transfers between devices: 101 us -> 59.4 us  [total(): return lax.psum(tuple(grads), 'ctx', axis_index_groups=ring)]
  transfers between devices with their start and end apart: 75 -> 102, of which waited for: 29 -> 46; matrix products, arithmetic and copies ran while one was open for 30% -> 12% of each run, Pallas kernels for 7% -> 25%
where the time goes in v3:
time: 941 us; the launch traced here: 926 us
  waiting for transfers between devices  360 us (38%)
  Pallas kernels  278 us (30%)
  starting transfers between devices  140 us (15%)
  local copies, waits for them, and re-layouts  66.6 us (7%)
  other arithmetic  44 us (5%)
  matrix products  21.4 us (2%)
  between operations  15.6 us (2%)
    ppermute x86, waiting for transfers between devices, swap(): return lax.ppermute(values, axis, [(i, i ^ mask) for i in range(count)])  286 us
    pallas_call x30, Pallas kernels, call(): pl.pallas_call(body, grid_spec=pltpu.PrefetchScalarGridSpec(num_scalar_pr...  278 us
    ppermute x86, starting transfers between devices, swap(): return lax.ppermute(values, axis, [(i, i ^ mask) for i in range(count)])  102 us
    psum x2, waiting for transfers between devices, total(): return lax.psum(tuple(grads), 'ctx', axis_index_groups=ring)  59.4 us
    all_to_all x4, starting transfers between devices, dispatch(): lax.all_to_all(values, BOTH, 0, 0, tiled=True, axis_index_groups=members)  24.7 us
  transfers between devices with their start and end apart: 102, of which 46 were waited for; matrix products, arithmetic and copies ran while one was open for 12% of the time, Pallas kernels for 25%

profile of v3, /device:TPU:0, one launch (start us, length us, event | category | flops | bytes accessed | tf_op | source)
XLA Modules:
  0.0 926.2 jit_solution(817241014324833994)
XLA Ops:
  24.7 8.4 all-to-all-start
  37.4 4.4 collective-permute-done.1
  43.7 44.9 %collective-permute-done.w2.rest_6_ = bf16[192,2304]{1,0:T(8,128)(2,1)S(1)} collective-permute-done((bf16[192,2304]{1,0:T(8,128)(2,1)S(1)}, bf16[192,2304]{1,0:T(8,128)(2,1)S(1)}, u32[]{:S(2)}, u32[]{:S(2)}) %collective-permute-start) | collective-permute-done | bytes 884768 | tf_op jit(solution)/shard_map/ppermute | solution.py:30
  92.3 5.8 shard_map.204
  99.5 5.1 reshape.206
  111.5 4.4 all-to-all-start.1
  115.9 4.5 collective-permute-start.7
  122.7 18.4 %collective-permute-done.7.refs_2_ = bf16[2,3,192,128]{3,2,1,0:T(8,128)(2,1)S(1)} collective-permute-done((bf16[2,3,192,128]{3,2,1,0:T(8,128)(2,1)}, bf16[2,3,192,128]{3,2,1,0:T(8,128)(2,1)S(1)}, u32[]{:S(2)}, u32[]{:S(2)}) %collective-permute-start.7) | collective-permute-done | bytes 294944 | tf_op jit(solution)/shard_map/ppermute | solution.py:30
  143.1 7.9 collective-permute-done.11.refs_6_
  151.8 4.3 collective-permute-done.12.refs_7_
  156.0 19.4 %shard_map.205 = (bf16[2,192,128]{2,1,0:T(8,128)(2,1)}, bf16[2,192,128]{2,1,0:T(8,128)(2,1)}, bf16[2,192,128]{2,1,0:T(8,128)(2,1)}, bf16[2,192,128]{2,1,0:T(8,12...) custom-call(s32[22]{0:T(128)} %concatenate.25.meta, bf16[2,3,192,128]{3,2,1,0:T(8,128)(2,1)} %get-tuple-element.240.refs_0_, ...), custom_call_target="tpu_custom_call" | custom-call | flops 1610612736 | bytes 3551232 | tf_op jit(solution)/shard_map/pallas_call | solution.py:91
  185.4 4.7 shard_map.206
  190.1 10.4 %shard_map.207 = (f32[256,768]{1,0:T(8,128)}, f32[2,256,2048]{2,1,0:T(8,128)}, bf16[2,256,512]{2,1,0:T(8,128)(2,1)}, bf16[2,256,512]{2,1,0:T(8,128)(2,1)}) custom-call(s32[22]{0:T(128)} %concatenate.25.meta, f32[256,768]{1,0:T(8,128)} %get-tuple-element.256.x, bf16[4,256,192]{2,1,0:T(8,128)(2,1)} %get-tuple-element.257.blocks, bf16[768,4096]{1,0:T(8,128)(2,1)} %bitcast.121, ...), custom_call_target="tpu_custom_call" | custom-call | flops 2415919104 | bytes 70123520 | tf_op jit(solution)/shard_map/pallas_call | solution.py:91
  200.6 5.8 shard_map.208
  206.4 7.0 collective-permute-done.16.refs_1_
  228.9 16.5 %collective-permute-done.17.refs_2_ = bf16[2,3,192,128]{3,2,1,0:T(8,128)(2,1)} collective-permute-done((bf16[2,3,192,128]{3,2,1,0:T(8,128)(2,1)S(1)}, bf16[2,3,192,128]{3,2,1,0:T(8,128)(2,1)}, u32[]{:S(2)}, u32[]{:S(2)}) %collective-permute-start.17) | collective-permute-done | bytes 294944 | tf_op jit(solution)/shard_map/ppermute | solution.py:30
  249.9 5.7 collective-permute-done.20.refs_5_
  255.6 6.3 collective-permute-done.21.refs_6_
  261.9 5.3 collective-permute-done.22.refs_7_
  267.2 29.3 %shard_map.209 = (bf16[2,192,128]{2,1,0:T(8,128)(2,1)}, bf16[2,192,128]{2,1,0:T(8,128)(2,1)}, bf16[2,192,128]{2,1,0:T(8,128)(2,1)}, bf16[2,192,128]{2,1,0:T(8,12...) custom-call(s32[22]{0:T(128)} %concatenate.25.meta, bf16[2,3,192,128]{3,2,1,0:T(8,128)(2,1)} %get-tuple-element.264.refs_0_, ...), custom_call_target="tpu_custom_call" | custom-call | flops 1610612736 | bytes 3551232 | tf_op jit(solution)/shard_map/pallas_call | solution.py:91
  305.9 5.1 shard_map.210
  313.8 4.7 all-to-all-start.3
  318.6 10.5 %shard_map.211 = (f32[256,768]{1,0:T(8,128)}, f32[2,256,2048]{2,1,0:T(8,128)}, bf16[2,256,512]{2,1,0:T(8,128)(2,1)}, bf16[2,256,512]{2,1,0:T(8,128)(2,1)}) custom-call(s32[22]{0:T(128)} %concatenate.25.meta, f32[256,768]{1,0:T(8,128)} %get-tuple-element.286.x, bf16[4,256,192]{2,1,0:T(8,128)(2,1)} %get-tuple-element.287.blocks, bf16[768,4096]{1,0:T(8,128)(2,1)} %bitcast.137, ...), custom_call_target="tpu_custom_call" | custom-call | flops 2415919104 | bytes 70123520 | tf_op jit(solution)/shard_map/pallas_call | solution.py:91
  330.1 10.8 %shard_map.212 = (bf16[2,256,2048]{2,1,0:T(8,128)(2,1)}, f32[256,768]{1,0:T(8,128)}) custom-call(s32[22]{0:T(128)} %concatenate.25.meta, bf16[1,256,768]{2,1,0:T(8,128)(2,1)} %right.1, f32[2,256,2048]{2,1,0:T(8,128)} %get-tuple-element.290.mixed, bf16[768,4096]{1,0:T(8,128)(2,1)} %bitcast.145, bf16[768,4096]{1,0:T(8,128)(2,1)} %bitcast.146, ...), custom_call_target="tpu_custom_call" | custom-call | flops 2415919104 | bytes 70385664 | tf_op jit(solution)/shard_map/pallas_call | solution.py:91
  341.7 4.3 shard_map.213
  345.9 5.8 all-to-all-done.3
  355.3 33.3 %shard_map.214 = (bf16[1024,768]{1,0:T(8,128)(2,1)}, bf16[1024,768]{1,0:T(8,128)(2,1)}, bf16[1024,768]{1,0:T(8,128)(2,1)}, bf16[1024,768]{1,0:T(8,128)(2,1)}, bf...) custom-call(s32[1]{0:T(128)} %bitcast.37.meta, ...), custom_call_target="tpu_custom_call" | custom-call | flops 19327352832 | bytes 36388864 | tf_op jit(solution)/shard_map/pallas_call | solution.py:91
  396.3 7.7 all-to-all-start.4
  406.5 8.6 shard_map.215
  417.4 6.7 convolution_convert_fusion.2
  434.2 7.0 all-to-all-done.4
  444.0 4.8 shard_map.216
  449.9 5.3 collective-permute-start.37
  455.2 4.7 collective-permute-start.38
  468.6 24.1 %shard_map.218 = (bf16[8,192,128]{2,1,0:T(8,128)(2,1)}, f32[8,2,192,128]{3,2,1,0:T(8,128)}, bf16[8,2,192,128]{3,2,1,0:T(8,128)(2,1)}) custom-call(s32[22]{0:T(128)} %concatenate.25.meta, bf16[2,3,192,128]{3,2,1,0:T(8,128)(2,1)} %get-tuple-element.264.refs_0_, bf16[2,3,192,128]{3,2,1,0:T(8,128)(2,1)} %collective-permute-done.16.refs_1_, ...), custom_call_target="tpu_custom_call" | custom-call | flops 4026531840 | bytes 6303744 | tf_op jit(solution)/shard_map/pallas_call | solution.py:91
  492.8 6.7 collective-permute-done.44
  503.5 4.4 collective-permute-done.42.rest_0_
  520.3 5.1 all-to-all-start.5
  525.5 10.4 %collective-permute-done.46.rest_2_ = bf16[2,3,192,128]{3,2,1,0:T(8,128)(2,1)S(1)} collective-permute-done((bf16[2,3,192,128]{3,2,1,0:T(8,128)(2,1)}, bf16[2,3,192,128]{3,2,1,0:T(8,128)(2,1)S(1)}, u32[]{:S(2)}, u32[]{:S(2)}) %collective-permute-start.46) | collective-permute-done | bytes 294944 | tf_op jit(solution)/shard_map/ppermute | solution.py:30
  536.8 7.1 shard_map.220
  545.8 11.4 %shard_map.221 = (bf16[2,256,2048]{2,1,0:T(8,128)(2,1)}, f32[256,768]{1,0:T(8,128)}) custom-call(s32[22]{0:T(128)} %concatenate.25.meta, bf16[1,256,768]{2,1,0:T(8,128)(2,1)} %convert_bitcast_fusion.1.branch.right, f32[2,256,2048]{2,1,0:T(8,128)} %get-tuple-element.367.mixed, bf16[768,4096]{1,0:T(8,128)(2,1)} %bitcast.129, bf16[768,4096]{1,0:T(8,128)(2,1)} %bitcast.130, ...), custom_call_target="tpu_custom_call" | custom-call | flops 2415919104 | bytes 70385664 | tf_op jit(solution)/shard_map/pallas_call | solution.py:91
  558.7 4.6 shard_map.222
  575.8 8.4 shard_map.224
  585.3 24.4 %shard_map.225 = (bf16[8,192,128]{2,1,0:T(8,128)(2,1)}, f32[8,2,192,128]{3,2,1,0:T(8,128)}, bf16[8,2,192,128]{3,2,1,0:T(8,128)(2,1)}) custom-call(s32[22]{0:T(128)} %concatenate.25.meta, bf16[2,3,192,128]{3,2,1,0:T(8,128)(2,1)} %get-tuple-element.240.refs_0_, bf16[2,3,192,128]{3,2,1,0:T(8,128)(2,1)} %collective-permute-done.6.refs_1_, ...), custom_call_target="tpu_custom_call" | custom-call | flops 4026531840 | bytes 6303744 | tf_op jit(solution)/shard_map/pallas_call | solution.py:91
  619.4 5.2 shard_map.226
  624.6 6.5 collective-permute-done.56.rest_0_
  634.2 30.1 %collective-permute-done.66 = bf16[512,768]{1,0:T(8,128)(2,1)} collective-permute-done((bf16[512,768]{1,0:T(8,128)(2,1)}, bf16[512,768]{1,0:T(8,128)(2,1)}, u32[]{:S(2)}, u32[]{:S(2)}) %collective-permute-start.66) | collective-permute-done | bytes 786464 | tf_op jit(solution)/shard_map/ppermute | solution.py:30
  670.3 8.0 collective-permute-start.61
  680.0 6.9 collective-permute-done.67
  692.1 4.6 copy.136
  700.3 5.2 all-reduce.8.cloned.1.call-done
  705.5 6.5 collective-permute-done.62.rest_2_
  712.0 7.2 shard_map.229
  725.2 5.1 collective-permute-start.82
  731.0 6.6 collective-permute-done.82
  737.7 10.4 %collective-permute-done.83 = f32[20,768]{1,0:T(8,128)S(1)} collective-permute-done((f32[20,768]{1,0:T(8,128)S(1)}, f32[20,768]{1,0:T(8,128)S(1)}, u32[]{:S(2)}, u32[]{:S(2)}) %collective-permute-start.83) | collective-permute-done | bytes 61472 | tf_op jit(solution)/shard_map/ppermute | solution.py:30
  749.3 5.2 shard_map.230
  759.9 6.3 slice_bitcast_fusion
  768.2 8.9 collective-permute-done.69.second
  786.6 10.7 %collective-permute-done.70.second = bf16[192,1152]{1,0:T(8,128)(2,1)S(1)} collective-permute-done((bf16[192,1152]{1,0:T(8,128)(2,1)}, bf16[192,1152]{1,0:T(8,128)(2,1)S(1)}, u32[]{:S(2)}, u32[]{:S(2)}) %collective-permute-start.70) | collective-permute-done | bytes 442400 | tf_op jit(solution)/shard_map/ppermute | solution.py:30
  805.4 5.0 collective-permute-done.71
  810.4 14.1 %collective-permute-done.72 = bf16[48,1152]{1,0:T(8,128)(2,1)S(1)} collective-permute-done((bf16[48,1152]{1,0:T(8,128)(2,1)}, bf16[48,1152]{1,0:T(8,128)(2,1)S(1)}, u32[]{:S(2)}, u32[]{:S(2)}) %collective-permute-start.72) | collective-permute-done | bytes 110624 | tf_op jit(solution)/shard_map/ppermute | solution.py:30
  833.5 11.6 %collective-permute-done.75.refs_2_ = bf16[48,1152]{1,0:T(8,128)(2,1)S(1)} collective-permute-done((bf16[48,1152]{1,0:T(8,128)(2,1)S(1)}, bf16[48,1152]{1,0:T(8,128)(2,1)S(1)}, u32[]{:S(2)}, u32[]{:S(2)}) %collective-permute-start.75) | collective-permute-done | bytes 110624 | tf_op jit(solution)/shard_map/ppermute | solution.py:30
  845.1 54.2 %all-reduce.10.cloned.1.call-done = (bf16[192,2304]{1,0:T(8,128)(2,1)}, bf16[192,4096]{1,0:T(8,128)(2,1)}, bf16[512,768]{1,0:T(8,128)(2,1)}, bf16[192,768]{1,0:T(8,128)(2,1)}) async-done(((bf16[192,2304]{1,0:T(8,128)(2,1)}, bf16[192,4096]{1,0:T(8,128)(2,1)}, bf16[512,768]{1,0:T(8,128)(2,1)}, bf16[192,768]{1,0:T(8,128)(2,1)}), (bf16[192,2304]{1,0:T(8,128)(2,1)}, bf16[192,4096]{1,0:T(8,128)(2,1)}, ...) | async-done | bytes 3538960 | tf_op jit(solution)/shard_map/psum | solution.py:913
  (490 shorter events, 247.6 us)
Async XLA Ops:
  7.2 172.8 %all-gather.15.cloned.1.call-start = ((), (), s32[]{:S(2)}) async-start(), calls=%async_computation.7 | async-start | bytes 1474560 | tf_op jit(solution)/shard_map/all_gather | solution.py:964
  13.4 176.7 %all-gather.19.cloned.1.call-start = ((), (), s32[]{:S(2)}) async-start(), calls=%async_computation.9 | async-start | bytes 3932160 | tf_op jit(solution)/shard_map/all_gather | solution.py:964
  14.7 175.4 %all-gather.17.cloned.1.call-start = ((), (), s32[]{:S(2)}) async-start(), calls=%async_computation.8 | async-start | bytes 7864320 | tf_op jit(solution)/shard_map/all_gather | solution.py:964
  18.9 181.7 %all-gather.21.cloned.1.call-start = ((), (), s32[]{:S(2)}) async-start(), calls=%async_computation.10 | async-start | bytes 4423680 | tf_op jit(solution)/shard_map/all_gather | solution.py:964
  19.9 281.1 %all-gather.23.cloned.1.call-start = ((), (), s32[]{:S(2)}) async-start(), calls=%async_computation.11 | async-start | bytes 1474560 | tf_op jit(solution)/shard_map/all_gather | solution.py:964
  20.5 298.1 %all-gather.27.cloned.1.call-start = ((), (), s32[]{:S(2)}) async-start(), calls=%async_computation.13 | async-start | bytes 3932160 | tf_op jit(solution)/shard_map/all_gather | solution.py:964
  24.7 83.8 %all-to-all-start = ((bf16[16,72,768]{2,1,0:T(8,128)(2,1)}), bf16[16,72,768]{2,1,0:T(8,128)(2,1)}, u32[]{:S(2)}, u32[]{:S(2)}) async-start(bf16[16,72,768]{2,1,0:T(8,128)(2,1)} %fusion.2), calls=%async_computation | async-start | bytes 3538944 | tf_op jit(solution)/shard_map/all_to_all | solution.py:952
  33.2 285.4 %all-gather.25.cloned.1.call-start = ((), (), s32[]{:S(2)}) async-start(), calls=%async_computation.12 | async-start | bytes 7864320 | tf_op jit(solution)/shard_map/all_gather | solution.py:964
  35.2 53.4 %collective-permute-start = (bf16[192,2304]{1,0:T(8,128)(2,1)S(1)}, bf16[192,2304]{1,0:T(8,128)(2,1)S(1)}, u32[]{:S(2)}, u32[]{:S(2)}) collective-permute-start(bf16[192,2304]{1,0:T(8,128)(2,1)S(1)} %slice_bitcast_fusion.2.w0.rest_4_), channel_id=1, source_target_pairs={{0,2},{1,3},{2,0},{3,1},{4,6},{5,7},{6,4},{7,5},{8,10},{9,11},{10,... | collective-permute-start | bytes 2654216 | tf_op jit(solution)/shard_map/ppermute | solution.py:30
  111.5 64.0 %all-to-all-start.1 = ((bf16[4,192,1024]{2,1,0:T(8,128)(2,1)}), bf16[4,192,1024]{2,1,0:T(8,128)(2,1)}, u32[]{:S(2)}, u32[]{:S(2)}) async-start(bf16[4,192,1024]{2,1,0:T(8,128)(2,1)} %bitcast.196), calls=%async_computation.1 | async-start | bytes 3145728 | tf_op jit(solution)/shard_map/all_to_all | solution.py:1054
  115.9 25.2 %collective-permute-start.7 = (bf16[2,3,192,128]{3,2,1,0:T(8,128)(2,1)}, bf16[2,3,192,128]{3,2,1,0:T(8,128)(2,1)S(1)}, u32[]{:S(2)}, u32[]{:S(2)}) collective-permute-start(bf16[2,3,192,128]{3,2,1,0:T(8,128)(2,1)} %get-tuple-element.243), channel_id=1, source_target_pairs={{0,16},{4,20},{8,24},{12,28},{16,0},{20,4},{24,8},{28,12},{1,17},{... | collective-permute-start | bytes 884744 | tf_op jit(solution)/shard_map/ppermute | solution.py:30
  120.5 22.1 %collective-permute-start.8 = (bf16[2,3,192,128]{3,2,1,0:T(8,128)(2,1)}, bf16[2,3,192,128]{3,2,1,0:T(8,128)(2,1)S(1)}, u32[]{:S(2)}, u32[]{:S(2)}) collective-permute-start(bf16[2,3,192,128]{3,2,1,0:T(8,128)(2,1)} %get-tuple-element.244), channel_id=1, source_target_pairs={{0,24},{4,28},{8,16},{12,20},{16,8},{20,12},{24,0},{28,4},{1,25},{... | collective-permute-start | bytes 884744 | tf_op jit(solution)/shard_map/ppermute | solution.py:30
  120.7 22.5 %collective-permute-start.9 = (bf16[2,3,192,128]{3,2,1,0:T(8,128)(2,1)}, bf16[2,3,192,128]{3,2,1,0:T(8,128)(2,1)S(1)}, u32[]{:S(2)}, u32[]{:S(2)}) collective-permute-start(bf16[2,3,192,128]{3,2,1,0:T(8,128)(2,1)} %get-tuple-element.240.refs_0_), channel_id=1, source_target_pairs={{0,4},{4,0},{8,12},{12,8},{16,20},{20,16},{24,28},{28,24},{1,5},{5... | collective-permute-start | bytes 884744 | tf_op jit(solution)/shard_map/ppermute | solution.py:30
  122.3 20.9 %collective-permute-start.10 = (bf16[2,3,192,128]{3,2,1,0:T(8,128)(2,1)}, bf16[2,3,192,128]{3,2,1,0:T(8,128)(2,1)S(1)}, u32[]{:S(2)}, u32[]{:S(2)}) collective-permute-start(bf16[2,3,192,128]{3,2,1,0:T(8,128)(2,1)} %collective-permute-done.6.refs_1_), channel_id=1, source_target_pairs={{0,4},{4,0},{8,12},{12,8},{16,20},{20,16},{24,28},{28,24},{1,5},{5... | collective-permute-start | bytes 884744 | tf_op jit(solution)/shard_map/ppermute | solution.py:30
  142.6 13.5 %collective-permute-start.12 = (bf16[2,3,192,128]{3,2,1,0:T(8,128)(2,1)S(1)}, bf16[2,3,192,128]{3,2,1,0:T(8,128)(2,1)}, u32[]{:S(2)}, u32[]{:S(2)}) collective-permute-start(bf16[2,3,192,128]{3,2,1,0:T(8,128)(2,1)S(1)} %collective-permute-done.8.refs_3_), channel_id=1, source_target_pairs={{0,4},{4,0},{8,12},{12,8},{16,20},{20,16},{24,28},{28,24},{1,5},{5... | collective-permute-start | bytes 884744 | tf_op jit(solution)/shard_map/ppermute | solution.py:30
  216.1 89.7 %all-to-all-start.2 = ((bf16[4,2,192,1024]{3,2,1,0:T(8,128)(2,1)}), bf16[4,2,192,1024]{3,2,1,0:T(8,128)(2,1)S(1)}, u32[]{:S(2)}, u32[]{:S(2)}) async-start(bf16[4,2,192,1024]{3,2,1,0:T(8,128)(2,1)} %bitcast.195), calls=%async_computation.2 | async-start | bytes 6291456 | tf_op jit(solution)/shard_map/all_to_all | solution.py:1071
  222.7 73.9 %collective-permute-start.23 = (bf16[1024,768]{1,0:T(8,128)(2,1)}, bf16[1024,768]{1,0:T(8,128)(2,1)}, u32[]{:S(2)}, u32[]{:S(2)}) collective-permute-start(bf16[1024,768]{1,0:T(8,128)(2,1)} %bitcast.29.refs_2_), channel_id=1, source_target_pairs={{0,1},{1,0},{2,3},{3,2},{4,5},{5,4},{6,7},{7,6},{8,9},{9,8},{10,11... | collective-permute-start | bytes 4718600 | tf_op jit(solution)/shard_map/ppermute | solution.py:30
  223.1 22.3 %collective-permute-start.17 = (bf16[2,3,192,128]{3,2,1,0:T(8,128)(2,1)S(1)}, bf16[2,3,192,128]{3,2,1,0:T(8,128)(2,1)}, u32[]{:S(2)}, u32[]{:S(2)}) collective-permute-start(bf16[2,3,192,128]{3,2,1,0:T(8,128)(2,1)S(1)} %copy-done.78), channel_id=1, source_target_pairs={{0,16},{4,20},{8,24},{12,28},{16,0},{20,4},{24,8},{28,12},{1,17},{... | collective-permute-start | bytes 884744 | tf_op jit(solution)/shard_map/ppermute | solution.py:30
  224.5 22.7 %collective-permute-start.18 = (bf16[2,3,192,128]{3,2,1,0:T(8,128)(2,1)S(1)}, bf16[2,3,192,128]{3,2,1,0:T(8,128)(2,1)}, u32[]{:S(2)}, u32[]{:S(2)}) collective-permute-start(bf16[2,3,192,128]{3,2,1,0:T(8,128)(2,1)S(1)} %copy-done.76), channel_id=1, source_target_pairs={{0,24},{4,28},{8,16},{12,20},{16,8},{20,12},{24,0},{28,4},{1,25},{... | collective-permute-start | bytes 884744 | tf_op jit(solution)/shard_map/ppermute | solution.py:30
  226.4 21.1 %collective-permute-start.24 = (f32[16,64]{1,0:T(8,128)S(1)}, f32[16,64]{1,0:T(8,128)S(1)}, u32[]{:S(2)}, u32[]{:S(2)}) collective-permute-start(f32[16,64]{1,0:T(8,128)S(1)} %bitcast.224), channel_id=1, source_target_pairs={{0,1},{1,0},{2,3},{3,2},{4,5},{5,4},{6,7},{7,6},{8,9},{9,8},{10,11... | collective-permute-start | bytes 12296 | tf_op jit(solution)/shard_map/ppermute | solution.py:30
  226.4 23.6 %collective-permute-start.19 = (bf16[2,3,192,128]{3,2,1,0:T(8,128)(2,1)}, bf16[2,3,192,128]{3,2,1,0:T(8,128)(2,1)}, u32[]{:S(2)}, u32[]{:S(2)}) collective-permute-start(bf16[2,3,192,128]{3,2,1,0:T(8,128)(2,1)} %get-tuple-element.264.refs_0_), channel_id=1, source_target_pairs={{0,4},{4,0},{8,12},{12,8},{16,20},{20,16},{24,28},{28,24},{1,5},{5... | collective-permute-start | bytes 884744 | tf_op jit(solution)/shard_map/ppermute | solution.py:30
  247.2 14.7 %collective-permute-start.21 = (bf16[2,3,192,128]{3,2,1,0:T(8,128)(2,1)}, bf16[2,3,192,128]{3,2,1,0:T(8,128)(2,1)}, u32[]{:S(2)}, u32[]{:S(2)}) collective-permute-start(bf16[2,3,192,128]{3,2,1,0:T(8,128)(2,1)} %collective-permute-done.17.refs_2_), channel_id=1, source_target_pairs={{0,4},{4,0},{8,12},{12,8},{16,20},{20,16},{24,28},{28,24},{1,5},{5... | collective-permute-start | bytes 884744 | tf_op jit(solution)/shard_map/ppermute | solution.py:30
  247.5 19.8 %collective-permute-start.22 = (bf16[2,3,192,128]{3,2,1,0:T(8,128)(2,1)}, bf16[2,3,192,128]{3,2,1,0:T(8,128)(2,1)}, u32[]{:S(2)}, u32[]{:S(2)}) collective-permute-start(bf16[2,3,192,128]{3,2,1,0:T(8,128)(2,1)} %collective-permute-done.18.refs_3_), channel_id=1, source_target_pairs={{0,4},{4,0},{8,12},{12,8},{16,20},{20,16},{24,28},{28,24},{1,5},{5... | collective-permute-start | bytes 884744 | tf_op jit(solution)/shard_map/ppermute | solution.py:30
  313.8 38.0 %all-to-all-start.3 = ((bf16[16,64,768]{2,1,0:T(8,128)(2,1)}), bf16[16,64,768]{2,1,0:T(8,128)(2,1)S(1)}, u32[]{:S(2)}, u32[]{:S(2)}) async-start(bf16[16,64,768]{2,1,0:T(8,128)(2,1)} %bitcast.212), calls=%async_computation.3 | async-start | bytes 3145728 | tf_op jit(solution)/shard_map/all_to_all | solution.py:952
  318.4 22.4 %collective-permute-start.29 = (bf16[1,256,768]{2,1,0:T(8,128)(2,1)S(1)}, bf16[1,256,768]{2,1,0:T(8,128)(2,1)}, u32[]{:S(2)}, u32[]{:S(2)}) collective-permute-start(bf16[1,256,768]{2,1,0:T(8,128)(2,1)S(1)} %copy-done.7), channel_id=1, source_target_pairs={{0,1},{1,0},{2,3},{3,2},{4,5},{5,4},{6,7},{7,6},{8,9},{9,8},{10,11... | collective-permute-start | bytes 1179656 | tf_op jit(solution)/shard_map/ppermute | solution.py:30
  388.8 17.0 %collective-permute-start.35 = (bf16[2,256,2048]{2,1,0:T(8,128)(2,1)}, bf16[2,256,2048]{2,1,0:T(8,128)(2,1)}, u32[]{:S(2)}, u32[]{:S(2)}) collective-permute-start(bf16[2,256,2048]{2,1,0:T(8,128)(2,1)} %get-tuple-element.324.right), channel_id=1, source_target_pairs={{0,1},{1,0},{2,3},{3,2},{4,5},{5,4},{6,7},{7,6},{8,9},{9,8},{10,11... | collective-permute-start | bytes 6291464 | tf_op jit(solution)/shard_map/ppermute | solution.py:30
  391.0 24.2 %collective-permute-start.36 = (bf16[512,768]{1,0:T(8,128)(2,1)}, bf16[512,768]{1,0:T(8,128)(2,1)}, u32[]{:S(2)}, u32[]{:S(2)}) collective-permute-start(bf16[512,768]{1,0:T(8,128)(2,1)} %get-tuple-element.328), channel_id=1, source_target_pairs={{0,2},{1,3},{2,0},{3,1},{4,6},{5,7},{6,4},{7,5},{8,10},{9,11},{10,... | collective-permute-start | bytes 2359304 | tf_op jit(solution)/shard_map/ppermute | solution.py:30
  396.3 44.9 %all-to-all-start.4 = ((bf16[16,72,768]{2,1,0:T(8,128)(2,1)}), bf16[16,72,768]{2,1,0:T(8,128)(2,1)S(1)}, u32[]{:S(2)}, u32[]{:S(2)}) async-start(bf16[16,72,768]{2,1,0:T(8,128)(2,1)} %fusion.3), calls=%async_computation.4 | async-start | bytes 3538944 | tf_op jit(solution)/shard_map/all_to_all | solution.py:952
  448.8 51.5 %collective-permute-start.43 = (bf16[192,4096]{1,0:T(8,128)(2,1)}, bf16[192,4096]{1,0:T(8,128)(2,1)}, u32[]{:S(2)}, u32[]{:S(2)}) collective-permute-start(bf16[192,4096]{1,0:T(8,128)(2,1)} %get-tuple-element.351), channel_id=1, source_target_pairs={{0,2},{1,3},{2,0},{3,1},{4,6},{5,7},{6,4},{7,5},{8,10},{9,11},{10,... | collective-permute-start | bytes 4718600 | tf_op jit(solution)/shard_map/ppermute | solution.py:30
  449.4 67.9 %collective-permute-start.48 = (bf16[1024,768]{1,0:T(8,128)(2,1)}, bf16[1024,768]{1,0:T(8,128)(2,1)}, u32[]{:S(2)}, u32[]{:S(2)}) collective-permute-start(bf16[1024,768]{1,0:T(8,128)(2,1)} %get-tuple-element.361), channel_id=1, source_target_pairs={{0,1},{1,0},{2,3},{3,2},{4,5},{5,4},{6,7},{7,6},{8,9},{9,8},{10,11... | collective-permute-start | bytes 4718600 | tf_op jit(solution)/shard_map/ppermute | solution.py:30
  449.9 14.0 %collective-permute-start.37 = (bf16[2,192,128]{2,1,0:T(8,128)(2,1)}, bf16[2,192,128]{2,1,0:T(8,128)(2,1)S(1)}, u32[]{:S(2)}, u32[]{:S(2)}) collective-permute-start(bf16[2,192,128]{2,1,0:T(8,128)(2,1)} %get-tuple-element.332), channel_id=1, source_target_pairs={{0,8},{4,12},{8,0},{12,4},{16,24},{20,28},{24,16},{28,20},{1,9},{5... | collective-permute-start | bytes 294920 | tf_op jit(solution)/shard_map/ppermute | solution.py:30
  455.2 12.7 %collective-permute-start.38 = (bf16[2,192,128]{2,1,0:T(8,128)(2,1)}, bf16[2,192,128]{2,1,0:T(8,128)(2,1)S(1)}, u32[]{:S(2)}, u32[]{:S(2)}) collective-permute-start(bf16[2,192,128]{2,1,0:T(8,128)(2,1)} %get-tuple-element.333), channel_id=1, source_target_pairs={{0,16},{4,20},{8,24},{12,28},{16,0},{20,4},{24,8},{28,12},{1,17},{... | collective-permute-start | bytes 294920 | tf_op jit(solution)/shard_map/ppermute | solution.py:30
  492.7 15.2 %collective-permute-start.42 = (bf16[8,2,192,128]{3,2,1,0:T(8,128)(2,1)}, bf16[8,2,192,128]{3,2,1,0:T(8,128)(2,1)S(1)}, u32[]{:S(2)}, u32[]{:S(2)}) collective-permute-start(bf16[8,2,192,128]{3,2,1,0:T(8,128)(2,1)} %get-tuple-element.348), channel_id=1, source_target_pairs={{0,4},{4,0},{8,12},{12,8},{16,20},{20,16},{24,28},{28,24},{1,5},{5... | collective-permute-start | bytes 2359304 | tf_op jit(solution)/shard_map/ppermute | solution.py:30
  512.2 13.2 %collective-permute-start.45 = (bf16[2,3,192,128]{3,2,1,0:T(8,128)(2,1)}, bf16[2,3,192,128]{3,2,1,0:T(8,128)(2,1)S(1)}, u32[]{:S(2)}, u32[]{:S(2)}) collective-permute-start(bf16[2,3,192,128]{3,2,1,0:T(8,128)(2,1)} %get-tuple-element.357), channel_id=1, source_target_pairs={{0,8},{4,12},{8,0},{12,4},{16,24},{20,28},{24,16},{28,20},{1,9},{5... | collective-permute-start | bytes 884744 | tf_op jit(solution)/shard_map/ppermute | solution.py:30
  515.0 21.0 %collective-permute-start.46 = (bf16[2,3,192,128]{3,2,1,0:T(8,128)(2,1)}, bf16[2,3,192,128]{3,2,1,0:T(8,128)(2,1)S(1)}, u32[]{:S(2)}, u32[]{:S(2)}) collective-permute-start(bf16[2,3,192,128]{3,2,1,0:T(8,128)(2,1)} %get-tuple-element.358), channel_id=1, source_target_pairs={{0,16},{4,20},{8,24},{12,28},{16,0},{20,4},{24,8},{28,12},{1,17},{... | collective-permute-start | bytes 884744 | tf_op jit(solution)/shard_map/ppermute | solution.py:30
  515.8 20.1 %collective-permute-start.47 = (bf16[2,3,192,128]{3,2,1,0:T(8,128)(2,1)}, bf16[2,3,192,128]{3,2,1,0:T(8,128)(2,1)S(1)}, u32[]{:S(2)}, u32[]{:S(2)}) collective-permute-start(bf16[2,3,192,128]{3,2,1,0:T(8,128)(2,1)} %get-tuple-element.359), channel_id=1, source_target_pairs={{0,24},{4,28},{8,16},{12,20},{16,8},{20,12},{24,0},{28,4},{1,25},{... | collective-permute-start | bytes 884744 | tf_op jit(solution)/shard_map/ppermute | solution.py:30
  520.3 110.8 %all-to-all-start.5 = ((bf16[4,3,192,1024]{3,2,1,0:T(8,128)(2,1)}), bf16[4,3,192,1024]{3,2,1,0:T(8,128)(2,1)}, u32[]{:S(2)}, u32[]{:S(2)}) async-start(bf16[4,3,192,1024]{3,2,1,0:T(8,128)(2,1)} %pad_maximum_fusion), calls=%async_computation.5 | async-start | bytes 9437184 | tf_op jit(solution)/shard_map/all_to_all | solution.py:1198
  525.4 180.1 %all-reduce.8.cloned.1.call-start = ((), (), s32[]{:S(2)}) async-start(), calls=%async_computation.14 | async-start | bytes 5308416 | tf_op jit(solution)/shard_map/psum | solution.py:913
  557.2 18.6 %collective-permute-start.55 = (bf16[2,256,2048]{2,1,0:T(8,128)(2,1)}, bf16[2,256,2048]{2,1,0:T(8,128)(2,1)}, u32[]{:S(2)}, u32[]{:S(2)}) collective-permute-start(bf16[2,256,2048]{2,1,0:T(8,128)(2,1)} %get-tuple-element.380.right), channel_id=1, source_target_pairs={{0,1},{1,0},{2,3},{3,2},{4,5},{5,4},{6,7},{7,6},{8,9},{9,8},{10,11... | collective-permute-start | bytes 6291464 | tf_op jit(solution)/shard_map/ppermute | solution.py:30
  557.9 341.5 %all-reduce.10.cloned.1.call-start = ((), (), s32[]{:S(2)}) async-start(), calls=%async_computation.15 | async-start | bytes 7077888 | tf_op jit(solution)/shard_map/psum | solution.py:913
  558.1 15.7 %collective-permute-start.54 = (bf16[2,256,192]{2,1,0:T(8,128)(2,1)S(1)}, bf16[2,256,192]{2,1,0:T(8,128)(2,1)S(1)}, u32[]{:S(2)}, u32[]{:S(2)}) collective-permute-start(bf16[2,256,192]{2,1,0:T(8,128)(2,1)S(1)} %copy-done.80), channel_id=1, source_target_pairs={{0,1},{1,0},{2,3},{3,2},{4,5},{5,4},{6,7},{7,6},{8,9},{9,8},{10,11... | collective-permute-start | bytes 589832 | tf_op jit(solution)/shard_map/ppermute | solution.py:30
  558.4 60.3 %collective-permute-start.58 = (bf16[1,256,2304]{2,1,0:T(8,128)(2,1)}, bf16[1,256,2304]{2,1,0:T(8,128)(2,1)}, u32[]{:S(2)}, u32[]{:S(2)}) collective-permute-start(bf16[1,256,2304]{2,1,0:T(8,128)(2,1)} %get-tuple-element.394.right), channel_id=1, source_target_pairs={{0,1},{1,0},{2,3},{3,2},{4,5},{5,4},{6,7},{7,6},{8,9},{9,8},{10,11... | collective-permute-start | bytes 3538952 | tf_op jit(solution)/shard_map/ppermute | solution.py:30
  563.3 20.9 %collective-permute-start.49 = (bf16[2,192,128]{2,1,0:T(8,128)(2,1)}, bf16[2,192,128]{2,1,0:T(8,128)(2,1)S(1)}, u32[]{:S(2)}, u32[]{:S(2)}) collective-permute-start(bf16[2,192,128]{2,1,0:T(8,128)(2,1)} %get-tuple-element.371), channel_id=1, source_target_pairs={{0,8},{4,12},{8,0},{12,4},{16,24},{20,28},{24,16},{28,20},{1,9},{5... | collective-permute-start | bytes 294920 | tf_op jit(solution)/shard_map/ppermute | solution.py:30
  567.5 16.7 %collective-permute-start.50 = (bf16[2,192,128]{2,1,0:T(8,128)(2,1)}, bf16[2,192,128]{2,1,0:T(8,128)(2,1)S(1)}, u32[]{:S(2)}, u32[]{:S(2)}) collective-permute-start(bf16[2,192,128]{2,1,0:T(8,128)(2,1)} %get-tuple-element.372), channel_id=1, source_target_pairs={{0,16},{4,20},{8,24},{12,28},{16,0},{20,4},{24,8},{28,12},{1,17},{... | collective-permute-start | bytes 294920 | tf_op jit(solution)/shard_map/ppermute | solution.py:30
  609.7 21.4 %collective-permute-start.56 = (bf16[8,2,192,128]{3,2,1,0:T(8,128)(2,1)}, bf16[8,2,192,128]{3,2,1,0:T(8,128)(2,1)S(1)}, u32[]{:S(2)}, u32[]{:S(2)}) collective-permute-start(bf16[8,2,192,128]{3,2,1,0:T(8,128)(2,1)} %get-tuple-element.391), channel_id=1, source_target_pairs={{0,4},{4,0},{8,12},{12,8},{16,20},{20,16},{24,28},{28,24},{1,5},{5... | collective-permute-start | bytes 2359304 | tf_op jit(solution)/shard_map/ppermute | solution.py:30
  609.7 87.8 %collective-permute-start.65 = (bf16[192,4096]{1,0:T(8,128)(2,1)}, bf16[192,4096]{1,0:T(8,128)(2,1)S(1)}, u32[]{:S(2)}, u32[]{:S(2)}) collective-permute-start(bf16[192,4096]{1,0:T(8,128)(2,1)} %get-tuple-element.416), channel_id=1, source_target_pairs={{0,2},{1,3},{2,0},{3,1},{4,6},{5,7},{6,4},{7,5},{8,10},{9,11},{10,... | collective-permute-start | bytes 4718600 | tf_op jit(solution)/shard_map/ppermute | solution.py:30
  613.9 50.4 %collective-permute-start.66 = (bf16[512,768]{1,0:T(8,128)(2,1)}, bf16[512,768]{1,0:T(8,128)(2,1)}, u32[]{:S(2)}, u32[]{:S(2)}) collective-permute-start(bf16[512,768]{1,0:T(8,128)(2,1)} %get-tuple-element.418), channel_id=1, source_target_pairs={{0,2},{1,3},{2,0},{3,1},{4,6},{5,7},{6,4},{7,5},{8,10},{9,11},{10,... | collective-permute-start | bytes 2359304 | tf_op jit(solution)/shard_map/ppermute | solution.py:30
  632.0 67.2 %collective-permute-start.64 = (bf16[192,2304]{1,0:T(8,128)(2,1)}, bf16[192,2304]{1,0:T(8,128)(2,1)S(1)}, u32[]{:S(2)}, u32[]{:S(2)}) collective-permute-start(bf16[192,2304]{1,0:T(8,128)(2,1)} %get-tuple-element.414), channel_id=1, source_target_pairs={{0,2},{1,3},{2,0},{3,1},{4,6},{5,7},{6,4},{7,5},{8,10},{9,11},{10,... | collective-permute-start | bytes 2654216 | tf_op jit(solution)/shard_map/ppermute | solution.py:30
  634.2 52.6 %collective-permute-start.67 = (bf16[192,768]{1,0:T(8,128)(2,1)S(1)}, bf16[192,768]{1,0:T(8,128)(2,1)S(1)}, u32[]{:S(2)}, u32[]{:S(2)}) collective-permute-start(bf16[192,768]{1,0:T(8,128)(2,1)S(1)} %copy-done.75), channel_id=1, source_target_pairs={{0,2},{1,3},{2,0},{3,1},{4,6},{5,7},{6,4},{7,5},{8,10},{9,11},{10,... | collective-permute-start | bytes 884744 | tf_op jit(solution)/shard_map/ppermute | solution.py:30
  670.3 35.3 %collective-permute-start.61 = (bf16[2,3,192,128]{3,2,1,0:T(8,128)(2,1)}, bf16[2,3,192,128]{3,2,1,0:T(8,128)(2,1)}, u32[]{:S(2)}, u32[]{:S(2)}) collective-permute-start(bf16[2,3,192,128]{3,2,1,0:T(8,128)(2,1)} %get-tuple-element.405), channel_id=1, source_target_pairs={{0,8},{4,12},{8,0},{12,4},{16,24},{20,28},{24,16},{28,20},{1,9},{5... | collective-permute-start | bytes 884744 | tf_op jit(solution)/shard_map/ppermute | solution.py:30
  678.3 33.7 %collective-permute-start.62 = (bf16[2,3,192,128]{3,2,1,0:T(8,128)(2,1)}, bf16[2,3,192,128]{3,2,1,0:T(8,128)(2,1)}, u32[]{:S(2)}, u32[]{:S(2)}) collective-permute-start(bf16[2,3,192,128]{3,2,1,0:T(8,128)(2,1)} %get-tuple-element.406), channel_id=1, source_target_pairs={{0,16},{4,20},{8,24},{12,28},{16,0},{20,4},{24,8},{28,12},{1,17},{... | collective-permute-start | bytes 884744 | tf_op jit(solution)/shard_map/ppermute | solution.py:30
  686.9 25.2 %collective-permute-start.63 = (bf16[2,3,192,128]{3,2,1,0:T(8,128)(2,1)}, bf16[2,3,192,128]{3,2,1,0:T(8,128)(2,1)}, u32[]{:S(2)}, u32[]{:S(2)}) collective-permute-start(bf16[2,3,192,128]{3,2,1,0:T(8,128)(2,1)} %get-tuple-element.407), channel_id=1, source_target_pairs={{0,24},{4,28},{8,16},{12,20},{16,8},{20,12},{24,0},{28,4},{1,25},{... | collective-permute-start | bytes 884744 | tf_op jit(solution)/shard_map/ppermute | solution.py:30
  719.2 29.0 %collective-permute-start.68 = (bf16[1,256,2304]{2,1,0:T(8,128)(2,1)}, bf16[1,256,2304]{2,1,0:T(8,128)(2,1)S(1)}, u32[]{:S(2)}, u32[]{:S(2)}) collective-permute-start(bf16[1,256,2304]{2,1,0:T(8,128)(2,1)} %get-tuple-element.425.right), channel_id=1, source_target_pairs={{0,1},{1,0},{2,3},{3,2},{4,5},{5,4},{6,7},{7,6},{8,9},{9,8},{10,11... | collective-permute-start | bytes 3538952 | tf_op jit(solution)/shard_map/ppermute | solution.py:30
  725.2 12.3 %collective-permute-start.82 = (f32[20,768]{1,0:T(8,128)S(1)}, f32[20,768]{1,0:T(8,128)S(1)}, u32[]{:S(2)}, u32[]{:S(2)}) collective-permute-start(f32[20,768]{1,0:T(8,128)S(1)} %add.203), channel_id=1, source_target_pairs={{0,8},{4,12},{8,0},{12,4},{16,24},{20,28},{24,16},{28,20},{1,9},{5... | collective-permute-start | bytes 184328 | tf_op jit(solution)/shard_map/ppermute | solution.py:30
  730.9 17.2 %collective-permute-start.30 = (bf16[2,256,192]{2,1,0:T(8,128)(2,1)S(1)}, bf16[2,256,192]{2,1,0:T(8,128)(2,1)S(1)}, u32[]{:S(2)}, u32[]{:S(2)}) collective-permute-start(bf16[2,256,192]{2,1,0:T(8,128)(2,1)S(1)} %copy-done.79), channel_id=1, source_target_pairs={{0,1},{1,0},{2,3},{3,2},{4,5},{5,4},{6,7},{7,6},{8,9},{9,8},{10,11... | collective-permute-start | bytes 589832 | tf_op jit(solution)/shard_map/ppermute | solution.py:30
  748.1 18.2 %collective-permute-start.84 = (f32[20,768]{1,0:T(8,128)S(1)}, f32[20,768]{1,0:T(8,128)S(1)}, u32[]{:S(2)}, u32[]{:S(2)}) collective-permute-start(f32[20,768]{1,0:T(8,128)S(1)} %add.205), channel_id=1, source_target_pairs={{0,1},{1,0},{2,3},{3,2},{4,5},{5,4},{6,7},{7,6},{8,9},{9,8},{10,11... | collective-permute-start | bytes 184328 | tf_op jit(solution)/shard_map/ppermute | solution.py:30
  754.5 22.7 %collective-permute-start.69 = (bf16[192,2304]{1,0:T(8,128)(2,1)}, bf16[192,2304]{1,0:T(8,128)(2,1)S(1)}, u32[]{:S(2)}, u32[]{:S(2)}) collective-permute-start(bf16[192,2304]{1,0:T(8,128)(2,1)} %get-tuple-element.433), channel_id=1, source_target_pairs={{0,2},{1,3},{2,0},{3,1},{4,6},{5,7},{6,4},{7,5},{8,10},{9,11},{10,... | collective-permute-start | bytes 2654216 | tf_op jit(solution)/shard_map/ppermute | solution.py:30
  756.0 160.5 %all-to-all-start.6 = ((bf16[16,64,768]{2,1,0:T(8,128)(2,1)}), bf16[16,64,768]{2,1,0:T(8,128)(2,1)S(1)}, u32[]{:S(2)}, u32[]{:S(2)}) async-start(bf16[16,64,768]{2,1,0:T(8,128)(2,1)} %bitcast.54), calls=%async_computation.6 | async-start | bytes 3145728 | tf_op jit(solution)/shard_map/all_to_all | solution.py:952
  766.3 39.1 %collective-permute-start.85 = (f32[20,768]{1,0:T(8,128)S(1)}, f32[20,768]{1,0:T(8,128)S(1)}, u32[]{:S(2)}, u32[]{:S(2)}) collective-permute-start(f32[20,768]{1,0:T(8,128)S(1)} %add.206), channel_id=1, source_target_pairs={{0,2},{1,3},{2,0},{3,1},{4,6},{5,7},{6,4},{7,5},{8,10},{9,11},{10,... | collective-permute-start | bytes 184328 | tf_op jit(solution)/shard_map/ppermute | solution.py:30
  781.3 16.1 %collective-permute-start.70 = (bf16[192,1152]{1,0:T(8,128)(2,1)}, bf16[192,1152]{1,0:T(8,128)(2,1)S(1)}, u32[]{:S(2)}, u32[]{:S(2)}) collective-permute-start(bf16[192,1152]{1,0:T(8,128)(2,1)} %get-tuple-element.435), channel_id=1, source_target_pairs={{0,4},{4,0},{8,12},{12,8},{16,20},{20,16},{24,28},{28,24},{1,5},{5... | collective-permute-start | bytes 1327112 | tf_op jit(solution)/shard_map/ppermute | solution.py:30
  800.9 23.5 %collective-permute-start.72 = (bf16[48,1152]{1,0:T(8,128)(2,1)}, bf16[48,1152]{1,0:T(8,128)(2,1)S(1)}, u32[]{:S(2)}, u32[]{:S(2)}) collective-permute-start(bf16[48,1152]{1,0:T(8,128)(2,1)} %get-tuple-element.438), channel_id=1, source_target_pairs={{0,16},{4,20},{8,24},{12,28},{16,0},{20,4},{24,8},{28,12},{1,17},{... | collective-permute-start | bytes 331784 | tf_op jit(solution)/shard_map/ppermute | solution.py:30
  803.5 21.0 %collective-permute-start.73 = (bf16[48,1152]{1,0:T(8,128)(2,1)}, bf16[48,1152]{1,0:T(8,128)(2,1)S(1)}, u32[]{:S(2)}, u32[]{:S(2)}) collective-permute-start(bf16[48,1152]{1,0:T(8,128)(2,1)} %get-tuple-element.439), channel_id=1, source_target_pairs={{0,24},{4,28},{8,16},{12,20},{16,8},{20,12},{24,0},{28,4},{1,25},{... | collective-permute-start | bytes 331784 | tf_op jit(solution)/shard_map/ppermute | solution.py:30
  828.2 16.9 %collective-permute-start.75 = (bf16[48,1152]{1,0:T(8,128)(2,1)S(1)}, bf16[48,1152]{1,0:T(8,128)(2,1)S(1)}, u32[]{:S(2)}, u32[]{:S(2)}) collective-permute-start(bf16[48,1152]{1,0:T(8,128)(2,1)S(1)} %add_convert_fusion.2.refs_0_), channel_id=1, source_target_pairs={{0,16},{4,20},{8,24},{12,28},{16,0},{20,4},{24,8},{28,12},{1,17},{... | collective-permute-start | bytes 331784 | tf_op jit(solution)/shard_map/ppermute | solution.py:30
  828.3 16.8 %collective-permute-start.76 = (bf16[48,1152]{1,0:T(8,128)(2,1)S(1)}, bf16[48,1152]{1,0:T(8,128)(2,1)S(1)}, u32[]{:S(2)}, u32[]{:S(2)}) collective-permute-start(bf16[48,1152]{1,0:T(8,128)(2,1)S(1)} %add_convert_fusion.2.refs_0_), channel_id=1, source_target_pairs={{0,24},{4,28},{8,16},{12,20},{16,8},{20,12},{24,0},{28,4},{1,25},{... | collective-permute-start | bytes 331784 | tf_op jit(solution)/shard_map/ppermute | solution.py:30
  (136 other events, 1269.3 us)
Sparse Core Ops, SparseCore 0:
  13.5 20.0 all-gather.14
  35.8 56.5 all-gather.18
  94.5 62.2 all-gather.16
  158.8 30.7 all-gather.20
  191.0 17.4 all-gather.22
  209.9 42.3 all-gather.26
  254.5 51.4 all-gather.24
  558.0 147.4 all-reduce.7
  722.4 176.9 all-reduce.9

commit v4 on v3

--- a/solution.py
+++ b/solution.py
@@ -717,14 +717,16 @@
     out[1] = other[...].astype(jnp.float32)
 
 
-def reduce_last(place, own, arrived, other, held):
+def reduce_last(place, own, arrived, other, held, small):
     lines = lax.axis_size("ctx") // 2
     rows, width = own.shape
     chunk, half = rows // lines, width // 2
     if chunk % 16:
         summed = lax.psum(own + arrived, "ctx")
-        return jnp.stack([summed, other]).astype(jnp.float32), held
+        return jnp.stack([summed, other]).astype(jnp.float32), held, total_small(small)
     sent, kept = call(_halve_kernel, place, (own, arrived), [_shape((rows, half))] * 2)
+    kept, small = lax.optimization_barrier((kept, small))
+    small = total_small(small)
     parts = call(
         _quarter_kernel,
         place,
@@ -744,13 +746,14 @@
             _place_kernel, place, (other, *parts), [_shape((2, rows, width), jnp.float32)]
         )[0],
         held,
+        small,
     )
 
 
 def _expert_kernel(units, meta, *refs):
     xs, cs = refs[:units], refs[units : 2 * units]
-    router, ids, w_in, w_out = refs[2 * units : 2 * units + 4]
-    outs = refs[2 * units + 4 :]
+    router, ids, w = refs[2 * units : 2 * units + 3]
+    outs = refs[2 * units + 3 :]
     parts, backs = outs[:units], outs[units : 2 * units]
     rows_out, grads_out, hidden_out, gate_out, up_out, dots_out = outs[2 * units : 2 * units + 6]
     gates, ups, downs, x, c = outs[2 * units + 6 :]
@@ -759,12 +762,12 @@
 
     @pl.when(step == 0)
     def _():
-        width = w_in.shape[2]
+        width = w.shape[2]
         for f in range(4):
             part = slice(f * width, (f + 1) * width)
-            gates[part, :] = w_in[f, 0]
-            ups[part, :] = w_in[f, 1]
-            downs[part, :] = w_out[f]
+            gates[part, :] = w[f, 0]
+            ups[part, :] = w[f, 1]
+            downs[part, :] = w[f, 2]
 
     for u in range(units):
 
@@ -808,9 +811,9 @@
             backs[u][...] = back.astype(jnp.bfloat16)
 
 
-def experts(meta, xs, cs, router, ids, w_in, w_out):
-    units, (rows, width), tile = len(xs), xs[0].shape, 256
-    tiles, hidden = rows // tile, w_out.shape[2]
+def experts(meta, xs, cs, router, ids, w):
+    units, (rows, width), tile = len(xs), xs[0].shape, 1024 // len(xs)
+    tiles, hidden = rows // tile, w.shape[3]
     total_rows = units * rows
     slabs = [
         pl.BlockSpec((tile, width), lambda i, m, u=u: (jnp.clip(i - u * tiles, 0, tiles - 1), 0))
@@ -823,7 +826,7 @@
     got = call(
         functools.partial(_expert_kernel, units),
         meta,
-        (*xs, *cs, router, ids, w_in, w_out),
+        (*xs, *cs, router, ids, w),
         [_shape((rows, width))] * (2 * units)
         + [_shape((total_rows, width))] * 2
         + [_shape((total_rows, hidden))] * 3
@@ -833,7 +836,7 @@
         flops=12 * total_rows * width * hidden,
         in_specs=slabs
         + slabs
-        + [_whole(router.shape), rowed(1), _whole(w_in.shape), _whole(w_out.shape)],
+        + [_whole(router.shape), rowed(1), _whole(w.shape)],
         out_specs=slabs + slabs + [rowed(width)] * 2 + [rowed(hidden)] * 3 + [rowed(1)],
         grid=(units * tiles,),
     )
@@ -893,8 +896,7 @@
     inputs = list(qkv)
     for part in range(1, head_parts()):
         inputs += [swap(values, "ctx", part) for values in qkv]
-    qkv[1], early = lax.optimization_barrier((qkv[1], early))
-    inputs[1] = qkv[1]
+    inputs, early = lax.optimization_barrier((inputs, early))
     heads, acc, lse = attend(meta, inputs, count)
     return heads, (keep, send, inputs, acc, lse), early
 
@@ -1023,53 +1025,51 @@
     gains = [small[i : i + 1].astype(jnp.float32) for i in range(4)]
     router_full = small[4:].T
     grad_rows = to_slots(cotangent[0]).reshape(num_experts, capacity, model_width)
-    grad_sent = dispatch(with_notes(grad_rows, other_ids.reshape(num_experts, capacity)))
-    far_shard, tables, meta, gains = lax.optimization_barrier((far_shard, tables, meta, gains))
+    grad_sent = with_notes(grad_rows, other_ids.reshape(num_experts, capacity))
+    stored = jnp.concatenate(
+        [jnp.swapaxes(expert_in, 1, 2), jnp.swapaxes(expert_out, 0, 1)[None]]
+    )
+    expert_part = jnp.stack(
+        [stored[:, :, f * hid_unit : (f + 1) * hid_unit] for f in range(fsdp_count)]
+    )
+    near_out, far_out = swap(attn_out[0], "fsdp", 1), swap(attn_out[0], "fsdp", 2)
+    far_shard, tables, meta, gains, expert_part = lax.optimization_barrier(
+        (far_shard, tables, meta, gains, expert_part)
+    )
     w_attn_in_one = (shard, near_shard, far_shard, swap(far_shard, "fsdp", 1))
-    near_shard, attn_in, attn_out, mlp_in, mlp_out = lax.optimization_barrier(
-        (near_shard, attn_in, attn_out, mlp_in, mlp_out)
-    )
-    w_attn_out_one, w_mlp_in_one, w_mlp_out_one = (
-        gathered(attn_out[0]), gathered(mlp_in[0]), gathered(mlp_out[0])
-    )
-    w_attn_in_two, w_attn_out_two = gathered(attn_in[1]), gathered(attn_out[1])
+    own_out = attn_out[0]
+    far_shard, far_out, attn_in, attn_out, mlp_in, mlp_out = lax.optimization_barrier(
+        (far_shard, far_out, attn_in, attn_out, mlp_in, mlp_out)
+    )
+    w_attn_out_one = (own_out, near_out, far_out, swap(far_out, "fsdp", 1))
+    w_mlp_in_one, w_mlp_out_one = gathered(mlp_in[0]), gathered(mlp_out[0])
     w_mlp_in_two, w_mlp_out_two = gathered(mlp_in[1]), gathered(mlp_out[1])
 
     resid_in = tokens[0].astype(jnp.float32)
-    heads_one, kept_one, (grad_sent, expert_parts) = attend_forward(
-        meta,
-        count,
-        resid_in,
-        gains[0],
-        tables,
-        w_attn_in_one,
-        (
-            grad_sent,
-            (
-                jnp.swapaxes(expert_in, 1, 2).reshape(2, shard_width, fsdp_count, hid_unit),
-                jnp.swapaxes(expert_out, 0, 1).reshape(shard_width, fsdp_count, hid_unit),
-            ),
-        ),
-    )
-    expert_w_out = lax.all_to_all(
-        jnp.transpose(expert_parts[1], (1, 0, 2)), "fsdp", 0, 0, tiled=True
-    )
-    heads_one, expert_w_out, expert_part = lax.optimization_barrier(
-        (heads_one, expert_w_out, expert_parts[0])
-    )
+    heads_one, kept_one, (grad_sent, attn_in, attn_out) = attend_forward(
+        meta, count, resid_in, gains[0], tables, w_attn_in_one, (grad_sent, attn_in, attn_out)
+    )
+    far_in, far_out = swap(attn_in[1], "fsdp", 2), swap(attn_out[1], "fsdp", 2)
+    grad_sent = dispatch(grad_sent)
     heads_one = exchange(heads_one)
+    heads_one, far_in, far_out = lax.optimization_barrier((heads_one, far_in, far_out))
+    w_attn_in_two, w_attn_out_two = [
+        (own, swap(own, "fsdp", 1), far, swap(far, "fsdp", 1))
+        for own, far in ((attn_in[1], far_in), (attn_out[1], far_out))
+    ]
     after_one, _, blocks_one, keep_one, send_one, att_keep_one, att_send_one = post(
         meta, resid_in, gains[1], heads_one, w_attn_out_one
     )
+    after_one, grad_sent, expert_part = lax.optimization_barrier(
+        (after_one, grad_sent, expert_part)
+    )
+    expert_w = lax.all_to_all(expert_part, "fsdp", 0, 0, tiled=True)
     middle, mixed_one, hid_keep_one, hid_send_one = mlp(
         meta, after_one, blocks_one, w_mlp_in_one, w_mlp_out_one
     )
     near_one = near(send_one, att_send_one, hid_send_one)
-    heads_two, kept_two, (expert_part, grad_sent) = attend_forward(
-        meta, count, middle, gains[2], tables, w_attn_in_two, (expert_part, grad_sent)
-    )
-    expert_w = lax.all_to_all(
-        jnp.transpose(expert_part, (2, 0, 1, 3)), "fsdp", 0, 0, tiled=True
+    heads_two, kept_two, grad_sent = attend_forward(
+        meta, count, middle, gains[2], tables, w_attn_in_two, grad_sent
     )
     grad_arrived = to_units(grad_sent[:, :capacity].reshape(slot_count, model_width))
     arrived_ids = jnp.concatenate(
@@ -1112,7 +1112,6 @@
         router_wide,
         arrived_ids,
         expert_w,
-        expert_w_out,
     )
     arrived, grad_rows, hidden_rows, grad_gate, grad_up, dots = kept_rows
     dots = from_units(dots.reshape(units, num_experts, capacity))
@@ -1181,89 +1180,110 @@
     grad_attn_out_two = weight_grad(
         meta, att_keep_two, *near(att_send_two), branch, *near(branch)
     )
-    grad_heads, grad_attn_out_two = lax.optimization_barrier((grad_heads, grad_attn_out_two))
+    sum_mlp_in_two = add_arrived(grad_mlp_in_two)
+    grad_heads, grad_attn_out_two, grad_experts, sum_mlp_in_two, sum_mlp_out_two = (
+        lax.optimization_barrier(
+            (grad_heads, grad_attn_out_two, grad_experts, sum_mlp_in_two, sum_mlp_out_two)
+        )
+    )
+    grad_experts = lax.all_to_all(grad_experts, "fsdp", 0, 0, tiled=True)
     grad_q, own, others = attend_back(
         meta, kept_two[2], grad_heads, kept_two[3], kept_two[4], count
     )
     arrived_kv = [swap(values, "ctx", part + 1) for part, values in enumerate(others)]
-    sum_mlp_in_two = add_arrived(grad_mlp_in_two)
     sum_attn_out_two = add_arrived(grad_attn_out_two)
-    arrived_kv, grad_experts, *sums_two = lax.optimization_barrier(
-        (arrived_kv, grad_experts, sum_mlp_in_two, sum_mlp_out_two, sum_attn_out_two)
-    )
-    sums_two = total(0, sums_two)
     grad_qkv = exchange(merge(meta, grad_q, own, arrived_kv))
     expert_rows = from_units(partial_rows).astype(jnp.bfloat16)
-    grad_qkv, expert_rows = lax.optimization_barrier((grad_qkv, expert_rows))
-    grad_experts = lax.all_to_all(grad_experts, "fsdp", 0, 0, tiled=True)
+    sums_two = jnp.concatenate(
+        [sum_mlp_in_two, sum_mlp_out_two.reshape(shard_width, -1)], axis=1
+    ).reshape(ctx_count, shard_width // ctx_count, -1)
+    grad_qkv, expert_rows, grad_experts, sums_two, sum_attn_out_two = lax.optimization_barrier(
+        (grad_qkv, expert_rows, grad_experts, sums_two, sum_attn_out_two)
+    )
+    sums_two = lax.all_to_all(sums_two, "ctx", 0, 0, tiled=True)
     grad_mixed, grad_resid, gain_two = pre_back(
         meta, middle, gains[2], tables, grad_resid, grad_qkv, w_attn_in_two
     )
+    near_qkv = near(kept_two[1], grad_mixed)
     branch = grad_resid.astype(jnp.bfloat16)[None]
     grad_mixed_one, grad_normed = mlp_back(
         meta, branch, mixed_one, w_mlp_in_one, w_mlp_out_one
     )
-    near_mixed = near(grad_mixed, branch, grad_mixed_one)
+    grad_attn_in_two = weight_grad(meta, kept_two[0], near_qkv[0], grad_mixed, near_qkv[1])
+    grad_normed, grad_attn_in_two = lax.optimization_barrier((grad_normed, grad_attn_in_two))
+    near_mixed = [None] + near(branch, grad_mixed_one)
     grad_heads, grad_resid, att_branch, gain_one = post_back(
         meta, after_one, gains[1], grad_resid, grad_normed, w_attn_out_one
     )
     near_branch = near(att_branch)[0]
     grad_heads = exchange(grad_heads)
     grad_mlp_in_one = weight_grad(meta, keep_one, near_one[0], grad_mixed_one, near_mixed[2])
-    grad_mlp_out_one = weight_grad(meta, hid_keep_one, near_one[2], branch, near_mixed[1])
-    grad_heads, grad_mlp_out_one, grad_mlp_in_one = lax.optimization_barrier(
-        (grad_heads, grad_mlp_out_one, grad_mlp_in_one)
-    )
+    first_sent = jnp.concatenate([grad_mlp_in_one[1], grad_attn_in_two[1]], axis=1)
+    grad_heads, first_sent, expert_rows, sums_two = lax.optimization_barrier(
+        (grad_heads, first_sent, expert_rows, sums_two)
+    )
+    sums_two = jnp.sum(sums_two.astype(jnp.float32), axis=0).astype(jnp.bfloat16)
+    sums_two = lax.all_gather(sums_two, "ctx", axis=0, tiled=True)
+    expert_rows = dispatch(expert_rows.reshape(num_experts, capacity, model_width))
+    expert_rows = expert_rows.reshape(slot_count, model_width)
+    first_arrived = swap(first_sent, "fsdp", 2)
     grad_q, own, others = attend_back(
         meta, kept_one[2], grad_heads, kept_one[3], kept_one[4], count
     )
     arrived_kv = [swap(values, "ctx", part + 1) for part, values in enumerate(others)]
-    grad_attn_in_two = weight_grad(
-        meta, kept_two[0], *near(kept_two[1]), grad_mixed, near_mixed[0]
-    )
+    grad_mlp_out_one = weight_grad(meta, hid_keep_one, near_one[2], branch, near_mixed[1])
     grad_attn_out_one = weight_grad(meta, att_keep_one, near_one[1], att_branch, near_branch)
-    arrived_kv, grad_attn_in_two, grad_attn_out_one, grad_experts = lax.optimization_barrier(
-        (arrived_kv, grad_attn_in_two, grad_attn_out_one, grad_experts)
+    second_sent = jnp.concatenate([grad_mlp_out_one[1], grad_attn_out_one[1]], axis=0)
+    wide = grad_mlp_in_one[0].shape[1]
+    first_sums = (
+        grad_attn_in_two[0] + first_arrived[:, wide:],
+        grad_mlp_in_one[0] + first_arrived[:, :wide],
+    )
+    arrived_kv, second_sent, first_sums = lax.optimization_barrier(
+        (arrived_kv, second_sent, first_sums)
     )
     grad_qkv = exchange(merge(meta, grad_q, own, arrived_kv))
+    second_arrived = swap(second_sent, "fsdp", 2)
+    tall = grad_mlp_out_one[0].shape[0]
     sums_one = [
-        add_arrived(g)
-        for g in (grad_attn_in_two, grad_mlp_in_one, grad_mlp_out_one, grad_attn_out_one)
+        *first_sums,
+        grad_mlp_out_one[0] + second_arrived[:tall],
+        grad_attn_out_one[0] + second_arrived[tall:],
+        sum_attn_out_two,
     ]
-    grad_experts = jnp.transpose(grad_experts, (1, 2, 0, 3)).astype(jnp.float32)
-    grad_experts = grad_experts.reshape(3, shard_width, hid_unit * fsdp_count)
-    grad_qkv, sums_two, expert_rows, grad_experts, *sums_one = lax.optimization_barrier(
-        (grad_qkv, sums_two, expert_rows, grad_experts, *sums_one)
+    grad_qkv, expert_rows, sums_two, *sums_one = lax.optimization_barrier(
+        (grad_qkv, expert_rows, sums_two, *sums_one)
     )
     sums_one = total(1, sums_one)
     grad_mixed, grad_resid, gain_zero = pre_back(
         meta, resid_in, gains[0], tables, grad_resid, grad_qkv, w_attn_in_one
     )
-    grad_attn_in_one = weight_grad(
-        meta, kept_one[0], *near(kept_one[1]), grad_mixed, *near(grad_mixed)
-    )
-    grad_attn_in_one, expert_rows = lax.optimization_barrier((grad_attn_in_one, expert_rows))
-    expert_rows = dispatch(expert_rows.reshape(num_experts, capacity, model_width))
-    expert_rows = expert_rows.reshape(slot_count, model_width)
+    near_qkv = near(kept_one[1], grad_mixed)
+    grad_attn_in_one = weight_grad(meta, kept_one[0], near_qkv[0], grad_mixed, near_qkv[1])
+    grad_attn_in_one, expert_rows, grad_experts = lax.optimization_barrier(
+        (grad_attn_in_one, expert_rows, grad_experts)
+    )
+    grad_experts = jnp.transpose(grad_experts, (1, 2, 0, 3)).astype(jnp.float32)
+    grad_experts = grad_experts.reshape(3, shard_width, hid_unit * fsdp_count)
     back_rows = [jnp.dot(p, expert_rows, preferred_element_type=jnp.float32) for p in of_token]
     output = shared + sum(gate_probs[:, k, None] * back_rows[k] for k in range(TOP))
-    small_grads = total_small(
-        jnp.concatenate([gain_zero, gain_one, gain_two, gain_three, grad_router])
-    )
-    small_grads = lax.dynamic_slice_in_dim(small_grads, own_fsdp * shard_width, shard_width, 1)
-    attn_in_grad, sums_one = reduce_last(
+    small_grads = jnp.concatenate([gain_zero, gain_one, gain_two, gain_three, grad_router])
+    attn_in_grad, sums_one, small_grads = reduce_last(
         at_ctx,
         grad_attn_in_one[0],
         swap(grad_attn_in_one[1], "fsdp", 2),
         sums_one[0],
         sums_one,
-    )
+        small_grads,
+    )
+    small_grads = lax.dynamic_slice_in_dim(small_grads, own_fsdp * shard_width, shard_width, 1)
+    wide = sums_one[1].shape[1]
     dense_grads = [attn_in_grad] + [
         jnp.stack(pair).astype(jnp.float32)
         for pair in (
-            (sums_one[3], sums_two[2]),
-            (sums_one[1], sums_two[0]),
-            (sums_one[2], sums_two[1]),
+            (sums_one[3], sums_one[4]),
+            (sums_one[1], sums_two[:, :wide]),
+            (sums_one[2], sums_two[:, wide:].reshape(sums_one[2].shape)),
         )
     ]
     return (

time: 941 us -> 910 us (0.967)
  waiting for transfers between devices: 360 us -> 334 us
  Pallas kernels: 278 us -> 253 us
  starting transfers between devices: 140 us -> 159 us
  other arithmetic: 44 us -> 62.7 us
  local copies, waits for them, and re-layouts: 66.6 us -> 52.2 us
    ppermute x86 -> x93, waiting for transfers between devices: 286 us -> 255 us  [swap(): return lax.ppermute(values, axis, [(i, i ^ mask) for i in range(count)])]
    pallas_call x30, Pallas kernels: 278 us -> 253 us  [call(): pl.pallas_call(body, grid_spec=pltpu.PrefetchScalarGridSpec(num_scalar_pr...]
    reshape x3 -> x0, local copies, waits for them, and re-layouts: 13.5 us -> none  [the longest x1 5.06 us: per_device(): jnp.swapaxes(expert_in, 1, 2).reshape(2, shard_width, fsdp_count, hid_unit)]
    ppermute x86 -> x93, starting transfers between devices: 102 us -> 112 us  [swap(): return lax.ppermute(values, axis, [(i, i ^ mask) for i in range(count)])]
    transpose x2 -> x0, local copies, waits for them, and re-layouts: 10.2 us -> none  [the longest x1 6.31 us: per_device(): jnp.swapaxes(grad_experts[:2], 1, 2)]
    all_to_all x2, waiting for transfers between devices: 0.01 us -> 9.63 us  [the longest x1 9.62 us: per_device(): expert_w = lax.all_to_all(expert_part, 'fsdp', 0, 0, tiled=True)]
    psum x2 -> x1, waiting for transfers between devices: 59.4 us -> 56.5 us  [total(): return lax.psum(tuple(grads), 'ctx', axis_index_groups=ring)]
  transfers between devices with their start and end apart: 102 -> 106, of which waited for: 46 -> 45; matrix products, arithmetic and copies ran while one was open for 12% -> 13% of each run, Pallas kernels for 25% -> 23%
where the time goes in v4:
time: 910 us; the launch traced here: 898 us
  waiting for transfers between devices  334 us (37%)
  Pallas kernels  253 us (28%)
  starting transfers between devices  159 us (17%)
  other arithmetic  62.7 us (7%)
  local copies, waits for them, and re-layouts  52.2 us (6%)
  matrix products  21.5 us (2%)
  between operations  15.8 us (2%)
    ppermute x93, waiting for transfers between devices, swap(): return lax.ppermute(values, axis, [(i, i ^ mask) for i in range(count)])  255 us
    pallas_call x30, Pallas kernels, call(): pl.pallas_call(body, grid_spec=pltpu.PrefetchScalarGridSpec(num_scalar_pr...  253 us
    ppermute x93, starting transfers between devices, swap(): return lax.ppermute(values, axis, [(i, i ^ mask) for i in range(count)])  112 us
    psum x1, waiting for transfers between devices, total(): return lax.psum(tuple(grads), 'ctx', axis_index_groups=ring)  56.5 us
    all_to_all x4, starting transfers between devices, dispatch(): lax.all_to_all(values, BOTH, 0, 0, tiled=True, axis_index_groups=members)  29.4 us
    unnamed x226, local copies, waits for them, and re-layouts  18.4 us
  transfers between devices with their start and end apart: 106, of which 45 were waited for; matrix products, arithmetic and copies ran while one was open for 13% of the time, Pallas kernels for 23%

profile of v4, /device:TPU:0, one launch (start us, length us, event | category | flops | bytes accessed | tf_op | source)
XLA Modules:
  0.0 898.2 jit_solution(8094085688009455864)
XLA Ops:
  25.1 10.3 %collective-permute-done.w2.rest_6_ = bf16[192,2304]{1,0:T(8,128)(2,1)S(1)} collective-permute-done((bf16[192,2304]{1,0:T(8,128)(2,1)S(1)}, bf16[192,2304]{1,0:T(8,128)(2,1)S(1)}, u32[]{:S(2)}, u32[]{:S(2)}) %collective-permute-start) | collective-permute-done | bytes 884768 | tf_op jit(solution)/shard_map/ppermute | solution.py:30
  35.4 5.9 collective-permute-done.13.w2
  57.2 5.8 shard_map.204
  69.4 8.6 collective-permute-done.6.refs_1_
  79.6 8.7 collective-permute-done.7.refs_2_
  98.9 7.3 all-to-all-start
  109.5 16.3 %shard_map.205 = (bf16[2,192,128]{2,1,0:T(8,128)(2,1)}, bf16[2,192,128]{2,1,0:T(8,128)(2,1)}, bf16[2,192,128]{2,1,0:T(8,128)(2,1)}, bf16[2,192,128]{2,1,0:T(8,12...) custom-call(s32[22]{0:T(128)} %concatenate.42.meta, bf16[2,3,192,128]{3,2,1,0:T(8,128)(2,1)} %get-tuple-element.270.refs_0_, ...), custom_call_target="tpu_custom_call" | custom-call | flops 1610612736 | bytes 3551232 | tf_op jit(solution)/shard_map/pallas_call | solution.py:91
  128.9 5.8 collective-permute-done.14.o1
  134.7 5.5 collective-permute-start.15
  140.2 9.2 %collective-permute-done.15.o2 = bf16[2,192,128]{2,1,0:T(8,128)(2,1)S(1)} collective-permute-done((bf16[2,192,128]{2,1,0:T(8,128)(2,1)}, bf16[2,192,128]{2,1,0:T(8,128)(2,1)S(1)}, u32[]{:S(2)}, u32[]{:S(2)}) %collective-permute-start.15) | collective-permute-done | bytes 98336 | tf_op jit(solution)/shard_map/ppermute | solution.py:30
  150.6 5.4 collective-permute-done.16.o3
  156.0 11.7 %collective-permute-done.18.w2 = bf16[192,768]{1,0:T(8,128)(2,1)S(1)} collective-permute-done((bf16[192,768]{1,0:T(8,128)(2,1)S(1)}, bf16[192,768]{1,0:T(8,128)(2,1)S(1)}, u32[]{:S(2)}, u32[]{:S(2)}) %collective-permute-start.18) | collective-permute-done | bytes 294944 | tf_op jit(solution)/shard_map/ppermute | solution.py:30
  169.2 4.6 shard_map.206
  173.8 5.0 all-to-all-start.1
  179.4 10.4 %shard_map.207 = (f32[256,768]{1,0:T(8,128)}, f32[2,256,2048]{2,1,0:T(8,128)}, bf16[2,256,512]{2,1,0:T(8,128)(2,1)}, bf16[2,256,512]{2,1,0:T(8,128)(2,1)}) custom-call(s32[22]{0:T(128)} %concatenate.42.meta, f32[256,768]{1,0:T(8,128)} %get-tuple-element.292.x, bf16[4,256,192]{2,1,0:T(8,128)(2,1)} %get-tuple-element.293.blocks, bf16[768,4096]{1,0:T(8,128)(2,1)} %bitcast.131, ...), custom_call_target="tpu_custom_call" | custom-call | flops 2415919104 | bytes 70123520 | tf_op jit(solution)/shard_map/pallas_call | solution.py:91
  189.8 5.9 shard_map.208
  201.5 9.6 %collective-permute-done.23.refs_1_ = bf16[2,3,192,128]{3,2,1,0:T(8,128)(2,1)S(1)} collective-permute-done((bf16[2,3,192,128]{3,2,1,0:T(8,128)(2,1)}, bf16[2,3,192,128]{3,2,1,0:T(8,128)(2,1)S(1)}, u32[]{:S(2)}, u32[]{:S(2)}) %collective-permute-start.23) | collective-permute-done | bytes 294944 | tf_op jit(solution)/shard_map/ppermute | solution.py:30
  212.5 8.3 collective-permute-done.24.refs_2_
  222.8 6.4 collective-permute-done.28.refs_6_
  234.9 15.9 %shard_map.209 = (bf16[2,192,128]{2,1,0:T(8,128)(2,1)}, bf16[2,192,128]{2,1,0:T(8,128)(2,1)}, bf16[2,192,128]{2,1,0:T(8,128)(2,1)}, bf16[2,192,128]{2,1,0:T(8,12...) custom-call(s32[22]{0:T(128)} %concatenate.42.meta, bf16[2,3,192,128]{3,2,1,0:T(8,128)(2,1)} %get-tuple-element.305.refs_0_, ...), custom_call_target="tpu_custom_call" | custom-call | flops 1610612736 | bytes 3551232 | tf_op jit(solution)/shard_map/pallas_call | solution.py:91
  256.7 9.6 %all-to-all-done.1.refs_6_ = bf16[4,3,192,1024]{3,2,1,0:T(8,128)(2,1)} async-done(((bf16[4,3,192,1024]{3,2,1,0:T(8,128)(2,1)}), bf16[4,3,192,1024]{3,2,1,0:T(8,128)(2,1)}, u32[]{:S(2)}, u32[]{:S(2)}) %all-to-all-start.1) | async-done | bytes 4718624 | tf_op jit(solution)/shard_map/all_to_all | solution.py:1066
  267.6 4.6 shard_map.210
  275.0 7.2 all-to-all-start.2
  282.4 10.5 %shard_map.211 = (f32[256,768]{1,0:T(8,128)}, f32[2,256,2048]{2,1,0:T(8,128)}, bf16[2,256,512]{2,1,0:T(8,128)(2,1)}, bf16[2,256,512]{2,1,0:T(8,128)(2,1)}) custom-call(s32[22]{0:T(128)} %concatenate.42.meta, f32[256,768]{1,0:T(8,128)} %get-tuple-element.332.x, bf16[4,256,192]{2,1,0:T(8,128)(2,1)} %get-tuple-element.333.blocks, bf16[768,4096]{1,0:T(8,128)(2,1)} %bitcast.147, ...), custom_call_target="tpu_custom_call" | custom-call | flops 2415919104 | bytes 70123520 | tf_op jit(solution)/shard_map/pallas_call | solution.py:91
  293.8 10.7 %shard_map.212 = (bf16[2,256,2048]{2,1,0:T(8,128)(2,1)}, f32[256,768]{1,0:T(8,128)}) custom-call(s32[22]{0:T(128)} %concatenate.42.meta, bf16[1,256,768]{2,1,0:T(8,128)(2,1)} %right.1, f32[2,256,2048]{2,1,0:T(8,128)} %get-tuple-element.336.mixed, bf16[768,4096]{1,0:T(8,128)(2,1)} %bitcast.155, bf16[768,4096]{1,0:T(8,128)(2,1)} %bitcast.156, ...), custom_call_target="tpu_custom_call" | custom-call | flops 2415919104 | bytes 70385664 | tf_op jit(solution)/shard_map/pallas_call | solution.py:91
  309.5 4.9 all-to-all-done.2
  318.0 33.8 %shard_map.214 = (bf16[1024,768]{1,0:T(8,128)(2,1)}, bf16[1024,768]{1,0:T(8,128)(2,1)}, bf16[1024,768]{1,0:T(8,128)(2,1)}, bf16[1024,768]{1,0:T(8,128)(2,1)}, bf...) custom-call(s32[1]{0:T(128)} %bitcast.40.meta, ...), custom_call_target="tpu_custom_call" | custom-call | flops 19327352832 | bytes 36388864 | tf_op jit(solution)/shard_map/pallas_call | solution.py:91
  359.6 7.4 all-to-all-start.3
  370.3 8.5 shard_map.215
  380.3 6.7 convolution_convert_fusion.2
  396.9 7.4 all-to-all-done.3
  407.7 4.7 shard_map.216
  412.9 5.3 collective-permute-start.46
  425.4 13.9 %collective-permute-done.51 = bf16[192,4096]{1,0:T(8,128)(2,1)} collective-permute-done((bf16[192,4096]{1,0:T(8,128)(2,1)}, bf16[192,4096]{1,0:T(8,128)(2,1)}, u32[]{:S(2)}, u32[]{:S(2)}) %collective-permute-start.51) | collective-permute-done | bytes 1572896 | tf_op jit(solution)/shard_map/ppermute | solution.py:30
  442.4 5.0 all-to-all-start.4
  447.9 20.0 %shard_map.218 = (bf16[8,192,128]{2,1,0:T(8,128)(2,1)}, f32[8,2,192,128]{3,2,1,0:T(8,128)}, bf16[8,2,192,128]{3,2,1,0:T(8,128)(2,1)}) custom-call(s32[22]{0:T(128)} %concatenate.42.meta, bf16[2,3,192,128]{3,2,1,0:T(8,128)(2,1)} %get-tuple-element.305.refs_0_, bf16[2,3,192,128]{3,2,1,0:T(8,128)(2,1)} %copy-done.87, bf16[2,3,192,128]{3,2,1,0:T(8,128)(2,1)} %copy-done.88, ...), custom_call_target="tpu_custom_call" | custom-call | flops 4026531840 | bytes 6303744 | tf_op jit(solution)/shard_map/pallas_call | solution.py:91
  474.8 5.6 collective-permute-start.57
  481.2 8.8 collective-permute-done.52.rest_0_
  493.4 5.2 collective-permute-start.53
  502.5 5.0 collective-permute-done.57
  511.1 11.2 %collective-permute-done.54.rest_2_ = bf16[2,3,192,128]{3,2,1,0:T(8,128)(2,1)} collective-permute-done((bf16[2,3,192,128]{3,2,1,0:T(8,128)(2,1)}, bf16[2,3,192,128]{3,2,1,0:T(8,128)(2,1)}, u32[]{:S(2)}, u32[]{:S(2)}) %collective-permute-start.54) | collective-permute-done | bytes 294944 | tf_op jit(solution)/shard_map/ppermute | solution.py:30
  522.4 7.1 all-to-all-start.5
  529.7 7.0 shard_map.220
  538.7 10.9 %shard_map.221 = (bf16[2,256,2048]{2,1,0:T(8,128)(2,1)}, f32[256,768]{1,0:T(8,128)}) custom-call(s32[22]{0:T(128)} %concatenate.42.meta, bf16[1,256,768]{2,1,0:T(8,128)(2,1)} %convert_bitcast_fusion.1.branch.right, f32[2,256,2048]{2,1,0:T(8,128)} %get-tuple-element.414.mixed, bf16[768,4096]{1,0:T(8,128)(2,1)} %bitcast.139, bf16[768,4096]{1,0:T(8,128)(2,1)} %bitcast.140, ...), custom_call_target="tpu_custom_call" | custom-call | flops 2415919104 | bytes 70385664 | tf_op jit(solution)/shard_map/pallas_call | solution.py:91
  556.6 5.2 shard_map.222
  561.8 4.6 shard_map.223
  571.6 8.4 shard_map.224
  583.4 7.3 collective-permute-done.61.refs_10_
  604.6 20.5 %shard_map.225 = (bf16[8,192,128]{2,1,0:T(8,128)(2,1)}, f32[8,2,192,128]{3,2,1,0:T(8,128)}, bf16[8,2,192,128]{3,2,1,0:T(8,128)(2,1)}) custom-call(s32[22]{0:T(128)} %concatenate.42.meta, bf16[2,3,192,128]{3,2,1,0:T(8,128)(2,1)} %get-tuple-element.270.refs_0_, bf16[2,3,192,128]{3,2,1,0:T(8,128)(2,1)} %copy-done.81, bf16[2,3,192,128]{3,2,1,0:T(8,128)(2,1)} %copy-done.82, ...), custom_call_target="tpu_custom_call" | custom-call | flops 4026531840 | bytes 6303744 | tf_op jit(solution)/shard_map/pallas_call | solution.py:91
  627.1 7.5 all-to-all-start.6
  634.6 12.0 %collective-permute-done.70 = bf16[192,6400]{1,0:T(8,128)(2,1)} collective-permute-done((bf16[192,6400]{1,0:T(8,128)(2,1)}, bf16[192,6400]{1,0:T(8,128)(2,1)}, u32[]{:S(2)}, u32[]{:S(2)}) %collective-permute-start.70) | collective-permute-done | bytes 2457632 | tf_op jit(solution)/shard_map/ppermute | solution.py:30
  651.8 10.1 %collective-permute-done.65.rest_0_ = bf16[8,2,192,128]{3,2,1,0:T(8,128)(2,1)} collective-permute-done((bf16[8,2,192,128]{3,2,1,0:T(8,128)(2,1)}, bf16[8,2,192,128]{3,2,1,0:T(8,128)(2,1)}, u32[]{:S(2)}, u32[]{:S(2)}) %collective-permute-start.65) | collective-permute-done | bytes 786464 | tf_op jit(solution)/shard_map/ppermute | solution.py:30
  668.1 5.3 collective-permute-start.72
  673.5 19.6 %collective-permute-done.74 = bf16[704,768]{1,0:T(8,128)(2,1)} collective-permute-done((bf16[704,768]{1,0:T(8,128)(2,1)S(1)}, bf16[704,768]{1,0:T(8,128)(2,1)}, u32[]{:S(2)}, u32[]{:S(2)}) %collective-permute-start.74) | collective-permute-done | bytes 1081376 | tf_op jit(solution)/shard_map/ppermute | solution.py:30
  698.1 7.2 shard_map.229
  710.0 5.3 shard_map.230
  718.0 19.2 %collective-permute-done.76.second = bf16[192,2304]{1,0:T(8,128)(2,1)} collective-permute-done((bf16[192,2304]{1,0:T(8,128)(2,1)}, bf16[192,2304]{1,0:T(8,128)(2,1)}, u32[]{:S(2)}, u32[]{:S(2)}) %collective-permute-start.76) | collective-permute-done | bytes 884768 | tf_op jit(solution)/shard_map/ppermute | solution.py:30
  745.5 6.0 collective-permute-start.89
  752.6 7.3 collective-permute-done.89
  762.0 4.6 collective-permute-done.90
  787.6 4.7 collective-permute-done.78
  792.3 4.6 collective-permute-done.79
  807.6 10.0 %collective-permute-done.82.refs_2_ = bf16[48,1152]{1,0:T(8,128)(2,1)S(1)} collective-permute-done((bf16[48,1152]{1,0:T(8,128)(2,1)S(1)}, bf16[48,1152]{1,0:T(8,128)(2,1)S(1)}, u32[]{:S(2)}, u32[]{:S(2)}) %collective-permute-start.82) | collective-permute-done | bytes 110624 | tf_op jit(solution)/shard_map/ppermute | solution.py:30
  817.6 56.5 %all-reduce.6.cloned.1.call-done = (bf16[192,2304]{1,0:T(8,128)(2,1)}, bf16[192,4096]{1,0:T(8,128)(2,1)}, bf16[512,768]{1,0:T(8,128)(2,1)}, bf16[192,768]{1,0:T(8,128)(2,1)}, bf16[192,768]{1,0:T(8,128)(2,1)}) async-done(((bf16[192,2304]{1,0:T(8,128)(2,1)}, bf16[192,4096]{1,0:T(8,128)(2,1)}, bf16[512,768]{1,0:T(8,128)(2,1)}, bf16[192,768]{1,0:T(8,128)(2,1)}, bf16[192,768]{1,0:T(8,128)(2,1)}), ...) | async-done | bytes 3833872 | tf_op jit(solution)/shard_map/psum | solution.py:915
  (530 shorter events, 269.0 us)
Async XLA Ops:
  7.2 172.2 %all-gather.14.cloned.1.call-start = ((), (), s32[]{:S(2)}) async-start(), calls=%async_computation.9 | async-start | bytes 3932160 | tf_op jit(solution)/shard_map/all_gather | solution.py:966
  8.6 14.4 %collective-permute-start.1 = (bf16[20,192]{1,0:T(8,128)(2,1)S(1)}, bf16[20,192]{1,0:T(8,128)(2,1)S(1)}, u32[]{:S(2)}, u32[]{:S(2)}) collective-permute-start(bf16[20,192]{1,0:T(8,128)(2,1)S(1)} %pad_maximum_fusion.11), channel_id=1, source_target_pairs={{0,2},{1,3},{2,0},{3,1},{4,6},{5,7},{6,4},{7,5},{8,10},{9,11},{10,... | collective-permute-start | bytes 23048 | tf_op jit(solution)/shard_map/ppermute | solution.py:30
  12.8 22.5 %collective-permute-start = (bf16[192,2304]{1,0:T(8,128)(2,1)S(1)}, bf16[192,2304]{1,0:T(8,128)(2,1)S(1)}, u32[]{:S(2)}, u32[]{:S(2)}) collective-permute-start(bf16[192,2304]{1,0:T(8,128)(2,1)S(1)} %slice_bitcast_fusion.3.w0.rest_4_), channel_id=1, source_target_pairs={{0,2},{1,3},{2,0},{3,1},{4,6},{5,7},{6,4},{7,5},{8,10},{9,11},{10,... | collective-permute-start | bytes 2654216 | tf_op jit(solution)/shard_map/ppermute | solution.py:30
  14.1 27.1 %collective-permute-start.13 = (bf16[192,768]{1,0:T(8,128)(2,1)S(1)}, bf16[192,768]{1,0:T(8,128)(2,1)S(1)}, u32[]{:S(2)}, u32[]{:S(2)}) collective-permute-start(bf16[192,768]{1,0:T(8,128)(2,1)S(1)} %slice_bitcast_fusion.5.w0), channel_id=1, source_target_pairs={{0,2},{1,3},{2,0},{3,1},{4,6},{5,7},{6,4},{7,5},{8,10},{9,11},{10,... | collective-permute-start | bytes 884744 | tf_op jit(solution)/shard_map/ppermute | solution.py:30
  44.0 135.3 %all-gather.12.cloned.1.call-start = ((), (), s32[]{:S(2)}) async-start(), calls=%async_computation.8 | async-start | bytes 7864320 | tf_op jit(solution)/shard_map/all_gather | solution.py:966
  48.0 234.3 %all-gather.18.cloned.1.call-start = ((), (), s32[]{:S(2)}) async-start(), calls=%async_computation.11 | async-start | bytes 3932160 | tf_op jit(solution)/shard_map/all_gather | solution.py:966
  48.8 233.6 %all-gather.16.cloned.1.call-start = ((), (), s32[]{:S(2)}) async-start(), calls=%async_computation.10 | async-start | bytes 7864320 | tf_op jit(solution)/shard_map/all_gather | solution.py:966
  63.0 15.0 %collective-permute-start.6 = (bf16[2,3,192,128]{3,2,1,0:T(8,128)(2,1)}, bf16[2,3,192,128]{3,2,1,0:T(8,128)(2,1)S(1)}, u32[]{:S(2)}, u32[]{:S(2)}) collective-permute-start(bf16[2,3,192,128]{3,2,1,0:T(8,128)(2,1)} %get-tuple-element.265), channel_id=1, source_target_pairs={{0,8},{4,12},{8,0},{12,4},{16,24},{20,28},{24,16},{28,20},{1,9},{5... | collective-permute-start | bytes 884744 | tf_op jit(solution)/shard_map/ppermute | solution.py:30
  64.6 23.6 %collective-permute-start.7 = (bf16[2,3,192,128]{3,2,1,0:T(8,128)(2,1)}, bf16[2,3,192,128]{3,2,1,0:T(8,128)(2,1)S(1)}, u32[]{:S(2)}, u32[]{:S(2)}) collective-permute-start(bf16[2,3,192,128]{3,2,1,0:T(8,128)(2,1)} %get-tuple-element.266), channel_id=1, source_target_pairs={{0,16},{4,20},{8,24},{12,28},{16,0},{20,4},{24,8},{28,12},{1,17},{... | collective-permute-start | bytes 884744 | tf_op jit(solution)/shard_map/ppermute | solution.py:30
  67.2 22.5 %collective-permute-start.8 = (bf16[2,3,192,128]{3,2,1,0:T(8,128)(2,1)}, bf16[2,3,192,128]{3,2,1,0:T(8,128)(2,1)S(1)}, u32[]{:S(2)}, u32[]{:S(2)}) collective-permute-start(bf16[2,3,192,128]{3,2,1,0:T(8,128)(2,1)} %get-tuple-element.267), channel_id=1, source_target_pairs={{0,24},{4,28},{8,16},{12,20},{16,8},{20,12},{24,0},{28,4},{1,25},{... | collective-permute-start | bytes 884744 | tf_op jit(solution)/shard_map/ppermute | solution.py:30
  67.9 24.4 %collective-permute-start.9 = (bf16[2,3,192,128]{3,2,1,0:T(8,128)(2,1)}, bf16[2,3,192,128]{3,2,1,0:T(8,128)(2,1)S(1)}, u32[]{:S(2)}, u32[]{:S(2)}) collective-permute-start(bf16[2,3,192,128]{3,2,1,0:T(8,128)(2,1)} %get-tuple-element.270.refs_0_), channel_id=1, source_target_pairs={{0,4},{4,0},{8,12},{12,8},{16,20},{20,16},{24,28},{28,24},{1,5},{5... | collective-permute-start | bytes 884744 | tf_op jit(solution)/shard_map/ppermute | solution.py:30
  98.9 74.9 %all-to-all-start = ((bf16[16,72,768]{2,1,0:T(8,128)(2,1)}), bf16[16,72,768]{2,1,0:T(8,128)(2,1)S(1)}, u32[]{:S(2)}, u32[]{:S(2)}) async-start(bf16[16,72,768]{2,1,0:T(8,128)(2,1)} %fusion.2), calls=%async_computation | async-start | bytes 3538944 | tf_op jit(solution)/shard_map/all_to_all | solution.py:954
  107.5 60.2 %collective-permute-start.17 = (bf16[192,2304]{1,0:T(8,128)(2,1)S(1)}, bf16[192,2304]{1,0:T(8,128)(2,1)}, u32[]{:S(2)}, u32[]{:S(2)}) collective-permute-start(bf16[192,2304]{1,0:T(8,128)(2,1)S(1)} %slice_bitcast_fusion.2.w0.rest_4_), channel_id=1, source_target_pairs={{0,2},{1,3},{2,0},{3,1},{4,6},{5,7},{6,4},{7,5},{8,10},{9,11},{10,... | collective-permute-start | bytes 2654216 | tf_op jit(solution)/shard_map/ppermute | solution.py:30
  128.2 39.5 %collective-permute-start.18 = (bf16[192,768]{1,0:T(8,128)(2,1)S(1)}, bf16[192,768]{1,0:T(8,128)(2,1)S(1)}, u32[]{:S(2)}, u32[]{:S(2)}) collective-permute-start(bf16[192,768]{1,0:T(8,128)(2,1)S(1)} %slice_bitcast_fusion.4.w0), channel_id=1, source_target_pairs={{0,2},{1,3},{2,0},{3,1},{4,6},{5,7},{6,4},{7,5},{8,10},{9,11},{10,... | collective-permute-start | bytes 884744 | tf_op jit(solution)/shard_map/ppermute | solution.py:30
  128.3 39.4 %collective-permute-start.19 = (bf16[192,768]{1,0:T(8,128)(2,1)S(1)}, bf16[192,768]{1,0:T(8,128)(2,1)S(1)}, u32[]{:S(2)}, u32[]{:S(2)}) collective-permute-start(bf16[192,768]{1,0:T(8,128)(2,1)S(1)} %slice_bitcast_fusion.5.w0), channel_id=1, source_target_pairs={{0,1},{1,0},{2,3},{3,2},{4,5},{5,4},{6,7},{7,6},{8,9},{9,8},{10,11... | collective-permute-start | bytes 884744 | tf_op jit(solution)/shard_map/ppermute | solution.py:30
  128.4 40.7 %collective-permute-start.20 = (bf16[192,768]{1,0:T(8,128)(2,1)S(1)}, bf16[192,768]{1,0:T(8,128)(2,1)}, u32[]{:S(2)}, u32[]{:S(2)}) collective-permute-start(bf16[192,768]{1,0:T(8,128)(2,1)S(1)} %copy-done.18), channel_id=1, source_target_pairs={{0,1},{1,0},{2,3},{3,2},{4,5},{5,4},{6,7},{7,6},{8,9},{9,8},{10,11... | collective-permute-start | bytes 884744 | tf_op jit(solution)/shard_map/ppermute | solution.py:30
  134.7 14.7 %collective-permute-start.15 = (bf16[2,192,128]{2,1,0:T(8,128)(2,1)}, bf16[2,192,128]{2,1,0:T(8,128)(2,1)S(1)}, u32[]{:S(2)}, u32[]{:S(2)}) collective-permute-start(bf16[2,192,128]{2,1,0:T(8,128)(2,1)} %get-tuple-element.280), channel_id=1, source_target_pairs={{0,16},{4,20},{8,24},{12,28},{16,0},{20,4},{24,8},{28,12},{1,17},{... | collective-permute-start | bytes 294920 | tf_op jit(solution)/shard_map/ppermute | solution.py:30
  173.8 92.5 %all-to-all-start.1 = ((bf16[4,3,192,1024]{3,2,1,0:T(8,128)(2,1)}), bf16[4,3,192,1024]{3,2,1,0:T(8,128)(2,1)}, u32[]{:S(2)}, u32[]{:S(2)}) async-start(bf16[4,3,192,1024]{3,2,1,0:T(8,128)(2,1)} %pad_maximum_fusion), calls=%async_computation.1 | async-start | bytes 9437184 | tf_op jit(solution)/shard_map/all_to_all | solution.py:1066
  195.7 15.4 %collective-permute-start.23 = (bf16[2,3,192,128]{3,2,1,0:T(8,128)(2,1)}, bf16[2,3,192,128]{3,2,1,0:T(8,128)(2,1)S(1)}, u32[]{:S(2)}, u32[]{:S(2)}) collective-permute-start(bf16[2,3,192,128]{3,2,1,0:T(8,128)(2,1)} %get-tuple-element.301), channel_id=1, source_target_pairs={{0,8},{4,12},{8,0},{12,4},{16,24},{20,28},{24,16},{28,20},{1,9},{5... | collective-permute-start | bytes 884744 | tf_op jit(solution)/shard_map/ppermute | solution.py:30
  197.1 23.6 %collective-permute-start.24 = (bf16[2,3,192,128]{3,2,1,0:T(8,128)(2,1)}, bf16[2,3,192,128]{3,2,1,0:T(8,128)(2,1)S(1)}, u32[]{:S(2)}, u32[]{:S(2)}) collective-permute-start(bf16[2,3,192,128]{3,2,1,0:T(8,128)(2,1)} %get-tuple-element.302), channel_id=1, source_target_pairs={{0,16},{4,20},{8,24},{12,28},{16,0},{20,4},{24,8},{28,12},{1,17},{... | collective-permute-start | bytes 884744 | tf_op jit(solution)/shard_map/ppermute | solution.py:30
  199.0 23.2 %collective-permute-start.25 = (bf16[2,3,192,128]{3,2,1,0:T(8,128)(2,1)}, bf16[2,3,192,128]{3,2,1,0:T(8,128)(2,1)S(1)}, u32[]{:S(2)}, u32[]{:S(2)}) collective-permute-start(bf16[2,3,192,128]{3,2,1,0:T(8,128)(2,1)} %get-tuple-element.303), channel_id=1, source_target_pairs={{0,24},{4,28},{8,16},{12,20},{16,8},{20,12},{24,0},{28,4},{1,25},{... | collective-permute-start | bytes 884744 | tf_op jit(solution)/shard_map/ppermute | solution.py:30
  200.1 22.7 %collective-permute-start.26 = (bf16[2,3,192,128]{3,2,1,0:T(8,128)(2,1)}, bf16[2,3,192,128]{3,2,1,0:T(8,128)(2,1)S(1)}, u32[]{:S(2)}, u32[]{:S(2)}) collective-permute-start(bf16[2,3,192,128]{3,2,1,0:T(8,128)(2,1)} %get-tuple-element.305.refs_0_), channel_id=1, source_target_pairs={{0,4},{4,0},{8,12},{12,8},{16,20},{20,16},{24,28},{28,24},{1,5},{5... | collective-permute-start | bytes 884744 | tf_op jit(solution)/shard_map/ppermute | solution.py:30
  233.8 17.7 %collective-permute-start.30 = (bf16[1024,768]{1,0:T(8,128)(2,1)}, bf16[1024,768]{1,0:T(8,128)(2,1)}, u32[]{:S(2)}, u32[]{:S(2)}) collective-permute-start(bf16[1024,768]{1,0:T(8,128)(2,1)} %bitcast.34.refs_2_), channel_id=1, source_target_pairs={{0,1},{1,0},{2,3},{3,2},{4,5},{5,4},{6,7},{7,6},{8,9},{9,8},{10,11... | collective-permute-start | bytes 4718600 | tf_op jit(solution)/shard_map/ppermute | solution.py:30
  233.8 22.8 %collective-permute-start.35 = (bf16[192,768]{1,0:T(8,128)(2,1)S(1)}, bf16[192,768]{1,0:T(8,128)(2,1)S(1)}, u32[]{:S(2)}, u32[]{:S(2)}) collective-permute-start(bf16[192,768]{1,0:T(8,128)(2,1)S(1)} %slice_bitcast_fusion.4.w0), channel_id=1, source_target_pairs={{0,1},{1,0},{2,3},{3,2},{4,5},{5,4},{6,7},{7,6},{8,9},{9,8},{10,11... | collective-permute-start | bytes 884744 | tf_op jit(solution)/shard_map/ppermute | solution.py:30
  234.3 22.3 %collective-permute-start.36 = (bf16[192,768]{1,0:T(8,128)(2,1)S(1)}, bf16[192,768]{1,0:T(8,128)(2,1)S(1)}, u32[]{:S(2)}, u32[]{:S(2)}) collective-permute-start(bf16[192,768]{1,0:T(8,128)(2,1)S(1)} %copy-done.21), channel_id=1, source_target_pairs={{0,1},{1,0},{2,3},{3,2},{4,5},{5,4},{6,7},{7,6},{8,9},{9,8},{10,11... | collective-permute-start | bytes 884744 | tf_op jit(solution)/shard_map/ppermute | solution.py:30
  234.4 16.4 %collective-permute-start.31 = (f32[16,64]{1,0:T(8,128)S(1)}, f32[16,64]{1,0:T(8,128)S(1)}, u32[]{:S(2)}, u32[]{:S(2)}) collective-permute-start(f32[16,64]{1,0:T(8,128)S(1)} %bitcast.208), channel_id=1, source_target_pairs={{0,1},{1,0},{2,3},{3,2},{4,5},{5,4},{6,7},{7,6},{8,9},{9,8},{10,11... | collective-permute-start | bytes 12296 | tf_op jit(solution)/shard_map/ppermute | solution.py:30
  251.5 14.8 %collective-permute-start.32 = (bf16[2,192,128]{2,1,0:T(8,128)(2,1)}, bf16[2,192,128]{2,1,0:T(8,128)(2,1)S(1)}, u32[]{:S(2)}, u32[]{:S(2)}) collective-permute-start(bf16[2,192,128]{2,1,0:T(8,128)(2,1)} %get-tuple-element.319), channel_id=1, source_target_pairs={{0,8},{4,12},{8,0},{12,4},{16,24},{20,28},{24,16},{28,20},{1,9},{5... | collective-permute-start | bytes 294920 | tf_op jit(solution)/shard_map/ppermute | solution.py:30
  275.0 39.4 %all-to-all-start.2 = ((bf16[16,64,768]{2,1,0:T(8,128)(2,1)}), bf16[16,64,768]{2,1,0:T(8,128)(2,1)S(1)}, u32[]{:S(2)}, u32[]{:S(2)}) async-start(bf16[16,64,768]{2,1,0:T(8,128)(2,1)} %bitcast.197), calls=%async_computation.2 | async-start | bytes 3145728 | tf_op jit(solution)/shard_map/all_to_all | solution.py:954
  282.2 22.4 %collective-permute-start.38 = (bf16[1,256,768]{2,1,0:T(8,128)(2,1)S(1)}, bf16[1,256,768]{2,1,0:T(8,128)(2,1)}, u32[]{:S(2)}, u32[]{:S(2)}) collective-permute-start(bf16[1,256,768]{2,1,0:T(8,128)(2,1)S(1)} %copy-done.9), channel_id=1, source_target_pairs={{0,1},{1,0},{2,3},{3,2},{4,5},{5,4},{6,7},{7,6},{8,9},{9,8},{10,11... | collective-permute-start | bytes 1179656 | tf_op jit(solution)/shard_map/ppermute | solution.py:30
  352.1 17.5 %collective-permute-start.44 = (bf16[2,256,2048]{2,1,0:T(8,128)(2,1)}, bf16[2,256,2048]{2,1,0:T(8,128)(2,1)}, u32[]{:S(2)}, u32[]{:S(2)}) collective-permute-start(bf16[2,256,2048]{2,1,0:T(8,128)(2,1)} %get-tuple-element.369.right), channel_id=1, source_target_pairs={{0,1},{1,0},{2,3},{3,2},{4,5},{5,4},{6,7},{7,6},{8,9},{9,8},{10,11... | collective-permute-start | bytes 6291464 | tf_op jit(solution)/shard_map/ppermute | solution.py:30
  354.2 24.6 %collective-permute-start.45 = (bf16[512,768]{1,0:T(8,128)(2,1)S(1)}, bf16[512,768]{1,0:T(8,128)(2,1)}, u32[]{:S(2)}, u32[]{:S(2)}) collective-permute-start(bf16[512,768]{1,0:T(8,128)(2,1)S(1)} %copy-done.78), channel_id=1, source_target_pairs={{0,2},{1,3},{2,0},{3,1},{4,6},{5,7},{6,4},{7,5},{8,10},{9,11},{10,... | collective-permute-start | bytes 2359304 | tf_op jit(solution)/shard_map/ppermute | solution.py:30
  359.6 44.7 %all-to-all-start.3 = ((bf16[16,72,768]{2,1,0:T(8,128)(2,1)}), bf16[16,72,768]{2,1,0:T(8,128)(2,1)S(1)}, u32[]{:S(2)}, u32[]{:S(2)}) async-start(bf16[16,72,768]{2,1,0:T(8,128)(2,1)} %fusion.3), calls=%async_computation.3 | async-start | bytes 3538944 | tf_op jit(solution)/shard_map/all_to_all | solution.py:954
  404.3 35.0 %collective-permute-start.51 = (bf16[192,4096]{1,0:T(8,128)(2,1)}, bf16[192,4096]{1,0:T(8,128)(2,1)}, u32[]{:S(2)}, u32[]{:S(2)}) collective-permute-start(bf16[192,4096]{1,0:T(8,128)(2,1)} %get-tuple-element.387), channel_id=1, source_target_pairs={{0,2},{1,3},{2,0},{3,1},{4,6},{5,7},{6,4},{7,5},{8,10},{9,11},{10,... | collective-permute-start | bytes 4718600 | tf_op jit(solution)/shard_map/ppermute | solution.py:30
  412.9 28.7 %collective-permute-start.46 = (bf16[2,192,128]{2,1,0:T(8,128)(2,1)}, bf16[2,192,128]{2,1,0:T(8,128)(2,1)S(1)}, u32[]{:S(2)}, u32[]{:S(2)}) collective-permute-start(bf16[2,192,128]{2,1,0:T(8,128)(2,1)} %get-tuple-element.377), channel_id=1, source_target_pairs={{0,8},{4,12},{8,0},{12,4},{16,24},{20,28},{24,16},{28,20},{1,9},{5... | collective-permute-start | bytes 294920 | tf_op jit(solution)/shard_map/ppermute | solution.py:30
  418.2 23.5 %collective-permute-start.47 = (bf16[2,192,128]{2,1,0:T(8,128)(2,1)}, bf16[2,192,128]{2,1,0:T(8,128)(2,1)S(1)}, u32[]{:S(2)}, u32[]{:S(2)}) collective-permute-start(bf16[2,192,128]{2,1,0:T(8,128)(2,1)} %get-tuple-element.378), channel_id=1, source_target_pairs={{0,16},{4,20},{8,24},{12,28},{16,0},{20,4},{24,8},{28,12},{1,17},{... | collective-permute-start | bytes 294920 | tf_op jit(solution)/shard_map/ppermute | solution.py:30
  419.8 21.9 %collective-permute-start.48 = (bf16[2,192,128]{2,1,0:T(8,128)(2,1)}, bf16[2,192,128]{2,1,0:T(8,128)(2,1)S(1)}, u32[]{:S(2)}, u32[]{:S(2)}) collective-permute-start(bf16[2,192,128]{2,1,0:T(8,128)(2,1)} %get-tuple-element.379), channel_id=1, source_target_pairs={{0,24},{4,28},{8,16},{12,20},{16,8},{20,12},{24,0},{28,4},{1,25},{... | collective-permute-start | bytes 294920 | tf_op jit(solution)/shard_map/ppermute | solution.py:30
  442.4 80.0 %all-to-all-start.4 = ((bf16[4,3,192,1024]{3,2,1,0:T(8,128)(2,1)}), bf16[4,3,192,1024]{3,2,1,0:T(8,128)(2,1)}, u32[]{:S(2)}, u32[]{:S(2)}) async-start(bf16[4,3,192,1024]{3,2,1,0:T(8,128)(2,1)} %pad_maximum_fusion.1), calls=%async_computation.4 | async-start | bytes 9437184 | tf_op jit(solution)/shard_map/all_to_all | solution.py:1189
  447.4 23.9 %collective-permute-start.56 = (bf16[1024,768]{1,0:T(8,128)(2,1)}, bf16[1024,768]{1,0:T(8,128)(2,1)}, u32[]{:S(2)}, u32[]{:S(2)}) collective-permute-start(bf16[1024,768]{1,0:T(8,128)(2,1)} %get-tuple-element.403), channel_id=1, source_target_pairs={{0,1},{1,0},{2,3},{3,2},{4,5},{5,4},{6,7},{7,6},{8,9},{9,8},{10,11... | collective-permute-start | bytes 4718600 | tf_op jit(solution)/shard_map/ppermute | solution.py:30
  467.9 22.1 %collective-permute-start.52 = (bf16[8,2,192,128]{3,2,1,0:T(8,128)(2,1)}, bf16[8,2,192,128]{3,2,1,0:T(8,128)(2,1)}, u32[]{:S(2)}, u32[]{:S(2)}) collective-permute-start(bf16[8,2,192,128]{3,2,1,0:T(8,128)(2,1)} %get-tuple-element.397), channel_id=1, source_target_pairs={{0,4},{4,0},{8,12},{12,8},{16,20},{20,16},{24,28},{28,24},{1,5},{5... | collective-permute-start | bytes 2359304 | tf_op jit(solution)/shard_map/ppermute | solution.py:30
  474.8 32.8 %collective-permute-start.57 = (bf16[192,768]{1,0:T(8,128)(2,1)}, bf16[192,768]{1,0:T(8,128)(2,1)}, u32[]{:S(2)}, u32[]{:S(2)}) collective-permute-start(bf16[192,768]{1,0:T(8,128)(2,1)} %get-tuple-element.408), channel_id=1, source_target_pairs={{0,2},{1,3},{2,0},{3,1},{4,6},{5,7},{6,4},{7,5},{8,10},{9,11},{10,... | collective-permute-start | bytes 884744 | tf_op jit(solution)/shard_map/ppermute | solution.py:30
  493.4 17.7 %collective-permute-start.53 = (bf16[2,3,192,128]{3,2,1,0:T(8,128)(2,1)}, bf16[2,3,192,128]{3,2,1,0:T(8,128)(2,1)S(1)}, u32[]{:S(2)}, u32[]{:S(2)}) collective-permute-start(bf16[2,3,192,128]{3,2,1,0:T(8,128)(2,1)} %get-tuple-element.399), channel_id=1, source_target_pairs={{0,8},{4,12},{8,0},{12,4},{16,24},{20,28},{24,16},{28,20},{1,9},{5... | collective-permute-start | bytes 884744 | tf_op jit(solution)/shard_map/ppermute | solution.py:30
  498.6 23.8 %collective-permute-start.54 = (bf16[2,3,192,128]{3,2,1,0:T(8,128)(2,1)}, bf16[2,3,192,128]{3,2,1,0:T(8,128)(2,1)}, u32[]{:S(2)}, u32[]{:S(2)}) collective-permute-start(bf16[2,3,192,128]{3,2,1,0:T(8,128)(2,1)} %get-tuple-element.400), channel_id=1, source_target_pairs={{0,16},{4,20},{8,24},{12,28},{16,0},{20,4},{24,8},{28,12},{1,17},{... | collective-permute-start | bytes 884744 | tf_op jit(solution)/shard_map/ppermute | solution.py:30
  499.8 22.6 %collective-permute-start.55 = (bf16[2,3,192,128]{3,2,1,0:T(8,128)(2,1)}, bf16[2,3,192,128]{3,2,1,0:T(8,128)(2,1)}, u32[]{:S(2)}, u32[]{:S(2)}) collective-permute-start(bf16[2,3,192,128]{3,2,1,0:T(8,128)(2,1)} %get-tuple-element.401), channel_id=1, source_target_pairs={{0,24},{4,28},{8,16},{12,20},{16,8},{20,12},{24,0},{28,4},{1,25},{... | collective-permute-start | bytes 884744 | tf_op jit(solution)/shard_map/ppermute | solution.py:30
  522.4 68.9 %all-to-all-start.5 = ((bf16[8,24,6144]{2,1,0:T(8,128)(2,1)}), bf16[8,24,6144]{2,1,0:T(8,128)(2,1)S(1)}, u32[]{:S(2)}, u32[]{:S(2)}) async-start(bf16[8,24,6144]{2,1,0:T(8,128)(2,1)} %pad_maximum_fusion.3), calls=%async_computation.5 | async-start | bytes 4718592 | tf_op jit(solution)/shard_map/all_to_all | solution.py:1203
  529.5 168.6 %all-gather.10.cloned.1.call-start = ((), (), s32[]{:S(2)}) async-start(), calls=%async_computation.7 | async-start | bytes 2654208 | tf_op jit(solution)/shard_map/all_gather | solution.py:1226
  549.6 21.4 %collective-permute-start.64 = (bf16[2,256,2048]{2,1,0:T(8,128)(2,1)}, bf16[2,256,2048]{2,1,0:T(8,128)(2,1)}, u32[]{:S(2)}, u32[]{:S(2)}) collective-permute-start(bf16[2,256,2048]{2,1,0:T(8,128)(2,1)} %get-tuple-element.429.right), channel_id=1, source_target_pairs={{0,1},{1,0},{2,3},{3,2},{4,5},{5,4},{6,7},{7,6},{8,9},{9,8},{10,11... | collective-permute-start | bytes 6291464 | tf_op jit(solution)/shard_map/ppermute | solution.py:30
  550.2 20.7 %collective-permute-start.63 = (bf16[2,256,192]{2,1,0:T(8,128)(2,1)S(1)}, bf16[2,256,192]{2,1,0:T(8,128)(2,1)S(1)}, u32[]{:S(2)}, u32[]{:S(2)}) collective-permute-start(bf16[2,256,192]{2,1,0:T(8,128)(2,1)S(1)} %copy-done.94), channel_id=1, source_target_pairs={{0,1},{1,0},{2,3},{3,2},{4,5},{5,4},{6,7},{7,6},{8,9},{9,8},{10,11... | collective-permute-start | bytes 589832 | tf_op jit(solution)/shard_map/ppermute | solution.py:30
  566.4 17.0 %collective-permute-start.60 = (bf16[2,192,128]{2,1,0:T(8,128)(2,1)}, bf16[2,192,128]{2,1,0:T(8,128)(2,1)S(1)}, u32[]{:S(2)}, u32[]{:S(2)}) collective-permute-start(bf16[2,192,128]{2,1,0:T(8,128)(2,1)} %get-tuple-element.424), channel_id=1, source_target_pairs={{0,8},{4,12},{8,0},{12,4},{16,24},{20,28},{24,16},{28,20},{1,9},{5... | collective-permute-start | bytes 294920 | tf_op jit(solution)/shard_map/ppermute | solution.py:30
  568.5 22.2 %collective-permute-start.61 = (bf16[2,192,128]{2,1,0:T(8,128)(2,1)}, bf16[2,192,128]{2,1,0:T(8,128)(2,1)S(1)}, u32[]{:S(2)}, u32[]{:S(2)}) collective-permute-start(bf16[2,192,128]{2,1,0:T(8,128)(2,1)} %get-tuple-element.425), channel_id=1, source_target_pairs={{0,16},{4,20},{8,24},{12,28},{16,0},{20,4},{24,8},{28,12},{1,17},{... | collective-permute-start | bytes 294920 | tf_op jit(solution)/shard_map/ppermute | solution.py:30
  570.8 20.5 %collective-permute-start.62 = (bf16[2,192,128]{2,1,0:T(8,128)(2,1)}, bf16[2,192,128]{2,1,0:T(8,128)(2,1)}, u32[]{:S(2)}, u32[]{:S(2)}) collective-permute-start(bf16[2,192,128]{2,1,0:T(8,128)(2,1)} %get-tuple-element.426), channel_id=1, source_target_pairs={{0,24},{4,28},{8,16},{12,20},{16,8},{20,12},{24,0},{28,4},{1,25},{... | collective-permute-start | bytes 294920 | tf_op jit(solution)/shard_map/ppermute | solution.py:30
  591.3 55.3 %collective-permute-start.70 = (bf16[192,6400]{1,0:T(8,128)(2,1)}, bf16[192,6400]{1,0:T(8,128)(2,1)}, u32[]{:S(2)}, u32[]{:S(2)}) collective-permute-start(bf16[192,6400]{1,0:T(8,128)(2,1)} %pad_maximum_fusion.2), channel_id=1, source_target_pairs={{0,2},{1,3},{2,0},{3,1},{4,6},{5,7},{6,4},{7,5},{8,10},{9,11},{10,... | collective-permute-start | bytes 7372808 | tf_op jit(solution)/shard_map/ppermute | solution.py:30
  625.1 36.8 %collective-permute-start.65 = (bf16[8,2,192,128]{3,2,1,0:T(8,128)(2,1)}, bf16[8,2,192,128]{3,2,1,0:T(8,128)(2,1)}, u32[]{:S(2)}, u32[]{:S(2)}) collective-permute-start(bf16[8,2,192,128]{3,2,1,0:T(8,128)(2,1)} %get-tuple-element.442), channel_id=1, source_target_pairs={{0,4},{4,0},{8,12},{12,8},{16,20},{20,16},{24,28},{28,24},{1,5},{5... | collective-permute-start | bytes 2359304 | tf_op jit(solution)/shard_map/ppermute | solution.py:30
  627.1 70.9 %all-to-all-start.6 = ((bf16[16,64,768]{2,1,0:T(8,128)(2,1)}), bf16[16,64,768]{2,1,0:T(8,128)(2,1)S(1)}, u32[]{:S(2)}, u32[]{:S(2)}) async-start(bf16[16,64,768]{2,1,0:T(8,128)(2,1)} %bitcast.57), calls=%async_computation.6 | async-start | bytes 3145728 | tf_op jit(solution)/shard_map/all_to_all | solution.py:954
  634.5 239.6 %all-reduce.6.cloned.1.call-start = ((), (), s32[]{:S(2)}) async-start(), calls=%async_computation.12 | async-start | bytes 7667712 | tf_op jit(solution)/shard_map/psum | solution.py:915
  661.9 31.2 %collective-permute-start.74 = (bf16[704,768]{1,0:T(8,128)(2,1)S(1)}, bf16[704,768]{1,0:T(8,128)(2,1)}, u32[]{:S(2)}, u32[]{:S(2)}) collective-permute-start(bf16[704,768]{1,0:T(8,128)(2,1)S(1)} %copy-done.24), channel_id=1, source_target_pairs={{0,2},{1,3},{2,0},{3,1},{4,6},{5,7},{6,4},{7,5},{8,10},{9,11},{10,... | collective-permute-start | bytes 3244040 | tf_op jit(solution)/shard_map/ppermute | solution.py:30
  668.1 29.0 %collective-permute-start.71 = (bf16[2,3,192,128]{3,2,1,0:T(8,128)(2,1)}, bf16[2,3,192,128]{3,2,1,0:T(8,128)(2,1)}, u32[]{:S(2)}, u32[]{:S(2)}) collective-permute-start(bf16[2,3,192,128]{3,2,1,0:T(8,128)(2,1)} %get-tuple-element.455), channel_id=1, source_target_pairs={{0,8},{4,12},{8,0},{12,4},{16,24},{20,28},{24,16},{28,20},{1,9},{5... | collective-permute-start | bytes 884744 | tf_op jit(solution)/shard_map/ppermute | solution.py:30
  668.1 29.9 %collective-permute-start.72 = (bf16[2,3,192,128]{3,2,1,0:T(8,128)(2,1)}, bf16[2,3,192,128]{3,2,1,0:T(8,128)(2,1)}, u32[]{:S(2)}, u32[]{:S(2)}) collective-permute-start(bf16[2,3,192,128]{3,2,1,0:T(8,128)(2,1)} %get-tuple-element.456), channel_id=1, source_target_pairs={{0,16},{4,20},{8,24},{12,28},{16,0},{20,4},{24,8},{28,12},{1,17},{... | collective-permute-start | bytes 884744 | tf_op jit(solution)/shard_map/ppermute | solution.py:30
  673.5 24.5 %collective-permute-start.73 = (bf16[2,3,192,128]{3,2,1,0:T(8,128)(2,1)}, bf16[2,3,192,128]{3,2,1,0:T(8,128)(2,1)}, u32[]{:S(2)}, u32[]{:S(2)}) collective-permute-start(bf16[2,3,192,128]{3,2,1,0:T(8,128)(2,1)} %get-tuple-element.457), channel_id=1, source_target_pairs={{0,24},{4,28},{8,16},{12,20},{16,8},{20,12},{24,0},{28,4},{1,25},{... | collective-permute-start | bytes 884744 | tf_op jit(solution)/shard_map/ppermute | solution.py:30
  715.3 22.0 %collective-permute-start.76 = (bf16[192,2304]{1,0:T(8,128)(2,1)}, bf16[192,2304]{1,0:T(8,128)(2,1)}, u32[]{:S(2)}, u32[]{:S(2)}) collective-permute-start(bf16[192,2304]{1,0:T(8,128)(2,1)} %get-tuple-element.479), channel_id=1, source_target_pairs={{0,2},{1,3},{2,0},{3,1},{4,6},{5,7},{6,4},{7,5},{8,10},{9,11},{10,... | collective-permute-start | bytes 2654216 | tf_op jit(solution)/shard_map/ppermute | solution.py:30
  745.5 14.4 %collective-permute-start.89 = (f32[20,768]{1,0:T(8,128)S(1)}, f32[20,768]{1,0:T(8,128)S(1)}, u32[]{:S(2)}, u32[]{:S(2)}) collective-permute-start(f32[20,768]{1,0:T(8,128)S(1)} %add.199), channel_id=1, source_target_pairs={{0,8},{4,12},{8,0},{12,4},{16,24},{20,28},{24,16},{28,20},{1,9},{5... | collective-permute-start | bytes 184328 | tf_op jit(solution)/shard_map/ppermute | solution.py:30
  761.5 18.0 %collective-permute-start.77 = (bf16[192,1152]{1,0:T(8,128)(2,1)S(1)}, bf16[192,1152]{1,0:T(8,128)(2,1)S(1)}, u32[]{:S(2)}, u32[]{:S(2)}) collective-permute-start(bf16[192,1152]{1,0:T(8,128)(2,1)S(1)} %copy-done.80), channel_id=1, source_target_pairs={{0,4},{4,0},{8,12},{12,8},{16,20},{20,16},{24,28},{28,24},{1,5},{5... | collective-permute-start | bytes 1327112 | tf_op jit(solution)/shard_map/ppermute | solution.py:30
  767.9 19.6 %collective-permute-start.92 = (f32[20,768]{1,0:T(8,128)S(1)}, f32[20,768]{1,0:T(8,128)S(1)}, u32[]{:S(2)}, u32[]{:S(2)}) collective-permute-start(f32[20,768]{1,0:T(8,128)S(1)} %add.202), channel_id=1, source_target_pairs={{0,2},{1,3},{2,0},{3,1},{4,6},{5,7},{6,4},{7,5},{8,10},{9,11},{10,... | collective-permute-start | bytes 184328 | tf_op jit(solution)/shard_map/ppermute | solution.py:30
  800.1 17.5 %collective-permute-start.82 = (bf16[48,1152]{1,0:T(8,128)(2,1)S(1)}, bf16[48,1152]{1,0:T(8,128)(2,1)S(1)}, u32[]{:S(2)}, u32[]{:S(2)}) collective-permute-start(bf16[48,1152]{1,0:T(8,128)(2,1)S(1)} %add_convert_fusion.2.refs_0_), channel_id=1, source_target_pairs={{0,16},{4,20},{8,24},{12,28},{16,0},{20,4},{24,8},{28,12},{1,17},{... | collective-permute-start | bytes 331784 | tf_op jit(solution)/shard_map/ppermute | solution.py:30
  800.1 17.5 %collective-permute-start.83 = (bf16[48,1152]{1,0:T(8,128)(2,1)S(1)}, bf16[48,1152]{1,0:T(8,128)(2,1)S(1)}, u32[]{:S(2)}, u32[]{:S(2)}) collective-permute-start(bf16[48,1152]{1,0:T(8,128)(2,1)S(1)} %add_convert_fusion.2.refs_0_), channel_id=1, source_target_pairs={{0,24},{4,28},{8,16},{12,20},{16,8},{20,12},{24,0},{28,4},{1,25},{... | collective-permute-start | bytes 331784 | tf_op jit(solution)/shard_map/ppermute | solution.py:30
  (154 other events, 2186.1 us)
Sparse Core Ops, SparseCore 0:
  44.1 28.8 all-gather.13
  75.2 73.3 all-gather.11
  150.7 33.5 all-gather.17
  186.2 80.7 all-gather.15
  594.2 71.5 all-gather.9
  709.4 164.7 all-reduce.5

commit v5 on v4

--- a/solution.py
+++ b/solution.py
@@ -717,37 +717,46 @@
     out[1] = other[...].astype(jnp.float32)
 
 
-def reduce_last(place, own, arrived, other, held, small):
+def reduce_last(place, grads, held, small):
     lines = lax.axis_size("ctx") // 2
-    rows, width = own.shape
-    chunk, half = rows // lines, width // 2
-    if chunk % 16:
-        summed = lax.psum(own + arrived, "ctx")
-        return jnp.stack([summed, other]).astype(jnp.float32), held, total_small(small)
-    sent, kept = call(_halve_kernel, place, (own, arrived), [_shape((rows, half))] * 2)
-    kept, small = lax.optimization_barrier((kept, small))
-    small = total_small(small)
-    parts = call(
-        _quarter_kernel,
-        place,
-        (kept, swap(sent, "ctx", 1)),
-        [_shape((chunk, half))] * lines,
-        [pltpu.VMEM((rows, half), jnp.bfloat16)],
-    )
-    summed = parts[0].astype(jnp.float32)
-    for k in range(1, lines):
-        summed = summed + swap(parts[k], "ctx", 2 * k).astype(jnp.float32)
-    summed = summed.astype(jnp.bfloat16)
-    column = [swap(summed, "ctx", 2 * k) if k else summed for k in range(lines)]
-    column, held = lax.optimization_barrier((column, held))
-    parts = column + [swap(c, "ctx", 1) for c in column]
-    return (
+    if any(own.shape[0] // lines % 16 for own, _, _ in grads):
+        outs = [
+            jnp.stack([lax.psum(own + arrived, "ctx"), other]).astype(jnp.float32)
+            for own, arrived, other in grads
+        ]
+        return outs, held, total_small(small)
+    columns = []
+    for i, (own, arrived, other) in enumerate(grads):
+        rows, width = own.shape
+        chunk, half = rows // lines, width // 2
+        sent, kept = call(_halve_kernel, place, (own, arrived), [_shape((rows, half))] * 2)
+        if i == 0:
+            kept, small = lax.optimization_barrier((kept, small))
+            small = total_small(small)
+        parts = call(
+            _quarter_kernel,
+            place,
+            (kept, swap(sent, "ctx", 1)),
+            [_shape((chunk, half))] * lines,
+            [pltpu.VMEM((rows, half), jnp.bfloat16)],
+        )
+        summed = parts[0].astype(jnp.float32)
+        for k in range(1, lines):
+            summed = summed + swap(parts[k], "ctx", 2 * k).astype(jnp.float32)
+        summed = summed.astype(jnp.bfloat16)
+        column = [swap(summed, "ctx", 2 * k) if k else summed for k in range(lines)]
+        columns.append(column + [swap(c, "ctx", 1) for c in column])
+    columns, held = lax.optimization_barrier((columns, held))
+    outs = [
         call(
-            _place_kernel, place, (other, *parts), [_shape((2, rows, width), jnp.float32)]
-        )[0],
-        held,
-        small,
-    )
+            _place_kernel,
+            place,
+            (other, *parts),
+            [_shape((2, *own.shape), jnp.float32)],
+        )[0]
+        for (own, _, other), parts in zip(grads, columns)
+    ]
+    return outs, held, small
 
 
 def _expert_kernel(units, meta, *refs):
@@ -1247,7 +1256,6 @@
     tall = grad_mlp_out_one[0].shape[0]
     sums_one = [
         *first_sums,
-        grad_mlp_out_one[0] + second_arrived[:tall],
         grad_attn_out_one[0] + second_arrived[tall:],
         sum_attn_out_two,
     ]
@@ -1268,32 +1276,33 @@
     back_rows = [jnp.dot(p, expert_rows, preferred_element_type=jnp.float32) for p in of_token]
     output = shared + sum(gate_probs[:, k, None] * back_rows[k] for k in range(TOP))
     small_grads = jnp.concatenate([gain_zero, gain_one, gain_two, gain_three, grad_router])
-    attn_in_grad, sums_one, small_grads = reduce_last(
+    wide = sums_one[1].shape[1]
+    (attn_in_grad, mlp_out_grad), sums_one, small_grads = reduce_last(
         at_ctx,
-        grad_attn_in_one[0],
-        swap(grad_attn_in_one[1], "fsdp", 2),
-        sums_one[0],
+        [
+            (grad_attn_in_one[0], swap(grad_attn_in_one[1], "fsdp", 2), sums_one[0]),
+            (
+                grad_mlp_out_one[0],
+                second_arrived[:tall],
+                sums_two[:, wide:].reshape(tall, model_width),
+            ),
+        ],
         sums_one,
         small_grads,
     )
     small_grads = lax.dynamic_slice_in_dim(small_grads, own_fsdp * shard_width, shard_width, 1)
-    wide = sums_one[1].shape[1]
-    dense_grads = [attn_in_grad] + [
+    attn_out_grad, mlp_in_grad = [
         jnp.stack(pair).astype(jnp.float32)
-        for pair in (
-            (sums_one[3], sums_one[4]),
-            (sums_one[1], sums_two[:, :wide]),
-            (sums_one[2], sums_two[:, wide:].reshape(sums_one[2].shape)),
-        )
+        for pair in ((sums_one[2], sums_one[3]), (sums_one[1], sums_two[:, :wide]))
     ]
     return (
         output[None],
         grad_resid[None],
-        dense_grads[0],
-        dense_grads[1],
+        attn_in_grad,
+        attn_out_grad,
         small_grads[:4].reshape(2, 2, shard_width),
-        dense_grads[2],
-        dense_grads[3],
+        mlp_in_grad,
+        mlp_out_grad,
         small_grads[4:].T,
         jnp.swapaxes(grad_experts[:2], 1, 2),
         grad_experts[2].T,

time: 910 us -> 917 us (level)
  waiting for transfers between devices: 334 us -> 305 us
  starting transfers between devices: 159 us -> 178 us
  Pallas kernels: 253 us -> 265 us
    ppermute x93 -> x104, starting transfers between devices: 112 us -> 133 us  [swap(): return lax.ppermute(values, axis, [(i, i ^ mask) for i in range(count)])]
    psum x1, waiting for transfers between devices: 56.5 us -> 36.8 us  [total(): return lax.psum(tuple(grads), 'ctx', axis_index_groups=ring)]
    pallas_call x30 -> x33, Pallas kernels: 253 us -> 265 us  [call(): pl.pallas_call(body, grid_spec=pltpu.PrefetchScalarGridSpec(num_scalar_pr...]
    ppermute x93 -> x104, waiting for transfers between devices: 255 us -> 245 us  [swap(): return lax.ppermute(values, axis, [(i, i ^ mask) for i in range(count)])]
    unnamed x226 -> x244, local copies, waits for them, and re-layouts: 18.4 us -> 23.4 us
  transfers between devices with their start and end apart: 106 -> 117, of which waited for: 45 -> 45; matrix products, arithmetic and copies ran while one was open for 13% -> 13% of each run, Pallas kernels for 23% -> 24%
where the time goes in v5:
time: 917 us; the launch traced here: 906 us
  waiting for transfers between devices  305 us (33%)
  Pallas kernels  265 us (29%)
  starting transfers between devices  178 us (19%)
  other arithmetic  61.4 us (7%)
  local copies, waits for them, and re-layouts  58.3 us (6%)
  matrix products  22.4 us (2%)
  between operations  15.9 us (2%)
    pallas_call x33, Pallas kernels, call(): pl.pallas_call(body, grid_spec=pltpu.PrefetchScalarGridSpec(num_scalar_pr...  265 us
    ppermute x104, waiting for transfers between devices, swap(): return lax.ppermute(values, axis, [(i, i ^ mask) for i in range(count)])  245 us
    ppermute x104, starting transfers between devices, swap(): return lax.ppermute(values, axis, [(i, i ^ mask) for i in range(count)])  133 us
    psum x1, waiting for transfers between devices, total(): return lax.psum(tuple(grads), 'ctx', axis_index_groups=ring)  36.8 us
    all_to_all x4, starting transfers between devices, dispatch(): lax.all_to_all(values, BOTH, 0, 0, tiled=True, axis_index_groups=members)  24.3 us
    unnamed x244, local copies, waits for them, and re-layouts  23.4 us
  transfers between devices with their start and end apart: 117, of which 45 were waited for; matrix products, arithmetic and copies ran while one was open for 13% of the time, Pallas kernels for 24%

profile of v5, /device:TPU:0, one launch (start us, length us, event | category | flops | bytes accessed | tf_op | source)
XLA Modules:
  0.0 906.3 jit_solution(1931296064810886132)
XLA Ops:
  25.1 10.3 %collective-permute-done.w2.rest_6_ = bf16[192,2304]{1,0:T(8,128)(2,1)S(1)} collective-permute-done((bf16[192,2304]{1,0:T(8,128)(2,1)S(1)}, bf16[192,2304]{1,0:T(8,128)(2,1)S(1)}, u32[]{:S(2)}, u32[]{:S(2)}) %collective-permute-start) | collective-permute-done | bytes 884768 | tf_op jit(solution)/shard_map/ppermute | solution.py:30
  35.4 5.9 collective-permute-done.13.w2
  57.2 5.8 shard_map.204
  69.4 8.6 collective-permute-done.6.refs_1_
  79.6 8.6 collective-permute-done.7.refs_2_
  98.9 7.3 all-to-all-start
  109.5 16.9 %shard_map.205 = (bf16[2,192,128]{2,1,0:T(8,128)(2,1)}, bf16[2,192,128]{2,1,0:T(8,128)(2,1)}, bf16[2,192,128]{2,1,0:T(8,128)(2,1)}, bf16[2,192,128]{2,1,0:T(8,12...) custom-call(s32[22]{0:T(128)} %concatenate.42.meta, bf16[2,3,192,128]{3,2,1,0:T(8,128)(2,1)} %get-tuple-element.286.refs_0_, ...), custom_call_target="tpu_custom_call" | custom-call | flops 1610612736 | bytes 3551232 | tf_op jit(solution)/shard_map/pallas_call | solution.py:91
  130.0 4.7 collective-permute-done.14.o1
  134.7 5.5 collective-permute-start.15
  140.2 9.2 %collective-permute-done.15.o2 = bf16[2,192,128]{2,1,0:T(8,128)(2,1)S(1)} collective-permute-done((bf16[2,192,128]{2,1,0:T(8,128)(2,1)}, bf16[2,192,128]{2,1,0:T(8,128)(2,1)S(1)}, u32[]{:S(2)}, u32[]{:S(2)}) %collective-permute-start.15) | collective-permute-done | bytes 98336 | tf_op jit(solution)/shard_map/ppermute | solution.py:30
  150.6 5.4 collective-permute-done.16.o3
  156.1 11.6 %collective-permute-done.18.w2 = bf16[192,768]{1,0:T(8,128)(2,1)S(1)} collective-permute-done((bf16[192,768]{1,0:T(8,128)(2,1)S(1)}, bf16[192,768]{1,0:T(8,128)(2,1)S(1)}, u32[]{:S(2)}, u32[]{:S(2)}) %collective-permute-start.18) | collective-permute-done | bytes 294944 | tf_op jit(solution)/shard_map/ppermute | solution.py:30
  169.2 4.6 shard_map.206
  173.8 4.9 all-to-all-start.1
  179.4 10.4 %shard_map.207 = (f32[256,768]{1,0:T(8,128)}, f32[2,256,2048]{2,1,0:T(8,128)}, bf16[2,256,512]{2,1,0:T(8,128)(2,1)}, bf16[2,256,512]{2,1,0:T(8,128)(2,1)}) custom-call(s32[22]{0:T(128)} %concatenate.42.meta, f32[256,768]{1,0:T(8,128)} %get-tuple-element.308.x, bf16[4,256,192]{2,1,0:T(8,128)(2,1)} %get-tuple-element.309.blocks, bf16[768,4096]{1,0:T(8,128)(2,1)} %bitcast.130, ...), custom_call_target="tpu_custom_call" | custom-call | flops 2415919104 | bytes 70123520 | tf_op jit(solution)/shard_map/pallas_call | solution.py:91
  189.8 5.9 shard_map.208
  201.5 9.5 %collective-permute-done.23.refs_1_ = bf16[2,3,192,128]{3,2,1,0:T(8,128)(2,1)S(1)} collective-permute-done((bf16[2,3,192,128]{3,2,1,0:T(8,128)(2,1)}, bf16[2,3,192,128]{3,2,1,0:T(8,128)(2,1)S(1)}, u32[]{:S(2)}, u32[]{:S(2)}) %collective-permute-start.23) | collective-permute-done | bytes 294944 | tf_op jit(solution)/shard_map/ppermute | solution.py:30
  212.4 8.4 collective-permute-done.24.refs_2_
  222.9 6.3 collective-permute-done.28.refs_6_
  234.8 16.6 %shard_map.209 = (bf16[2,192,128]{2,1,0:T(8,128)(2,1)}, bf16[2,192,128]{2,1,0:T(8,128)(2,1)}, bf16[2,192,128]{2,1,0:T(8,128)(2,1)}, bf16[2,192,128]{2,1,0:T(8,12...) custom-call(s32[22]{0:T(128)} %concatenate.42.meta, bf16[2,3,192,128]{3,2,1,0:T(8,128)(2,1)} %get-tuple-element.321.refs_0_, ...), custom_call_target="tpu_custom_call" | custom-call | flops 1610612736 | bytes 3551232 | tf_op jit(solution)/shard_map/pallas_call | solution.py:91
  257.4 8.9 all-to-all-done.1.refs_6_
  267.6 4.6 shard_map.210
  275.1 5.1 all-to-all-start.2
  280.4 10.5 %shard_map.211 = (f32[256,768]{1,0:T(8,128)}, f32[2,256,2048]{2,1,0:T(8,128)}, bf16[2,256,512]{2,1,0:T(8,128)(2,1)}, bf16[2,256,512]{2,1,0:T(8,128)(2,1)}) custom-call(s32[22]{0:T(128)} %concatenate.42.meta, f32[256,768]{1,0:T(8,128)} %get-tuple-element.348.x, bf16[4,256,192]{2,1,0:T(8,128)(2,1)} %get-tuple-element.349.blocks, bf16[768,4096]{1,0:T(8,128)(2,1)} %bitcast.146, ...), custom_call_target="tpu_custom_call" | custom-call | flops 2415919104 | bytes 70123520 | tf_op jit(solution)/shard_map/pallas_call | solution.py:91
  291.8 10.7 %shard_map.212 = (bf16[2,256,2048]{2,1,0:T(8,128)(2,1)}, f32[256,768]{1,0:T(8,128)}) custom-call(s32[22]{0:T(128)} %concatenate.42.meta, bf16[1,256,768]{2,1,0:T(8,128)(2,1)} %right.1, f32[2,256,2048]{2,1,0:T(8,128)} %get-tuple-element.352.mixed, bf16[768,4096]{1,0:T(8,128)(2,1)} %bitcast.154, bf16[768,4096]{1,0:T(8,128)(2,1)} %bitcast.155, ...), custom_call_target="tpu_custom_call" | custom-call | flops 2415919104 | bytes 70385664 | tf_op jit(solution)/shard_map/pallas_call | solution.py:91
  307.5 6.7 all-to-all-done.2
  317.8 33.8 %shard_map.214 = (bf16[1024,768]{1,0:T(8,128)(2,1)}, bf16[1024,768]{1,0:T(8,128)(2,1)}, bf16[1024,768]{1,0:T(8,128)(2,1)}, bf16[1024,768]{1,0:T(8,128)(2,1)}, bf...) custom-call(s32[1]{0:T(128)} %bitcast.40.meta, ...), custom_call_target="tpu_custom_call" | custom-call | flops 19327352832 | bytes 36388864 | tf_op jit(solution)/shard_map/pallas_call | solution.py:91
  359.4 7.8 all-to-all-start.3
  370.4 8.5 shard_map.215
  380.5 6.7 convolution_convert_fusion.2
  397.0 7.4 all-to-all-done.3
  407.8 4.8 shard_map.216
  413.1 5.3 collective-permute-start.46
  425.5 13.8 %collective-permute-done.51 = bf16[192,4096]{1,0:T(8,128)(2,1)} collective-permute-done((bf16[192,4096]{1,0:T(8,128)(2,1)}, bf16[192,4096]{1,0:T(8,128)(2,1)}, u32[]{:S(2)}, u32[]{:S(2)}) %collective-permute-start.51) | collective-permute-done | bytes 1572896 | tf_op jit(solution)/shard_map/ppermute | solution.py:30
  442.5 4.9 all-to-all-start.4
  447.9 20.8 %shard_map.218 = (bf16[8,192,128]{2,1,0:T(8,128)(2,1)}, f32[8,2,192,128]{3,2,1,0:T(8,128)}, bf16[8,2,192,128]{3,2,1,0:T(8,128)(2,1)}) custom-call(s32[22]{0:T(128)} %concatenate.42.meta, bf16[2,3,192,128]{3,2,1,0:T(8,128)(2,1)} %get-tuple-element.321.refs_0_, bf16[2,3,192,128]{3,2,1,0:T(8,128)(2,1)} %copy-done.95, bf16[2,3,192,128]{3,2,1,0:T(8,128)(2,1)} %copy-done.96, ...), custom_call_target="tpu_custom_call" | custom-call | flops 4026531840 | bytes 6303744 | tf_op jit(solution)/shard_map/pallas_call | solution.py:91
  476.6 8.0 collective-permute-done.52.rest_0_
  488.0 5.0 collective-permute-start.53
  493.0 4.7 collective-permute-start.54
  500.7 6.9 collective-permute-done.57
  509.4 9.7 %collective-permute-done.55.rest_3_ = bf16[2,3,192,128]{3,2,1,0:T(8,128)(2,1)} collective-permute-done((bf16[2,3,192,128]{3,2,1,0:T(8,128)(2,1)}, bf16[2,3,192,128]{3,2,1,0:T(8,128)(2,1)}, u32[]{:S(2)}, u32[]{:S(2)}) %collective-permute-start.55) | collective-permute-done | bytes 294944 | tf_op jit(solution)/shard_map/ppermute | solution.py:30
  519.1 9.8 %all-to-all-start.5 = ((bf16[8,24,6144]{2,1,0:T(8,128)(2,1)}), bf16[8,24,6144]{2,1,0:T(8,128)(2,1)S(1)}, u32[]{:S(2)}, u32[]{:S(2)}) async-start(bf16[8,24,6144]{2,1,0:T(8,128)(2,1)} %pad_maximum_fusion.3), calls=%async_computation.5 | async-start | bytes 4718592 | tf_op jit(solution)/shard_map/all_to_all | solution.py:1212
  529.4 7.0 shard_map.220
  538.4 10.9 %shard_map.221 = (bf16[2,256,2048]{2,1,0:T(8,128)(2,1)}, f32[256,768]{1,0:T(8,128)}) custom-call(s32[22]{0:T(128)} %concatenate.42.meta, bf16[1,256,768]{2,1,0:T(8,128)(2,1)} %convert_bitcast_fusion.1.branch.right, f32[2,256,2048]{2,1,0:T(8,128)} %get-tuple-element.430.mixed, bf16[768,4096]{1,0:T(8,128)(2,1)} %bitcast.138, bf16[768,4096]{1,0:T(8,128)(2,1)} %bitcast.139, ...), custom_call_target="tpu_custom_call" | custom-call | flops 2415919104 | bytes 70385664 | tf_op jit(solution)/shard_map/pallas_call | solution.py:91
  556.3 5.2 shard_map.222
  561.5 4.6 shard_map.223
  571.3 8.4 shard_map.224
  583.0 7.5 collective-permute-done.61.refs_10_
  608.3 21.0 %shard_map.225 = (bf16[8,192,128]{2,1,0:T(8,128)(2,1)}, f32[8,2,192,128]{3,2,1,0:T(8,128)}, bf16[8,2,192,128]{3,2,1,0:T(8,128)(2,1)}) custom-call(s32[22]{0:T(128)} %concatenate.42.meta, bf16[2,3,192,128]{3,2,1,0:T(8,128)(2,1)} %get-tuple-element.286.refs_0_, bf16[2,3,192,128]{3,2,1,0:T(8,128)(2,1)} %copy-done.89, bf16[2,3,192,128]{3,2,1,0:T(8,128)(2,1)} %copy-done.90, ...), custom_call_target="tpu_custom_call" | custom-call | flops 4026531840 | bytes 6303744 | tf_op jit(solution)/shard_map/pallas_call | solution.py:91
  634.1 13.5 %collective-permute-done.70 = bf16[192,6400]{1,0:T(8,128)(2,1)} collective-permute-done((bf16[192,6400]{1,0:T(8,128)(2,1)}, bf16[192,6400]{1,0:T(8,128)(2,1)}, u32[]{:S(2)}, u32[]{:S(2)}) %collective-permute-start.70) | collective-permute-done | bytes 2457632 | tf_op jit(solution)/shard_map/ppermute | solution.py:30
  652.7 6.2 collective-permute-done.65.rest_0_
  658.9 5.0 collective-permute-start.74
  667.3 4.6 collective-permute-start.72
  671.9 22.2 %collective-permute-done.74 = bf16[704,768]{1,0:T(8,128)(2,1)S(1)} collective-permute-done((bf16[704,768]{1,0:T(8,128)(2,1)}, bf16[704,768]{1,0:T(8,128)(2,1)S(1)}, u32[]{:S(2)}, u32[]{:S(2)}) %collective-permute-start.74) | collective-permute-done | bytes 1081376 | tf_op jit(solution)/shard_map/ppermute | solution.py:30
  696.8 7.0 shard_map.229
  711.8 10.0 %collective-permute-done.88.second = bf16[512,384]{1,0:T(8,128)(2,1)S(1)} collective-permute-done((bf16[512,384]{1,0:T(8,128)(2,1)}, bf16[512,384]{1,0:T(8,128)(2,1)S(1)}, u32[]{:S(2)}, u32[]{:S(2)}) %collective-permute-start.88) | collective-permute-done | bytes 393248 | tf_op jit(solution)/shard_map/ppermute | solution.py:30
  725.2 5.8 collective-permute-start.89
  734.8 6.2 collective-permute-done.90
  746.1 5.2 shard_map.230
  756.3 16.0 %collective-permute-done.76.second = bf16[192,2304]{1,0:T(8,128)(2,1)} collective-permute-done((bf16[192,2304]{1,0:T(8,128)(2,1)}, bf16[192,2304]{1,0:T(8,128)(2,1)}, u32[]{:S(2)}, u32[]{:S(2)}) %collective-permute-start.76) | collective-permute-done | bytes 884768 | tf_op jit(solution)/shard_map/ppermute | solution.py:30
  813.8 4.4 copy.132
  835.7 4.2 collective-permute-start.85
  848.4 36.8 %all-reduce.6.cloned.1.call-done = (bf16[192,2304]{1,0:T(8,128)(2,1)}, bf16[192,4096]{1,0:T(8,128)(2,1)}, bf16[192,768]{1,0:T(8,128)(2,1)}, bf16[192,768]{1,0:T(8,128)(2,1)}) async-done(((bf16[192,2304]{1,0:T(8,128)(2,1)}, bf16[192,4096]{1,0:T(8,128)(2,1)}, bf16[192,768]{1,0:T(8,128)(2,1)}, bf16[192,768]{1,0:T(8,128)(2,1)}), (bf16[192,2304]{1,0:T(8,128)(2,1)}, bf16[192,4096]{1,0:T(8,128)(2,1)}, ...) | async-done | bytes 3047440 | tf_op jit(solution)/shard_map/psum | solution.py:924
  885.2 4.6 maximum_convert_fusion
  (574 shorter events, 302.9 us)
Async XLA Ops:
  7.2 172.2 %all-gather.14.cloned.1.call-start = ((), (), s32[]{:S(2)}) async-start(), calls=%async_computation.9 | async-start | bytes 3932160 | tf_op jit(solution)/shard_map/all_gather | solution.py:975
  12.8 22.5 %collective-permute-start = (bf16[192,2304]{1,0:T(8,128)(2,1)S(1)}, bf16[192,2304]{1,0:T(8,128)(2,1)S(1)}, u32[]{:S(2)}, u32[]{:S(2)}) collective-permute-start(bf16[192,2304]{1,0:T(8,128)(2,1)S(1)} %slice_bitcast_fusion.3.w0.rest_4_), channel_id=1, source_target_pairs={{0,2},{1,3},{2,0},{3,1},{4,6},{5,7},{6,4},{7,5},{8,10},{9,11},{10,... | collective-permute-start | bytes 2654216 | tf_op jit(solution)/shard_map/ppermute | solution.py:30
  14.1 27.1 %collective-permute-start.13 = (bf16[192,768]{1,0:T(8,128)(2,1)S(1)}, bf16[192,768]{1,0:T(8,128)(2,1)S(1)}, u32[]{:S(2)}, u32[]{:S(2)}) collective-permute-start(bf16[192,768]{1,0:T(8,128)(2,1)S(1)} %slice_bitcast_fusion.5.w0), channel_id=1, source_target_pairs={{0,2},{1,3},{2,0},{3,1},{4,6},{5,7},{6,4},{7,5},{8,10},{9,11},{10,... | collective-permute-start | bytes 884744 | tf_op jit(solution)/shard_map/ppermute | solution.py:30
  44.0 135.3 %all-gather.12.cloned.1.call-start = ((), (), s32[]{:S(2)}) async-start(), calls=%async_computation.8 | async-start | bytes 7864320 | tf_op jit(solution)/shard_map/all_gather | solution.py:975
  48.0 232.3 %all-gather.18.cloned.1.call-start = ((), (), s32[]{:S(2)}) async-start(), calls=%async_computation.11 | async-start | bytes 3932160 | tf_op jit(solution)/shard_map/all_gather | solution.py:975
  48.8 231.5 %all-gather.16.cloned.1.call-start = ((), (), s32[]{:S(2)}) async-start(), calls=%async_computation.10 | async-start | bytes 7864320 | tf_op jit(solution)/shard_map/all_gather | solution.py:975
  63.0 15.0 %collective-permute-start.6 = (bf16[2,3,192,128]{3,2,1,0:T(8,128)(2,1)}, bf16[2,3,192,128]{3,2,1,0:T(8,128)(2,1)S(1)}, u32[]{:S(2)}, u32[]{:S(2)}) collective-permute-start(bf16[2,3,192,128]{3,2,1,0:T(8,128)(2,1)} %get-tuple-element.281), channel_id=1, source_target_pairs={{0,8},{4,12},{8,0},{12,4},{16,24},{20,28},{24,16},{28,20},{1,9},{5... | collective-permute-start | bytes 884744 | tf_op jit(solution)/shard_map/ppermute | solution.py:30
  64.6 23.6 %collective-permute-start.7 = (bf16[2,3,192,128]{3,2,1,0:T(8,128)(2,1)}, bf16[2,3,192,128]{3,2,1,0:T(8,128)(2,1)S(1)}, u32[]{:S(2)}, u32[]{:S(2)}) collective-permute-start(bf16[2,3,192,128]{3,2,1,0:T(8,128)(2,1)} %get-tuple-element.282), channel_id=1, source_target_pairs={{0,16},{4,20},{8,24},{12,28},{16,0},{20,4},{24,8},{28,12},{1,17},{... | collective-permute-start | bytes 884744 | tf_op jit(solution)/shard_map/ppermute | solution.py:30
  67.2 22.6 %collective-permute-start.8 = (bf16[2,3,192,128]{3,2,1,0:T(8,128)(2,1)}, bf16[2,3,192,128]{3,2,1,0:T(8,128)(2,1)S(1)}, u32[]{:S(2)}, u32[]{:S(2)}) collective-permute-start(bf16[2,3,192,128]{3,2,1,0:T(8,128)(2,1)} %get-tuple-element.283), channel_id=1, source_target_pairs={{0,24},{4,28},{8,16},{12,20},{16,8},{20,12},{24,0},{28,4},{1,25},{... | collective-permute-start | bytes 884744 | tf_op jit(solution)/shard_map/ppermute | solution.py:30
  67.9 24.4 %collective-permute-start.9 = (bf16[2,3,192,128]{3,2,1,0:T(8,128)(2,1)}, bf16[2,3,192,128]{3,2,1,0:T(8,128)(2,1)S(1)}, u32[]{:S(2)}, u32[]{:S(2)}) collective-permute-start(bf16[2,3,192,128]{3,2,1,0:T(8,128)(2,1)} %get-tuple-element.286.refs_0_), channel_id=1, source_target_pairs={{0,4},{4,0},{8,12},{12,8},{16,20},{20,16},{24,28},{28,24},{1,5},{5... | collective-permute-start | bytes 884744 | tf_op jit(solution)/shard_map/ppermute | solution.py:30
  98.9 74.9 %all-to-all-start = ((bf16[16,72,768]{2,1,0:T(8,128)(2,1)}), bf16[16,72,768]{2,1,0:T(8,128)(2,1)S(1)}, u32[]{:S(2)}, u32[]{:S(2)}) async-start(bf16[16,72,768]{2,1,0:T(8,128)(2,1)} %fusion.2), calls=%async_computation | async-start | bytes 3538944 | tf_op jit(solution)/shard_map/all_to_all | solution.py:963
  107.5 60.2 %collective-permute-start.17 = (bf16[192,2304]{1,0:T(8,128)(2,1)S(1)}, bf16[192,2304]{1,0:T(8,128)(2,1)}, u32[]{:S(2)}, u32[]{:S(2)}) collective-permute-start(bf16[192,2304]{1,0:T(8,128)(2,1)S(1)} %slice_bitcast_fusion.2.w0.rest_4_), channel_id=1, source_target_pairs={{0,2},{1,3},{2,0},{3,1},{4,6},{5,7},{6,4},{7,5},{8,10},{9,11},{10,... | collective-permute-start | bytes 2654216 | tf_op jit(solution)/shard_map/ppermute | solution.py:30
  128.9 38.8 %collective-permute-start.18 = (bf16[192,768]{1,0:T(8,128)(2,1)S(1)}, bf16[192,768]{1,0:T(8,128)(2,1)S(1)}, u32[]{:S(2)}, u32[]{:S(2)}) collective-permute-start(bf16[192,768]{1,0:T(8,128)(2,1)S(1)} %slice_bitcast_fusion.4.w0), channel_id=1, source_target_pairs={{0,2},{1,3},{2,0},{3,1},{4,6},{5,7},{6,4},{7,5},{8,10},{9,11},{10,... | collective-permute-start | bytes 884744 | tf_op jit(solution)/shard_map/ppermute | solution.py:30
  129.5 38.2 %collective-permute-start.19 = (bf16[192,768]{1,0:T(8,128)(2,1)S(1)}, bf16[192,768]{1,0:T(8,128)(2,1)S(1)}, u32[]{:S(2)}, u32[]{:S(2)}) collective-permute-start(bf16[192,768]{1,0:T(8,128)(2,1)S(1)} %slice_bitcast_fusion.5.w0), channel_id=1, source_target_pairs={{0,1},{1,0},{2,3},{3,2},{4,5},{5,4},{6,7},{7,6},{8,9},{9,8},{10,11... | collective-permute-start | bytes 884744 | tf_op jit(solution)/shard_map/ppermute | solution.py:30
  129.5 39.6 %collective-permute-start.20 = (bf16[192,768]{1,0:T(8,128)(2,1)S(1)}, bf16[192,768]{1,0:T(8,128)(2,1)}, u32[]{:S(2)}, u32[]{:S(2)}) collective-permute-start(bf16[192,768]{1,0:T(8,128)(2,1)S(1)} %copy-done.18), channel_id=1, source_target_pairs={{0,1},{1,0},{2,3},{3,2},{4,5},{5,4},{6,7},{7,6},{8,9},{9,8},{10,11... | collective-permute-start | bytes 884744 | tf_op jit(solution)/shard_map/ppermute | solution.py:30
  134.7 14.7 %collective-permute-start.15 = (bf16[2,192,128]{2,1,0:T(8,128)(2,1)}, bf16[2,192,128]{2,1,0:T(8,128)(2,1)S(1)}, u32[]{:S(2)}, u32[]{:S(2)}) collective-permute-start(bf16[2,192,128]{2,1,0:T(8,128)(2,1)} %get-tuple-element.296), channel_id=1, source_target_pairs={{0,16},{4,20},{8,24},{12,28},{16,0},{20,4},{24,8},{28,12},{1,17},{... | collective-permute-start | bytes 294920 | tf_op jit(solution)/shard_map/ppermute | solution.py:30
  173.8 92.5 %all-to-all-start.1 = ((bf16[4,3,192,1024]{3,2,1,0:T(8,128)(2,1)}), bf16[4,3,192,1024]{3,2,1,0:T(8,128)(2,1)}, u32[]{:S(2)}, u32[]{:S(2)}) async-start(bf16[4,3,192,1024]{3,2,1,0:T(8,128)(2,1)} %pad_maximum_fusion), calls=%async_computation.1 | async-start | bytes 9437184 | tf_op jit(solution)/shard_map/all_to_all | solution.py:1075
  195.7 15.4 %collective-permute-start.23 = (bf16[2,3,192,128]{3,2,1,0:T(8,128)(2,1)}, bf16[2,3,192,128]{3,2,1,0:T(8,128)(2,1)S(1)}, u32[]{:S(2)}, u32[]{:S(2)}) collective-permute-start(bf16[2,3,192,128]{3,2,1,0:T(8,128)(2,1)} %get-tuple-element.317), channel_id=1, source_target_pairs={{0,8},{4,12},{8,0},{12,4},{16,24},{20,28},{24,16},{28,20},{1,9},{5... | collective-permute-start | bytes 884744 | tf_op jit(solution)/shard_map/ppermute | solution.py:30
  197.1 23.7 %collective-permute-start.24 = (bf16[2,3,192,128]{3,2,1,0:T(8,128)(2,1)}, bf16[2,3,192,128]{3,2,1,0:T(8,128)(2,1)S(1)}, u32[]{:S(2)}, u32[]{:S(2)}) collective-permute-start(bf16[2,3,192,128]{3,2,1,0:T(8,128)(2,1)} %get-tuple-element.318), channel_id=1, source_target_pairs={{0,16},{4,20},{8,24},{12,28},{16,0},{20,4},{24,8},{28,12},{1,17},{... | collective-permute-start | bytes 884744 | tf_op jit(solution)/shard_map/ppermute | solution.py:30
  199.1 23.2 %collective-permute-start.25 = (bf16[2,3,192,128]{3,2,1,0:T(8,128)(2,1)}, bf16[2,3,192,128]{3,2,1,0:T(8,128)(2,1)S(1)}, u32[]{:S(2)}, u32[]{:S(2)}) collective-permute-start(bf16[2,3,192,128]{3,2,1,0:T(8,128)(2,1)} %get-tuple-element.319), channel_id=1, source_target_pairs={{0,24},{4,28},{8,16},{12,20},{16,8},{20,12},{24,0},{28,4},{1,25},{... | collective-permute-start | bytes 884744 | tf_op jit(solution)/shard_map/ppermute | solution.py:30
  200.1 22.8 %collective-permute-start.26 = (bf16[2,3,192,128]{3,2,1,0:T(8,128)(2,1)}, bf16[2,3,192,128]{3,2,1,0:T(8,128)(2,1)S(1)}, u32[]{:S(2)}, u32[]{:S(2)}) collective-permute-start(bf16[2,3,192,128]{3,2,1,0:T(8,128)(2,1)} %get-tuple-element.321.refs_0_), channel_id=1, source_target_pairs={{0,4},{4,0},{8,12},{12,8},{16,20},{20,16},{24,28},{28,24},{1,5},{5... | collective-permute-start | bytes 884744 | tf_op jit(solution)/shard_map/ppermute | solution.py:30
  233.8 18.4 %collective-permute-start.30 = (bf16[1024,768]{1,0:T(8,128)(2,1)}, bf16[1024,768]{1,0:T(8,128)(2,1)}, u32[]{:S(2)}, u32[]{:S(2)}) collective-permute-start(bf16[1024,768]{1,0:T(8,128)(2,1)} %bitcast.34.refs_2_), channel_id=1, source_target_pairs={{0,1},{1,0},{2,3},{3,2},{4,5},{5,4},{6,7},{7,6},{8,9},{9,8},{10,11... | collective-permute-start | bytes 4718600 | tf_op jit(solution)/shard_map/ppermute | solution.py:30
  233.8 23.6 %collective-permute-start.35 = (bf16[192,768]{1,0:T(8,128)(2,1)S(1)}, bf16[192,768]{1,0:T(8,128)(2,1)S(1)}, u32[]{:S(2)}, u32[]{:S(2)}) collective-permute-start(bf16[192,768]{1,0:T(8,128)(2,1)S(1)} %slice_bitcast_fusion.4.w0), channel_id=1, source_target_pairs={{0,1},{1,0},{2,3},{3,2},{4,5},{5,4},{6,7},{7,6},{8,9},{9,8},{10,11... | collective-permute-start | bytes 884744 | tf_op jit(solution)/shard_map/ppermute | solution.py:30
  234.3 23.1 %collective-permute-start.36 = (bf16[192,768]{1,0:T(8,128)(2,1)S(1)}, bf16[192,768]{1,0:T(8,128)(2,1)S(1)}, u32[]{:S(2)}, u32[]{:S(2)}) collective-permute-start(bf16[192,768]{1,0:T(8,128)(2,1)S(1)} %copy-done.21), channel_id=1, source_target_pairs={{0,1},{1,0},{2,3},{3,2},{4,5},{5,4},{6,7},{7,6},{8,9},{9,8},{10,11... | collective-permute-start | bytes 884744 | tf_op jit(solution)/shard_map/ppermute | solution.py:30
  234.4 17.1 %collective-permute-start.31 = (f32[16,64]{1,0:T(8,128)S(1)}, f32[16,64]{1,0:T(8,128)S(1)}, u32[]{:S(2)}, u32[]{:S(2)}) collective-permute-start(f32[16,64]{1,0:T(8,128)S(1)} %bitcast.208), channel_id=1, source_target_pairs={{0,1},{1,0},{2,3},{3,2},{4,5},{5,4},{6,7},{7,6},{8,9},{9,8},{10,11... | collective-permute-start | bytes 12296 | tf_op jit(solution)/shard_map/ppermute | solution.py:30
  275.1 39.2 %all-to-all-start.2 = ((bf16[16,64,768]{2,1,0:T(8,128)(2,1)}), bf16[16,64,768]{2,1,0:T(8,128)(2,1)S(1)}, u32[]{:S(2)}, u32[]{:S(2)}) async-start(bf16[16,64,768]{2,1,0:T(8,128)(2,1)} %bitcast.198), calls=%async_computation.2 | async-start | bytes 3145728 | tf_op jit(solution)/shard_map/all_to_all | solution.py:963
  280.1 22.4 %collective-permute-start.38 = (bf16[1,256,768]{2,1,0:T(8,128)(2,1)S(1)}, bf16[1,256,768]{2,1,0:T(8,128)(2,1)}, u32[]{:S(2)}, u32[]{:S(2)}) collective-permute-start(bf16[1,256,768]{2,1,0:T(8,128)(2,1)S(1)} %copy-done.10), channel_id=1, source_target_pairs={{0,1},{1,0},{2,3},{3,2},{4,5},{5,4},{6,7},{7,6},{8,9},{9,8},{10,11... | collective-permute-start | bytes 1179656 | tf_op jit(solution)/shard_map/ppermute | solution.py:30
  351.9 17.8 %collective-permute-start.44 = (bf16[2,256,2048]{2,1,0:T(8,128)(2,1)}, bf16[2,256,2048]{2,1,0:T(8,128)(2,1)}, u32[]{:S(2)}, u32[]{:S(2)}) collective-permute-start(bf16[2,256,2048]{2,1,0:T(8,128)(2,1)} %get-tuple-element.385.right), channel_id=1, source_target_pairs={{0,1},{1,0},{2,3},{3,2},{4,5},{5,4},{6,7},{7,6},{8,9},{9,8},{10,11... | collective-permute-start | bytes 6291464 | tf_op jit(solution)/shard_map/ppermute | solution.py:30
  354.0 24.9 %collective-permute-start.45 = (bf16[512,768]{1,0:T(8,128)(2,1)S(1)}, bf16[512,768]{1,0:T(8,128)(2,1)}, u32[]{:S(2)}, u32[]{:S(2)}) collective-permute-start(bf16[512,768]{1,0:T(8,128)(2,1)S(1)} %copy-done.85), channel_id=1, source_target_pairs={{0,2},{1,3},{2,0},{3,1},{4,6},{5,7},{6,4},{7,5},{8,10},{9,11},{10,... | collective-permute-start | bytes 2359304 | tf_op jit(solution)/shard_map/ppermute | solution.py:30
  359.4 45.0 %all-to-all-start.3 = ((bf16[16,72,768]{2,1,0:T(8,128)(2,1)}), bf16[16,72,768]{2,1,0:T(8,128)(2,1)S(1)}, u32[]{:S(2)}, u32[]{:S(2)}) async-start(bf16[16,72,768]{2,1,0:T(8,128)(2,1)} %fusion.3), calls=%async_computation.3 | async-start | bytes 3538944 | tf_op jit(solution)/shard_map/all_to_all | solution.py:963
  404.4 35.0 %collective-permute-start.51 = (bf16[192,4096]{1,0:T(8,128)(2,1)}, bf16[192,4096]{1,0:T(8,128)(2,1)}, u32[]{:S(2)}, u32[]{:S(2)}) collective-permute-start(bf16[192,4096]{1,0:T(8,128)(2,1)} %get-tuple-element.403), channel_id=1, source_target_pairs={{0,2},{1,3},{2,0},{3,1},{4,6},{5,7},{6,4},{7,5},{8,10},{9,11},{10,... | collective-permute-start | bytes 4718600 | tf_op jit(solution)/shard_map/ppermute | solution.py:30
  413.1 28.7 %collective-permute-start.46 = (bf16[2,192,128]{2,1,0:T(8,128)(2,1)}, bf16[2,192,128]{2,1,0:T(8,128)(2,1)S(1)}, u32[]{:S(2)}, u32[]{:S(2)}) collective-permute-start(bf16[2,192,128]{2,1,0:T(8,128)(2,1)} %get-tuple-element.393), channel_id=1, source_target_pairs={{0,8},{4,12},{8,0},{12,4},{16,24},{20,28},{24,16},{28,20},{1,9},{5... | collective-permute-start | bytes 294920 | tf_op jit(solution)/shard_map/ppermute | solution.py:30
  418.3 23.5 %collective-permute-start.47 = (bf16[2,192,128]{2,1,0:T(8,128)(2,1)}, bf16[2,192,128]{2,1,0:T(8,128)(2,1)S(1)}, u32[]{:S(2)}, u32[]{:S(2)}) collective-permute-start(bf16[2,192,128]{2,1,0:T(8,128)(2,1)} %get-tuple-element.394), channel_id=1, source_target_pairs={{0,16},{4,20},{8,24},{12,28},{16,0},{20,4},{24,8},{28,12},{1,17},{... | collective-permute-start | bytes 294920 | tf_op jit(solution)/shard_map/ppermute | solution.py:30
  419.9 21.9 %collective-permute-start.48 = (bf16[2,192,128]{2,1,0:T(8,128)(2,1)}, bf16[2,192,128]{2,1,0:T(8,128)(2,1)S(1)}, u32[]{:S(2)}, u32[]{:S(2)}) collective-permute-start(bf16[2,192,128]{2,1,0:T(8,128)(2,1)} %get-tuple-element.395), channel_id=1, source_target_pairs={{0,24},{4,28},{8,16},{12,20},{16,8},{20,12},{24,0},{28,4},{1,25},{... | collective-permute-start | bytes 294920 | tf_op jit(solution)/shard_map/ppermute | solution.py:30
  442.5 76.6 %all-to-all-start.4 = ((bf16[4,3,192,1024]{3,2,1,0:T(8,128)(2,1)}), bf16[4,3,192,1024]{3,2,1,0:T(8,128)(2,1)}, u32[]{:S(2)}, u32[]{:S(2)}) async-start(bf16[4,3,192,1024]{3,2,1,0:T(8,128)(2,1)} %pad_maximum_fusion.1), calls=%async_computation.4 | async-start | bytes 9437184 | tf_op jit(solution)/shard_map/all_to_all | solution.py:1198
  447.5 23.2 %collective-permute-start.56 = (bf16[1024,768]{1,0:T(8,128)(2,1)}, bf16[1024,768]{1,0:T(8,128)(2,1)}, u32[]{:S(2)}, u32[]{:S(2)}) collective-permute-start(bf16[1024,768]{1,0:T(8,128)(2,1)} %get-tuple-element.419), channel_id=1, source_target_pairs={{0,1},{1,0},{2,3},{3,2},{4,5},{5,4},{6,7},{7,6},{8,9},{9,8},{10,11... | collective-permute-start | bytes 4718600 | tf_op jit(solution)/shard_map/ppermute | solution.py:30
  468.7 15.9 %collective-permute-start.52 = (bf16[8,2,192,128]{3,2,1,0:T(8,128)(2,1)}, bf16[8,2,192,128]{3,2,1,0:T(8,128)(2,1)}, u32[]{:S(2)}, u32[]{:S(2)}) collective-permute-start(bf16[8,2,192,128]{3,2,1,0:T(8,128)(2,1)} %get-tuple-element.413), channel_id=1, source_target_pairs={{0,4},{4,0},{8,12},{12,8},{16,20},{20,16},{24,28},{28,24},{1,5},{5... | collective-permute-start | bytes 2359304 | tf_op jit(solution)/shard_map/ppermute | solution.py:30
  474.0 33.6 %collective-permute-start.57 = (bf16[192,768]{1,0:T(8,128)(2,1)}, bf16[192,768]{1,0:T(8,128)(2,1)}, u32[]{:S(2)}, u32[]{:S(2)}) collective-permute-start(bf16[192,768]{1,0:T(8,128)(2,1)} %get-tuple-element.424), channel_id=1, source_target_pairs={{0,2},{1,3},{2,0},{3,1},{4,6},{5,7},{6,4},{7,5},{8,10},{9,11},{10,... | collective-permute-start | bytes 884744 | tf_op jit(solution)/shard_map/ppermute | solution.py:30
  488.0 21.4 %collective-permute-start.53 = (bf16[2,3,192,128]{3,2,1,0:T(8,128)(2,1)}, bf16[2,3,192,128]{3,2,1,0:T(8,128)(2,1)S(1)}, u32[]{:S(2)}, u32[]{:S(2)}) collective-permute-start(bf16[2,3,192,128]{3,2,1,0:T(8,128)(2,1)} %get-tuple-element.415), channel_id=1, source_target_pairs={{0,8},{4,12},{8,0},{12,4},{16,24},{20,28},{24,16},{28,20},{1,9},{5... | collective-permute-start | bytes 884744 | tf_op jit(solution)/shard_map/ppermute | solution.py:30
  493.0 16.4 %collective-permute-start.54 = (bf16[2,3,192,128]{3,2,1,0:T(8,128)(2,1)}, bf16[2,3,192,128]{3,2,1,0:T(8,128)(2,1)}, u32[]{:S(2)}, u32[]{:S(2)}) collective-permute-start(bf16[2,3,192,128]{3,2,1,0:T(8,128)(2,1)} %get-tuple-element.416), channel_id=1, source_target_pairs={{0,16},{4,20},{8,24},{12,28},{16,0},{20,4},{24,8},{28,12},{1,17},{... | collective-permute-start | bytes 884744 | tf_op jit(solution)/shard_map/ppermute | solution.py:30
  497.7 21.4 %collective-permute-start.55 = (bf16[2,3,192,128]{3,2,1,0:T(8,128)(2,1)}, bf16[2,3,192,128]{3,2,1,0:T(8,128)(2,1)}, u32[]{:S(2)}, u32[]{:S(2)}) collective-permute-start(bf16[2,3,192,128]{3,2,1,0:T(8,128)(2,1)} %get-tuple-element.417), channel_id=1, source_target_pairs={{0,24},{4,28},{8,16},{12,20},{16,8},{20,12},{24,0},{28,4},{1,25},{... | collective-permute-start | bytes 884744 | tf_op jit(solution)/shard_map/ppermute | solution.py:30
  519.1 72.0 %all-to-all-start.5 = ((bf16[8,24,6144]{2,1,0:T(8,128)(2,1)}), bf16[8,24,6144]{2,1,0:T(8,128)(2,1)S(1)}, u32[]{:S(2)}, u32[]{:S(2)}) async-start(bf16[8,24,6144]{2,1,0:T(8,128)(2,1)} %pad_maximum_fusion.3), calls=%async_computation.5 | async-start | bytes 4718592 | tf_op jit(solution)/shard_map/all_to_all | solution.py:1212
  529.0 167.9 %all-gather.10.cloned.1.call-start = ((), (), s32[]{:S(2)}) async-start(), calls=%async_computation.7 | async-start | bytes 2654208 | tf_op jit(solution)/shard_map/all_gather | solution.py:1235
  549.3 21.3 %collective-permute-start.64 = (bf16[2,256,2048]{2,1,0:T(8,128)(2,1)}, bf16[2,256,2048]{2,1,0:T(8,128)(2,1)}, u32[]{:S(2)}, u32[]{:S(2)}) collective-permute-start(bf16[2,256,2048]{2,1,0:T(8,128)(2,1)} %get-tuple-element.445.right), channel_id=1, source_target_pairs={{0,1},{1,0},{2,3},{3,2},{4,5},{5,4},{6,7},{7,6},{8,9},{9,8},{10,11... | collective-permute-start | bytes 6291464 | tf_op jit(solution)/shard_map/ppermute | solution.py:30
  549.9 20.6 %collective-permute-start.63 = (bf16[2,256,192]{2,1,0:T(8,128)(2,1)S(1)}, bf16[2,256,192]{2,1,0:T(8,128)(2,1)S(1)}, u32[]{:S(2)}, u32[]{:S(2)}) collective-permute-start(bf16[2,256,192]{2,1,0:T(8,128)(2,1)S(1)} %copy-done.101), channel_id=1, source_target_pairs={{0,1},{1,0},{2,3},{3,2},{4,5},{5,4},{6,7},{7,6},{8,9},{9,8},{10,11... | collective-permute-start | bytes 589832 | tf_op jit(solution)/shard_map/ppermute | solution.py:30
  566.2 16.8 %collective-permute-start.60 = (bf16[2,192,128]{2,1,0:T(8,128)(2,1)}, bf16[2,192,128]{2,1,0:T(8,128)(2,1)S(1)}, u32[]{:S(2)}, u32[]{:S(2)}) collective-permute-start(bf16[2,192,128]{2,1,0:T(8,128)(2,1)} %get-tuple-element.440), channel_id=1, source_target_pairs={{0,8},{4,12},{8,0},{12,4},{16,24},{20,28},{24,16},{28,20},{1,9},{5... | collective-permute-start | bytes 294920 | tf_op jit(solution)/shard_map/ppermute | solution.py:30
  568.1 22.4 %collective-permute-start.61 = (bf16[2,192,128]{2,1,0:T(8,128)(2,1)}, bf16[2,192,128]{2,1,0:T(8,128)(2,1)S(1)}, u32[]{:S(2)}, u32[]{:S(2)}) collective-permute-start(bf16[2,192,128]{2,1,0:T(8,128)(2,1)} %get-tuple-element.441), channel_id=1, source_target_pairs={{0,16},{4,20},{8,24},{12,28},{16,0},{20,4},{24,8},{28,12},{1,17},{... | collective-permute-start | bytes 294920 | tf_op jit(solution)/shard_map/ppermute | solution.py:30
  570.5 20.6 %collective-permute-start.62 = (bf16[2,192,128]{2,1,0:T(8,128)(2,1)}, bf16[2,192,128]{2,1,0:T(8,128)(2,1)}, u32[]{:S(2)}, u32[]{:S(2)}) collective-permute-start(bf16[2,192,128]{2,1,0:T(8,128)(2,1)} %get-tuple-element.442), channel_id=1, source_target_pairs={{0,24},{4,28},{8,16},{12,20},{16,8},{20,12},{24,0},{28,4},{1,25},{... | collective-permute-start | bytes 294920 | tf_op jit(solution)/shard_map/ppermute | solution.py:30
  591.2 56.5 %collective-permute-start.70 = (bf16[192,6400]{1,0:T(8,128)(2,1)}, bf16[192,6400]{1,0:T(8,128)(2,1)}, u32[]{:S(2)}, u32[]{:S(2)}) collective-permute-start(bf16[192,6400]{1,0:T(8,128)(2,1)} %pad_maximum_fusion.2), channel_id=1, source_target_pairs={{0,2},{1,3},{2,0},{3,1},{4,6},{5,7},{6,4},{7,5},{8,10},{9,11},{10,... | collective-permute-start | bytes 7372808 | tf_op jit(solution)/shard_map/ppermute | solution.py:30
  629.3 29.6 %collective-permute-start.65 = (bf16[8,2,192,128]{3,2,1,0:T(8,128)(2,1)}, bf16[8,2,192,128]{3,2,1,0:T(8,128)(2,1)}, u32[]{:S(2)}, u32[]{:S(2)}) collective-permute-start(bf16[8,2,192,128]{3,2,1,0:T(8,128)(2,1)} %get-tuple-element.458), channel_id=1, source_target_pairs={{0,4},{4,0},{8,12},{12,8},{16,20},{20,16},{24,28},{28,24},{1,5},{5... | collective-permute-start | bytes 2359304 | tf_op jit(solution)/shard_map/ppermute | solution.py:30
  630.0 66.8 %all-to-all-start.6 = ((bf16[16,64,768]{2,1,0:T(8,128)(2,1)}), bf16[16,64,768]{2,1,0:T(8,128)(2,1)S(1)}, u32[]{:S(2)}, u32[]{:S(2)}) async-start(bf16[16,64,768]{2,1,0:T(8,128)(2,1)} %bitcast.57), calls=%async_computation.6 | async-start | bytes 3145728 | tf_op jit(solution)/shard_map/all_to_all | solution.py:963
  634.1 251.1 %all-reduce.6.cloned.1.call-start = ((), (), s32[]{:S(2)}) async-start(), calls=%async_computation.12 | async-start | bytes 6094848 | tf_op jit(solution)/shard_map/psum | solution.py:924
  658.9 35.2 %collective-permute-start.74 = (bf16[704,768]{1,0:T(8,128)(2,1)}, bf16[704,768]{1,0:T(8,128)(2,1)S(1)}, u32[]{:S(2)}, u32[]{:S(2)}) collective-permute-start(bf16[704,768]{1,0:T(8,128)(2,1)} %pad_maximum_fusion.5), channel_id=1, source_target_pairs={{0,2},{1,3},{2,0},{3,1},{4,6},{5,7},{6,4},{7,5},{8,10},{9,11},{10,... | collective-permute-start | bytes 3244040 | tf_op jit(solution)/shard_map/ppermute | solution.py:30
  667.3 27.6 %collective-permute-start.71 = (bf16[2,3,192,128]{3,2,1,0:T(8,128)(2,1)}, bf16[2,3,192,128]{3,2,1,0:T(8,128)(2,1)}, u32[]{:S(2)}, u32[]{:S(2)}) collective-permute-start(bf16[2,3,192,128]{3,2,1,0:T(8,128)(2,1)} %get-tuple-element.471), channel_id=1, source_target_pairs={{0,8},{4,12},{8,0},{12,4},{16,24},{20,28},{24,16},{28,20},{1,9},{5... | collective-permute-start | bytes 884744 | tf_op jit(solution)/shard_map/ppermute | solution.py:30
  667.3 29.5 %collective-permute-start.72 = (bf16[2,3,192,128]{3,2,1,0:T(8,128)(2,1)}, bf16[2,3,192,128]{3,2,1,0:T(8,128)(2,1)}, u32[]{:S(2)}, u32[]{:S(2)}) collective-permute-start(bf16[2,3,192,128]{3,2,1,0:T(8,128)(2,1)} %get-tuple-element.472), channel_id=1, source_target_pairs={{0,16},{4,20},{8,24},{12,28},{16,0},{20,4},{24,8},{28,12},{1,17},{... | collective-permute-start | bytes 884744 | tf_op jit(solution)/shard_map/ppermute | solution.py:30
  671.9 24.9 %collective-permute-start.73 = (bf16[2,3,192,128]{3,2,1,0:T(8,128)(2,1)}, bf16[2,3,192,128]{3,2,1,0:T(8,128)(2,1)}, u32[]{:S(2)}, u32[]{:S(2)}) collective-permute-start(bf16[2,3,192,128]{3,2,1,0:T(8,128)(2,1)} %get-tuple-element.473), channel_id=1, source_target_pairs={{0,24},{4,28},{8,16},{12,20},{16,8},{20,12},{24,0},{28,4},{1,25},{... | collective-permute-start | bytes 884744 | tf_op jit(solution)/shard_map/ppermute | solution.py:30
  703.9 41.1 %collective-permute-start.75 = (bf16[1,256,2304]{2,1,0:T(8,128)(2,1)}, bf16[1,256,2304]{2,1,0:T(8,128)(2,1)S(1)}, u32[]{:S(2)}, u32[]{:S(2)}) collective-permute-start(bf16[1,256,2304]{2,1,0:T(8,128)(2,1)} %get-tuple-element.485.right), channel_id=1, source_target_pairs={{0,1},{1,0},{2,3},{3,2},{4,5},{5,4},{6,7},{7,6},{8,9},{9,8},{10,11... | collective-permute-start | bytes 3538952 | tf_op jit(solution)/shard_map/ppermute | solution.py:30
  711.8 33.2 %collective-permute-start.39 = (bf16[2,256,192]{2,1,0:T(8,128)(2,1)}, bf16[2,256,192]{2,1,0:T(8,128)(2,1)S(1)}, u32[]{:S(2)}, u32[]{:S(2)}) collective-permute-start(bf16[2,256,192]{2,1,0:T(8,128)(2,1)} %get-tuple-element.360), channel_id=1, source_target_pairs={{0,1},{1,0},{2,3},{3,2},{4,5},{5,4},{6,7},{7,6},{8,9},{9,8},{10,11... | collective-permute-start | bytes 589832 | tf_op jit(solution)/shard_map/ppermute | solution.py:30
  742.6 76.5 %collective-permute-start.92 = (bf16[128,384]{1,0:T(8,128)(2,1)}, bf16[128,384]{1,0:T(8,128)(2,1)}, u32[]{:S(2)}, u32[]{:S(2)}) collective-permute-start(bf16[128,384]{1,0:T(8,128)(2,1)} %add_convert_fusion.3.refs_0_), channel_id=1, source_target_pairs={{0,8},{4,12},{8,0},{12,4},{16,24},{20,28},{24,16},{28,20},{1,9},{5... | collective-permute-start | bytes 294920 | tf_op jit(solution)/shard_map/ppermute | solution.py:30
  744.2 76.1 %collective-permute-start.93 = (bf16[128,384]{1,0:T(8,128)(2,1)}, bf16[128,384]{1,0:T(8,128)(2,1)}, u32[]{:S(2)}, u32[]{:S(2)}) collective-permute-start(bf16[128,384]{1,0:T(8,128)(2,1)} %add_convert_fusion.3.refs_0_), channel_id=1, source_target_pairs={{0,16},{4,20},{8,24},{12,28},{16,0},{20,4},{24,8},{28,12},{1,17},{... | collective-permute-start | bytes 294920 | tf_op jit(solution)/shard_map/ppermute | solution.py:30
  751.3 21.0 %collective-permute-start.76 = (bf16[192,2304]{1,0:T(8,128)(2,1)}, bf16[192,2304]{1,0:T(8,128)(2,1)}, u32[]{:S(2)}, u32[]{:S(2)}) collective-permute-start(bf16[192,2304]{1,0:T(8,128)(2,1)} %get-tuple-element.494), channel_id=1, source_target_pairs={{0,2},{1,3},{2,0},{3,1},{4,6},{5,7},{6,4},{7,5},{8,10},{9,11},{10,... | collective-permute-start | bytes 2654216 | tf_op jit(solution)/shard_map/ppermute | solution.py:30
  800.5 21.3 %collective-permute-start.78 = (bf16[48,1152]{1,0:T(8,128)(2,1)}, bf16[48,1152]{1,0:T(8,128)(2,1)S(1)}, u32[]{:S(2)}, u32[]{:S(2)}) collective-permute-start(bf16[48,1152]{1,0:T(8,128)(2,1)} %get-tuple-element.503), channel_id=1, source_target_pairs={{0,8},{4,12},{8,0},{12,4},{16,24},{20,28},{24,16},{28,20},{1,9},{5... | collective-permute-start | bytes 331784 | tf_op jit(solution)/shard_map/ppermute | solution.py:30
  802.2 20.1 %collective-permute-start.79 = (bf16[48,1152]{1,0:T(8,128)(2,1)}, bf16[48,1152]{1,0:T(8,128)(2,1)S(1)}, u32[]{:S(2)}, u32[]{:S(2)}) collective-permute-start(bf16[48,1152]{1,0:T(8,128)(2,1)} %get-tuple-element.504), channel_id=1, source_target_pairs={{0,16},{4,20},{8,24},{12,28},{16,0},{20,4},{24,8},{28,12},{1,17},{... | collective-permute-start | bytes 331784 | tf_op jit(solution)/shard_map/ppermute | solution.py:30
  802.2 21.7 %collective-permute-start.80 = (bf16[48,1152]{1,0:T(8,128)(2,1)}, bf16[48,1152]{1,0:T(8,128)(2,1)S(1)}, u32[]{:S(2)}, u32[]{:S(2)}) collective-permute-start(bf16[48,1152]{1,0:T(8,128)(2,1)} %get-tuple-element.505), channel_id=1, source_target_pairs={{0,24},{4,28},{8,16},{12,20},{16,8},{20,12},{24,0},{28,4},{1,25},{... | collective-permute-start | bytes 331784 | tf_op jit(solution)/shard_map/ppermute | solution.py:30
  (174 other events, 2563.1 us)
Sparse Core Ops, SparseCore 0:
  44.1 28.8 all-gather.13
  75.2 73.3 all-gather.11
  150.7 33.5 all-gather.17
  186.3 80.7 all-gather.15
  595.2 65.3 all-gather.9
  745.1 140.0 all-reduce.5

commit v6 on v5

--- a/solution.py
+++ b/solution.py
@@ -1254,15 +1254,8 @@
     grad_qkv = exchange(merge(meta, grad_q, own, arrived_kv))
     second_arrived = swap(second_sent, "fsdp", 2)
     tall = grad_mlp_out_one[0].shape[0]
-    sums_one = [
-        *first_sums,
-        grad_attn_out_one[0] + second_arrived[tall:],
-        sum_attn_out_two,
-    ]
-    grad_qkv, expert_rows, sums_two, *sums_one = lax.optimization_barrier(
-        (grad_qkv, expert_rows, sums_two, *sums_one)
-    )
-    sums_one = total(1, sums_one)
+    sums_one = total(1, (*first_sums, sum_attn_out_two))
+    grad_qkv, expert_rows, sums_two = lax.optimization_barrier((grad_qkv, expert_rows, sums_two))
     grad_mixed, grad_resid, gain_zero = pre_back(
         meta, resid_in, gains[0], tables, grad_resid, grad_qkv, w_attn_in_one
     )
@@ -1277,10 +1270,17 @@
     output = shared + sum(gate_probs[:, k, None] * back_rows[k] for k in range(TOP))
     small_grads = jnp.concatenate([gain_zero, gain_one, gain_two, gain_three, grad_router])
     wide = sums_one[1].shape[1]
-    (attn_in_grad, mlp_out_grad), sums_one, small_grads = reduce_last(
+    (attn_grad, mlp_out_grad), sums_one, small_grads = reduce_last(
         at_ctx,
         [
-            (grad_attn_in_one[0], swap(grad_attn_in_one[1], "fsdp", 2), sums_one[0]),
+            tuple(
+                jnp.concatenate(pair, axis=1)
+                for pair in (
+                    (grad_attn_in_one[0], grad_attn_out_one[0]),
+                    (swap(grad_attn_in_one[1], "fsdp", 2), second_arrived[tall:]),
+                    (sums_one[0], sums_one[2]),
+                )
+            ),
             (
                 grad_mlp_out_one[0],
                 second_arrived[:tall],
@@ -1291,10 +1291,8 @@
         small_grads,
     )
     small_grads = lax.dynamic_slice_in_dim(small_grads, own_fsdp * shard_width, shard_width, 1)
-    attn_out_grad, mlp_in_grad = [
-        jnp.stack(pair).astype(jnp.float32)
-        for pair in ((sums_one[2], sums_one[3]), (sums_one[1], sums_two[:, :wide]))
-    ]
+    attn_in_grad, attn_out_grad = attn_grad[:, :, :-model_width], attn_grad[:, :, -model_width:]
+    mlp_in_grad = jnp.stack([sums_one[1], sums_two[:, :wide]]).astype(jnp.float32)
     return (
         output[None],
         grad_resid[None],

time: 917 us -> 946 us (1.032)
  local copies, waits for them, and re-layouts: 58.3 us -> 71.8 us
  starting transfers between devices: 178 us -> 189 us
    ppermute x104, waiting for transfers between devices: 245 us -> 263 us  [swap(): return lax.ppermute(values, axis, [(i, i ^ mask) for i in range(count)])]
    ppermute x104, starting transfers between devices: 133 us -> 148 us  [swap(): return lax.ppermute(values, axis, [(i, i ^ mask) for i in range(count)])]
    psum x1, waiting for transfers between devices: 36.8 us -> 24.2 us  [total(): return lax.psum(tuple(grads), 'ctx', axis_index_groups=ring)]
    unnamed x244 -> x256, local copies, waits for them, and re-layouts: 23.4 us -> 24.6 us
  transfers between devices with their start and end apart: 117 -> 117, of which waited for: 45 -> 51; matrix products, arithmetic and copies ran while one was open for 13% -> 13% of each run, Pallas kernels for 24% -> 23%
where the time goes in v6:
time: 946 us; the launch traced here: 932 us
  waiting for transfers between devices  313 us (33%)
  Pallas kernels  259 us (27%)
  starting transfers between devices  189 us (20%)
  local copies, waits for them, and re-layouts  71.8 us (8%)
  other arithmetic  59 us (6%)
  matrix products  24.2 us (3%)
  between operations  16 us (2%)
    ppermute x104, waiting for transfers between devices, swap(): return lax.ppermute(values, axis, [(i, i ^ mask) for i in range(count)])  263 us
    pallas_call x33, Pallas kernels, call(): pl.pallas_call(body, grid_spec=pltpu.PrefetchScalarGridSpec(num_scalar_pr...  259 us
    ppermute x104, starting transfers between devices, swap(): return lax.ppermute(values, axis, [(i, i ^ mask) for i in range(count)])  148 us
    unnamed x256, local copies, waits for them, and re-layouts  24.6 us
    psum x1, waiting for transfers between devices, total(): return lax.psum(tuple(grads), 'ctx', axis_index_groups=ring)  24.2 us
    all_to_all x4, starting transfers between devices, dispatch(): lax.all_to_all(values, BOTH, 0, 0, tiled=True, axis_index_groups=members)  23.7 us
  transfers between devices with their start and end apart: 117, of which 51 were waited for; matrix products, arithmetic and copies ran while one was open for 13% of the time, Pallas kernels for 23%

profile of v6, /device:TPU:0, one launch (start us, length us, event | category | flops | bytes accessed | tf_op | source)
XLA Modules:
  0.0 931.5 jit_solution(9159056480655416650)
XLA Ops:
  25.1 10.3 %collective-permute-done.w2.rest_6_ = bf16[192,2304]{1,0:T(8,128)(2,1)S(1)} collective-permute-done((bf16[192,2304]{1,0:T(8,128)(2,1)S(1)}, bf16[192,2304]{1,0:T(8,128)(2,1)S(1)}, u32[]{:S(2)}, u32[]{:S(2)}) %collective-permute-start) | collective-permute-done | bytes 884768 | tf_op jit(solution)/shard_map/ppermute | solution.py:30
  35.4 5.9 collective-permute-done.13.w2
  57.2 5.8 shard_map.204
  69.4 8.6 collective-permute-done.6.refs_1_
  79.6 8.6 collective-permute-done.7.refs_2_
  98.9 7.4 all-to-all-start
  109.6 15.0 %shard_map.205 = (bf16[2,192,128]{2,1,0:T(8,128)(2,1)}, bf16[2,192,128]{2,1,0:T(8,128)(2,1)}, bf16[2,192,128]{2,1,0:T(8,128)(2,1)}, bf16[2,192,128]{2,1,0:T(8,12...) custom-call(s32[22]{0:T(128)} %concatenate.51.meta, bf16[2,3,192,128]{3,2,1,0:T(8,128)(2,1)} %get-tuple-element.280.refs_0_, ...), custom_call_target="tpu_custom_call" | custom-call | flops 1610612736 | bytes 3551232 | tf_op jit(solution)/shard_map/pallas_call | solution.py:91
  126.9 5.2 collective-permute-start.18
  134.7 5.5 collective-permute-start.15
  140.2 9.2 collective-permute-done.15.o2
  150.6 5.4 collective-permute-done.16.o3
  156.1 11.7 %collective-permute-done.18.w2 = bf16[192,768]{1,0:T(8,128)(2,1)S(1)} collective-permute-done((bf16[192,768]{1,0:T(8,128)(2,1)S(1)}, bf16[192,768]{1,0:T(8,128)(2,1)S(1)}, u32[]{:S(2)}, u32[]{:S(2)}) %collective-permute-start.18) | collective-permute-done | bytes 294944 | tf_op jit(solution)/shard_map/ppermute | solution.py:30
  169.2 4.7 shard_map.206
  173.9 5.0 all-to-all-start.1
  179.5 10.4 %shard_map.207 = (f32[256,768]{1,0:T(8,128)}, f32[2,256,2048]{2,1,0:T(8,128)}, bf16[2,256,512]{2,1,0:T(8,128)(2,1)}, bf16[2,256,512]{2,1,0:T(8,128)(2,1)}) custom-call(s32[22]{0:T(128)} %concatenate.51.meta, f32[256,768]{1,0:T(8,128)} %get-tuple-element.302.x, bf16[4,256,192]{2,1,0:T(8,128)(2,1)} %get-tuple-element.303.blocks, bf16[768,4096]{1,0:T(8,128)(2,1)} %bitcast.128, ...), custom_call_target="tpu_custom_call" | custom-call | flops 2415919104 | bytes 70123520 | tf_op jit(solution)/shard_map/pallas_call | solution.py:91
  189.9 6.0 shard_map.208
  201.6 9.6 %collective-permute-done.23.refs_1_ = bf16[2,3,192,128]{3,2,1,0:T(8,128)(2,1)S(1)} collective-permute-done((bf16[2,3,192,128]{3,2,1,0:T(8,128)(2,1)}, bf16[2,3,192,128]{3,2,1,0:T(8,128)(2,1)S(1)}, u32[]{:S(2)}, u32[]{:S(2)}) %collective-permute-start.23) | collective-permute-done | bytes 294944 | tf_op jit(solution)/shard_map/ppermute | solution.py:30
  212.6 8.3 collective-permute-done.24.refs_2_
  223.0 6.5 collective-permute-done.28.refs_6_
  235.0 14.7 %shard_map.209 = (bf16[2,192,128]{2,1,0:T(8,128)(2,1)}, bf16[2,192,128]{2,1,0:T(8,128)(2,1)}, bf16[2,192,128]{2,1,0:T(8,128)(2,1)}, bf16[2,192,128]{2,1,0:T(8,12...) custom-call(s32[22]{0:T(128)} %concatenate.51.meta, bf16[2,3,192,128]{3,2,1,0:T(8,128)(2,1)} %get-tuple-element.315.refs_0_, ...), custom_call_target="tpu_custom_call" | custom-call | flops 1610612736 | bytes 3551232 | tf_op jit(solution)/shard_map/pallas_call | solution.py:91
  255.6 10.9 %all-to-all-done.1.refs_6_ = bf16[4,3,192,1024]{3,2,1,0:T(8,128)(2,1)} async-done(((bf16[4,3,192,1024]{3,2,1,0:T(8,128)(2,1)}), bf16[4,3,192,1024]{3,2,1,0:T(8,128)(2,1)}, u32[]{:S(2)}, u32[]{:S(2)}) %all-to-all-start.1) | async-done | bytes 4718624 | tf_op jit(solution)/shard_map/all_to_all | solution.py:1075
  267.7 4.6 shard_map.210
  275.2 5.0 all-to-all-start.2
  280.4 10.5 %shard_map.211 = (f32[256,768]{1,0:T(8,128)}, f32[2,256,2048]{2,1,0:T(8,128)}, bf16[2,256,512]{2,1,0:T(8,128)(2,1)}, bf16[2,256,512]{2,1,0:T(8,128)(2,1)}) custom-call(s32[22]{0:T(128)} %concatenate.51.meta, f32[256,768]{1,0:T(8,128)} %get-tuple-element.342.x, bf16[4,256,192]{2,1,0:T(8,128)(2,1)} %get-tuple-element.343.blocks, bf16[768,4096]{1,0:T(8,128)(2,1)} %bitcast.144, ...), custom_call_target="tpu_custom_call" | custom-call | flops 2415919104 | bytes 70123520 | tf_op jit(solution)/shard_map/pallas_call | solution.py:91
  291.8 10.7 %shard_map.212 = (bf16[2,256,2048]{2,1,0:T(8,128)(2,1)}, f32[256,768]{1,0:T(8,128)}) custom-call(s32[22]{0:T(128)} %concatenate.51.meta, bf16[1,256,768]{2,1,0:T(8,128)(2,1)} %right.1, f32[2,256,2048]{2,1,0:T(8,128)} %get-tuple-element.346.mixed, bf16[768,4096]{1,0:T(8,128)(2,1)} %bitcast.152, bf16[768,4096]{1,0:T(8,128)(2,1)} %bitcast.153, ...), custom_call_target="tpu_custom_call" | custom-call | flops 2415919104 | bytes 70385664 | tf_op jit(solution)/shard_map/pallas_call | solution.py:91
  307.6 6.6 all-to-all-done.2
  317.7 33.8 %shard_map.214 = (bf16[1024,768]{1,0:T(8,128)(2,1)}, bf16[1024,768]{1,0:T(8,128)(2,1)}, bf16[1024,768]{1,0:T(8,128)(2,1)}, bf16[1024,768]{1,0:T(8,128)(2,1)}, bf...) custom-call(s32[1]{0:T(128)} %bitcast.40.meta, ...), custom_call_target="tpu_custom_call" | custom-call | flops 19327352832 | bytes 36388864 | tf_op jit(solution)/shard_map/pallas_call | solution.py:91
  359.3 7.5 all-to-all-start.3
  370.1 8.5 shard_map.215
  380.2 6.7 convolution_convert_fusion.2
  396.7 7.3 all-to-all-done.3
  407.5 4.8 shard_map.216
  412.7 5.3 collective-permute-start.46
  425.2 13.8 %collective-permute-done.51 = bf16[192,4096]{1,0:T(8,128)(2,1)} collective-permute-done((bf16[192,4096]{1,0:T(8,128)(2,1)}, bf16[192,4096]{1,0:T(8,128)(2,1)}, u32[]{:S(2)}, u32[]{:S(2)}) %collective-permute-start.51) | collective-permute-done | bytes 1572896 | tf_op jit(solution)/shard_map/ppermute | solution.py:30
  442.2 4.9 all-to-all-start.4
  447.6 18.4 %shard_map.218 = (bf16[8,192,128]{2,1,0:T(8,128)(2,1)}, f32[8,2,192,128]{3,2,1,0:T(8,128)}, bf16[8,2,192,128]{3,2,1,0:T(8,128)(2,1)}) custom-call(s32[22]{0:T(128)} %concatenate.51.meta, bf16[2,3,192,128]{3,2,1,0:T(8,128)(2,1)} %get-tuple-element.315.refs_0_, bf16[2,3,192,128]{3,2,1,0:T(8,128)(2,1)} %copy-done.101, bf16[2,3,192,128]{3,2,1,0:T(8,128)(2,1)} %copy-done.102, ...), custom_call_target="tpu_custom_call" | custom-call | flops 4026531840 | bytes 6303744 | tf_op jit(solution)/shard_map/pallas_call | solution.py:91
  466.0 6.6 collective-permute-start.52
  477.5 12.5 %collective-permute-done.52.rest_0_ = bf16[8,2,192,128]{3,2,1,0:T(8,128)(2,1)} collective-permute-done((bf16[8,2,192,128]{3,2,1,0:T(8,128)(2,1)}, bf16[8,2,192,128]{3,2,1,0:T(8,128)(2,1)}, u32[]{:S(2)}, u32[]{:S(2)}) %collective-permute-start.52) | collective-permute-done | bytes 786464 | tf_op jit(solution)/shard_map/ppermute | solution.py:30
  493.4 5.3 collective-permute-start.53
  502.6 4.6 collective-permute-done.57
  509.2 13.3 %collective-permute-done.54.rest_2_ = bf16[2,3,192,128]{3,2,1,0:T(8,128)(2,1)} collective-permute-done((bf16[2,3,192,128]{3,2,1,0:T(8,128)(2,1)}, bf16[2,3,192,128]{3,2,1,0:T(8,128)(2,1)}, u32[]{:S(2)}, u32[]{:S(2)}) %collective-permute-start.54) | collective-permute-done | bytes 294944 | tf_op jit(solution)/shard_map/ppermute | solution.py:30
  522.5 6.5 all-to-all-start.5
  529.5 7.0 shard_map.220
  538.4 10.9 %shard_map.221 = (bf16[2,256,2048]{2,1,0:T(8,128)(2,1)}, f32[256,768]{1,0:T(8,128)}) custom-call(s32[22]{0:T(128)} %concatenate.51.meta, bf16[1,256,768]{2,1,0:T(8,128)(2,1)} %convert_bitcast_fusion.1.branch.right, f32[2,256,2048]{2,1,0:T(8,128)} %get-tuple-element.424.mixed, bf16[768,4096]{1,0:T(8,128)(2,1)} %bitcast.136, bf16[768,4096]{1,0:T(8,128)(2,1)} %bitcast.137, ...), custom_call_target="tpu_custom_call" | custom-call | flops 2415919104 | bytes 70385664 | tf_op jit(solution)/shard_map/pallas_call | solution.py:91
  556.3 5.3 shard_map.222
  561.6 4.7 shard_map.223
  571.4 8.4 shard_map.224
  583.0 5.0 collective-permute-done.61.refs_10_
  607.6 18.7 %shard_map.225 = (bf16[8,192,128]{2,1,0:T(8,128)(2,1)}, f32[8,2,192,128]{3,2,1,0:T(8,128)}, bf16[8,2,192,128]{3,2,1,0:T(8,128)(2,1)}) custom-call(s32[22]{0:T(128)} %concatenate.51.meta, bf16[2,3,192,128]{3,2,1,0:T(8,128)(2,1)} %get-tuple-element.280.refs_0_, bf16[2,3,192,128]{3,2,1,0:T(8,128)(2,1)} %copy-done.95, bf16[2,3,192,128]{3,2,1,0:T(8,128)(2,1)} %copy-done.96, ...), custom_call_target="tpu_custom_call" | custom-call | flops 4026531840 | bytes 6303744 | tf_op jit(solution)/shard_map/pallas_call | solution.py:91
  626.4 5.8 collective-permute-start.65
  632.2 20.9 %collective-permute-done.70 = bf16[192,6400]{1,0:T(8,128)(2,1)} collective-permute-done((bf16[192,6400]{1,0:T(8,128)(2,1)}, bf16[192,6400]{1,0:T(8,128)(2,1)}, u32[]{:S(2)}, u32[]{:S(2)}) %collective-permute-start.70) | collective-permute-done | bytes 2457632 | tf_op jit(solution)/shard_map/ppermute | solution.py:30
  658.1 4.9 collective-permute-done.65.rest_0_
  674.2 17.1 %collective-permute-done.71.rest_1_ = bf16[2,3,192,128]{3,2,1,0:T(8,128)(2,1)S(1)} collective-permute-done((bf16[2,3,192,128]{3,2,1,0:T(8,128)(2,1)}, bf16[2,3,192,128]{3,2,1,0:T(8,128)(2,1)S(1)}, u32[]{:S(2)}, u32[]{:S(2)}) %collective-permute-start.71) | collective-permute-done | bytes 294944 | tf_op jit(solution)/shard_map/ppermute | solution.py:30
  691.3 12.4 %collective-permute-done.72.rest_2_ = bf16[2,3,192,128]{3,2,1,0:T(8,128)(2,1)S(1)} collective-permute-done((bf16[2,3,192,128]{3,2,1,0:T(8,128)(2,1)}, bf16[2,3,192,128]{3,2,1,0:T(8,128)(2,1)S(1)}, u32[]{:S(2)}, u32[]{:S(2)}) %collective-permute-start.72) | collective-permute-done | bytes 294944 | tf_op jit(solution)/shard_map/ppermute | solution.py:30
  708.7 7.1 shard_map.229
  723.4 9.2 collective-permute-done.88.second
  736.2 18.9 %collective-permute-start.89 = (bf16[128,384]{1,0:T(8,128)(2,1)}, bf16[128,384]{1,0:T(8,128)(2,1)S(1)}, u32[]{:S(2)}, u32[]{:S(2)}) collective-permute-start(bf16[128,384]{1,0:T(8,128)(2,1)} %get-tuple-element.502), channel_id=1, source_target_pairs={{0,8},{4,12},{8,0},{12,4},{16,24},{20,28},{24,16},{28,20},{1,9},{5... | collective-permute-start | bytes 294920 | tf_op jit(solution)/shard_map/ppermute | solution.py:30
  758.8 10.2 %collective-permute-done.90 = bf16[128,384]{1,0:T(8,128)(2,1)S(1)} collective-permute-done((bf16[128,384]{1,0:T(8,128)(2,1)}, bf16[128,384]{1,0:T(8,128)(2,1)S(1)}, u32[]{:S(2)}, u32[]{:S(2)}) %collective-permute-start.90) | collective-permute-done | bytes 98336 | tf_op jit(solution)/shard_map/ppermute | solution.py:30
  769.9 4.7 collective-permute-start.92
  775.3 5.2 shard_map.230
  791.4 24.2 %all-reduce.6.cloned.1.call-done = (bf16[192,768]{1,0:T(8,128)(2,1)}, bf16[192,2304]{1,0:T(8,128)(2,1)}, bf16[192,4096]{1,0:T(8,128)(2,1)}) async-done(((bf16[192,768]{1,0:T(8,128)(2,1)}, bf16[192,2304]{1,0:T(8,128)(2,1)}, bf16[192,4096]{1,0:T(8,128)(2,1)}), (bf16[192,768]{1,0:T(8,128)(2,1)}, bf16[192,2304]{1,0:T(8,128)(2,1)}, bf16[192,4096]{1,0:T(8,128)(2,1)})) %all-reduce.6.cloned.1.call-update) | async-done | bytes 2752528 | tf_op jit(solution)/shard_map/psum | solution.py:924
  856.3 9.6 %collective-permute-done.79 = bf16[48,1536]{1,0:T(8,128)(2,1)S(1)} collective-permute-done((bf16[48,1536]{1,0:T(8,128)(2,1)}, bf16[48,1536]{1,0:T(8,128)(2,1)S(1)}, u32[]{:S(2)}, u32[]{:S(2)}) %collective-permute-start.79) | collective-permute-done | bytes 147488 | tf_op jit(solution)/shard_map/ppermute | solution.py:30
  880.9 4.4 copy.132
  905.7 4.9 shard_map.235
  (590 shorter events, 324.2 us)
Async XLA Ops:
  7.2 172.3 %all-gather.14.cloned.1.call-start = ((), (), s32[]{:S(2)}) async-start(), calls=%async_computation.9 | async-start | bytes 3932160 | tf_op jit(solution)/shard_map/all_gather | solution.py:975
  12.8 22.5 %collective-permute-start = (bf16[192,2304]{1,0:T(8,128)(2,1)S(1)}, bf16[192,2304]{1,0:T(8,128)(2,1)S(1)}, u32[]{:S(2)}, u32[]{:S(2)}) collective-permute-start(bf16[192,2304]{1,0:T(8,128)(2,1)S(1)} %slice_bitcast_fusion.3.w0.rest_4_), channel_id=1, source_target_pairs={{0,2},{1,3},{2,0},{3,1},{4,6},{5,7},{6,4},{7,5},{8,10},{9,11},{10,... | collective-permute-start | bytes 2654216 | tf_op jit(solution)/shard_map/ppermute | solution.py:30
  14.1 27.1 %collective-permute-start.13 = (bf16[192,768]{1,0:T(8,128)(2,1)S(1)}, bf16[192,768]{1,0:T(8,128)(2,1)S(1)}, u32[]{:S(2)}, u32[]{:S(2)}) collective-permute-start(bf16[192,768]{1,0:T(8,128)(2,1)S(1)} %slice_bitcast_fusion.5.w0), channel_id=1, source_target_pairs={{0,2},{1,3},{2,0},{3,1},{4,6},{5,7},{6,4},{7,5},{8,10},{9,11},{10,... | collective-permute-start | bytes 884744 | tf_op jit(solution)/shard_map/ppermute | solution.py:30
  44.0 135.4 %all-gather.12.cloned.1.call-start = ((), (), s32[]{:S(2)}) async-start(), calls=%async_computation.8 | async-start | bytes 7864320 | tf_op jit(solution)/shard_map/all_gather | solution.py:975
  48.0 232.3 %all-gather.18.cloned.1.call-start = ((), (), s32[]{:S(2)}) async-start(), calls=%async_computation.11 | async-start | bytes 3932160 | tf_op jit(solution)/shard_map/all_gather | solution.py:975
  48.8 231.6 %all-gather.16.cloned.1.call-start = ((), (), s32[]{:S(2)}) async-start(), calls=%async_computation.10 | async-start | bytes 7864320 | tf_op jit(solution)/shard_map/all_gather | solution.py:975
  64.6 23.6 %collective-permute-start.7 = (bf16[2,3,192,128]{3,2,1,0:T(8,128)(2,1)}, bf16[2,3,192,128]{3,2,1,0:T(8,128)(2,1)S(1)}, u32[]{:S(2)}, u32[]{:S(2)}) collective-permute-start(bf16[2,3,192,128]{3,2,1,0:T(8,128)(2,1)} %get-tuple-element.276), channel_id=1, source_target_pairs={{0,16},{4,20},{8,24},{12,28},{16,0},{20,4},{24,8},{28,12},{1,17},{... | collective-permute-start | bytes 884744 | tf_op jit(solution)/shard_map/ppermute | solution.py:30
  67.2 22.5 %collective-permute-start.8 = (bf16[2,3,192,128]{3,2,1,0:T(8,128)(2,1)}, bf16[2,3,192,128]{3,2,1,0:T(8,128)(2,1)S(1)}, u32[]{:S(2)}, u32[]{:S(2)}) collective-permute-start(bf16[2,3,192,128]{3,2,1,0:T(8,128)(2,1)} %get-tuple-element.277), channel_id=1, source_target_pairs={{0,24},{4,28},{8,16},{12,20},{16,8},{20,12},{24,0},{28,4},{1,25},{... | collective-permute-start | bytes 884744 | tf_op jit(solution)/shard_map/ppermute | solution.py:30
  67.9 24.4 %collective-permute-start.9 = (bf16[2,3,192,128]{3,2,1,0:T(8,128)(2,1)}, bf16[2,3,192,128]{3,2,1,0:T(8,128)(2,1)S(1)}, u32[]{:S(2)}, u32[]{:S(2)}) collective-permute-start(bf16[2,3,192,128]{3,2,1,0:T(8,128)(2,1)} %get-tuple-element.280.refs_0_), channel_id=1, source_target_pairs={{0,4},{4,0},{8,12},{12,8},{16,20},{20,16},{24,28},{28,24},{1,5},{5... | collective-permute-start | bytes 884744 | tf_op jit(solution)/shard_map/ppermute | solution.py:30
  98.9 75.0 %all-to-all-start = ((bf16[16,72,768]{2,1,0:T(8,128)(2,1)}), bf16[16,72,768]{2,1,0:T(8,128)(2,1)S(1)}, u32[]{:S(2)}, u32[]{:S(2)}) async-start(bf16[16,72,768]{2,1,0:T(8,128)(2,1)} %fusion.2), calls=%async_computation | async-start | bytes 3538944 | tf_op jit(solution)/shard_map/all_to_all | solution.py:963
  107.6 60.2 %collective-permute-start.17 = (bf16[192,2304]{1,0:T(8,128)(2,1)S(1)}, bf16[192,2304]{1,0:T(8,128)(2,1)}, u32[]{:S(2)}, u32[]{:S(2)}) collective-permute-start(bf16[192,2304]{1,0:T(8,128)(2,1)S(1)} %slice_bitcast_fusion.2.w0.rest_4_), channel_id=1, source_target_pairs={{0,2},{1,3},{2,0},{3,1},{4,6},{5,7},{6,4},{7,5},{8,10},{9,11},{10,... | collective-permute-start | bytes 2654216 | tf_op jit(solution)/shard_map/ppermute | solution.py:30
  126.9 40.8 %collective-permute-start.18 = (bf16[192,768]{1,0:T(8,128)(2,1)S(1)}, bf16[192,768]{1,0:T(8,128)(2,1)S(1)}, u32[]{:S(2)}, u32[]{:S(2)}) collective-permute-start(bf16[192,768]{1,0:T(8,128)(2,1)S(1)} %slice_bitcast_fusion.4.w0), channel_id=1, source_target_pairs={{0,2},{1,3},{2,0},{3,1},{4,6},{5,7},{6,4},{7,5},{8,10},{9,11},{10,... | collective-permute-start | bytes 884744 | tf_op jit(solution)/shard_map/ppermute | solution.py:30
  132.2 35.6 %collective-permute-start.19 = (bf16[192,768]{1,0:T(8,128)(2,1)S(1)}, bf16[192,768]{1,0:T(8,128)(2,1)S(1)}, u32[]{:S(2)}, u32[]{:S(2)}) collective-permute-start(bf16[192,768]{1,0:T(8,128)(2,1)S(1)} %slice_bitcast_fusion.5.w0), channel_id=1, source_target_pairs={{0,1},{1,0},{2,3},{3,2},{4,5},{5,4},{6,7},{7,6},{8,9},{9,8},{10,11... | collective-permute-start | bytes 884744 | tf_op jit(solution)/shard_map/ppermute | solution.py:30
  132.2 37.0 %collective-permute-start.20 = (bf16[192,768]{1,0:T(8,128)(2,1)S(1)}, bf16[192,768]{1,0:T(8,128)(2,1)}, u32[]{:S(2)}, u32[]{:S(2)}) collective-permute-start(bf16[192,768]{1,0:T(8,128)(2,1)S(1)} %copy-done.18), channel_id=1, source_target_pairs={{0,1},{1,0},{2,3},{3,2},{4,5},{5,4},{6,7},{7,6},{8,9},{9,8},{10,11... | collective-permute-start | bytes 884744 | tf_op jit(solution)/shard_map/ppermute | solution.py:30
  173.9 92.5 %all-to-all-start.1 = ((bf16[4,3,192,1024]{3,2,1,0:T(8,128)(2,1)}), bf16[4,3,192,1024]{3,2,1,0:T(8,128)(2,1)}, u32[]{:S(2)}, u32[]{:S(2)}) async-start(bf16[4,3,192,1024]{3,2,1,0:T(8,128)(2,1)} %pad_maximum_fusion), calls=%async_computation.1 | async-start | bytes 9437184 | tf_op jit(solution)/shard_map/all_to_all | solution.py:1075
  197.3 23.6 %collective-permute-start.24 = (bf16[2,3,192,128]{3,2,1,0:T(8,128)(2,1)}, bf16[2,3,192,128]{3,2,1,0:T(8,128)(2,1)S(1)}, u32[]{:S(2)}, u32[]{:S(2)}) collective-permute-start(bf16[2,3,192,128]{3,2,1,0:T(8,128)(2,1)} %get-tuple-element.312), channel_id=1, source_target_pairs={{0,16},{4,20},{8,24},{12,28},{16,0},{20,4},{24,8},{28,12},{1,17},{... | collective-permute-start | bytes 884744 | tf_op jit(solution)/shard_map/ppermute | solution.py:30
  199.2 23.2 %collective-permute-start.25 = (bf16[2,3,192,128]{3,2,1,0:T(8,128)(2,1)}, bf16[2,3,192,128]{3,2,1,0:T(8,128)(2,1)S(1)}, u32[]{:S(2)}, u32[]{:S(2)}) collective-permute-start(bf16[2,3,192,128]{3,2,1,0:T(8,128)(2,1)} %get-tuple-element.313), channel_id=1, source_target_pairs={{0,24},{4,28},{8,16},{12,20},{16,8},{20,12},{24,0},{28,4},{1,25},{... | collective-permute-start | bytes 884744 | tf_op jit(solution)/shard_map/ppermute | solution.py:30
  200.3 22.7 %collective-permute-start.26 = (bf16[2,3,192,128]{3,2,1,0:T(8,128)(2,1)}, bf16[2,3,192,128]{3,2,1,0:T(8,128)(2,1)S(1)}, u32[]{:S(2)}, u32[]{:S(2)}) collective-permute-start(bf16[2,3,192,128]{3,2,1,0:T(8,128)(2,1)} %get-tuple-element.315.refs_0_), channel_id=1, source_target_pairs={{0,4},{4,0},{8,12},{12,8},{16,20},{20,16},{24,28},{28,24},{1,5},{5... | collective-permute-start | bytes 884744 | tf_op jit(solution)/shard_map/ppermute | solution.py:30
  234.0 16.4 %collective-permute-start.30 = (bf16[1024,768]{1,0:T(8,128)(2,1)}, bf16[1024,768]{1,0:T(8,128)(2,1)}, u32[]{:S(2)}, u32[]{:S(2)}) collective-permute-start(bf16[1024,768]{1,0:T(8,128)(2,1)} %bitcast.34.refs_2_), channel_id=1, source_target_pairs={{0,1},{1,0},{2,3},{3,2},{4,5},{5,4},{6,7},{7,6},{8,9},{9,8},{10,11... | collective-permute-start | bytes 4718600 | tf_op jit(solution)/shard_map/ppermute | solution.py:30
  234.0 21.6 %collective-permute-start.35 = (bf16[192,768]{1,0:T(8,128)(2,1)S(1)}, bf16[192,768]{1,0:T(8,128)(2,1)S(1)}, u32[]{:S(2)}, u32[]{:S(2)}) collective-permute-start(bf16[192,768]{1,0:T(8,128)(2,1)S(1)} %slice_bitcast_fusion.4.w0), channel_id=1, source_target_pairs={{0,1},{1,0},{2,3},{3,2},{4,5},{5,4},{6,7},{7,6},{8,9},{9,8},{10,11... | collective-permute-start | bytes 884744 | tf_op jit(solution)/shard_map/ppermute | solution.py:30
  234.5 21.1 %collective-permute-start.36 = (bf16[192,768]{1,0:T(8,128)(2,1)S(1)}, bf16[192,768]{1,0:T(8,128)(2,1)S(1)}, u32[]{:S(2)}, u32[]{:S(2)}) collective-permute-start(bf16[192,768]{1,0:T(8,128)(2,1)S(1)} %copy-done.21), channel_id=1, source_target_pairs={{0,1},{1,0},{2,3},{3,2},{4,5},{5,4},{6,7},{7,6},{8,9},{9,8},{10,11... | collective-permute-start | bytes 884744 | tf_op jit(solution)/shard_map/ppermute | solution.py:30
  275.2 39.0 %all-to-all-start.2 = ((bf16[16,64,768]{2,1,0:T(8,128)(2,1)}), bf16[16,64,768]{2,1,0:T(8,128)(2,1)S(1)}, u32[]{:S(2)}, u32[]{:S(2)}) async-start(bf16[16,64,768]{2,1,0:T(8,128)(2,1)} %bitcast.196), calls=%async_computation.2 | async-start | bytes 3145728 | tf_op jit(solution)/shard_map/all_to_all | solution.py:963
  280.2 22.4 %collective-permute-start.38 = (bf16[1,256,768]{2,1,0:T(8,128)(2,1)S(1)}, bf16[1,256,768]{2,1,0:T(8,128)(2,1)}, u32[]{:S(2)}, u32[]{:S(2)}) collective-permute-start(bf16[1,256,768]{2,1,0:T(8,128)(2,1)S(1)} %copy-done.8), channel_id=1, source_target_pairs={{0,1},{1,0},{2,3},{3,2},{4,5},{5,4},{6,7},{7,6},{8,9},{9,8},{10,11... | collective-permute-start | bytes 1179656 | tf_op jit(solution)/shard_map/ppermute | solution.py:30
  351.8 17.6 %collective-permute-start.44 = (bf16[2,256,2048]{2,1,0:T(8,128)(2,1)}, bf16[2,256,2048]{2,1,0:T(8,128)(2,1)}, u32[]{:S(2)}, u32[]{:S(2)}) collective-permute-start(bf16[2,256,2048]{2,1,0:T(8,128)(2,1)} %get-tuple-element.379.right), channel_id=1, source_target_pairs={{0,1},{1,0},{2,3},{3,2},{4,5},{5,4},{6,7},{7,6},{8,9},{9,8},{10,11... | collective-permute-start | bytes 6291464 | tf_op jit(solution)/shard_map/ppermute | solution.py:30
  353.9 24.7 %collective-permute-start.45 = (bf16[512,768]{1,0:T(8,128)(2,1)S(1)}, bf16[512,768]{1,0:T(8,128)(2,1)}, u32[]{:S(2)}, u32[]{:S(2)}) collective-permute-start(bf16[512,768]{1,0:T(8,128)(2,1)S(1)} %copy-done.90), channel_id=1, source_target_pairs={{0,2},{1,3},{2,0},{3,1},{4,6},{5,7},{6,4},{7,5},{8,10},{9,11},{10,... | collective-permute-start | bytes 2359304 | tf_op jit(solution)/shard_map/ppermute | solution.py:30
  359.3 44.7 %all-to-all-start.3 = ((bf16[16,72,768]{2,1,0:T(8,128)(2,1)}), bf16[16,72,768]{2,1,0:T(8,128)(2,1)S(1)}, u32[]{:S(2)}, u32[]{:S(2)}) async-start(bf16[16,72,768]{2,1,0:T(8,128)(2,1)} %fusion.3), calls=%async_computation.3 | async-start | bytes 3538944 | tf_op jit(solution)/shard_map/all_to_all | solution.py:963
  404.1 35.0 %collective-permute-start.51 = (bf16[192,4096]{1,0:T(8,128)(2,1)}, bf16[192,4096]{1,0:T(8,128)(2,1)}, u32[]{:S(2)}, u32[]{:S(2)}) collective-permute-start(bf16[192,4096]{1,0:T(8,128)(2,1)} %get-tuple-element.397), channel_id=1, source_target_pairs={{0,2},{1,3},{2,0},{3,1},{4,6},{5,7},{6,4},{7,5},{8,10},{9,11},{10,... | collective-permute-start | bytes 4718600 | tf_op jit(solution)/shard_map/ppermute | solution.py:30
  412.7 28.7 %collective-permute-start.46 = (bf16[2,192,128]{2,1,0:T(8,128)(2,1)}, bf16[2,192,128]{2,1,0:T(8,128)(2,1)S(1)}, u32[]{:S(2)}, u32[]{:S(2)}) collective-permute-start(bf16[2,192,128]{2,1,0:T(8,128)(2,1)} %get-tuple-element.387), channel_id=1, source_target_pairs={{0,8},{4,12},{8,0},{12,4},{16,24},{20,28},{24,16},{28,20},{1,9},{5... | collective-permute-start | bytes 294920 | tf_op jit(solution)/shard_map/ppermute | solution.py:30
  418.0 23.5 %collective-permute-start.47 = (bf16[2,192,128]{2,1,0:T(8,128)(2,1)}, bf16[2,192,128]{2,1,0:T(8,128)(2,1)S(1)}, u32[]{:S(2)}, u32[]{:S(2)}) collective-permute-start(bf16[2,192,128]{2,1,0:T(8,128)(2,1)} %get-tuple-element.388), channel_id=1, source_target_pairs={{0,16},{4,20},{8,24},{12,28},{16,0},{20,4},{24,8},{28,12},{1,17},{... | collective-permute-start | bytes 294920 | tf_op jit(solution)/shard_map/ppermute | solution.py:30
  419.6 21.9 %collective-permute-start.48 = (bf16[2,192,128]{2,1,0:T(8,128)(2,1)}, bf16[2,192,128]{2,1,0:T(8,128)(2,1)S(1)}, u32[]{:S(2)}, u32[]{:S(2)}) collective-permute-start(bf16[2,192,128]{2,1,0:T(8,128)(2,1)} %get-tuple-element.389), channel_id=1, source_target_pairs={{0,24},{4,28},{8,16},{12,20},{16,8},{20,12},{24,0},{28,4},{1,25},{... | collective-permute-start | bytes 294920 | tf_op jit(solution)/shard_map/ppermute | solution.py:30
  442.2 80.3 %all-to-all-start.4 = ((bf16[4,3,192,1024]{3,2,1,0:T(8,128)(2,1)}), bf16[4,3,192,1024]{3,2,1,0:T(8,128)(2,1)}, u32[]{:S(2)}, u32[]{:S(2)}) async-start(bf16[4,3,192,1024]{3,2,1,0:T(8,128)(2,1)} %pad_maximum_fusion.1), calls=%async_computation.4 | async-start | bytes 9437184 | tf_op jit(solution)/shard_map/all_to_all | solution.py:1198
  447.1 25.5 %collective-permute-start.56 = (bf16[1024,768]{1,0:T(8,128)(2,1)}, bf16[1024,768]{1,0:T(8,128)(2,1)}, u32[]{:S(2)}, u32[]{:S(2)}) collective-permute-start(bf16[1024,768]{1,0:T(8,128)(2,1)} %get-tuple-element.413), channel_id=1, source_target_pairs={{0,1},{1,0},{2,3},{3,2},{4,5},{5,4},{6,7},{7,6},{8,9},{9,8},{10,11... | collective-permute-start | bytes 4718600 | tf_op jit(solution)/shard_map/ppermute | solution.py:30
  466.0 23.9 %collective-permute-start.52 = (bf16[8,2,192,128]{3,2,1,0:T(8,128)(2,1)}, bf16[8,2,192,128]{3,2,1,0:T(8,128)(2,1)}, u32[]{:S(2)}, u32[]{:S(2)}) collective-permute-start(bf16[8,2,192,128]{3,2,1,0:T(8,128)(2,1)} %get-tuple-element.407), channel_id=1, source_target_pairs={{0,4},{4,0},{8,12},{12,8},{16,20},{20,16},{24,28},{28,24},{1,5},{5... | collective-permute-start | bytes 2359304 | tf_op jit(solution)/shard_map/ppermute | solution.py:30
  476.0 31.3 %collective-permute-start.57 = (bf16[192,768]{1,0:T(8,128)(2,1)}, bf16[192,768]{1,0:T(8,128)(2,1)}, u32[]{:S(2)}, u32[]{:S(2)}) collective-permute-start(bf16[192,768]{1,0:T(8,128)(2,1)} %get-tuple-element.418), channel_id=1, source_target_pairs={{0,2},{1,3},{2,0},{3,1},{4,6},{5,7},{6,4},{7,5},{8,10},{9,11},{10,... | collective-permute-start | bytes 884744 | tf_op jit(solution)/shard_map/ppermute | solution.py:30
  498.7 23.8 %collective-permute-start.54 = (bf16[2,3,192,128]{3,2,1,0:T(8,128)(2,1)}, bf16[2,3,192,128]{3,2,1,0:T(8,128)(2,1)}, u32[]{:S(2)}, u32[]{:S(2)}) collective-permute-start(bf16[2,3,192,128]{3,2,1,0:T(8,128)(2,1)} %get-tuple-element.410), channel_id=1, source_target_pairs={{0,16},{4,20},{8,24},{12,28},{16,0},{20,4},{24,8},{28,12},{1,17},{... | collective-permute-start | bytes 884744 | tf_op jit(solution)/shard_map/ppermute | solution.py:30
  500.3 22.3 %collective-permute-start.55 = (bf16[2,3,192,128]{3,2,1,0:T(8,128)(2,1)}, bf16[2,3,192,128]{3,2,1,0:T(8,128)(2,1)}, u32[]{:S(2)}, u32[]{:S(2)}) collective-permute-start(bf16[2,3,192,128]{3,2,1,0:T(8,128)(2,1)} %get-tuple-element.411), channel_id=1, source_target_pairs={{0,24},{4,28},{8,16},{12,20},{16,8},{20,12},{24,0},{28,4},{1,25},{... | collective-permute-start | bytes 884744 | tf_op jit(solution)/shard_map/ppermute | solution.py:30
  522.5 66.2 %all-to-all-start.5 = ((bf16[8,24,6144]{2,1,0:T(8,128)(2,1)}), bf16[8,24,6144]{2,1,0:T(8,128)(2,1)S(1)}, u32[]{:S(2)}, u32[]{:S(2)}) async-start(bf16[8,24,6144]{2,1,0:T(8,128)(2,1)} %pad_maximum_fusion.3), calls=%async_computation.5 | async-start | bytes 4718592 | tf_op jit(solution)/shard_map/all_to_all | solution.py:1212
  529.0 179.7 %all-gather.10.cloned.1.call-start = ((), (), s32[]{:S(2)}) async-start(), calls=%async_computation.7 | async-start | bytes 2654208 | tf_op jit(solution)/shard_map/all_gather | solution.py:1235
  549.3 21.3 %collective-permute-start.64 = (bf16[2,256,2048]{2,1,0:T(8,128)(2,1)}, bf16[2,256,2048]{2,1,0:T(8,128)(2,1)}, u32[]{:S(2)}, u32[]{:S(2)}) collective-permute-start(bf16[2,256,2048]{2,1,0:T(8,128)(2,1)} %get-tuple-element.439.right), channel_id=1, source_target_pairs={{0,1},{1,0},{2,3},{3,2},{4,5},{5,4},{6,7},{7,6},{8,9},{9,8},{10,11... | collective-permute-start | bytes 6291464 | tf_op jit(solution)/shard_map/ppermute | solution.py:30
  550.0 20.7 %collective-permute-start.63 = (bf16[2,256,192]{2,1,0:T(8,128)(2,1)S(1)}, bf16[2,256,192]{2,1,0:T(8,128)(2,1)S(1)}, u32[]{:S(2)}, u32[]{:S(2)}) collective-permute-start(bf16[2,256,192]{2,1,0:T(8,128)(2,1)S(1)} %copy-done.107), channel_id=1, source_target_pairs={{0,1},{1,0},{2,3},{3,2},{4,5},{5,4},{6,7},{7,6},{8,9},{9,8},{10,11... | collective-permute-start | bytes 589832 | tf_op jit(solution)/shard_map/ppermute | solution.py:30
  566.2 16.8 %collective-permute-start.60 = (bf16[2,192,128]{2,1,0:T(8,128)(2,1)}, bf16[2,192,128]{2,1,0:T(8,128)(2,1)S(1)}, u32[]{:S(2)}, u32[]{:S(2)}) collective-permute-start(bf16[2,192,128]{2,1,0:T(8,128)(2,1)} %get-tuple-element.434), channel_id=1, source_target_pairs={{0,8},{4,12},{8,0},{12,4},{16,24},{20,28},{24,16},{28,20},{1,9},{5... | collective-permute-start | bytes 294920 | tf_op jit(solution)/shard_map/ppermute | solution.py:30
  568.2 19.8 %collective-permute-start.61 = (bf16[2,192,128]{2,1,0:T(8,128)(2,1)}, bf16[2,192,128]{2,1,0:T(8,128)(2,1)S(1)}, u32[]{:S(2)}, u32[]{:S(2)}) collective-permute-start(bf16[2,192,128]{2,1,0:T(8,128)(2,1)} %get-tuple-element.435), channel_id=1, source_target_pairs={{0,16},{4,20},{8,24},{12,28},{16,0},{20,4},{24,8},{28,12},{1,17},{... | collective-permute-start | bytes 294920 | tf_op jit(solution)/shard_map/ppermute | solution.py:30
  570.6 18.1 %collective-permute-start.62 = (bf16[2,192,128]{2,1,0:T(8,128)(2,1)}, bf16[2,192,128]{2,1,0:T(8,128)(2,1)}, u32[]{:S(2)}, u32[]{:S(2)}) collective-permute-start(bf16[2,192,128]{2,1,0:T(8,128)(2,1)} %get-tuple-element.436), channel_id=1, source_target_pairs={{0,24},{4,28},{8,16},{12,20},{16,8},{20,12},{24,0},{28,4},{1,25},{... | collective-permute-start | bytes 294920 | tf_op jit(solution)/shard_map/ppermute | solution.py:30
  588.7 64.5 %collective-permute-start.70 = (bf16[192,6400]{1,0:T(8,128)(2,1)}, bf16[192,6400]{1,0:T(8,128)(2,1)}, u32[]{:S(2)}, u32[]{:S(2)}) collective-permute-start(bf16[192,6400]{1,0:T(8,128)(2,1)} %pad_maximum_fusion.2), channel_id=1, source_target_pairs={{0,2},{1,3},{2,0},{3,1},{4,6},{5,7},{6,4},{7,5},{8,10},{9,11},{10,... | collective-permute-start | bytes 7372808 | tf_op jit(solution)/shard_map/ppermute | solution.py:30
  602.7 106.1 %all-to-all-start.6 = ((bf16[16,64,768]{2,1,0:T(8,128)(2,1)}), bf16[16,64,768]{2,1,0:T(8,128)(2,1)S(1)}, u32[]{:S(2)}, u32[]{:S(2)}) async-start(bf16[16,64,768]{2,1,0:T(8,128)(2,1)} %bitcast.57), calls=%async_computation.6 | async-start | bytes 3145728 | tf_op jit(solution)/shard_map/all_to_all | solution.py:963
  606.5 209.0 %all-reduce.6.cloned.1.call-start = ((), (), s32[]{:S(2)}) async-start(), calls=%async_computation.12 | async-start | bytes 5505024 | tf_op jit(solution)/shard_map/psum | solution.py:924
  626.4 36.6 %collective-permute-start.65 = (bf16[8,2,192,128]{3,2,1,0:T(8,128)(2,1)}, bf16[8,2,192,128]{3,2,1,0:T(8,128)(2,1)}, u32[]{:S(2)}, u32[]{:S(2)}) collective-permute-start(bf16[8,2,192,128]{3,2,1,0:T(8,128)(2,1)} %get-tuple-element.452), channel_id=1, source_target_pairs={{0,4},{4,0},{8,12},{12,8},{16,20},{20,16},{24,28},{28,24},{1,5},{5... | collective-permute-start | bytes 2359304 | tf_op jit(solution)/shard_map/ppermute | solution.py:30
  663.0 53.4 %collective-permute-start.76 = (bf16[704,768]{1,0:T(8,128)(2,1)}, bf16[704,768]{1,0:T(8,128)(2,1)S(1)}, u32[]{:S(2)}, u32[]{:S(2)}) collective-permute-start(bf16[704,768]{1,0:T(8,128)(2,1)} %pad_maximum_fusion.8), channel_id=1, source_target_pairs={{0,2},{1,3},{2,0},{3,1},{4,6},{5,7},{6,4},{7,5},{8,10},{9,11},{10,... | collective-permute-start | bytes 3244040 | tf_op jit(solution)/shard_map/ppermute | solution.py:30
  667.4 23.9 %collective-permute-start.71 = (bf16[2,3,192,128]{3,2,1,0:T(8,128)(2,1)}, bf16[2,3,192,128]{3,2,1,0:T(8,128)(2,1)S(1)}, u32[]{:S(2)}, u32[]{:S(2)}) collective-permute-start(bf16[2,3,192,128]{3,2,1,0:T(8,128)(2,1)} %get-tuple-element.465), channel_id=1, source_target_pairs={{0,8},{4,12},{8,0},{12,4},{16,24},{20,28},{24,16},{28,20},{1,9},{5... | collective-permute-start | bytes 884744 | tf_op jit(solution)/shard_map/ppermute | solution.py:30
  671.5 32.3 %collective-permute-start.72 = (bf16[2,3,192,128]{3,2,1,0:T(8,128)(2,1)}, bf16[2,3,192,128]{3,2,1,0:T(8,128)(2,1)S(1)}, u32[]{:S(2)}, u32[]{:S(2)}) collective-permute-start(bf16[2,3,192,128]{3,2,1,0:T(8,128)(2,1)} %get-tuple-element.466), channel_id=1, source_target_pairs={{0,16},{4,20},{8,24},{12,28},{16,0},{20,4},{24,8},{28,12},{1,17},{... | collective-permute-start | bytes 884744 | tf_op jit(solution)/shard_map/ppermute | solution.py:30
  672.8 36.0 %collective-permute-start.73 = (bf16[2,3,192,128]{3,2,1,0:T(8,128)(2,1)}, bf16[2,3,192,128]{3,2,1,0:T(8,128)(2,1)}, u32[]{:S(2)}, u32[]{:S(2)}) collective-permute-start(bf16[2,3,192,128]{3,2,1,0:T(8,128)(2,1)} %get-tuple-element.467), channel_id=1, source_target_pairs={{0,24},{4,28},{8,16},{12,20},{16,8},{20,12},{24,0},{28,4},{1,25},{... | collective-permute-start | bytes 884744 | tf_op jit(solution)/shard_map/ppermute | solution.py:30
  715.8 58.8 %collective-permute-start.74 = (bf16[1,256,2304]{2,1,0:T(8,128)(2,1)}, bf16[1,256,2304]{2,1,0:T(8,128)(2,1)}, u32[]{:S(2)}, u32[]{:S(2)}) collective-permute-start(bf16[1,256,2304]{2,1,0:T(8,128)(2,1)} %get-tuple-element.474.right), channel_id=1, source_target_pairs={{0,1},{1,0},{2,3},{3,2},{4,5},{5,4},{6,7},{7,6},{8,9},{9,8},{10,11... | collective-permute-start | bytes 3538952 | tf_op jit(solution)/shard_map/ppermute | solution.py:30
  722.6 52.0 %collective-permute-start.39 = (bf16[2,256,192]{2,1,0:T(8,128)(2,1)}, bf16[2,256,192]{2,1,0:T(8,128)(2,1)S(1)}, u32[]{:S(2)}, u32[]{:S(2)}) collective-permute-start(bf16[2,256,192]{2,1,0:T(8,128)(2,1)} %get-tuple-element.354), channel_id=1, source_target_pairs={{0,1},{1,0},{2,3},{3,2},{4,5},{5,4},{6,7},{7,6},{8,9},{9,8},{10,11... | collective-permute-start | bytes 589832 | tf_op jit(solution)/shard_map/ppermute | solution.py:30
  736.2 22.6 %collective-permute-start.89 = (bf16[128,384]{1,0:T(8,128)(2,1)}, bf16[128,384]{1,0:T(8,128)(2,1)S(1)}, u32[]{:S(2)}, u32[]{:S(2)}) collective-permute-start(bf16[128,384]{1,0:T(8,128)(2,1)} %get-tuple-element.502), channel_id=1, source_target_pairs={{0,8},{4,12},{8,0},{12,4},{16,24},{20,28},{24,16},{28,20},{1,9},{5... | collective-permute-start | bytes 294920 | tf_op jit(solution)/shard_map/ppermute | solution.py:30
  769.9 98.1 %collective-permute-start.92 = (bf16[128,384]{1,0:T(8,128)(2,1)S(1)}, bf16[128,384]{1,0:T(8,128)(2,1)}, u32[]{:S(2)}, u32[]{:S(2)}) collective-permute-start(bf16[128,384]{1,0:T(8,128)(2,1)S(1)} %add_convert_fusion.3.refs_0_), channel_id=1, source_target_pairs={{0,8},{4,12},{8,0},{12,4},{16,24},{20,28},{24,16},{28,20},{1,9},{5... | collective-permute-start | bytes 294920 | tf_op jit(solution)/shard_map/ppermute | solution.py:30
  780.5 38.8 %collective-permute-start.75 = (bf16[192,2304]{1,0:T(8,128)(2,1)}, bf16[192,2304]{1,0:T(8,128)(2,1)}, u32[]{:S(2)}, u32[]{:S(2)}) collective-permute-start(bf16[192,2304]{1,0:T(8,128)(2,1)} %get-tuple-element.485), channel_id=1, source_target_pairs={{0,2},{1,3},{2,0},{3,1},{4,6},{5,7},{6,4},{7,5},{8,10},{9,11},{10,... | collective-permute-start | bytes 2654216 | tf_op jit(solution)/shard_map/ppermute | solution.py:30
  848.3 17.6 %collective-permute-start.79 = (bf16[48,1536]{1,0:T(8,128)(2,1)}, bf16[48,1536]{1,0:T(8,128)(2,1)S(1)}, u32[]{:S(2)}, u32[]{:S(2)}) collective-permute-start(bf16[48,1536]{1,0:T(8,128)(2,1)} %get-tuple-element.496), channel_id=1, source_target_pairs={{0,16},{4,20},{8,24},{12,28},{16,0},{20,4},{24,8},{28,12},{1,17},{... | collective-permute-start | bytes 442376 | tf_op jit(solution)/shard_map/ppermute | solution.py:30
  854.5 16.8 %collective-permute-start.93 = (bf16[128,384]{1,0:T(8,128)(2,1)S(1)}, bf16[128,384]{1,0:T(8,128)(2,1)S(1)}, u32[]{:S(2)}, u32[]{:S(2)}) collective-permute-start(bf16[128,384]{1,0:T(8,128)(2,1)S(1)} %add_convert_fusion.3.refs_0_), channel_id=1, source_target_pairs={{0,16},{4,20},{8,24},{12,28},{16,0},{20,4},{24,8},{28,12},{1,17},{... | collective-permute-start | bytes 294920 | tf_op jit(solution)/shard_map/ppermute | solution.py:30
  855.2 16.9 %collective-permute-start.94 = (bf16[128,384]{1,0:T(8,128)(2,1)S(1)}, bf16[128,384]{1,0:T(8,128)(2,1)S(1)}, u32[]{:S(2)}, u32[]{:S(2)}) collective-permute-start(bf16[128,384]{1,0:T(8,128)(2,1)S(1)} %add_convert_fusion.3.refs_0_), channel_id=1, source_target_pairs={{0,24},{4,28},{8,16},{12,20},{16,8},{20,12},{24,0},{28,4},{1,25},{... | collective-permute-start | bytes 294920 | tf_op jit(solution)/shard_map/ppermute | solution.py:30
  865.9 19.4 %collective-permute-start.95 = (bf16[128,384]{1,0:T(8,128)(2,1)S(1)}, bf16[128,384]{1,0:T(8,128)(2,1)S(1)}, u32[]{:S(2)}, u32[]{:S(2)}) collective-permute-start(bf16[128,384]{1,0:T(8,128)(2,1)S(1)} %add_convert_fusion.3.refs_0_), channel_id=1, source_target_pairs={{0,4},{4,0},{8,12},{12,8},{16,20},{20,16},{24,28},{28,24},{1,5},{5... | collective-permute-start | bytes 294920 | tf_op jit(solution)/shard_map/ppermute | solution.py:30
  866.5 19.4 %collective-permute-start.103 = (f32[20,768]{1,0:T(8,128)S(1)}, f32[20,768]{1,0:T(8,128)S(1)}, u32[]{:S(2)}, u32[]{:S(2)}) collective-permute-start(f32[20,768]{1,0:T(8,128)S(1)} %add.202), channel_id=1, source_target_pairs={{0,2},{1,3},{2,0},{3,1},{4,6},{5,7},{6,4},{7,5},{8,10},{9,11},{10,... | collective-permute-start | bytes 184328 | tf_op jit(solution)/shard_map/ppermute | solution.py:30
  868.0 25.6 %collective-permute-start.81 = (bf16[48,1536]{1,0:T(8,128)(2,1)S(1)}, bf16[48,1536]{1,0:T(8,128)(2,1)S(1)}, u32[]{:S(2)}, u32[]{:S(2)}) collective-permute-start(bf16[48,1536]{1,0:T(8,128)(2,1)S(1)} %add_convert_fusion.2.refs_0_), channel_id=1, source_target_pairs={{0,8},{4,12},{8,0},{12,4},{16,24},{20,28},{24,16},{28,20},{1,9},{5... | collective-permute-start | bytes 442376 | tf_op jit(solution)/shard_map/ppermute | solution.py:30
  871.3 24.0 %collective-permute-start.82 = (bf16[48,1536]{1,0:T(8,128)(2,1)S(1)}, bf16[48,1536]{1,0:T(8,128)(2,1)S(1)}, u32[]{:S(2)}, u32[]{:S(2)}) collective-permute-start(bf16[48,1536]{1,0:T(8,128)(2,1)S(1)} %add_convert_fusion.2.refs_0_), channel_id=1, source_target_pairs={{0,16},{4,20},{8,24},{12,28},{16,0},{20,4},{24,8},{28,12},{1,17},{... | collective-permute-start | bytes 442376 | tf_op jit(solution)/shard_map/ppermute | solution.py:30
  872.2 23.5 %collective-permute-start.83 = (bf16[48,1536]{1,0:T(8,128)(2,1)S(1)}, bf16[48,1536]{1,0:T(8,128)(2,1)S(1)}, u32[]{:S(2)}, u32[]{:S(2)}) collective-permute-start(bf16[48,1536]{1,0:T(8,128)(2,1)S(1)} %add_convert_fusion.2.refs_0_), channel_id=1, source_target_pairs={{0,24},{4,28},{8,16},{12,20},{16,8},{20,12},{24,0},{28,4},{1,25},{... | collective-permute-start | bytes 442376 | tf_op jit(solution)/shard_map/ppermute | solution.py:30
  (180 other events, 2379.7 us)
Sparse Core Ops, SparseCore 0:
  44.1 28.8 all-gather.13
  75.2 73.3 all-gather.11
  150.7 33.6 all-gather.17
  186.4 80.6 all-gather.15
  590.7 73.8 all-gather.9
  668.9 146.5 all-reduce.5

commit v7 on v5

--- a/solution.py
+++ b/solution.py
@@ -1061,21 +1061,21 @@
     far_in, far_out = swap(attn_in[1], "fsdp", 2), swap(attn_out[1], "fsdp", 2)
     grad_sent = dispatch(grad_sent)
     heads_one = exchange(heads_one)
-    heads_one, far_in, far_out = lax.optimization_barrier((heads_one, far_in, far_out))
+    after_one, _, blocks_one, keep_one, send_one, att_keep_one, att_send_one = post(
+        meta, resid_in, gains[1], heads_one, w_attn_out_one
+    )
+    after_one, grad_sent, expert_part = lax.optimization_barrier(
+        (after_one, grad_sent, expert_part)
+    )
+    expert_w = lax.all_to_all(expert_part, "fsdp", 0, 0, tiled=True)
+    middle, mixed_one, hid_keep_one, hid_send_one = mlp(
+        meta, after_one, blocks_one, w_mlp_in_one, w_mlp_out_one
+    )
+    middle, far_in, far_out = lax.optimization_barrier((middle, far_in, far_out))
     w_attn_in_two, w_attn_out_two = [
         (own, swap(own, "fsdp", 1), far, swap(far, "fsdp", 1))
         for own, far in ((attn_in[1], far_in), (attn_out[1], far_out))
     ]
-    after_one, _, blocks_one, keep_one, send_one, att_keep_one, att_send_one = post(
-        meta, resid_in, gains[1], heads_one, w_attn_out_one
-    )
-    after_one, grad_sent, expert_part = lax.optimization_barrier(
-        (after_one, grad_sent, expert_part)
-    )
-    expert_w = lax.all_to_all(expert_part, "fsdp", 0, 0, tiled=True)
-    middle, mixed_one, hid_keep_one, hid_send_one = mlp(
-        meta, after_one, blocks_one, w_mlp_in_one, w_mlp_out_one
-    )
     near_one = near(send_one, att_send_one, hid_send_one)
     heads_two, kept_two, grad_sent = attend_forward(
         meta, count, middle, gains[2], tables, w_attn_in_two, grad_sent

time: 917 us -> 994 us (1.084)
  waiting for transfers between devices: 305 us -> 383 us
    ppermute x104, waiting for transfers between devices: 245 us -> 331 us  [swap(): return lax.ppermute(values, axis, [(i, i ^ mask) for i in range(count)])]
    unnamed x244 -> x242, local copies, waits for them, and re-layouts: 23.4 us -> 22 us
  transfers between devices with their start and end apart: 117 -> 117, of which waited for: 45 -> 49; matrix products, arithmetic and copies ran while one was open for 13% -> 12% of each run, Pallas kernels for 24% -> 22%
where the time goes in v7:
time: 994 us; the launch traced here: 983 us
  waiting for transfers between devices  383 us (39%)
  Pallas kernels  265 us (27%)
  starting transfers between devices  178 us (18%)
  other arithmetic  61.3 us (6%)
  local copies, waits for them, and re-layouts  56.3 us (6%)
  matrix products  22.4 us (2%)
  between operations  15.9 us (2%)
    ppermute x104, waiting for transfers between devices, swap(): return lax.ppermute(values, axis, [(i, i ^ mask) for i in range(count)])  331 us
    pallas_call x33, Pallas kernels, call(): pl.pallas_call(body, grid_spec=pltpu.PrefetchScalarGridSpec(num_scalar_pr...  265 us
    ppermute x104, starting transfers between devices, swap(): return lax.ppermute(values, axis, [(i, i ^ mask) for i in range(count)])  129 us
    psum x1, waiting for transfers between devices, total(): return lax.psum(tuple(grads), 'ctx', axis_index_groups=ring)  37.7 us
    all_to_all x4, starting transfers between devices, dispatch(): lax.all_to_all(values, BOTH, 0, 0, tiled=True, axis_index_groups=members)  29.3 us
    unnamed x242, local copies, waits for them, and re-layouts  22 us
  transfers between devices with their start and end apart: 117, of which 49 were waited for; matrix products, arithmetic and copies ran while one was open for 12% of the time, Pallas kernels for 22%

profile of v7, /device:TPU:0, one launch (start us, length us, event | category | flops | bytes accessed | tf_op | source)
XLA Modules:
  0.0 983.0 jit_solution(16845654870098397490)
XLA Ops:
  25.1 10.3 %collective-permute-done.w2.rest_6_ = bf16[192,2304]{1,0:T(8,128)(2,1)S(1)} collective-permute-done((bf16[192,2304]{1,0:T(8,128)(2,1)S(1)}, bf16[192,2304]{1,0:T(8,128)(2,1)S(1)}, u32[]{:S(2)}, u32[]{:S(2)}) %collective-permute-start) | collective-permute-done | bytes 884768 | tf_op jit(solution)/shard_map/ppermute | solution.py:30
  35.4 5.9 collective-permute-done.13.w2
  57.2 5.8 shard_map.204
  69.5 8.5 collective-permute-done.6.refs_1_
  79.6 8.7 collective-permute-done.7.refs_2_
  99.6 7.3 all-to-all-start
  110.4 16.9 %shard_map.205 = (bf16[2,192,128]{2,1,0:T(8,128)(2,1)}, bf16[2,192,128]{2,1,0:T(8,128)(2,1)}, bf16[2,192,128]{2,1,0:T(8,128)(2,1)}, bf16[2,192,128]{2,1,0:T(8,12...) custom-call(s32[22]{0:T(128)} %concatenate.42.meta, bf16[2,3,192,128]{3,2,1,0:T(8,128)(2,1)} %get-tuple-element.283.refs_0_, ...), custom_call_target="tpu_custom_call" | custom-call | flops 1610612736 | bytes 3551232 | tf_op jit(solution)/shard_map/pallas_call | solution.py:91
  131.7 5.8 collective-permute-done.14.o1
  137.5 15.6 %collective-permute-done.15.o2 = bf16[2,192,128]{2,1,0:T(8,128)(2,1)S(1)} collective-permute-done((bf16[2,192,128]{2,1,0:T(8,128)(2,1)}, bf16[2,192,128]{2,1,0:T(8,128)(2,1)S(1)}, u32[]{:S(2)}, u32[]{:S(2)}) %collective-permute-start.15) | collective-permute-done | bytes 98336 | tf_op jit(solution)/shard_map/ppermute | solution.py:30
  153.8 4.7 shard_map.206
  158.5 5.0 all-to-all-start.1
  166.5 10.4 %shard_map.207 = (f32[256,768]{1,0:T(8,128)}, f32[2,256,2048]{2,1,0:T(8,128)}, bf16[2,256,512]{2,1,0:T(8,128)(2,1)}, bf16[2,256,512]{2,1,0:T(8,128)(2,1)}) custom-call(s32[22]{0:T(128)} %concatenate.42.meta, f32[256,768]{1,0:T(8,128)} %get-tuple-element.299.x, bf16[4,256,192]{2,1,0:T(8,128)(2,1)} %get-tuple-element.300.blocks, bf16[768,4096]{1,0:T(8,128)(2,1)} %bitcast.130, ...), custom_call_target="tpu_custom_call" | custom-call | flops 2415919104 | bytes 70123520 | tf_op jit(solution)/shard_map/pallas_call | solution.py:91
  176.9 87.0 %collective-permute-done.20.w2 = bf16[192,768]{1,0:T(8,128)(2,1)S(1)} collective-permute-done((bf16[192,768]{1,0:T(8,128)(2,1)S(1)}, bf16[192,768]{1,0:T(8,128)(2,1)S(1)}, u32[]{:S(2)}, u32[]{:S(2)}) %collective-permute-start.20) | collective-permute-done | bytes 294944 | tf_op jit(solution)/shard_map/ppermute | solution.py:30
  266.7 5.9 shard_map.208
  278.4 9.1 collective-permute-done.23.refs_1_
  289.0 8.7 collective-permute-done.24.refs_2_
  299.7 5.5 collective-permute-done.28.refs_6_
  310.8 16.6 %shard_map.209 = (bf16[2,192,128]{2,1,0:T(8,128)(2,1)}, bf16[2,192,128]{2,1,0:T(8,128)(2,1)}, bf16[2,192,128]{2,1,0:T(8,128)(2,1)}, bf16[2,192,128]{2,1,0:T(8,12...) custom-call(s32[22]{0:T(128)} %concatenate.42.meta, bf16[2,3,192,128]{3,2,1,0:T(8,128)(2,1)} %get-tuple-element.315.refs_0_, ...), custom_call_target="tpu_custom_call" | custom-call | flops 1610612736 | bytes 3551232 | tf_op jit(solution)/shard_map/pallas_call | solution.py:91
  340.4 4.6 shard_map.210
  347.8 7.3 all-to-all-start.2
  355.4 10.5 %shard_map.211 = (f32[256,768]{1,0:T(8,128)}, f32[2,256,2048]{2,1,0:T(8,128)}, bf16[2,256,512]{2,1,0:T(8,128)(2,1)}, bf16[2,256,512]{2,1,0:T(8,128)(2,1)}) custom-call(s32[22]{0:T(128)} %concatenate.42.meta, f32[256,768]{1,0:T(8,128)} %get-tuple-element.342.x, bf16[4,256,192]{2,1,0:T(8,128)(2,1)} %get-tuple-element.343.blocks, bf16[768,4096]{1,0:T(8,128)(2,1)} %bitcast.146, ...), custom_call_target="tpu_custom_call" | custom-call | flops 2415919104 | bytes 70123520 | tf_op jit(solution)/shard_map/pallas_call | solution.py:91
  366.7 10.7 %shard_map.212 = (bf16[2,256,2048]{2,1,0:T(8,128)(2,1)}, f32[256,768]{1,0:T(8,128)}) custom-call(s32[22]{0:T(128)} %concatenate.42.meta, bf16[1,256,768]{2,1,0:T(8,128)(2,1)} %right.1, f32[2,256,2048]{2,1,0:T(8,128)} %get-tuple-element.346.mixed, bf16[768,4096]{1,0:T(8,128)(2,1)} %bitcast.154, bf16[768,4096]{1,0:T(8,128)(2,1)} %bitcast.155, ...), custom_call_target="tpu_custom_call" | custom-call | flops 2415919104 | bytes 70385664 | tf_op jit(solution)/shard_map/pallas_call | solution.py:91
  378.3 4.1 shard_map.213
  382.4 6.8 all-to-all-done.2
  392.8 33.8 %shard_map.214 = (bf16[1024,768]{1,0:T(8,128)(2,1)}, bf16[1024,768]{1,0:T(8,128)(2,1)}, bf16[1024,768]{1,0:T(8,128)(2,1)}, bf16[1024,768]{1,0:T(8,128)(2,1)}, bf...) custom-call(s32[1]{0:T(128)} %bitcast.40.meta, ...), custom_call_target="tpu_custom_call" | custom-call | flops 19327352832 | bytes 36388864 | tf_op jit(solution)/shard_map/pallas_call | solution.py:91
  434.4 8.4 all-to-all-start.3
  446.0 8.5 shard_map.215
  456.1 6.7 convolution_convert_fusion.2
  472.6 7.4 all-to-all-done.3
  483.4 4.8 shard_map.216
  488.7 5.3 collective-permute-start.46
  501.1 13.8 %collective-permute-done.51 = bf16[192,4096]{1,0:T(8,128)(2,1)} collective-permute-done((bf16[192,4096]{1,0:T(8,128)(2,1)}, bf16[192,4096]{1,0:T(8,128)(2,1)}, u32[]{:S(2)}, u32[]{:S(2)}) %collective-permute-start.51) | collective-permute-done | bytes 1572896 | tf_op jit(solution)/shard_map/ppermute | solution.py:30
  518.1 4.9 all-to-all-start.4
  523.5 20.8 %shard_map.218 = (bf16[8,192,128]{2,1,0:T(8,128)(2,1)}, f32[8,2,192,128]{3,2,1,0:T(8,128)}, bf16[8,2,192,128]{3,2,1,0:T(8,128)(2,1)}) custom-call(s32[22]{0:T(128)} %concatenate.42.meta, bf16[2,3,192,128]{3,2,1,0:T(8,128)(2,1)} %get-tuple-element.315.refs_0_, bf16[2,3,192,128]{3,2,1,0:T(8,128)(2,1)} %copy-done.94, bf16[2,3,192,128]{3,2,1,0:T(8,128)(2,1)} %copy-done.95, ...), custom_call_target="tpu_custom_call" | custom-call | flops 4026531840 | bytes 6303744 | tf_op jit(solution)/shard_map/pallas_call | solution.py:91
  554.5 7.2 collective-permute-done.52.rest_0_
  565.2 5.0 collective-permute-start.53
  570.2 4.7 collective-permute-start.54
  578.0 5.2 collective-permute-done.57
  585.0 11.6 %collective-permute-done.55.rest_3_ = bf16[2,3,192,128]{3,2,1,0:T(8,128)(2,1)} collective-permute-done((bf16[2,3,192,128]{3,2,1,0:T(8,128)(2,1)}, bf16[2,3,192,128]{3,2,1,0:T(8,128)(2,1)}, u32[]{:S(2)}, u32[]{:S(2)}) %collective-permute-start.55) | collective-permute-done | bytes 294944 | tf_op jit(solution)/shard_map/ppermute | solution.py:30
  596.6 9.2 all-to-all-start.5
  606.3 7.0 shard_map.220
  615.3 10.8 %shard_map.221 = (bf16[2,256,2048]{2,1,0:T(8,128)(2,1)}, f32[256,768]{1,0:T(8,128)}) custom-call(s32[22]{0:T(128)} %concatenate.42.meta, bf16[1,256,768]{2,1,0:T(8,128)(2,1)} %convert_bitcast_fusion.1.branch.right, f32[2,256,2048]{2,1,0:T(8,128)} %get-tuple-element.424.mixed, bf16[768,4096]{1,0:T(8,128)(2,1)} %bitcast.138, bf16[768,4096]{1,0:T(8,128)(2,1)} %bitcast.139, ...), custom_call_target="tpu_custom_call" | custom-call | flops 2415919104 | bytes 70385664 | tf_op jit(solution)/shard_map/pallas_call | solution.py:91
  633.1 5.2 shard_map.222
  638.4 4.6 shard_map.223
  648.1 8.4 shard_map.224
  659.7 7.4 collective-permute-done.61.refs_10_
  671.6 4.1 shard_map.226
  682.2 21.0 %shard_map.225 = (bf16[8,192,128]{2,1,0:T(8,128)(2,1)}, f32[8,2,192,128]{3,2,1,0:T(8,128)}, bf16[8,2,192,128]{3,2,1,0:T(8,128)(2,1)}) custom-call(s32[22]{0:T(128)} %concatenate.42.meta, bf16[2,3,192,128]{3,2,1,0:T(8,128)(2,1)} %get-tuple-element.283.refs_0_, bf16[2,3,192,128]{3,2,1,0:T(8,128)(2,1)} %copy-done.87, bf16[2,3,192,128]{3,2,1,0:T(8,128)(2,1)} %copy-done.88, ...), custom_call_target="tpu_custom_call" | custom-call | flops 4026531840 | bytes 6303744 | tf_op jit(solution)/shard_map/pallas_call | solution.py:91
  703.9 6.2 all-to-all-start.6
  710.2 12.9 %collective-permute-done.70 = bf16[192,6400]{1,0:T(8,128)(2,1)} collective-permute-done((bf16[192,6400]{1,0:T(8,128)(2,1)}, bf16[192,6400]{1,0:T(8,128)(2,1)}, u32[]{:S(2)}, u32[]{:S(2)}) %collective-permute-start.70) | collective-permute-done | bytes 2457632 | tf_op jit(solution)/shard_map/ppermute | solution.py:30
  728.2 8.8 collective-permute-done.65.rest_0_
  747.9 21.6 %collective-permute-done.74 = bf16[704,768]{1,0:T(8,128)(2,1)S(1)} collective-permute-done((bf16[704,768]{1,0:T(8,128)(2,1)}, bf16[704,768]{1,0:T(8,128)(2,1)S(1)}, u32[]{:S(2)}, u32[]{:S(2)}) %collective-permute-start.74) | collective-permute-done | bytes 1081376 | tf_op jit(solution)/shard_map/ppermute | solution.py:30
  770.2 4.1 collective-permute-done.72.rest_2_
  774.4 7.0 shard_map.229
  787.9 10.0 %collective-permute-done.88.second = bf16[512,384]{1,0:T(8,128)(2,1)S(1)} collective-permute-done((bf16[512,384]{1,0:T(8,128)(2,1)}, bf16[512,384]{1,0:T(8,128)(2,1)S(1)}, u32[]{:S(2)}, u32[]{:S(2)}) %collective-permute-start.88) | collective-permute-done | bytes 393248 | tf_op jit(solution)/shard_map/ppermute | solution.py:30
  801.4 6.8 collective-permute-start.89
  811.8 6.5 collective-permute-done.90
  823.4 5.5 shard_map.230
  834.4 14.7 %collective-permute-done.76.second = bf16[192,2304]{1,0:T(8,128)(2,1)} collective-permute-done((bf16[192,2304]{1,0:T(8,128)(2,1)}, bf16[192,2304]{1,0:T(8,128)(2,1)}, u32[]{:S(2)}, u32[]{:S(2)}) %collective-permute-start.76) | collective-permute-done | bytes 884768 | tf_op jit(solution)/shard_map/ppermute | solution.py:30
  889.8 4.4 copy.132
  908.7 5.9 collective-permute-start.98
  924.2 37.7 %all-reduce.6.cloned.1.call-done = (bf16[192,2304]{1,0:T(8,128)(2,1)}, bf16[192,4096]{1,0:T(8,128)(2,1)}, bf16[192,768]{1,0:T(8,128)(2,1)}, bf16[192,768]{1,0:T(8,128)(2,1)}) async-done(((bf16[192,2304]{1,0:T(8,128)(2,1)}, bf16[192,4096]{1,0:T(8,128)(2,1)}, bf16[192,768]{1,0:T(8,128)(2,1)}, bf16[192,768]{1,0:T(8,128)(2,1)}), (bf16[192,2304]{1,0:T(8,128)(2,1)}, bf16[192,4096]{1,0:T(8,128)(2,1)}, ...) | async-done | bytes 3047440 | tf_op jit(solution)/shard_map/psum | solution.py:924
  961.9 4.6 maximum_convert_fusion
  967.7 4.2 shard_map.235
  (572 shorter events, 298.4 us)
Async XLA Ops:
  7.2 159.3 %all-gather.14.cloned.1.call-start = ((), (), s32[]{:S(2)}) async-start(), calls=%async_computation.9 | async-start | bytes 3932160 | tf_op jit(solution)/shard_map/all_gather | solution.py:975
  12.8 22.5 %collective-permute-start = (bf16[192,2304]{1,0:T(8,128)(2,1)S(1)}, bf16[192,2304]{1,0:T(8,128)(2,1)S(1)}, u32[]{:S(2)}, u32[]{:S(2)}) collective-permute-start(bf16[192,2304]{1,0:T(8,128)(2,1)S(1)} %slice_bitcast_fusion.3.w0.rest_4_), channel_id=1, source_target_pairs={{0,2},{1,3},{2,0},{3,1},{4,6},{5,7},{6,4},{7,5},{8,10},{9,11},{10,... | collective-permute-start | bytes 2654216 | tf_op jit(solution)/shard_map/ppermute | solution.py:30
  14.1 27.1 %collective-permute-start.13 = (bf16[192,768]{1,0:T(8,128)(2,1)S(1)}, bf16[192,768]{1,0:T(8,128)(2,1)S(1)}, u32[]{:S(2)}, u32[]{:S(2)}) collective-permute-start(bf16[192,768]{1,0:T(8,128)(2,1)S(1)} %slice_bitcast_fusion.5.w0), channel_id=1, source_target_pairs={{0,2},{1,3},{2,0},{3,1},{4,6},{5,7},{6,4},{7,5},{8,10},{9,11},{10,... | collective-permute-start | bytes 884744 | tf_op jit(solution)/shard_map/ppermute | solution.py:30
  44.0 122.4 %all-gather.12.cloned.1.call-start = ((), (), s32[]{:S(2)}) async-start(), calls=%async_computation.8 | async-start | bytes 7864320 | tf_op jit(solution)/shard_map/all_gather | solution.py:975
  48.0 307.3 %all-gather.18.cloned.1.call-start = ((), (), s32[]{:S(2)}) async-start(), calls=%async_computation.11 | async-start | bytes 3932160 | tf_op jit(solution)/shard_map/all_gather | solution.py:975
  48.8 306.6 %all-gather.16.cloned.1.call-start = ((), (), s32[]{:S(2)}) async-start(), calls=%async_computation.10 | async-start | bytes 7864320 | tf_op jit(solution)/shard_map/all_gather | solution.py:975
  64.6 23.6 %collective-permute-start.7 = (bf16[2,3,192,128]{3,2,1,0:T(8,128)(2,1)}, bf16[2,3,192,128]{3,2,1,0:T(8,128)(2,1)S(1)}, u32[]{:S(2)}, u32[]{:S(2)}) collective-permute-start(bf16[2,3,192,128]{3,2,1,0:T(8,128)(2,1)} %get-tuple-element.279), channel_id=1, source_target_pairs={{0,16},{4,20},{8,24},{12,28},{16,0},{20,4},{24,8},{28,12},{1,17},{... | collective-permute-start | bytes 884744 | tf_op jit(solution)/shard_map/ppermute | solution.py:30
  67.2 22.6 %collective-permute-start.8 = (bf16[2,3,192,128]{3,2,1,0:T(8,128)(2,1)}, bf16[2,3,192,128]{3,2,1,0:T(8,128)(2,1)S(1)}, u32[]{:S(2)}, u32[]{:S(2)}) collective-permute-start(bf16[2,3,192,128]{3,2,1,0:T(8,128)(2,1)} %get-tuple-element.280), channel_id=1, source_target_pairs={{0,24},{4,28},{8,16},{12,20},{16,8},{20,12},{24,0},{28,4},{1,25},{... | collective-permute-start | bytes 884744 | tf_op jit(solution)/shard_map/ppermute | solution.py:30
  67.9 24.4 %collective-permute-start.9 = (bf16[2,3,192,128]{3,2,1,0:T(8,128)(2,1)}, bf16[2,3,192,128]{3,2,1,0:T(8,128)(2,1)S(1)}, u32[]{:S(2)}, u32[]{:S(2)}) collective-permute-start(bf16[2,3,192,128]{3,2,1,0:T(8,128)(2,1)} %get-tuple-element.283.refs_0_), channel_id=1, source_target_pairs={{0,4},{4,0},{8,12},{12,8},{16,20},{20,16},{24,28},{28,24},{1,5},{5... | collective-permute-start | bytes 884744 | tf_op jit(solution)/shard_map/ppermute | solution.py:30
  99.6 58.9 %all-to-all-start = ((bf16[16,72,768]{2,1,0:T(8,128)(2,1)}), bf16[16,72,768]{2,1,0:T(8,128)(2,1)S(1)}, u32[]{:S(2)}, u32[]{:S(2)}) async-start(bf16[16,72,768]{2,1,0:T(8,128)(2,1)} %fusion.2), calls=%async_computation | async-start | bytes 3538944 | tf_op jit(solution)/shard_map/all_to_all | solution.py:963
  106.9 24.3 %collective-permute-start.17 = (bf16[192,768]{1,0:T(8,128)(2,1)S(1)}, bf16[192,768]{1,0:T(8,128)(2,1)S(1)}, u32[]{:S(2)}, u32[]{:S(2)}) collective-permute-start(bf16[192,768]{1,0:T(8,128)(2,1)S(1)} %slice_bitcast_fusion.5.w0), channel_id=1, source_target_pairs={{0,1},{1,0},{2,3},{3,2},{4,5},{5,4},{6,7},{7,6},{8,9},{9,8},{10,11... | collective-permute-start | bytes 884744 | tf_op jit(solution)/shard_map/ppermute | solution.py:30
  108.2 155.7 %collective-permute-start.19 = (bf16[192,2304]{1,0:T(8,128)(2,1)S(1)}, bf16[192,2304]{1,0:T(8,128)(2,1)}, u32[]{:S(2)}, u32[]{:S(2)}) collective-permute-start(bf16[192,2304]{1,0:T(8,128)(2,1)S(1)} %slice_bitcast_fusion.2.w0.rest_4_), channel_id=1, source_target_pairs={{0,2},{1,3},{2,0},{3,1},{4,6},{5,7},{6,4},{7,5},{8,10},{9,11},{10,... | collective-permute-start | bytes 2654216 | tf_op jit(solution)/shard_map/ppermute | solution.py:30
  110.2 21.5 %collective-permute-start.18 = (bf16[192,768]{1,0:T(8,128)(2,1)S(1)}, bf16[192,768]{1,0:T(8,128)(2,1)}, u32[]{:S(2)}, u32[]{:S(2)}) collective-permute-start(bf16[192,768]{1,0:T(8,128)(2,1)S(1)} %copy-done.18), channel_id=1, source_target_pairs={{0,1},{1,0},{2,3},{3,2},{4,5},{5,4},{6,7},{7,6},{8,9},{9,8},{10,11... | collective-permute-start | bytes 884744 | tf_op jit(solution)/shard_map/ppermute | solution.py:30
  128.8 24.3 %collective-permute-start.15 = (bf16[2,192,128]{2,1,0:T(8,128)(2,1)}, bf16[2,192,128]{2,1,0:T(8,128)(2,1)S(1)}, u32[]{:S(2)}, u32[]{:S(2)}) collective-permute-start(bf16[2,192,128]{2,1,0:T(8,128)(2,1)} %get-tuple-element.293), channel_id=1, source_target_pairs={{0,16},{4,20},{8,24},{12,28},{16,0},{20,4},{24,8},{28,12},{1,17},{... | collective-permute-start | bytes 294920 | tf_op jit(solution)/shard_map/ppermute | solution.py:30
  131.2 21.9 %collective-permute-start.16 = (bf16[2,192,128]{2,1,0:T(8,128)(2,1)}, bf16[2,192,128]{2,1,0:T(8,128)(2,1)S(1)}, u32[]{:S(2)}, u32[]{:S(2)}) collective-permute-start(bf16[2,192,128]{2,1,0:T(8,128)(2,1)} %get-tuple-element.294), channel_id=1, source_target_pairs={{0,24},{4,28},{8,16},{12,20},{16,8},{20,12},{24,0},{28,4},{1,25},{... | collective-permute-start | bytes 294920 | tf_op jit(solution)/shard_map/ppermute | solution.py:30
  158.5 174.7 %all-to-all-start.1 = ((bf16[4,3,192,1024]{3,2,1,0:T(8,128)(2,1)}), bf16[4,3,192,1024]{3,2,1,0:T(8,128)(2,1)}, u32[]{:S(2)}, u32[]{:S(2)}) async-start(bf16[4,3,192,1024]{3,2,1,0:T(8,128)(2,1)} %pad_maximum_fusion), calls=%async_computation.1 | async-start | bytes 9437184 | tf_op jit(solution)/shard_map/all_to_all | solution.py:1070
  164.4 99.5 %collective-permute-start.20 = (bf16[192,768]{1,0:T(8,128)(2,1)S(1)}, bf16[192,768]{1,0:T(8,128)(2,1)S(1)}, u32[]{:S(2)}, u32[]{:S(2)}) collective-permute-start(bf16[192,768]{1,0:T(8,128)(2,1)S(1)} %slice_bitcast_fusion.4.w0), channel_id=1, source_target_pairs={{0,2},{1,3},{2,0},{3,1},{4,6},{5,7},{6,4},{7,5},{8,10},{9,11},{10,... | collective-permute-start | bytes 884744 | tf_op jit(solution)/shard_map/ppermute | solution.py:30
  166.5 97.4 %collective-permute-start.21 = (bf16[192,2304]{1,0:T(8,128)(2,1)S(1)}, bf16[192,2304]{1,0:T(8,128)(2,1)}, u32[]{:S(2)}, u32[]{:S(2)}) collective-permute-start(bf16[192,2304]{1,0:T(8,128)(2,1)S(1)} %slice_bitcast_fusion.2.w0.rest_4_), channel_id=1, source_target_pairs={{0,1},{1,0},{2,3},{3,2},{4,5},{5,4},{6,7},{7,6},{8,9},{9,8},{10,11... | collective-permute-start | bytes 2654216 | tf_op jit(solution)/shard_map/ppermute | solution.py:30
  274.0 23.6 %collective-permute-start.24 = (bf16[2,3,192,128]{3,2,1,0:T(8,128)(2,1)}, bf16[2,3,192,128]{3,2,1,0:T(8,128)(2,1)S(1)}, u32[]{:S(2)}, u32[]{:S(2)}) collective-permute-start(bf16[2,3,192,128]{3,2,1,0:T(8,128)(2,1)} %get-tuple-element.312), channel_id=1, source_target_pairs={{0,16},{4,20},{8,24},{12,28},{16,0},{20,4},{24,8},{28,12},{1,17},{... | collective-permute-start | bytes 884744 | tf_op jit(solution)/shard_map/ppermute | solution.py:30
  276.5 22.7 %collective-permute-start.25 = (bf16[2,3,192,128]{3,2,1,0:T(8,128)(2,1)}, bf16[2,3,192,128]{3,2,1,0:T(8,128)(2,1)S(1)}, u32[]{:S(2)}, u32[]{:S(2)}) collective-permute-start(bf16[2,3,192,128]{3,2,1,0:T(8,128)(2,1)} %get-tuple-element.313), channel_id=1, source_target_pairs={{0,24},{4,28},{8,16},{12,20},{16,8},{20,12},{24,0},{28,4},{1,25},{... | collective-permute-start | bytes 884744 | tf_op jit(solution)/shard_map/ppermute | solution.py:30
  277.0 22.8 %collective-permute-start.26 = (bf16[2,3,192,128]{3,2,1,0:T(8,128)(2,1)}, bf16[2,3,192,128]{3,2,1,0:T(8,128)(2,1)S(1)}, u32[]{:S(2)}, u32[]{:S(2)}) collective-permute-start(bf16[2,3,192,128]{3,2,1,0:T(8,128)(2,1)} %get-tuple-element.315.refs_0_), channel_id=1, source_target_pairs={{0,4},{4,0},{8,12},{12,8},{16,20},{20,16},{24,28},{28,24},{1,5},{5... | collective-permute-start | bytes 884744 | tf_op jit(solution)/shard_map/ppermute | solution.py:30
  309.8 17.7 %collective-permute-start.30 = (bf16[1024,768]{1,0:T(8,128)(2,1)}, bf16[1024,768]{1,0:T(8,128)(2,1)}, u32[]{:S(2)}, u32[]{:S(2)}) collective-permute-start(bf16[1024,768]{1,0:T(8,128)(2,1)} %bitcast.34.refs_2_), channel_id=1, source_target_pairs={{0,1},{1,0},{2,3},{3,2},{4,5},{5,4},{6,7},{7,6},{8,9},{9,8},{10,11... | collective-permute-start | bytes 4718600 | tf_op jit(solution)/shard_map/ppermute | solution.py:30
  309.8 23.3 %collective-permute-start.35 = (bf16[192,768]{1,0:T(8,128)(2,1)S(1)}, bf16[192,768]{1,0:T(8,128)(2,1)S(1)}, u32[]{:S(2)}, u32[]{:S(2)}) collective-permute-start(bf16[192,768]{1,0:T(8,128)(2,1)S(1)} %slice_bitcast_fusion.4.w0), channel_id=1, source_target_pairs={{0,1},{1,0},{2,3},{3,2},{4,5},{5,4},{6,7},{7,6},{8,9},{9,8},{10,11... | collective-permute-start | bytes 884744 | tf_op jit(solution)/shard_map/ppermute | solution.py:30
  310.3 22.8 %collective-permute-start.36 = (bf16[192,768]{1,0:T(8,128)(2,1)S(1)}, bf16[192,768]{1,0:T(8,128)(2,1)S(1)}, u32[]{:S(2)}, u32[]{:S(2)}) collective-permute-start(bf16[192,768]{1,0:T(8,128)(2,1)S(1)} %collective-permute-done.20.w2), channel_id=1, source_target_pairs={{0,1},{1,0},{2,3},{3,2},{4,5},{5,4},{6,7},{7,6},{8,9},{9,8},{10,11... | collective-permute-start | bytes 884744 | tf_op jit(solution)/shard_map/ppermute | solution.py:30
  310.4 17.0 %collective-permute-start.31 = (f32[16,64]{1,0:T(8,128)S(1)}, f32[16,64]{1,0:T(8,128)S(1)}, u32[]{:S(2)}, u32[]{:S(2)}) collective-permute-start(f32[16,64]{1,0:T(8,128)S(1)} %bitcast.208), channel_id=1, source_target_pairs={{0,1},{1,0},{2,3},{3,2},{4,5},{5,4},{6,7},{7,6},{8,9},{9,8},{10,11... | collective-permute-start | bytes 12296 | tf_op jit(solution)/shard_map/ppermute | solution.py:30
  347.8 41.5 %all-to-all-start.2 = ((bf16[16,64,768]{2,1,0:T(8,128)(2,1)}), bf16[16,64,768]{2,1,0:T(8,128)(2,1)S(1)}, u32[]{:S(2)}, u32[]{:S(2)}) async-start(bf16[16,64,768]{2,1,0:T(8,128)(2,1)} %bitcast.198), calls=%async_computation.2 | async-start | bytes 3145728 | tf_op jit(solution)/shard_map/all_to_all | solution.py:963
  355.1 22.4 %collective-permute-start.38 = (bf16[1,256,768]{2,1,0:T(8,128)(2,1)S(1)}, bf16[1,256,768]{2,1,0:T(8,128)(2,1)}, u32[]{:S(2)}, u32[]{:S(2)}) collective-permute-start(bf16[1,256,768]{2,1,0:T(8,128)(2,1)S(1)} %copy-done.10), channel_id=1, source_target_pairs={{0,1},{1,0},{2,3},{3,2},{4,5},{5,4},{6,7},{7,6},{8,9},{9,8},{10,11... | collective-permute-start | bytes 1179656 | tf_op jit(solution)/shard_map/ppermute | solution.py:30
  426.9 18.4 %collective-permute-start.44 = (bf16[2,256,2048]{2,1,0:T(8,128)(2,1)}, bf16[2,256,2048]{2,1,0:T(8,128)(2,1)}, u32[]{:S(2)}, u32[]{:S(2)}) collective-permute-start(bf16[2,256,2048]{2,1,0:T(8,128)(2,1)} %get-tuple-element.379.right), channel_id=1, source_target_pairs={{0,1},{1,0},{2,3},{3,2},{4,5},{5,4},{6,7},{7,6},{8,9},{9,8},{10,11... | collective-permute-start | bytes 6291464 | tf_op jit(solution)/shard_map/ppermute | solution.py:30
  429.0 25.5 %collective-permute-start.45 = (bf16[512,768]{1,0:T(8,128)(2,1)S(1)}, bf16[512,768]{1,0:T(8,128)(2,1)}, u32[]{:S(2)}, u32[]{:S(2)}) collective-permute-start(bf16[512,768]{1,0:T(8,128)(2,1)S(1)} %copy-done.83), channel_id=1, source_target_pairs={{0,2},{1,3},{2,0},{3,1},{4,6},{5,7},{6,4},{7,5},{8,10},{9,11},{10,... | collective-permute-start | bytes 2359304 | tf_op jit(solution)/shard_map/ppermute | solution.py:30
  434.4 45.6 %all-to-all-start.3 = ((bf16[16,72,768]{2,1,0:T(8,128)(2,1)}), bf16[16,72,768]{2,1,0:T(8,128)(2,1)S(1)}, u32[]{:S(2)}, u32[]{:S(2)}) async-start(bf16[16,72,768]{2,1,0:T(8,128)(2,1)} %fusion.3), calls=%async_computation.3 | async-start | bytes 3538944 | tf_op jit(solution)/shard_map/all_to_all | solution.py:963
  480.0 35.0 %collective-permute-start.51 = (bf16[192,4096]{1,0:T(8,128)(2,1)}, bf16[192,4096]{1,0:T(8,128)(2,1)}, u32[]{:S(2)}, u32[]{:S(2)}) collective-permute-start(bf16[192,4096]{1,0:T(8,128)(2,1)} %get-tuple-element.397), channel_id=1, source_target_pairs={{0,2},{1,3},{2,0},{3,1},{4,6},{5,7},{6,4},{7,5},{8,10},{9,11},{10,... | collective-permute-start | bytes 4718600 | tf_op jit(solution)/shard_map/ppermute | solution.py:30
  488.7 28.7 %collective-permute-start.46 = (bf16[2,192,128]{2,1,0:T(8,128)(2,1)}, bf16[2,192,128]{2,1,0:T(8,128)(2,1)S(1)}, u32[]{:S(2)}, u32[]{:S(2)}) collective-permute-start(bf16[2,192,128]{2,1,0:T(8,128)(2,1)} %get-tuple-element.387), channel_id=1, source_target_pairs={{0,8},{4,12},{8,0},{12,4},{16,24},{20,28},{24,16},{28,20},{1,9},{5... | collective-permute-start | bytes 294920 | tf_op jit(solution)/shard_map/ppermute | solution.py:30
  493.9 23.5 %collective-permute-start.47 = (bf16[2,192,128]{2,1,0:T(8,128)(2,1)}, bf16[2,192,128]{2,1,0:T(8,128)(2,1)S(1)}, u32[]{:S(2)}, u32[]{:S(2)}) collective-permute-start(bf16[2,192,128]{2,1,0:T(8,128)(2,1)} %get-tuple-element.388), channel_id=1, source_target_pairs={{0,16},{4,20},{8,24},{12,28},{16,0},{20,4},{24,8},{28,12},{1,17},{... | collective-permute-start | bytes 294920 | tf_op jit(solution)/shard_map/ppermute | solution.py:30
  495.6 21.9 %collective-permute-start.48 = (bf16[2,192,128]{2,1,0:T(8,128)(2,1)}, bf16[2,192,128]{2,1,0:T(8,128)(2,1)S(1)}, u32[]{:S(2)}, u32[]{:S(2)}) collective-permute-start(bf16[2,192,128]{2,1,0:T(8,128)(2,1)} %get-tuple-element.389), channel_id=1, source_target_pairs={{0,24},{4,28},{8,16},{12,20},{16,8},{20,12},{24,0},{28,4},{1,25},{... | collective-permute-start | bytes 294920 | tf_op jit(solution)/shard_map/ppermute | solution.py:30
  518.1 78.5 %all-to-all-start.4 = ((bf16[4,3,192,1024]{3,2,1,0:T(8,128)(2,1)}), bf16[4,3,192,1024]{3,2,1,0:T(8,128)(2,1)}, u32[]{:S(2)}, u32[]{:S(2)}) async-start(bf16[4,3,192,1024]{3,2,1,0:T(8,128)(2,1)} %pad_maximum_fusion.1), calls=%async_computation.4 | async-start | bytes 9437184 | tf_op jit(solution)/shard_map/all_to_all | solution.py:1198
  523.1 23.1 %collective-permute-start.56 = (bf16[1024,768]{1,0:T(8,128)(2,1)}, bf16[1024,768]{1,0:T(8,128)(2,1)}, u32[]{:S(2)}, u32[]{:S(2)}) collective-permute-start(bf16[1024,768]{1,0:T(8,128)(2,1)} %get-tuple-element.413), channel_id=1, source_target_pairs={{0,1},{1,0},{2,3},{3,2},{4,5},{5,4},{6,7},{7,6},{8,9},{9,8},{10,11... | collective-permute-start | bytes 4718600 | tf_op jit(solution)/shard_map/ppermute | solution.py:30
  544.3 17.4 %collective-permute-start.52 = (bf16[8,2,192,128]{3,2,1,0:T(8,128)(2,1)}, bf16[8,2,192,128]{3,2,1,0:T(8,128)(2,1)}, u32[]{:S(2)}, u32[]{:S(2)}) collective-permute-start(bf16[8,2,192,128]{3,2,1,0:T(8,128)(2,1)} %get-tuple-element.407), channel_id=1, source_target_pairs={{0,4},{4,0},{8,12},{12,8},{16,20},{20,16},{24,28},{28,24},{1,5},{5... | collective-permute-start | bytes 2359304 | tf_op jit(solution)/shard_map/ppermute | solution.py:30
  549.6 33.6 %collective-permute-start.57 = (bf16[192,768]{1,0:T(8,128)(2,1)}, bf16[192,768]{1,0:T(8,128)(2,1)}, u32[]{:S(2)}, u32[]{:S(2)}) collective-permute-start(bf16[192,768]{1,0:T(8,128)(2,1)} %get-tuple-element.418), channel_id=1, source_target_pairs={{0,2},{1,3},{2,0},{3,1},{4,6},{5,7},{6,4},{7,5},{8,10},{9,11},{10,... | collective-permute-start | bytes 884744 | tf_op jit(solution)/shard_map/ppermute | solution.py:30
  565.2 19.8 %collective-permute-start.53 = (bf16[2,3,192,128]{3,2,1,0:T(8,128)(2,1)}, bf16[2,3,192,128]{3,2,1,0:T(8,128)(2,1)S(1)}, u32[]{:S(2)}, u32[]{:S(2)}) collective-permute-start(bf16[2,3,192,128]{3,2,1,0:T(8,128)(2,1)} %get-tuple-element.409), channel_id=1, source_target_pairs={{0,8},{4,12},{8,0},{12,4},{16,24},{20,28},{24,16},{28,20},{1,9},{5... | collective-permute-start | bytes 884744 | tf_op jit(solution)/shard_map/ppermute | solution.py:30
  575.0 21.6 %collective-permute-start.55 = (bf16[2,3,192,128]{3,2,1,0:T(8,128)(2,1)}, bf16[2,3,192,128]{3,2,1,0:T(8,128)(2,1)}, u32[]{:S(2)}, u32[]{:S(2)}) collective-permute-start(bf16[2,3,192,128]{3,2,1,0:T(8,128)(2,1)} %get-tuple-element.411), channel_id=1, source_target_pairs={{0,24},{4,28},{8,16},{12,20},{16,8},{20,12},{24,0},{28,4},{1,25},{... | collective-permute-start | bytes 884744 | tf_op jit(solution)/shard_map/ppermute | solution.py:30
  596.6 71.1 %all-to-all-start.5 = ((bf16[8,24,6144]{2,1,0:T(8,128)(2,1)}), bf16[8,24,6144]{2,1,0:T(8,128)(2,1)S(1)}, u32[]{:S(2)}, u32[]{:S(2)}) async-start(bf16[8,24,6144]{2,1,0:T(8,128)(2,1)} %pad_maximum_fusion.3), calls=%async_computation.5 | async-start | bytes 4718592 | tf_op jit(solution)/shard_map/all_to_all | solution.py:1212
  605.8 168.5 %all-gather.10.cloned.1.call-start = ((), (), s32[]{:S(2)}) async-start(), calls=%async_computation.7 | async-start | bytes 2654208 | tf_op jit(solution)/shard_map/all_gather | solution.py:1235
  626.1 21.3 %collective-permute-start.64 = (bf16[2,256,2048]{2,1,0:T(8,128)(2,1)}, bf16[2,256,2048]{2,1,0:T(8,128)(2,1)}, u32[]{:S(2)}, u32[]{:S(2)}) collective-permute-start(bf16[2,256,2048]{2,1,0:T(8,128)(2,1)} %get-tuple-element.439.right), channel_id=1, source_target_pairs={{0,1},{1,0},{2,3},{3,2},{4,5},{5,4},{6,7},{7,6},{8,9},{9,8},{10,11... | collective-permute-start | bytes 6291464 | tf_op jit(solution)/shard_map/ppermute | solution.py:30
  626.8 20.6 %collective-permute-start.63 = (bf16[2,256,192]{2,1,0:T(8,128)(2,1)S(1)}, bf16[2,256,192]{2,1,0:T(8,128)(2,1)S(1)}, u32[]{:S(2)}, u32[]{:S(2)}) collective-permute-start(bf16[2,256,192]{2,1,0:T(8,128)(2,1)S(1)} %copy-done.100), channel_id=1, source_target_pairs={{0,1},{1,0},{2,3},{3,2},{4,5},{5,4},{6,7},{7,6},{8,9},{9,8},{10,11... | collective-permute-start | bytes 589832 | tf_op jit(solution)/shard_map/ppermute | solution.py:30
  643.0 16.8 %collective-permute-start.60 = (bf16[2,192,128]{2,1,0:T(8,128)(2,1)}, bf16[2,192,128]{2,1,0:T(8,128)(2,1)S(1)}, u32[]{:S(2)}, u32[]{:S(2)}) collective-permute-start(bf16[2,192,128]{2,1,0:T(8,128)(2,1)} %get-tuple-element.434), channel_id=1, source_target_pairs={{0,8},{4,12},{8,0},{12,4},{16,24},{20,28},{24,16},{28,20},{1,9},{5... | collective-permute-start | bytes 294920 | tf_op jit(solution)/shard_map/ppermute | solution.py:30
  644.9 22.2 %collective-permute-start.61 = (bf16[2,192,128]{2,1,0:T(8,128)(2,1)}, bf16[2,192,128]{2,1,0:T(8,128)(2,1)S(1)}, u32[]{:S(2)}, u32[]{:S(2)}) collective-permute-start(bf16[2,192,128]{2,1,0:T(8,128)(2,1)} %get-tuple-element.435), channel_id=1, source_target_pairs={{0,16},{4,20},{8,24},{12,28},{16,0},{20,4},{24,8},{28,12},{1,17},{... | collective-permute-start | bytes 294920 | tf_op jit(solution)/shard_map/ppermute | solution.py:30
  647.3 20.4 %collective-permute-start.62 = (bf16[2,192,128]{2,1,0:T(8,128)(2,1)}, bf16[2,192,128]{2,1,0:T(8,128)(2,1)}, u32[]{:S(2)}, u32[]{:S(2)}) collective-permute-start(bf16[2,192,128]{2,1,0:T(8,128)(2,1)} %get-tuple-element.436), channel_id=1, source_target_pairs={{0,24},{4,28},{8,16},{12,20},{16,8},{20,12},{24,0},{28,4},{1,25},{... | collective-permute-start | bytes 294920 | tf_op jit(solution)/shard_map/ppermute | solution.py:30
  667.7 55.4 %collective-permute-start.70 = (bf16[192,6400]{1,0:T(8,128)(2,1)}, bf16[192,6400]{1,0:T(8,128)(2,1)}, u32[]{:S(2)}, u32[]{:S(2)}) collective-permute-start(bf16[192,6400]{1,0:T(8,128)(2,1)} %pad_maximum_fusion.2), channel_id=1, source_target_pairs={{0,2},{1,3},{2,0},{3,1},{4,6},{5,7},{6,4},{7,5},{8,10},{9,11},{10,... | collective-permute-start | bytes 7372808 | tf_op jit(solution)/shard_map/ppermute | solution.py:30
  703.2 33.8 %collective-permute-start.65 = (bf16[8,2,192,128]{3,2,1,0:T(8,128)(2,1)}, bf16[8,2,192,128]{3,2,1,0:T(8,128)(2,1)}, u32[]{:S(2)}, u32[]{:S(2)}) collective-permute-start(bf16[8,2,192,128]{3,2,1,0:T(8,128)(2,1)} %get-tuple-element.452), channel_id=1, source_target_pairs={{0,4},{4,0},{8,12},{12,8},{16,20},{20,16},{24,28},{28,24},{1,5},{5... | collective-permute-start | bytes 2359304 | tf_op jit(solution)/shard_map/ppermute | solution.py:30
  703.9 70.5 %all-to-all-start.6 = ((bf16[16,64,768]{2,1,0:T(8,128)(2,1)}), bf16[16,64,768]{2,1,0:T(8,128)(2,1)S(1)}, u32[]{:S(2)}, u32[]{:S(2)}) async-start(bf16[16,64,768]{2,1,0:T(8,128)(2,1)} %bitcast.57), calls=%async_computation.6 | async-start | bytes 3145728 | tf_op jit(solution)/shard_map/all_to_all | solution.py:963
  710.1 251.8 %all-reduce.6.cloned.1.call-start = ((), (), s32[]{:S(2)}) async-start(), calls=%async_computation.12 | async-start | bytes 6094848 | tf_op jit(solution)/shard_map/psum | solution.py:924
  737.0 32.5 %collective-permute-start.74 = (bf16[704,768]{1,0:T(8,128)(2,1)}, bf16[704,768]{1,0:T(8,128)(2,1)S(1)}, u32[]{:S(2)}, u32[]{:S(2)}) collective-permute-start(bf16[704,768]{1,0:T(8,128)(2,1)} %pad_maximum_fusion.5), channel_id=1, source_target_pairs={{0,2},{1,3},{2,0},{3,1},{4,6},{5,7},{6,4},{7,5},{8,10},{9,11},{10,... | collective-permute-start | bytes 3244040 | tf_op jit(solution)/shard_map/ppermute | solution.py:30
  743.5 26.7 %collective-permute-start.71 = (bf16[2,3,192,128]{3,2,1,0:T(8,128)(2,1)}, bf16[2,3,192,128]{3,2,1,0:T(8,128)(2,1)}, u32[]{:S(2)}, u32[]{:S(2)}) collective-permute-start(bf16[2,3,192,128]{3,2,1,0:T(8,128)(2,1)} %get-tuple-element.465), channel_id=1, source_target_pairs={{0,8},{4,12},{8,0},{12,4},{16,24},{20,28},{24,16},{28,20},{1,9},{5... | collective-permute-start | bytes 884744 | tf_op jit(solution)/shard_map/ppermute | solution.py:30
  743.5 30.8 %collective-permute-start.72 = (bf16[2,3,192,128]{3,2,1,0:T(8,128)(2,1)}, bf16[2,3,192,128]{3,2,1,0:T(8,128)(2,1)}, u32[]{:S(2)}, u32[]{:S(2)}) collective-permute-start(bf16[2,3,192,128]{3,2,1,0:T(8,128)(2,1)} %get-tuple-element.466), channel_id=1, source_target_pairs={{0,16},{4,20},{8,24},{12,28},{16,0},{20,4},{24,8},{28,12},{1,17},{... | collective-permute-start | bytes 884744 | tf_op jit(solution)/shard_map/ppermute | solution.py:30
  747.3 27.1 %collective-permute-start.73 = (bf16[2,3,192,128]{3,2,1,0:T(8,128)(2,1)}, bf16[2,3,192,128]{3,2,1,0:T(8,128)(2,1)}, u32[]{:S(2)}, u32[]{:S(2)}) collective-permute-start(bf16[2,3,192,128]{3,2,1,0:T(8,128)(2,1)} %get-tuple-element.467), channel_id=1, source_target_pairs={{0,24},{4,28},{8,16},{12,20},{16,8},{20,12},{24,0},{28,4},{1,25},{... | collective-permute-start | bytes 884744 | tf_op jit(solution)/shard_map/ppermute | solution.py:30
  781.4 40.9 %collective-permute-start.75 = (bf16[1,256,2304]{2,1,0:T(8,128)(2,1)}, bf16[1,256,2304]{2,1,0:T(8,128)(2,1)S(1)}, u32[]{:S(2)}, u32[]{:S(2)}) collective-permute-start(bf16[1,256,2304]{2,1,0:T(8,128)(2,1)} %get-tuple-element.479.right), channel_id=1, source_target_pairs={{0,1},{1,0},{2,3},{3,2},{4,5},{5,4},{6,7},{7,6},{8,9},{9,8},{10,11... | collective-permute-start | bytes 3538952 | tf_op jit(solution)/shard_map/ppermute | solution.py:30
  787.9 34.4 %collective-permute-start.39 = (bf16[2,256,192]{2,1,0:T(8,128)(2,1)}, bf16[2,256,192]{2,1,0:T(8,128)(2,1)S(1)}, u32[]{:S(2)}, u32[]{:S(2)}) collective-permute-start(bf16[2,256,192]{2,1,0:T(8,128)(2,1)} %get-tuple-element.354), channel_id=1, source_target_pairs={{0,1},{1,0},{2,3},{3,2},{4,5},{5,4},{6,7},{7,6},{8,9},{9,8},{10,11... | collective-permute-start | bytes 589832 | tf_op jit(solution)/shard_map/ppermute | solution.py:30
  819.8 75.3 %collective-permute-start.92 = (bf16[128,384]{1,0:T(8,128)(2,1)}, bf16[128,384]{1,0:T(8,128)(2,1)}, u32[]{:S(2)}, u32[]{:S(2)}) collective-permute-start(bf16[128,384]{1,0:T(8,128)(2,1)} %add_convert_fusion.3.refs_0_), channel_id=1, source_target_pairs={{0,8},{4,12},{8,0},{12,4},{16,24},{20,28},{24,16},{28,20},{1,9},{5... | collective-permute-start | bytes 294920 | tf_op jit(solution)/shard_map/ppermute | solution.py:30
  821.8 75.2 %collective-permute-start.93 = (bf16[128,384]{1,0:T(8,128)(2,1)}, bf16[128,384]{1,0:T(8,128)(2,1)}, u32[]{:S(2)}, u32[]{:S(2)}) collective-permute-start(bf16[128,384]{1,0:T(8,128)(2,1)} %add_convert_fusion.3.refs_0_), channel_id=1, source_target_pairs={{0,16},{4,20},{8,24},{12,28},{16,0},{20,4},{24,8},{28,12},{1,17},{... | collective-permute-start | bytes 294920 | tf_op jit(solution)/shard_map/ppermute | solution.py:30
  828.9 20.2 %collective-permute-start.76 = (bf16[192,2304]{1,0:T(8,128)(2,1)}, bf16[192,2304]{1,0:T(8,128)(2,1)}, u32[]{:S(2)}, u32[]{:S(2)}) collective-permute-start(bf16[192,2304]{1,0:T(8,128)(2,1)} %get-tuple-element.488), channel_id=1, source_target_pairs={{0,2},{1,3},{2,0},{3,1},{4,6},{5,7},{6,4},{7,5},{8,10},{9,11},{10,... | collective-permute-start | bytes 2654216 | tf_op jit(solution)/shard_map/ppermute | solution.py:30
  876.5 22.9 %collective-permute-start.78 = (bf16[48,1152]{1,0:T(8,128)(2,1)}, bf16[48,1152]{1,0:T(8,128)(2,1)S(1)}, u32[]{:S(2)}, u32[]{:S(2)}) collective-permute-start(bf16[48,1152]{1,0:T(8,128)(2,1)} %get-tuple-element.497), channel_id=1, source_target_pairs={{0,8},{4,12},{8,0},{12,4},{16,24},{20,28},{24,16},{28,20},{1,9},{5... | collective-permute-start | bytes 331784 | tf_op jit(solution)/shard_map/ppermute | solution.py:30
  878.6 20.9 %collective-permute-start.79 = (bf16[48,1152]{1,0:T(8,128)(2,1)}, bf16[48,1152]{1,0:T(8,128)(2,1)S(1)}, u32[]{:S(2)}, u32[]{:S(2)}) collective-permute-start(bf16[48,1152]{1,0:T(8,128)(2,1)} %get-tuple-element.498), channel_id=1, source_target_pairs={{0,16},{4,20},{8,24},{12,28},{16,0},{20,4},{24,8},{28,12},{1,17},{... | collective-permute-start | bytes 331784 | tf_op jit(solution)/shard_map/ppermute | solution.py:30
  878.9 22.5 %collective-permute-start.80 = (bf16[48,1152]{1,0:T(8,128)(2,1)}, bf16[48,1152]{1,0:T(8,128)(2,1)S(1)}, u32[]{:S(2)}, u32[]{:S(2)}) collective-permute-start(bf16[48,1152]{1,0:T(8,128)(2,1)} %get-tuple-element.499), channel_id=1, source_target_pairs={{0,24},{4,28},{8,16},{12,20},{16,8},{20,12},{24,0},{28,4},{1,25},{... | collective-permute-start | bytes 331784 | tf_op jit(solution)/shard_map/ppermute | solution.py:30
  899.5 15.1 %collective-permute-start.97 = (bf16[128,384]{1,0:T(8,128)(2,1)}, bf16[128,384]{1,0:T(8,128)(2,1)S(1)}, u32[]{:S(2)}, u32[]{:S(2)}) collective-permute-start(bf16[128,384]{1,0:T(8,128)(2,1)} %collective-permute-done.93.refs_2_), channel_id=1, source_target_pairs={{0,4},{4,0},{8,12},{12,8},{16,20},{20,16},{24,28},{28,24},{1,5},{5... | collective-permute-start | bytes 294920 | tf_op jit(solution)/shard_map/ppermute | solution.py:30
  (173 other events, 2597.3 us)
Sparse Core Ops, SparseCore 0:
  44.1 28.8 all-gather.13
  75.2 71.7 all-gather.11
  149.1 40.1 all-gather.17
  191.3 78.0 all-gather.15
  669.1 64.9 all-gather.9
  822.4 139.4 all-reduce.5
